TPU v7x, 32 devices: a whole 2x2x4 slice. The times are simulated.
32 devices in a mesh: dp: 2 (over y), seq: 16 (over z, x, core).
Axes of the slice: x: 2, y: 2, z: 4, core: 2. Of those that a mesh axis runs over, the one named last changes fastest.
Arguments:
- tokens: bfloat16 [4096, 2048], P(('dp', 'seq')), may hold values from -6 to 6
- cotangent: bfloat16 [4096, 2048], P(('dp', 'seq')), may hold values from -6 to 6
- doc_lengths: int32 [2, 4], P('dp'), may hold values from 1 to 2045, as said below
- attn_gain: bfloat16 [2048], P(('dp', 'seq')), may hold values from 0.099609375 to 1.8984375
- mlp_gain: bfloat16 [2048], P(('dp', 'seq')), may hold values from 0.099609375 to 1.8984375
- query_weight: bfloat16 [2048, 2048], P(('dp', 'seq')), may hold values from -0.125 to 0.125
- key_weight: bfloat16 [2048, 512], P(('dp', 'seq')), may hold values from -0.125 to 0.125
- value_weight: bfloat16 [2048, 512], P(('dp', 'seq')), may hold values from -0.125 to 0.125
- output_weight: bfloat16 [2048, 2048], P(('dp', 'seq')), may hold values from -0.75 to 0.75
- gate_weight: bfloat16 [2048, 8192], P(('dp', 'seq')), may hold values from -0.125 to 0.125
- up_weight: bfloat16 [2048, 8192], P(('dp', 'seq')), may hold values from -0.125 to 0.125
- down_weight: bfloat16 [8192, 2048], P(('dp', 'seq')), may hold values from -0.0625 to 0.0625
Outputs:
- mixed: float32 [4096, 2048], P(('dp', 'seq'))
- token_grad: float32 [4096, 2048], P(('dp', 'seq'))
- attn_gain_grad: float32 [2048], P(('dp', 'seq'))
- mlp_gain_grad: float32 [2048], P(('dp', 'seq'))
- query_grad: float32 [2048, 2048], P(('dp', 'seq'))
- key_grad: float32 [2048, 512], P(('dp', 'seq'))
- value_grad: float32 [2048, 512], P(('dp', 'seq'))
- output_grad: float32 [2048, 2048], P(('dp', 'seq'))
- gate_grad: float32 [2048, 8192], P(('dp', 'seq'))
- up_grad: float32 [2048, 8192], P(('dp', 'seq'))
- down_grad: float32 [8192, 2048], P(('dp', 'seq'))
Inputs may be any that keep to these rules, and one draw needn't show every extreme that they name: `doc_lengths`: row b lists the lengths of the 4 documents packed in order from the start of bucket b; the places after them, at most 16, are padding.
All inputs are finite; a program needn't handle non-finite values.
Results may differ from a plain program's by a relative error of at most 0.017.
Values may be sent and summed in bfloat16 or wider, within the bound.
A program may use at most 512 MiB of HBM per device.

v0:
```python
import math

import jax
import jax.numpy as jnp
from jax import lax
from jax.sharding import PartitionSpec as P

HEADS = 32
KV_HEADS = 8
HEAD_DIM = 64
DOCS = 4


EPS = 1e-05


def rotary_table(head_dim):
    exponent = jnp.arange(0, head_dim, 2, dtype=jnp.float32) / head_dim
    inverse = jnp.power(jnp.float32(500000.0), -exponent)
    wavelength = 2.0 * math.pi / inverse
    smooth = (8192.0 / wavelength - 1.0) / 3.0
    blended = (1.0 - smooth) * inverse / 32.0 + smooth * inverse
    scaled = jnp.where(
        wavelength < 2048.0, inverse, jnp.where(wavelength > 8192.0, inverse / 32.0, blended)
    )
    return scaled


def segment_of(doc_ends, places):
    return jnp.sum((doc_ends[None, :] <= places[:, None]).astype(jnp.int32), axis=1)


def opening_of(doc_ends, places):
    return jnp.max(jnp.where(doc_ends[None, :] <= places[:, None], doc_ends[None, :], 0), axis=1)


def rotate(values, cosine_table, sine_table):
    middle = values.shape[-1] // 2
    leading, trailing = (values[..., :middle], values[..., middle:])
    return jnp.concatenate(
        [
            leading * cosine_table - trailing * sine_table,
            trailing * cosine_table + leading * sine_table,
        ],
        axis=-1,
    )


def unrotate(gradients, cosine_table, sine_table):
    middle = gradients.shape[-1] // 2
    leading, trailing = (gradients[..., :middle], gradients[..., middle:])
    return jnp.concatenate(
        [
            leading * cosine_table + trailing * sine_table,
            trailing * cosine_table - leading * sine_table,
        ],
        axis=-1,
    )


def normalize(inputs):
    factor = lax.rsqrt(jnp.mean(inputs * inputs, axis=-1, keepdims=True) + EPS)
    return (inputs * factor, factor)


def norm_back(inputs, factor, gain_row, upstream):
    scaled_up = gain_row * upstream
    inner_mean = jnp.mean(scaled_up * inputs, axis=-1, keepdims=True)
    grad_in = factor * scaled_up - inputs * factor * factor * factor * inner_mean
    grad_gain = jnp.sum(upstream * inputs * factor, axis=0)
    return (grad_in, grad_gain)


def gather_attention(attn_gain, mlp_gain, query_weight, key_weight, value_weight, output_weight):
    return (
        lax.all_gather(attn_gain, ("dp", "seq"), axis=0, tiled=True),
        lax.all_gather(mlp_gain, ("dp", "seq"), axis=0, tiled=True),
        lax.all_gather(query_weight, ("dp", "seq"), axis=0, tiled=True),
        lax.all_gather(key_weight, ("dp", "seq"), axis=0, tiled=True),
        lax.all_gather(value_weight, ("dp", "seq"), axis=0, tiled=True),
        lax.all_gather(output_weight, ("dp", "seq"), axis=0, tiled=True),
    )


def gather_feed(gate_weight, up_weight, down_weight):
    return (
        lax.all_gather(gate_weight, ("dp", "seq"), axis=0, tiled=True),
        lax.all_gather(up_weight, ("dp", "seq"), axis=0, tiled=True),
        lax.all_gather(down_weight, ("dp", "seq"), axis=0, tiled=True),
    )


def fold_keys(key_rows, value_rows, combine, initial):
    return combine(
        initial,
        (
            lax.all_gather(key_rows, "seq", axis=0, tiled=True),
            lax.all_gather(value_rows, "seq", axis=0, tiled=True),
        ),
        jnp.int32(0),
    )


def contract_rows(chosen, upstream):
    return lax.dot_general(
        chosen, upstream, (((0,), (0,)), ((), ())), preferred_element_type=jnp.float32
    )


def seq_share(activation, upstream):
    dp_count = lax.axis_size("dp")
    seq_count = lax.axis_size("seq")
    tok_count = activation.shape[0]
    per_device = activation.shape[1] // (dp_count * seq_count)
    blocked = activation.reshape(tok_count, dp_count, seq_count, per_device)
    stride = dp_count * per_device
    chosen = blocked
    chosen = jnp.transpose(chosen, (0, 2, 1, 3)).reshape(tok_count, stride * lax.axis_size("seq"))
    return lax.psum_scatter(contract_rows(chosen, upstream), "seq", scatter_dimension=0, tiled=True)


def seq_order(vector):
    return jnp.transpose(
        vector.reshape(lax.axis_size("dp"), lax.axis_size("seq"), -1), (1, 0, 2)
    ).reshape(-1)


def pick_data(summed, per_device):
    return lax.dynamic_slice_in_dim(summed, lax.axis_index("dp") * per_device, per_device, 0)


def shards(
    tokens,
    cotangent,
    doc_lengths,
    attn_gain,
    mlp_gain,
    query_weight,
    key_weight,
    value_weight,
    output_weight,
    gate_weight,
    up_weight,
    down_weight,
):
    tok_count = tokens.shape[0]
    width = tokens.shape[1]
    kv_width = key_weight.shape[1]
    group_size = HEADS // KV_HEADS
    score_scale = 1.0 / math.sqrt(HEAD_DIM)
    bucket_rows = tok_count * lax.axis_size("seq")
    doc_ends = jnp.cumsum(doc_lengths[0])
    query_place = lax.axis_index("seq") * tok_count + jnp.arange(tok_count, dtype=jnp.int32)
    last_place = lax.axis_index("seq") * tok_count + tok_count - 1
    query_seg = segment_of(doc_ends, query_place)
    position = query_place - opening_of(doc_ends, query_place)
    angles = position.astype(jnp.float32)[:, None] * rotary_table(HEAD_DIM)[None, :]
    cosine_table = jnp.cos(angles)[:, None, :]
    sine_table = jnp.sin(angles)[:, None, :]
    inputs = tokens.astype(jnp.float32)
    attention_full = gather_attention(
        attn_gain, mlp_gain, query_weight, key_weight, value_weight, output_weight
    )
    gain_one = attention_full[0].astype(jnp.float32)
    gain_two = attention_full[1].astype(jnp.float32)
    normed_raw, factor_one = normalize(inputs)
    normed_one = (normed_raw * gain_one).astype(jnp.bfloat16)
    query_lin = jnp.dot(normed_one, attention_full[2], preferred_element_type=jnp.float32)
    key_lin = jnp.dot(normed_one, attention_full[3], preferred_element_type=jnp.float32)
    value_rows = jnp.dot(normed_one, attention_full[4], preferred_element_type=jnp.float32).astype(
        jnp.bfloat16
    )
    grouped = rotate(
        query_lin.reshape(tok_count, HEADS, HEAD_DIM), cosine_table, sine_table
    ).astype(jnp.bfloat16)
    grouped = grouped.reshape(tok_count, KV_HEADS, group_size, HEAD_DIM)
    key_rows = rotate(
        key_lin.reshape(tok_count, KV_HEADS, HEAD_DIM), cosine_table, sine_table
    ).astype(jnp.bfloat16)
    key_rows = key_rows.reshape(tok_count, kv_width)

    def score_piece(key_piece):
        piece_rows = key_piece.shape[0]
        key_place = jnp.arange(piece_rows, dtype=jnp.int32)
        same_doc = query_seg[:, None] == segment_of(doc_ends, key_place)[None, :]
        allowed = (same_doc & (key_place[None, :] <= query_place[:, None]))[:, None, None, :]
        scores = (
            jnp.einsum(
                "tkgd,ukd->tkgu",
                grouped,
                key_piece.reshape(piece_rows, KV_HEADS, HEAD_DIM),
                preferred_element_type=jnp.float32,
            )
            * score_scale
        )
        return (jnp.where(allowed, scores, -1e30), allowed)

    def when_needed(step_fn):

        def guarded(running, pieces, first_row):
            return lax.cond(
                first_row <= last_place,
                lambda: step_fn(running, pieces, first_row),
                lambda: running,
            )

        return guarded

    def gather_stats(running, pieces, first_row):
        row_peak, row_total = running
        masked, allowed = score_piece(pieces[0])
        new_peak = jnp.maximum(row_peak, jnp.max(masked, axis=-1))
        spread = jnp.where(allowed, jnp.exp(masked - new_peak[..., None]), 0.0)
        return (new_peak, jnp.sum(spread, axis=-1))

    stat_shape = (tok_count, KV_HEADS, group_size)
    row_peak, row_total = fold_keys(
        key_rows,
        value_rows,
        when_needed(gather_stats),
        (jnp.full(stat_shape, -1e30, jnp.float32), jnp.zeros(stat_shape, jnp.float32)),
    )
    log_total = row_peak + jnp.log(row_total)

    def gather_output(running, pieces, first_row):
        masked, allowed = score_piece(pieces[0])
        weights = jnp.where(allowed, jnp.exp(masked - log_total[..., None]), 0.0).astype(
            jnp.bfloat16
        )
        value_piece = pieces[1].reshape(pieces[1].shape[0], KV_HEADS, HEAD_DIM)
        return jnp.einsum(
            "tkgu,ukd->tkgd", weights, value_piece, preferred_element_type=jnp.float32
        )

    attended_sum = fold_keys(
        key_rows,
        value_rows,
        when_needed(gather_output),
        jnp.zeros((tok_count, KV_HEADS, group_size, HEAD_DIM), jnp.float32),
    )
    attended = attended_sum.reshape(tok_count, width).astype(jnp.bfloat16)
    middle = inputs + jnp.dot(attended, attention_full[5], preferred_element_type=jnp.float32)
    normed_raw_two, factor_two = normalize(middle)
    normed_two = (normed_raw_two * gain_two).astype(jnp.bfloat16)
    feed_full = gather_feed(gate_weight, up_weight, down_weight)
    gate_lin = jnp.dot(normed_two, feed_full[0], preferred_element_type=jnp.float32)
    upward = jnp.dot(normed_two, feed_full[1], preferred_element_type=jnp.float32)
    hidden = (jax.nn.silu(gate_lin) * upward).astype(jnp.bfloat16)
    mixed = middle + jnp.dot(hidden, feed_full[2], preferred_element_type=jnp.float32)
    keeping = (query_seg < DOCS).astype(jnp.float32)[:, None]
    grad_out = (cotangent.astype(jnp.float32) * keeping).astype(jnp.bfloat16)
    hidden_grad = jnp.dot(grad_out, feed_full[2].T, preferred_element_type=jnp.float32)
    sigmoid = jax.nn.sigmoid(gate_lin)
    gate_back = (hidden_grad * upward * sigmoid * (1.0 + gate_lin * (1.0 - sigmoid))).astype(
        jnp.bfloat16
    )
    up_back = (hidden_grad * gate_lin * sigmoid).astype(jnp.bfloat16)
    normed_two_grad = jnp.dot(
        gate_back, feed_full[0].T, preferred_element_type=jnp.float32
    ) + jnp.dot(up_back, feed_full[1].T, preferred_element_type=jnp.float32)
    middle_in, gain_two_full = norm_back(middle, factor_two, gain_two, normed_two_grad)
    middle_grad = grad_out.astype(jnp.float32) + middle_in
    middle_back = middle_grad.astype(jnp.bfloat16)
    attended_grad = jnp.dot(
        middle_back, attention_full[5].T, preferred_element_type=jnp.float32
    ).astype(jnp.bfloat16)
    attended_grad = attended_grad.reshape(tok_count, KV_HEADS, group_size, HEAD_DIM)
    row_sum = jnp.sum(attended_grad.astype(jnp.float32) * attended_sum, axis=-1)

    def gather_grads(running, pieces, first_row):
        piece_rows = pieces[0].shape[0]
        masked, allowed = score_piece(pieces[0])
        chance = jnp.where(allowed, jnp.exp(masked - log_total[..., None]), 0.0)
        key_piece = pieces[0].reshape(piece_rows, KV_HEADS, HEAD_DIM)
        value_piece = pieces[1].reshape(piece_rows, KV_HEADS, HEAD_DIM)
        prob_grad = jnp.einsum(
            "tkgd,ukd->tkgu", attended_grad, value_piece, preferred_element_type=jnp.float32
        )
        score_grad = (chance * (prob_grad - row_sum[..., None])).astype(jnp.bfloat16)
        query_acc = jnp.einsum(
            "tkgu,ukd->tkgd", score_grad, key_piece, preferred_element_type=jnp.float32
        )
        key_part = (
            jnp.einsum("tkgu,tkgd->ukd", score_grad, grouped, preferred_element_type=jnp.float32)
            * score_scale
        )
        value_part = jnp.einsum(
            "tkgu,tkgd->ukd",
            chance.astype(jnp.bfloat16),
            attended_grad,
            preferred_element_type=jnp.float32,
        )
        update = jnp.concatenate(
            [key_part.reshape(piece_rows, kv_width), value_part.reshape(piece_rows, kv_width)],
            axis=1,
        )
        return (query_acc, update)

    query_acc, kv_acc = fold_keys(
        key_rows,
        value_rows,
        when_needed(gather_grads),
        (
            jnp.zeros((tok_count, KV_HEADS, group_size, HEAD_DIM), jnp.float32),
            jnp.zeros((bucket_rows, 2 * kv_width), jnp.float32),
        ),
    )
    own_kv = lax.psum_scatter(kv_acc, "seq", scatter_dimension=0, tiled=True)
    query_back = unrotate(
        (query_acc * score_scale).reshape(tok_count, HEADS, HEAD_DIM), cosine_table, sine_table
    )
    query_back = query_back.reshape(tok_count, width).astype(jnp.bfloat16)
    key_back = unrotate(
        own_kv[:, :kv_width].reshape(tok_count, KV_HEADS, HEAD_DIM), cosine_table, sine_table
    )
    key_back = key_back.reshape(tok_count, kv_width).astype(jnp.bfloat16)
    value_back = own_kv[:, kv_width:].astype(jnp.bfloat16)
    normed_one_grad = jnp.dot(query_back, attention_full[2].T, preferred_element_type=jnp.float32)
    normed_one_grad = normed_one_grad + jnp.dot(
        key_back, attention_full[3].T, preferred_element_type=jnp.float32
    )
    normed_one_grad = normed_one_grad + jnp.dot(
        value_back, attention_full[4].T, preferred_element_type=jnp.float32
    )
    input_in, gain_one_full = norm_back(inputs, factor_one, gain_one, normed_one_grad)
    token_grad = middle_grad + input_in
    qkv_up = jnp.concatenate([query_back, key_back, value_back], axis=1)
    gate_up = jnp.concatenate([gate_back, up_back], axis=1)
    per_width = width // (lax.axis_size("dp") * lax.axis_size("seq"))
    per_hidden = down_weight.shape[0]
    qkv_part = seq_share(normed_one, qkv_up)
    output_part = seq_share(attended, middle_back)
    feed_part = seq_share(normed_two, gate_up)
    down_part = seq_share(hidden, grad_out)
    gain_parts = (
        lax.psum_scatter(seq_order(gain_one_full), "seq", scatter_dimension=0, tiled=True),
        lax.psum_scatter(seq_order(gain_two_full), "seq", scatter_dimension=0, tiled=True),
    )
    summed = (
        lax.psum(qkv_part.astype(jnp.bfloat16), "dp").astype(jnp.float32),
        lax.psum(output_part.astype(jnp.bfloat16), "dp").astype(jnp.float32),
        lax.psum(feed_part.astype(jnp.bfloat16), "dp").astype(jnp.float32),
        lax.psum(down_part.astype(jnp.bfloat16), "dp").astype(jnp.float32),
        lax.psum(gain_parts[0].astype(jnp.bfloat16), "dp").astype(jnp.float32),
        lax.psum(gain_parts[1].astype(jnp.bfloat16), "dp").astype(jnp.float32),
    )
    qkv_share = pick_data(summed[0], per_width)
    output_share = pick_data(summed[1], per_width)
    feed_share = pick_data(summed[2], per_width)
    down_share = pick_data(summed[3], per_hidden)
    gain_one_share = pick_data(summed[4], per_width)
    gain_two_share = pick_data(summed[5], per_width)
    feed_width = gate_weight.shape[1]
    return (
        mixed,
        token_grad,
        gain_one_share,
        gain_two_share,
        qkv_share[:, :width],
        qkv_share[:, width : width + kv_width],
        qkv_share[:, width + kv_width :],
        output_share,
        feed_share[:, :feed_width],
        feed_share[:, feed_width:],
        down_share,
    )


def solution(mesh):
    return jax.shard_map(
        shards,
        mesh=mesh,
        in_specs=(
            P(("dp", "seq"), None),
            P(("dp", "seq"), None),
            P("dp", None),
            P(("dp", "seq")),
            P(("dp", "seq")),
            P(("dp", "seq"), None),
            P(("dp", "seq"), None),
            P(("dp", "seq"), None),
            P(("dp", "seq"), None),
            P(("dp", "seq"), None),
            P(("dp", "seq"), None),
            P(("dp", "seq"), None),
        ),
        out_specs=(
            P(("dp", "seq"), None),
            P(("dp", "seq"), None),
            P(("dp", "seq")),
            P(("dp", "seq")),
            P(("dp", "seq"), None),
            P(("dp", "seq"), None),
            P(("dp", "seq"), None),
            P(("dp", "seq"), None),
            P(("dp", "seq"), None),
            P(("dp", "seq"), None),
            P(("dp", "seq"), None),
        ),
        check_vma=False,
    )
```

profile of v0, /device:TPU:0, one launch (start us, length us, event | category | flops | bytes accessed | tf_op | source)
XLA Modules:
  0.0 3715.8 jit_solution(10710532629755974175)
XLA Ops:
  11.2 42.2 %all-reduce.5 = (bf16[2048]{0:T(1024)(128)(2,1)S(1)}, bf16[2048]{0:T(1024)(128)(2,1)S(1)}) all-reduce(bf16[2048]{0:T(1024)(128)(2,1)S(1)} %dynamic-update-slice, bf16[2048]{0:T(1024)(128)(2,1)S(1)} %dynamic-update-slice.1), channel_id=1, replica_groups=mesh['dp'=2,'seq'=16] {'dp','seq'}, use_global_device_ids=true, to_apply=%add | all-reduce | flops 4096 | bytes 16384
  57.1 13.0 all-gather.10.cloned.1.call-done
  73.4 54.9 %all-gather.16.cloned.1.call-done = bf16[2048,512]{1,0:T(8,128)(2,1)} async-done(((bf16[64,512]{1,0:T(8,128)(2,1)}), bf16[2048,512]{1,0:T(8,128)(2,1)}) %all-gather.16.cloned.1.call-update) | async-done | bytes 2097168 | tf_op jit(solution)/shard_map/all_gather | solution.py:80
  134.0 73.6 %all-gather.14.cloned.1.call-done = bf16[2048,2048]{1,0:T(8,128)(2,1)} async-done(((bf16[64,2048]{1,0:T(8,128)(2,1)}), bf16[2048,2048]{1,0:T(8,128)(2,1)}) %all-gather.14.cloned.1.call-update) | async-done | bytes 8388624 | tf_op jit(solution)/shard_map/all_gather | solution.py:78
  207.6 6.8 fusion.60
  214.7 35.3 all-gather.12.cloned.1.call-done
  250.0 31.2 conditional.3
  250.4 15.3 fusion
  266.3 14.9 select_reduce_fusion
  282.5 10.4 all-gather.18.cloned.1.call-done
  292.9 16.9 conditional.4
  292.9 4.2 copy.96
  297.5 12.3 fusion.7
  309.9 62.0 %all-gather.20.cloned.1.call-done = bf16[2048,2048]{1,0:T(8,128)(2,1)} async-done(((bf16[64,2048]{1,0:T(8,128)(2,1)}), bf16[2048,2048]{1,0:T(8,128)(2,1)}) %all-gather.20.cloned.1.call-update) | async-done | bytes 8388624 | tf_op jit(solution)/shard_map/all_gather | solution.py:81
  371.9 4.7 multiply_reduce_fusion.3
  376.9 191.3 %all-gather.22.cloned.1.call-done = bf16[2048,8192]{1,0:T(8,128)(2,1)} async-done(((bf16[64,8192]{1,0:T(8,128)(2,1)}), bf16[2048,8192]{1,0:T(8,128)(2,1)}) %all-gather.22.cloned.1.call-update) | async-done | bytes 33554448 | tf_op jit(solution)/shard_map/all_gather | solution.py:87
  568.2 18.2 fusion.61
  586.4 177.7 %all-gather.24.cloned.1.call-done = bf16[2048,8192]{1,0:T(8,128)(2,1)} async-done(((bf16[64,8192]{1,0:T(8,128)(2,1)}), bf16[2048,8192]{1,0:T(8,128)(2,1)}) %all-gather.24.cloned.1.call-update) | async-done | bytes 33554448 | tf_op jit(solution)/shard_map/all_gather | solution.py:88
  764.1 17.8 fusion.62
  781.9 178.1 %all-gather.26.cloned.1.call-done = bf16[8192,2048]{1,0:T(8,128)(2,1)} async-done(((bf16[256,2048]{1,0:T(8,128)(2,1)}), bf16[8192,2048]{1,0:T(8,128)(2,1)}) %all-gather.26.cloned.1.call-update) | async-done | bytes 33554448 | tf_op jit(solution)/shard_map/all_gather | solution.py:89
  959.9 20.9 multiply_convert_fusion
  980.8 16.4 fusion.63
  997.3 17.3 multiply_reduce_fusion.1
  1016.4 6.7 convolution_convert_fusion
  1023.1 75.8 %conditional.5 = (f32[128,8,4,64]{0,3,2,1:T(8,128)}, f32[2048,1024]{0,1:T(8,128)}) conditional(s32[]{:T(128)} %convert_element_type.153, () %tuple.39, (s32[128]{0:T(128)S(1)}, s32[4]{0:T(128)S(1)}, s32[128]{0:T(128)S(1)}, bf16[2048,512]{0,1:T(8,128)(2,1)S(1)}, bf16[128,8,4,64]{0,3,2,1:T(8,128)(2,1)S(1)}, /*index=5*/f32[128,8,4]{0,2,1:T(4,128)}, ...), branch_computations={%region_14.15_spmd, %region_15.18_spmd} | conditional | flops 5474109440 | bytes 277169344 | solution.py:201
  1023.1 13.1 fusion.58
  1036.2 4.0 copy.97
  1044.5 16.0 fusion.13
  1060.5 5.7 copy-done
  1066.2 3.9 convolution_bitcast_fusion
  1070.1 16.0 fusion.18
  1086.1 8.8 bitcast_multiply_fusion
  1095.0 3.9 pad_maximum_fusion
  1100.2 9.5 fusion.46
  1112.9 89.2 %reduce-scatter.6.cloned.1.call-done = f32[128,1024]{0,1:T(8,128)} async-done(((f32[2048,1024]{0,1:T(8,128)}), f32[128,1024]{0,1:T(8,128)}) %reduce-scatter.6.cloned.1.call-update) | async-done | bytes 524304 | tf_op jit(solution)/shard_map/reduce_scatter | solution.py:308
  1204.1 12.9 fusion.40
  1224.7 26.7 fusion.53
  1254.5 48.3 %fusion.25 = f32[2048,16384]{1,0:T(8,128)} fusion(bf16[128,2048]{0,1:T(8,128)(2,1)S(1)} %bitcast.176, bf16[128,8192]{1,0:T(8,128)(2,1)} %get-tuple-element.210, bf16[128,8192]{1,0:T(8,128)(2,1)S(1)} %copy-done.11), kind=kOutput, calls=%fused_computation.43 | convolution fusion | flops 8598323200 | bytes 138936320 | tf_op jit(solution)/shard_map/dot_general | solution.py:105
  1303.0 81.5 %reduce-scatter.10.cloned.1.call-done = f32[128,2048]{1,0:T(8,128)} async-done(((f32[2048,2048]{1,0:T(8,128)}), f32[128,2048]{1,0:T(8,128)}) %reduce-scatter.10.cloned.1.call-update) | async-done | bytes 1048592 | tf_op jit(solution)/shard_map/reduce_scatter | solution.py:119
  1386.6 244.8 %reduce-scatter.8.cloned.1.call-done = f32[128,3072]{1,0:T(8,128)} async-done(((f32[2048,3072]{1,0:T(8,128)}), f32[128,3072]{1,0:T(8,128)}) %reduce-scatter.8.cloned.1.call-update) | async-done | bytes 1572880 | tf_op jit(solution)/shard_map/reduce_scatter | solution.py:119
  1633.8 638.1 %reduce-scatter.14.cloned.1.call-done = f32[512,2048]{1,0:T(8,128)} async-done(((f32[8192,2048]{1,0:T(8,128)}), f32[512,2048]{1,0:T(8,128)}) %reduce-scatter.14.cloned.1.call-update) | async-done | bytes 4194320 | tf_op jit(solution)/shard_map/reduce_scatter | solution.py:119
  2275.7 1235.5 %reduce-scatter.12.cloned.1.call-done = f32[128,16384]{1,0:T(8,128)} async-done(((f32[2048,16384]{1,0:T(8,128)}), f32[128,16384]{1,0:T(8,128)}) %reduce-scatter.12.cloned.1.call-update) | async-done | bytes 8388624 | tf_op jit(solution)/shard_map/reduce_scatter | solution.py:119
  3511.2 5.8 convert_element_type.184
  3518.5 6.6 fusion.64
  3525.2 17.2 convolution_add_fusion.3
  3544.5 59.0 %all-reduce.4 = (bf16[2048]{0:T(1024)(128)(2,1)S(1)}, bf16[2048]{0:T(1024)(128)(2,1)S(1)}) all-reduce(f32[2048]{0:T(1024)S(1)} %reshape.386, f32[2048]{0:T(1024)S(1)} %reshape.388), channel_id=3, replica_groups=mesh['dp'=2,'seq'=16] {'seq'}, use_global_device_ids=true, to_apply=%region_21.22.clone | all-reduce | flops 4096 | bytes 24576
  3603.6 4.9 all-reduce.6
  3611.1 87.8 %all-reduce.10.cloned.1.call-done = (bf16[128,3072]{1,0:T(8,128)(2,1)}, bf16[128,2048]{1,0:T(8,128)(2,1)}, bf16[128,16384]{1,0:T(8,128)(2,1)}, bf16[512,2048]{1,0:T(8,128)(2,1)}) async-done(((bf16[128,3072]{1,0:T(8,128)(2,1)}, bf16[128,2048]{1,0:T(8,128)(2,1)}, bf16[128,16384]{1,0:T(8,128)(2,1)}, bf16[512,2048]{1,0:T(8,128)(2,1)}), (bf16[128,3072]{1,0:T(8,128)(2,1)}, bf16[128,2048]{1,0:T(8,128)(2,1)}, ...) | async-done | bytes 7602192 | tf_op jit(solution)/shard_map/psum | solution.py:340
  (190 shorter events, 67.1 us)
Async XLA Ops:
  7.2 63.0 %all-gather.10.cloned.1.call-start = ((), (), s32[]{:S(2)}) async-start(), calls=%async_computation.5 | async-start | bytes 2162688 | tf_op jit(solution)/shard_map/all_gather | solution.py:79
  7.9 120.5 %all-gather.16.cloned.1.call-start = ((), (), s32[]{:S(2)}) async-start(), calls=%async_computation.8 | async-start | bytes 2162688 | tf_op jit(solution)/shard_map/all_gather | solution.py:80
  8.7 198.9 %all-gather.14.cloned.1.call-start = ((), (), s32[]{:S(2)}) async-start(), calls=%async_computation.7 | async-start | bytes 8650752 | tf_op jit(solution)/shard_map/all_gather | solution.py:78
  9.4 240.6 %all-gather.12.cloned.1.call-start = ((), (), s32[]{:S(2)}) async-start(), calls=%async_computation.6 | async-start | bytes 2228224 | tf_op jit(solution)/shard_map/all_gather | solution.py:97
  53.3 161.1 %copy-start.32 = (f32[2048]{0:T(1024)}, f32[2048]{0:T(1024)S(1)}, u32[]{:S(2)}) copy-start(f32[2048]{0:T(1024)S(1)} %convert_element_type.155) | copy-start | bytes 24580
  55.7 158.7 %copy-start.36 = (f32[128]{0:T(128)}, f32[128]{0:T(128)S(1)}, u32[]{:S(2)}) copy-start(f32[128]{0:T(128)S(1)} %add_rsqrt_fusion.1) | copy-start | bytes 1540
  55.8 158.6 %copy-start.28 = (f32[128,32]{0,1:T(8,128)}, f32[128,32]{0,1:T(8,128)S(1)}, u32[]{:S(2)}) copy-start(f32[128,32]{0,1:T(8,128)S(1)} %get-tuple-element.225) | copy-start | bytes 49156
  55.9 158.6 %copy-start.30 = (f32[128,32]{0,1:T(8,128)}, f32[128,32]{0,1:T(8,128)S(1)}, u32[]{:S(2)}) copy-start(f32[128,32]{0,1:T(8,128)S(1)} %get-tuple-element.226) | copy-start | bytes 49156
  57.1 157.3 %copy-start.9 = (bf16[128,2048]{1,0:T(8,128)(2,1)}, bf16[128,2048]{1,0:T(8,128)(2,1)S(1)}, u32[]{:S(2)}) copy-start(bf16[128,2048]{1,0:T(8,128)(2,1)S(1)} %fusion.31) | copy-start | bytes 1572868
  73.4 219.5 %all-gather.18.cloned.1.call-start = ((), (), s32[]{:S(2)}) async-start(), calls=%async_computation.9 | async-start | bytes 2228224 | tf_op jit(solution)/shard_map/all_gather | solution.py:98
  131.1 240.8 %all-gather.20.cloned.1.call-start = ((), (), s32[]{:S(2)}) async-start(), calls=%async_computation.10 | async-start | bytes 8650752 | tf_op jit(solution)/shard_map/all_gather | solution.py:81
  131.7 436.5 %all-gather.22.cloned.1.call-start = ((), (), s32[]{:S(2)}) async-start(), calls=%async_computation.11 | async-start | bytes 34603008 | tf_op jit(solution)/shard_map/all_gather | solution.py:87
  132.4 631.6 %all-gather.24.cloned.1.call-start = ((), (), s32[]{:S(2)}) async-start(), calls=%async_computation.12 | async-start | bytes 34603008 | tf_op jit(solution)/shard_map/all_gather | solution.py:88
  133.2 826.7 %all-gather.26.cloned.1.call-start = ((), (), s32[]{:S(2)}) async-start(), calls=%async_computation.13 | async-start | bytes 34603008 | tf_op jit(solution)/shard_map/all_gather | solution.py:89
  133.9 1068.2 %reduce-scatter.6.cloned.1.call-start = ((), (), s32[]{:S(2)}) async-start(), calls=%async_computation.14 | async-start | bytes 8912896 | tf_op jit(solution)/shard_map/reduce_scatter | solution.py:308
  134.0 825.9 %copy-start.38 = (f32[128]{0:T(128)}, f32[128]{0:T(128)S(1)}, u32[]{:S(2)}) copy-start(f32[128]{0:T(128)S(1)} %compare_convert_fusion.1) | copy-start | bytes 1540
  292.9 79.0 %copy-start.7 = (bf16[128,2048]{1,0:T(8,128)(2,1)S(1)}, bf16[128,2048]{1,0:T(8,128)(2,1)}, u32[]{:S(2)}) copy-start(bf16[128,2048]{1,0:T(8,128)(2,1)} %param.18) | copy-start | bytes 1572868
  309.8 62.1 %copy-start.13 = (f32[128,8,4,64]{0,3,2,1:T(8,128)}, f32[128,8,4,64]{0,3,2,1:T(8,128)S(1)}, u32[]{:S(2)}) copy-start(f32[128,8,4,64]{0,3,2,1:T(8,128)S(1)} %get-tuple-element.243) | copy-start | bytes 3145732
  309.9 66.8 %copy-start.18 = (bf16[128,8,4,64]{0,3,2,1:T(8,128)(2,1)}, bf16[128,8,4,64]{0,3,2,1:T(8,128)(2,1)S(1)}, u32[]{:S(2)}) copy-start(bf16[128,8,4,64]{0,3,2,1:T(8,128)(2,1)S(1)} %convert_element_type.160) | copy-start | bytes 1572868
  376.7 620.6 %copy-start.2 = (f32[128,2048]{1,0:T(8,128)}, f32[128,2048]{1,0:T(8,128)S(1)}, u32[]{:S(2)}) copy-start(f32[128,2048]{1,0:T(8,128)S(1)} %get-tuple-element.228) | copy-start | bytes 3145732
  376.9 387.2 %copy-start.14 = (bf16[128,2048]{1,0:T(8,128)(2,1)}, bf16[128,2048]{1,0:T(8,128)(2,1)S(1)}, u32[]{:S(2)}) copy-start(bf16[128,2048]{1,0:T(8,128)(2,1)S(1)} %multiply_convert_fusion.4) | copy-start | bytes 1572868
  586.4 373.5 %copy-start.21 = (bf16[128,2048]{1,0:T(8,128)(2,1)S(1)}, bf16[128,2048]{1,0:T(8,128)(2,1)}, u32[]{:S(2)}) copy-start(bf16[128,2048]{1,0:T(8,128)(2,1)} %param.19) | copy-start | bytes 1572868
  997.3 17.3 copy-start.22
  997.3 17.3 copy-start.39
  1014.5 8.5 copy-start.1
  1016.4 6.7 copy-start.4
  1023.1 13.2 copy-start.35
  1086.1 8.8 copy-start.20
  1098.9 285.7 %reduce-scatter.10.cloned.1.call-start = ((), (), s32[]{:S(2)}) async-start(), calls=%async_computation.16 | async-start | bytes 17825792 | tf_op jit(solution)/shard_map/reduce_scatter | solution.py:119
  1109.8 521.6 %reduce-scatter.8.cloned.1.call-start = ((), (), s32[]{:S(2)}) async-start(), calls=%async_computation.15 | async-start | bytes 26738688 | tf_op jit(solution)/shard_map/reduce_scatter | solution.py:119
  1204.1 12.9 copy-start.24
  1217.0 7.7 copy-start.23
  1217.0 7.7 copy-start.40
  1217.0 1054.9 %reduce-scatter.14.cloned.1.call-start = ((), (), s32[]{:S(2)}) async-start(), calls=%async_computation.18 | async-start | bytes 71303168 | tf_op jit(solution)/shard_map/reduce_scatter | solution.py:119
  1251.4 2259.8 %reduce-scatter.12.cloned.1.call-start = ((), (), s32[]{:S(2)}) async-start(), calls=%async_computation.17 | async-start | bytes 142606336 | tf_op jit(solution)/shard_map/reduce_scatter | solution.py:119
  1302.8 2396.1 %all-reduce.10.cloned.1.call-start = ((), (), s32[]{:S(2)}) async-start(), calls=%async_computation.19 | async-start | bytes 15204352 | tf_op jit(solution)/shard_map/psum | solution.py:340
  2275.7 1241.4 %copy-start.41 = (u32[32]{0:T(128)S(1)}, u32[32]{0:T(128)}, u32[]{:S(2)}) copy-start(u32[32]{0:T(128)} %constant.122) | copy-start | bytes 388
  2275.7 1242.6 %copy-start.34 = (f32[2048]{0:T(1024)S(1)}, f32[2048]{0:T(1024)}, u32[]{:S(2)}) copy-start(f32[2048]{0:T(1024)} %get-tuple-element.192) | copy-start | bytes 24580
  3517.1 8.1 copy-start.3
  3525.1 17.3 copy-start.16
  3525.1 17.2 copy-start.25
  3525.1 18.1 copy-start.8
  3525.2 18.1 copy-start.17
  3525.2 18.1 copy-start.26
  3525.2 18.1 copy-start.33
  3525.2 18.1 copy-start.37
  3542.4 67.4 %copy-start.6 = (f32[128,2048]{1,0:T(8,128)S(1)}, f32[128,2048]{1,0:T(8,128)}, u32[]{:S(2)}) copy-start(f32[128,2048]{1,0:T(8,128)} %copy-done.4) | copy-start | bytes 3145732
  3700.0 7.5 copy-start.27
  (9 other events, 21.2 us)
Sparse Core Ops, SparseCore 0:
  10.8 59.2 all-gather.9
  73.0 55.3 all-gather.15
  131.2 76.3 all-gather.13
  210.2 39.7 all-gather.11
  252.6 40.3 all-gather.17
  295.6 76.2 all-gather.19
  374.8 193.3 all-gather.21
  571.0 192.9 all-gather.23
  766.9 192.9 all-gather.25
  1099.0 103.0 reduce-scatter.5
  1206.2 178.3 reduce-scatter.9
  1388.5 242.8 reduce-scatter.7
  1635.7 636.1 reduce-scatter.13
  2276.0 1235.1 reduce-scatter.11
  3517.2 181.6 all-reduce.9
where the time goes:
time: 3730 us; the launch traced here: 3720 us
  waiting for transfers between devices  3180 us (85%)
  matrix products  322 us (9%)
  blocking collectives  106 us (3%)
  other arithmetic  55 us (1%)
  local copies, waits for them, and re-layouts  37.6 us (1%)
    reduce_scatter x4, waiting for transfers between devices, seq_share(): lax.psum_scatter(contract_rows(chosen, upstream), 'seq', scatter_dimensio...  2200 us
    all_gather x1, waiting for transfers between devices, gather_feed(): lax.all_gather(gate_weight, ('dp', 'seq'), axis=0, tiled=True)  191 us
    all_gather x1, waiting for transfers between devices, gather_feed(): lax.all_gather(down_weight, ('dp', 'seq'), axis=0, tiled=True)  178 us
    all_gather x1, waiting for transfers between devices, gather_feed(): lax.all_gather(up_weight, ('dp', 'seq'), axis=0, tiled=True)  178 us
    unnamed x2, blocking collectives  101 us
    dot_general x4, matrix products, contract_rows(): lax.dot_general(chosen, upstream, (((0,), (0,)), ((), ())), preferred_ele...  97.4 us
    reduce_scatter x1, waiting for transfers between devices, shards(): own_kv = lax.psum_scatter(kv_acc, 'seq', scatter_dimension=0, tiled=True)  89.2 us
    psum x1, waiting for transfers between devices, shards(): lax.psum(qkv_part.astype(jnp.bfloat16), 'dp').astype(jnp.float32)  87.8 us
  transfers between devices with their start and end apart: 15, of which 15 were waited for; matrix products, arithmetic and copies ran while one was open for 7% of the time, Pallas kernels for 0%

commit v1 on v0

v1 whole, which is shorter than its diff:
```python
import functools
import math

import jax
import jax.numpy as jnp
from jax import lax
from jax.experimental import pallas as pl
from jax.experimental.pallas import tpu as pltpu
from jax.sharding import PartitionSpec as P

HEADS = 32
KV_HEADS = 8
HEAD_DIM = 64
DOCS = 4
EPS = 1e-05
NEG = -1e30
F32 = jnp.float32
BF16 = jnp.bfloat16


def rotary_table(head_dim):
    exponent = jnp.arange(0, head_dim, 2, dtype=F32) / head_dim
    inverse = jnp.power(F32(500000.0), -exponent)
    wavelength = 2.0 * math.pi / inverse
    smooth = (8192.0 / wavelength - 1.0) / 3.0
    blended = (1.0 - smooth) * inverse / 32.0 + smooth * inverse
    return jnp.where(
        wavelength < 2048.0, inverse, jnp.where(wavelength > 8192.0, inverse / 32.0, blended)
    )


def swap_halves(values):
    rows, cols = values.shape
    halves = values.reshape(rows, cols // HEAD_DIM, 2, HEAD_DIM // 2)
    return halves[:, :, ::-1].reshape(rows, cols)


def dot(a, b):
    return jnp.dot(a, b, preferred_element_type=F32)


def dot_t(a, b):
    return lax.dot_general(a, b, (((1,), (1,)), ((), ())), preferred_element_type=F32)


def t_dot(a, b):
    return lax.dot_general(a, b, (((0,), (0,)), ((), ())), preferred_element_type=F32)


def allowed_tile(opening, q_first, k_first, shape):
    rows = q_first + lax.broadcasted_iota(jnp.int32, shape, 0)
    cols = k_first + lax.broadcasted_iota(jnp.int32, shape, 1)
    return (cols <= rows) & (cols >= opening)


def attention_kernel(block, q_ref, k_ref, v_ref, open_ref, out_ref, lse_ref):
    tile = pl.program_id(0)
    opening = open_ref[...]
    for head in range(q_ref.shape[1] // HEAD_DIM):
        lanes = slice(head * HEAD_DIM, (head + 1) * HEAD_DIM)
        query = q_ref[:, lanes]

        def step(j, carry, lanes=lanes, query=query):
            peak, total, acc = carry
            first = pl.multiple_of(j * block, block)
            scores = dot_t(query, k_ref[pl.ds(first, block), lanes])
            allowed = allowed_tile(opening, tile * block, first, scores.shape)
            scores = jnp.where(allowed, scores, NEG)
            new_peak = jnp.maximum(peak, jnp.max(scores, axis=1, keepdims=True))
            spread = jnp.where(allowed, jnp.exp(scores - new_peak), 0.0)
            fade = jnp.exp(peak - new_peak)
            total = total * fade + jnp.sum(spread, axis=1, keepdims=True)
            acc = acc * fade + dot(spread.astype(BF16), v_ref[pl.ds(first, block), lanes])
            return new_peak, total, acc

        peak, total, acc = lax.fori_loop(
            0,
            tile + 1,
            step,
            (
                jnp.full((block, 1), NEG, F32),
                jnp.zeros((block, 1), F32),
                jnp.zeros((block, HEAD_DIM), F32),
            ),
        )
        out_ref[:, lanes] = acc / total
        lse_ref[:, head : head + 1] = peak + jnp.log(total)


def attention(queries, keys, values, opening, block):
    rows, cols = queries.shape
    heads = cols // HEAD_DIM
    tiled = lambda width: pl.BlockSpec((block, width), lambda i: (i, 0))
    whole = pl.BlockSpec((rows, cols), lambda i: (0, 0))
    return pl.pallas_call(
        functools.partial(attention_kernel, block),
        grid=(rows // block,),
        in_specs=[tiled(cols), whole, whole, tiled(1)],
        out_specs=[tiled(cols), tiled(heads)],
        out_shape=[
            jax.ShapeDtypeStruct((rows, cols), F32),
            jax.ShapeDtypeStruct((rows, heads), F32),
        ],
        compiler_params=pltpu.CompilerParams(vmem_limit_bytes=48 << 20),
        cost_estimate=pl.CostEstimate(
            flops=2 * rows * rows * cols, bytes_accessed=10 * rows * cols, transcendentals=0
        ),
    )(queries, keys, values, opening)


def attention_back_kernel(
    block, q_ref, k_ref, v_ref, g_ref, att_ref, lse_ref, open_ref, dq_ref, dk_ref, dv_ref
):
    tile = pl.program_id(0)

    @pl.when(tile == 0)
    def _():
        dk_ref[...] = jnp.zeros_like(dk_ref)
        dv_ref[...] = jnp.zeros_like(dv_ref)

    opening = open_ref[...]
    for head in range(q_ref.shape[1] // HEAD_DIM):
        lanes = slice(head * HEAD_DIM, (head + 1) * HEAD_DIM)
        query = q_ref[:, lanes]
        grad = g_ref[:, lanes]
        log_total = lse_ref[:, head : head + 1]
        row_sum = jnp.sum(grad.astype(F32) * att_ref[:, lanes], axis=1, keepdims=True)

        def step(j, acc, lanes=lanes, query=query, grad=grad, log_total=log_total, row_sum=row_sum):
            first = pl.multiple_of(j * block, block)
            here = pl.ds(first, block)
            key = k_ref[here, lanes]
            scores = dot_t(query, key)
            allowed = allowed_tile(opening, tile * block, first, scores.shape)
            chance = jnp.where(allowed, jnp.exp(scores - log_total), 0.0)
            prob_grad = dot_t(grad, v_ref[here, lanes])
            score_grad = (chance * (prob_grad - row_sum)).astype(BF16)
            dk_ref[here, lanes] += t_dot(score_grad, query)
            dv_ref[here, lanes] += t_dot(chance.astype(BF16), grad)
            return acc + dot(score_grad, key)

        acc = lax.fori_loop(0, tile + 1, step, jnp.zeros((block, HEAD_DIM), F32))
        dq_ref[:, lanes] = acc


def attention_back(queries, keys, values, grads, attended, log_total, opening, block):
    rows, cols = queries.shape
    heads = cols // HEAD_DIM
    tiled = lambda width: pl.BlockSpec((block, width), lambda i: (i, 0))
    whole = pl.BlockSpec((rows, cols), lambda i: (0, 0))
    return pl.pallas_call(
        functools.partial(attention_back_kernel, block),
        grid=(rows // block,),
        in_specs=[tiled(cols), whole, whole, tiled(cols), tiled(cols), tiled(heads), tiled(1)],
        out_specs=[tiled(cols), whole, whole],
        out_shape=[jax.ShapeDtypeStruct((rows, cols), F32)] * 3,
        compiler_params=pltpu.CompilerParams(vmem_limit_bytes=60 << 20),
        cost_estimate=pl.CostEstimate(
            flops=5 * rows * rows * cols, bytes_accessed=20 * rows * cols, transcendentals=0
        ),
    )(queries, keys, values, grads, attended, log_total, opening)


def swap_dp(values):
    count = lax.axis_size("dp")
    return lax.ppermute(values, "dp", [(i, (i + 1) % count) for i in range(count)])


def gather_dp(values):
    return lax.all_gather(values, "dp", axis=0, tiled=True)


def sum_dp(partial):
    half = partial.shape[0] // 2
    mine = lax.axis_index("dp")
    away = lax.dynamic_slice_in_dim(partial, (1 - mine) * half, half, 0).astype(BF16)
    kept = lax.dynamic_slice_in_dim(partial, mine * half, half, 0)
    return kept + swap_dp(away).astype(F32)


def gather_rows(values):
    return lax.all_gather(values, "seq", axis=0, tiled=True)


def scatter_rows(partial):
    return lax.psum_scatter(partial.astype(BF16), "seq", scatter_dimension=0, tiled=True).astype(F32)


def exchange(blocks):
    return lax.all_to_all(blocks, "seq", split_axis=0, concat_axis=0, tiled=True)


def norm_factor(values):
    return lax.rsqrt(jnp.mean(values * values, axis=-1, keepdims=True) + EPS)


def norm_back(inputs, factor, gain_row, upstream):
    scaled_up = gain_row * upstream
    inner_mean = jnp.mean(scaled_up * inputs, axis=-1, keepdims=True)
    grad_in = factor * scaled_up - inputs * factor * factor * factor * inner_mean
    grad_gain = jnp.sum(upstream * inputs * factor, axis=0)
    return grad_in, grad_gain


def shards(
    tokens,
    cotangent,
    doc_lengths,
    attn_gain,
    mlp_gain,
    query_weight,
    key_weight,
    value_weight,
    output_weight,
    gate_weight,
    up_weight,
    down_weight,
):
    dp = lax.axis_size("dp")
    seq = lax.axis_size("seq")
    mine = lax.axis_index("seq")
    tok_count, width = tokens.shape
    rows = tok_count * seq
    slab = query_weight.shape[0]
    share = HEAD_DIM // slab
    half_heads = HEADS // dp
    half_kv = KV_HEADS // dp
    hidden_dev = down_weight.shape[0]
    block = 512

    doc_ends = jnp.cumsum(doc_lengths[0])
    place = jnp.arange(rows, dtype=jnp.int32)
    passed = doc_ends[None, :] <= place[:, None]
    opening = jnp.max(jnp.where(passed, doc_ends[None, :], 0), axis=1)
    position = place - opening
    keeping = place < doc_ends[DOCS - 1]
    angles = position.astype(F32)[:, None] * rotary_table(HEAD_DIM)[None, :]
    cosine = jnp.cos(angles)
    sine = jnp.sin(angles)
    cos_heads = jnp.tile(cosine, (1, 2 * dp))
    sin_heads = jnp.tile(jnp.concatenate([-sine, sine], axis=1), (1, dp))
    own_keeping = lax.dynamic_slice_in_dim(keeping, mine * tok_count, tok_count, 0)

    def head_columns(weight, kept):
        split = weight.reshape(slab, dp, kept, HEAD_DIM)
        return jnp.repeat(split, seq // kept, axis=2)

    qkv_blocks = jnp.stack(
        [
            head_columns(query_weight, half_heads),
            head_columns(key_weight, half_kv),
            head_columns(value_weight, half_kv),
        ],
        axis=1,
    )
    qkv_blocks = jnp.transpose(qkv_blocks, (3, 0, 1, 2, 4)).reshape(seq * slab, 3 * dp * HEAD_DIM)
    qkv_weight = gather_dp(exchange(qkv_blocks))
    feed_blocks = jnp.stack(
        [w.reshape(slab, dp, seq, hidden_dev) for w in (gate_weight, up_weight)], axis=1
    )
    feed_blocks = jnp.transpose(feed_blocks, (3, 0, 1, 2, 4)).reshape(
        seq * slab, 2 * dp * hidden_dev
    )
    feed_weight = gather_dp(exchange(feed_blocks))
    down_own = gather_dp(down_weight)
    output_own = output_weight
    if share > 1:
        groups = [list(range(i, i + share)) for i in range(0, seq, share)]
        output_own = lax.all_gather(
            output_own, "seq", axis=0, tiled=True, axis_index_groups=groups
        )
    output_own = gather_dp(output_own)
    gains = lax.all_gather(
        jnp.stack([attn_gain, mlp_gain]), ("dp", "seq"), axis=1, tiled=True
    ).astype(F32)
    gain_one, gain_two = gains[0], gains[1]

    inputs_all = gather_rows(tokens).astype(F32)
    normed_one = (inputs_all * norm_factor(inputs_all) * gain_one).astype(BF16)
    qkv = dot(normed_one, qkv_weight)
    head_cols = dp * HEAD_DIM
    query_lin, key_lin = qkv[:, :head_cols], qkv[:, head_cols : 2 * head_cols]
    values = qkv[:, 2 * head_cols :].astype(BF16)
    scale = 1.0 / math.sqrt(HEAD_DIM)
    queries = (query_lin * cos_heads + swap_halves(query_lin) * sin_heads).astype(BF16) * BF16(scale)
    keys = (key_lin * cos_heads + swap_halves(key_lin) * sin_heads).astype(BF16)
    attended_sum, log_total = attention(queries, keys, values, opening[:, None], block)
    if share > 1:
        own_rows = ((place // tok_count) % share == mine % share)[:, None]
        attended_sum = jnp.where(own_rows, attended_sum, 0.0)
    attended = attended_sum.astype(BF16)
    inputs = tokens.astype(F32)
    middle = inputs + scatter_rows(dot(attended, output_own))

    factor_two = norm_factor(middle)
    normed_two = gather_rows((middle * factor_two * gain_two).astype(BF16))
    grad_own = jnp.where(own_keeping[:, None], cotangent, BF16(0))
    grad_out = gather_rows(grad_own)
    feed = dot(normed_two, feed_weight)
    feed_cols = dp * hidden_dev
    gate_lin, upward = feed[:, :feed_cols], feed[:, feed_cols:]
    sigmoid = jax.nn.sigmoid(gate_lin)
    hidden = (gate_lin * sigmoid * upward).astype(BF16)
    hidden_grad = dot_t(grad_out, down_own)
    gate_back = (hidden_grad * upward * sigmoid * (1.0 + gate_lin * (1.0 - sigmoid))).astype(BF16)
    up_back = (hidden_grad * gate_lin * sigmoid).astype(BF16)
    feed_back = jnp.concatenate([gate_back, up_back], axis=1)
    normed_two_grad = scatter_rows(dot_t(feed_back, feed_weight))
    mixed = middle + scatter_rows(dot(hidden, down_own))
    middle_in, gain_two_part = norm_back(middle, factor_two, gain_two, normed_two_grad)
    middle_grad = grad_own.astype(F32) + middle_in
    middle_back = gather_rows(middle_grad.astype(BF16))

    attended_grad = dot_t(middle_back, output_own).astype(BF16)
    if share > 1:
        attended_grad = jnp.where(own_rows, attended_grad, BF16(0))
    query_acc, key_acc, value_acc = attention_back(
        queries, keys, values, attended_grad, attended_sum, log_total, opening[:, None], block
    )
    query_acc = query_acc * scale
    query_back = query_acc * cos_heads - swap_halves(query_acc) * sin_heads
    key_back = key_acc * cos_heads - swap_halves(key_acc) * sin_heads
    qkv_back = jnp.concatenate([query_back, key_back, value_acc], axis=1).astype(BF16)
    normed_one_grad = scatter_rows(dot_t(qkv_back, qkv_weight))
    input_in, gain_one_part = norm_back(inputs, norm_factor(inputs), gain_one, normed_one_grad)
    token_grad = middle_grad + input_in

    feed_grad = exchange(sum_dp(t_dot(normed_two, feed_back)).astype(BF16)).astype(F32)
    feed_grad = feed_grad.reshape(seq, slab, 2, dp, hidden_dev)
    feed_grad = jnp.transpose(feed_grad, (2, 1, 3, 0, 4)).reshape(2, slab, dp * seq * hidden_dev)
    down_grad = sum_dp(t_dot(hidden, grad_out))
    output_part = t_dot(attended, middle_back)
    if share > 1:
        split = output_part.reshape(dp, share, slab, width)
        split = jnp.transpose(split, (1, 0, 2, 3)).reshape(share * dp * slab, width)
        output_part = lax.psum_scatter(
            split, "seq", scatter_dimension=0, tiled=True, axis_index_groups=groups
        )
    output_grad = sum_dp(output_part)
    qkv_grad = exchange(sum_dp(t_dot(normed_one, qkv_back)).astype(BF16)).astype(F32)
    qkv_grad = qkv_grad.reshape(seq, slab, 3, dp, HEAD_DIM)

    def own_columns(part, kept):
        summed = jnp.sum(part.reshape(kept, seq // kept, slab, dp, HEAD_DIM), axis=1)
        return jnp.transpose(summed, (1, 2, 0, 3)).reshape(slab, dp * kept * HEAD_DIM)

    query_grad = own_columns(qkv_grad[:, :, 0], half_heads)
    key_grad = own_columns(qkv_grad[:, :, 1], half_kv)
    value_grad = own_columns(qkv_grad[:, :, 2], half_kv)
    gain_parts = lax.psum(jnp.stack([gain_one_part, gain_two_part]), ("dp", "seq"))
    own = lax.axis_index("dp") * seq + mine
    gain_grads = lax.dynamic_slice_in_dim(gain_parts, own * slab, slab, 1)
    return (
        mixed,
        token_grad,
        gain_grads[0],
        gain_grads[1],
        query_grad,
        key_grad,
        value_grad,
        output_grad,
        feed_grad[0],
        feed_grad[1],
        down_grad,
    )


def solution(mesh):
    both = P(("dp", "seq"), None)
    line = P(("dp", "seq"))
    return jax.shard_map(
        shards,
        mesh=mesh,
        in_specs=(both, both, P("dp", None), line, line) + (both,) * 7,
        out_specs=(both, both, line, line) + (both,) * 7,
        check_vma=False,
    )
```

time: 3730 us -> 1120 us (0.30)
  waiting for transfers between devices: 3180 us -> 557 us
  matrix products: 322 us -> 107 us
  blocking collectives: 106 us -> 207 us
  local copies, waits for them, and re-layouts: 37.6 us -> 91.1 us
  Pallas kernels: 0 us -> 51.8 us
    reduce_scatter x5 -> x4, waiting for transfers between devices: 2290 us -> 142 us  [scatter_rows(): lax.psum_scatter(partial.astype(BF16), 'seq', scatter_dimension=0, tiled=...]
    all_gather x9 -> x7, waiting for transfers between devices: 796 us -> 323 us  [the longest x4 231 us: gather_rows(): return lax.all_gather(values, 'seq', axis=0, tiled=True)]
    dot_general x25 -> x12, matrix products: 322 us -> 107 us  [the longest x4 38.8 us: dot_t(): lax.dot_general(a, b, (((1,), (1,)), ((), ())), preferred_element_type=F32)]
    unnamed x2 -> x0, blocking collectives: 101 us -> none
    psum x1 -> x0, waiting for transfers between devices: 87.8 us -> none  [shards(): lax.psum(qkv_part.astype(jnp.bfloat16), 'dp').astype(jnp.float32)]
    all_to_all x0 -> x1, blocking collectives: none -> 84.3 us  [exchange(): lax.all_to_all(blocks, 'seq', split_axis=0, concat_axis=0, tiled=True)]
    all_gather x0 -> x2, blocking collectives: none -> 70.6 us  [the longest x1 60.8 us: shards(): lax.all_gather(jnp.stack([attn_gain, mlp_gain]), ('dp', 'seq'), axis=1, t...]
    ppermute x0 -> x4, waiting for transfers between devices: none -> 61.7 us  [swap_dp(): lax.ppermute(values, 'dp', [(i, (i + 1) % count) for i in range(count)])]
  transfers between devices with their start and end apart: 15 -> 18, of which waited for: 15 -> 14; matrix products, arithmetic and copies ran while one was open for 7% -> 12% of each run, Pallas kernels for 0% -> 0%
where the time goes in v1:
time: 1120 us; the launch traced here: 1110 us
  waiting for transfers between devices  557 us (50%)
  blocking collectives  207 us (18%)
  matrix products  107 us (10%)
  local copies, waits for them, and re-layouts  91.1 us (8%)
  other arithmetic  54.5 us (5%)
  Pallas kernels  51.8 us (5%)
  starting transfers between devices  28.6 us (3%)
  between operations  14.8 us (1%)
    all_gather x4, waiting for transfers between devices, gather_rows(): return lax.all_gather(values, 'seq', axis=0, tiled=True)  231 us
    reduce_scatter x4, waiting for transfers between devices, scatter_rows(): lax.psum_scatter(partial.astype(BF16), 'seq', scatter_dimension=0, tiled=...  142 us
    all_gather x3, waiting for transfers between devices, gather_dp(): return lax.all_gather(values, 'dp', axis=0, tiled=True)  92.3 us
    all_to_all x1, blocking collectives, exchange(): lax.all_to_all(blocks, 'seq', split_axis=0, concat_axis=0, tiled=True)  84.3 us
    ppermute x4, waiting for transfers between devices, swap_dp(): lax.ppermute(values, 'dp', [(i, (i + 1) % count) for i in range(count)])  61.7 us
    all_gather x1, blocking collectives, shards(): lax.all_gather(jnp.stack([attn_gain, mlp_gain]), ('dp', 'seq'), axis=1, t...  60.8 us
    psum x1, blocking collectives, shards(): lax.psum(jnp.stack([gain_one_part, gain_two_part]), ('dp', 'seq'))  51.6 us
    dot_general x4, matrix products, dot_t(): lax.dot_general(a, b, (((1,), (1,)), ((), ())), preferred_element_type=F32)  38.8 us
  transfers between devices with their start and end apart: 18, of which 14 were waited for; matrix products, arithmetic and copies ran while one was open for 12% of the time, Pallas kernels for 0%

profile of v1, /device:TPU:0, one launch (start us, length us, event | category | flops | bytes accessed | tf_op | source)
XLA Modules:
  0.0 1112.1 jit_solution(11929038120192244028)
XLA Ops:
  12.9 3.1 maximum_bitcast_fusion.1
  17.8 7.4 all-to-all-start
  25.2 60.8 %all-gather = bf16[32,64,2]{1,2,0:T(2,128)(2,1)S(1)} all-gather(bf16[1,64,2]{1,2,0:T(2,128)(2,1)S(1)} %maximum_bitcast_fusion.2), channel_id=1, replica_groups=mesh['dp'=2,'seq'=16] {'dp','seq'}, dimensions={0}, use_global_device_ids=true | all-gather | bytes 8448 | tf_op jit(solution)/shard_map/all_gather | solution.py:273
  91.9 9.8 all_gather.30
  102.6 5.1 fusion
  107.7 22.6 %all-gather.11.cloned.1.call-done = bf16[2048,384]{1,0:T(8,128)(2,1)} async-done(((bf16[1024,384]{1,0:T(8,128)(2,1)}), bf16[2048,384]{1,0:T(8,128)(2,1)}) %all-gather.11.cloned.1.call-update) | async-done | bytes 1572880 | tf_op jit(solution)/shard_map/all_gather | solution.py:170
  130.3 7.5 fusion.6
  147.7 3.4 add_convert_fusion.2
  151.1 2.7 copy.160
  161.3 22.4 %shard_map.203 = (f32[2048,128]{1,0:T(8,128)S(1)}, f32[2048,2]{1,0:T(8,128)S(1)}) custom-call(bf16[2048,128]{1,0:T(8,128)(2,1)S(1)} %get-tuple-element.35.q_ref, bf16[2048,128]{1,0:T(8,128)(2,1)S(1)} %get-tuple-element.36.k_ref, bf16[2048,128]{1,0:T(8,128)(2,1)S(1)} %get-tuple-element.34.v_ref, s32[2048,1]{1,0:T(8,128)S(1)} %copy.169.open_ref), custom_call_target="tpu_custom_call" | custom-call | flops 1073741824 | bytes 2621440 | tf_op jit(solution)/shard_map/pallas_call | solution.py:95
  184.6 5.6 convolution_convert_fusion.3
  194.0 2.7 maximum_bitcast_fusion
  196.7 2.7 all_to_all.31
  199.4 84.3 %all_to_all.42 = bf16[16,64,1024]{2,1,0:T(8,128)(2,1)} all-to-all(bf16[16,64,1024]{2,1,0:T(8,128)(2,1)} %all_to_all.31), channel_id=1, replica_groups=mesh['dp'=2,'seq'=16] {'seq'}, dimensions={0} | all-to-all | bytes 4194304 | tf_op jit(solution)/shard_map/all_to_all | solution.py:190
  283.8 39.1 %reduce-scatter.5.cloned.1.call-done = bf16[128,2048]{1,0:T(8,128)(2,1)} async-done(((bf16[2048,2048]{1,0:T(8,128)(2,1)}), bf16[128,2048]{1,0:T(8,128)(2,1)}) %reduce-scatter.5.cloned.1.call-update) | async-done | bytes 524304 | tf_op jit(solution)/shard_map/reduce_scatter | solution.py:186
  329.4 51.5 %all-gather.15.cloned.1.call-done = bf16[2048,1024]{1,0:T(8,128)(2,1)} async-done(((bf16[1024,1024]{1,0:T(8,128)(2,1)}), bf16[2048,1024]{1,0:T(8,128)(2,1)}) %all-gather.15.cloned.1.call-update) | async-done | bytes 4194320 | tf_op jit(solution)/shard_map/all_gather | solution.py:170
  380.8 77.5 %all-gather.13.cloned.1.call-done = bf16[2048,2048]{1,0:T(8,128)(2,1)} async-done(((bf16[128,2048]{1,0:T(8,128)(2,1)}), bf16[2048,2048]{1,0:T(8,128)(2,1)}) %all-gather.13.cloned.1.call-update) | async-done | bytes 8388624 | tf_op jit(solution)/shard_map/all_gather | solution.py:182
  458.3 14.5 %fusion.39 = f32[2048,1024]{0,1:T(8,128)} fusion(bf16[2048,2048]{1,0:T(8,128)(2,1)} %all-gather.13.cloned.1.call-done, bf16[2048,1024]{1,0:T(8,128)(2,1)} %all-gather.15.cloned.1.call-done), kind=kOutput, calls=%fused_computation.100 | convolution fusion | flops 8589934592 | bytes 20971520 | tf_op jit(solution)/shard_map/dot_general | solution.py:39
  472.9 18.3 %all-gather.17.cloned.1.call-done = bf16[512,2048]{1,0:T(8,128)(2,1)} async-done(((bf16[256,2048]{1,0:T(8,128)(2,1)}), bf16[512,2048]{1,0:T(8,128)(2,1)}) %all-gather.17.cloned.1.call-update) | async-done | bytes 2097168 | tf_op jit(solution)/shard_map/all_gather | solution.py:170
  491.1 77.7 %all-gather.19.cloned.1.call-done = bf16[2048,2048]{1,0:T(8,128)(2,1)} async-done(((bf16[128,2048]{1,0:T(8,128)(2,1)}), bf16[2048,2048]{1,0:T(8,128)(2,1)}) %all-gather.19.cloned.1.call-update) | async-done | bytes 8388624 | tf_op jit(solution)/shard_map/all_gather | solution.py:182
  568.8 13.8 %multiply_convert_fusion.1 = (bf16[2048,512]{0,1:T(8,128)(2,1)S(1)}, bf16[2048,512]{0,1:T(8,128)(2,1)S(1)}, bf16[2048,512]{0,1:T(8,128)(2,1)}) fusion(f32[2048,1024]{0,1:T(8,128)} %fusion.39, bf16[2048,2048]{1,0:T(8,128)(2,1)} %all-gather.19.cloned.1.call-done, bf16[512,2048]{1,0:T(8,128)(2,1)} %all-gather.17.cloned.1.call-done), kind=kOutput, calls=%fused_computation.14 | convolution fusion | flops 4311744512 | bytes 25165824 | tf_op jit(solution)/shard_map/dot_general | solution.py:43
  583.9 11.6 %convolution_convert_fusion.1 = bf16[2048,2048]{1,0:T(8,128)(2,1)} fusion(bf16[2048,1024]{1,0:T(8,128)(2,1)S(1)} %copy-done.35, bf16[2048,512]{0,1:T(8,128)(2,1)S(1)} %get-tuple-element.27, bf16[2048,512]{0,1:T(8,128)(2,1)S(1)} %get-tuple-element.26), kind=kOutput, calls=%fused_computation.6 | convolution fusion | flops 8602517504 | bytes 16777216 | tf_op jit(solution)/shard_map/dot_general | solution.py:43
  595.6 103.1 %reduce-scatter.9.cloned.1.call-done = bf16[128,2048]{1,0:T(8,128)(2,1)} async-done(((bf16[2048,2048]{1,0:T(8,128)(2,1)}), bf16[128,2048]{1,0:T(8,128)(2,1)}) %reduce-scatter.9.cloned.1.call-update) | async-done | bytes 524304 | tf_op jit(solution)/shard_map/reduce_scatter | solution.py:186
  702.6 74.8 %all-gather.21.cloned.1.call-done = bf16[2048,2048]{1,0:T(8,128)(2,1)} async-done(((bf16[128,2048]{1,0:T(8,128)(2,1)}), bf16[2048,2048]{1,0:T(8,128)(2,1)}) %all-gather.21.cloned.1.call-update) | async-done | bytes 8388624 | tf_op jit(solution)/shard_map/all_gather | solution.py:182
  777.4 6.5 convolution_convert_fusion.4.g_ref
  783.9 29.4 %shard_map.204 = (f32[2048,128]{1,0:T(8,128)}, f32[2048,128]{1,0:T(8,128)}, f32[2048,128]{1,0:T(8,128)}) custom-call(bf16[2048,128]{1,0:T(8,128)(2,1)} %copy-done.5, bf16[2048,128]{1,0:T(8,128)(2,1)} %copy-done.3, bf16[2048,128]{1,0:T(8,128)(2,1)} %copy-done.4, bf16[2048,128]{1,0:T(8,128)(2,1)} %convolution_convert_fusion.4.g_ref, f32[2048,128]{1,0:T(8,128)} %copy-done, ...), custom_call_target="tpu_custom_call" | custom-call | flops 2684354560 | bytes 5242880 | tf_op jit(solution)/shard_map/pallas_call | solution.py:151
  828.9 6.8 convolution_convert_fusion
  837.4 8.6 convolution_convert_fusion.2
  847.8 12.6 %fusion.3 = f32[2048,1024]{1,0:T(8,128)S(1)} fusion(bf16[2048,2048]{1,0:T(8,128)(2,1)} %all-gather.13.cloned.1.call-done, bf16[2048,512]{0,1:T(8,128)(2,1)} %copy-done.43, bf16[2048,512]{0,1:T(8,128)(2,1)S(1)} %copy-done.42), kind=kOutput, calls=%fused_computation.17 | convolution fusion | flops 8598323200 | bytes 20971520 | tf_op jit(solution)/shard_map/dot_general | solution.py:47
  860.4 3.3 copy-done.15
  865.5 46.4 %collective-permute-done.2 = bf16[1024,1024]{1,0:T(8,128)(2,1)} collective-permute-done((bf16[1024,1024]{1,0:T(8,128)(2,1)S(1)}, bf16[1024,1024]{1,0:T(8,128)(2,1)}, u32[]{:S(2)}, u32[]{:S(2)}) %collective-permute-start.2) | collective-permute-done | bytes 2097184 | tf_op jit(solution)/shard_map/ppermute | solution.py:166
  911.9 4.9 add_convert_fusion
  916.8 3.9 all-to-all-start.3
  920.8 7.7 fusion.40
  933.1 7.3 fusion.4
  943.5 14.4 %collective-permute-done.3 = bf16[256,2048]{1,0:T(8,128)(2,1)} collective-permute-done((bf16[256,2048]{1,0:T(8,128)(2,1)}, bf16[256,2048]{1,0:T(8,128)(2,1)}, u32[]{:S(2)}, u32[]{:S(2)}) %collective-permute-start.3) | collective-permute-done | bytes 1048608 | tf_op jit(solution)/shard_map/ppermute | solution.py:166
  957.9 3.6 convert_add_fusion
  961.5 14.3 %all-to-all-done.3 = bf16[16,64,1024]{2,1,0:T(8,128)(2,1)S(1)} async-done(((bf16[16,64,1024]{2,1,0:T(8,128)(2,1)}), bf16[16,64,1024]{2,1,0:T(8,128)(2,1)S(1)}, u32[]{:S(2)}, u32[]{:S(2)}) %all-to-all-start.3) | async-done | bytes 2097184 | tf_op jit(solution)/shard_map/all_to_all | solution.py:190
  975.7 5.2 reshape.207
  980.9 7.2 copy.196
  990.5 11.2 %all-to-all-start.2 = ((bf16[16,64,384]{2,1,0:T(8,128)(2,1)}), bf16[16,64,384]{2,1,0:T(8,128)(2,1)}, u32[]{:S(2)}, u32[]{:S(2)}) async-start(bf16[16,64,384]{2,1,0:T(8,128)(2,1)} %bitcast.31), calls=%async_computation.6 | async-start | bytes 1572864 | tf_op jit(solution)/shard_map/all_to_all | solution.py:190
  1001.7 4.9 fusion.26
  1011.1 2.7 squeeze.19
  1018.2 14.8 %all-to-all-done.2 = bf16[16,64,384]{2,1,0:T(8,128)(2,1)} async-done(((bf16[16,64,384]{2,1,0:T(8,128)(2,1)}), bf16[16,64,384]{2,1,0:T(8,128)(2,1)}, u32[]{:S(2)}, u32[]{:S(2)}) %all-to-all-start.2) | async-done | bytes 786464 | tf_op jit(solution)/shard_map/all_to_all | solution.py:190
  1033.0 4.2 reshape.206
  1037.2 3.5 fusion.36
  1049.6 51.6 %psum.7 = f32[2,2048]{1,0:T(2,128)S(1)} all-reduce(f32[2,2048]{1,0:T(2,128)S(1)} %pad_maximum_fusion.7), channel_id=1, replica_groups=mesh['dp'=2,'seq'=16] {'dp','seq'}, use_global_device_ids=true, to_apply=%region_13.14 | all-reduce | flops 4096 | bytes 32768 | tf_op jit(solution)/shard_map/psum | solution.py:350
  1101.8 3.5 fusion.12
  (195 shorter events, 97.1 us)
Async XLA Ops:
  7.2 95.4 %all-gather.9.cloned.1.call-start = ((), (), s32[]{:S(2)}) async-start(), calls=%async_computation.8 | async-start | bytes 8912896 | tf_op jit(solution)/shard_map/all_gather | solution.py:182
  12.1 13.1 %copy-start.38 = (bf16[64]{0:T(256)(128)(2,1)S(1)}, bf16[64]{0:T(256)(128)(2,1)}, u32[]{:S(2)}) copy-start(bf16[64]{0:T(256)(128)(2,1)} %param.16) | copy-start | bytes 388
  12.1 13.1 %copy-start.39 = (bf16[64]{0:T(256)(128)(2,1)S(1)}, bf16[64]{0:T(256)(128)(2,1)}, u32[]{:S(2)}) copy-start(bf16[64]{0:T(256)(128)(2,1)} %param.15) | copy-start | bytes 388
  12.1 74.0 %copy-start.40 = (s32[1,4]{1,0:T(1,128)S(1)}, s32[1,4]{1,0:T(1,128)}, u32[]{:S(2)}) copy-start(s32[1,4]{1,0:T(1,128)} %param.14) | copy-start | bytes 52
  17.8 70.5 %all-to-all-start = ((bf16[16,64,384]{2,1,0:T(8,128)(2,1)}), bf16[16,64,384]{2,1,0:T(8,128)(2,1)S(1)}, u32[]{:S(2)}, u32[]{:S(2)}) async-start(bf16[16,64,384]{2,1,0:T(8,128)(2,1)} %all_to_all.28), calls=%async_computation | async-start | bytes 1572864 | tf_op jit(solution)/shard_map/all_to_all | solution.py:190
  25.1 105.2 %all-gather.11.cloned.1.call-start = ((), (), s32[]{:S(2)}) async-start(), calls=%async_computation.9 | async-start | bytes 2359296 | tf_op jit(solution)/shard_map/all_gather | solution.py:170
  89.1 233.8 %reduce-scatter.5.cloned.1.call-start = ((), (), s32[]{:S(2)}) async-start(), calls=%async_computation.10 | async-start | bytes 8912896 | tf_op jit(solution)/shard_map/reduce_scatter | solution.py:186
  89.2 2.7 copy-start.34
  89.7 69.0 %copy-start.9 = (f32[2048,128]{1,0:T(8,128)}, f32[2048,128]{1,0:T(8,128)S(1)}, u32[]{:S(2)}) copy-start(f32[2048,128]{1,0:T(8,128)S(1)} %copy.162) | copy-start | bytes 3145732
  91.9 69.3 %copy-start.2 = (s32[2048,1]{1,0:T(8,128)}, s32[2048,1]{1,0:T(8,128)S(1)}, u32[]{:S(2)}) copy-start(s32[2048,1]{1,0:T(8,128)S(1)} %copy.169.open_ref) | copy-start | bytes 24580
  151.1 10.1 copy-start.3
  158.7 25.9 %copy-start.21 = (bf16[128,2048]{1,0:T(8,128)(2,1)S(1)}, bf16[128,2048]{1,0:T(8,128)(2,1)}, u32[]{:S(2)}) copy-start(bf16[128,2048]{1,0:T(8,128)(2,1)} %all_gather.30) | copy-start | bytes 1572868
  161.2 22.4 %copy-start.5 = (bf16[2048,128]{1,0:T(8,128)(2,1)}, bf16[2048,128]{1,0:T(8,128)(2,1)S(1)}, u32[]{:S(2)}) copy-start(bf16[2048,128]{1,0:T(8,128)(2,1)S(1)} %get-tuple-element.35.q_ref) | copy-start | bytes 1572868
  161.2 29.0 %copy-start.4 = (bf16[2048,128]{1,0:T(8,128)(2,1)}, bf16[2048,128]{1,0:T(8,128)(2,1)S(1)}, u32[]{:S(2)}) copy-start(bf16[2048,128]{1,0:T(8,128)(2,1)S(1)} %get-tuple-element.34.v_ref) | copy-start | bytes 1572868
  184.6 5.6 copy-start
  190.3 190.6 %all-gather.15.cloned.1.call-start = ((), (), s32[]{:S(2)}) async-start(), calls=%async_computation.12 | async-start | bytes 6291456 | tf_op jit(solution)/shard_map/all_gather | solution.py:170
  199.4 123.5 %copy-start.7 = (bf16[128,2048]{1,0:T(8,128)(2,1)S(1)}, bf16[128,2048]{1,0:T(8,128)(2,1)}, u32[]{:S(2)}) copy-start(bf16[128,2048]{1,0:T(8,128)(2,1)} %param.12) | copy-start | bytes 1572868
  283.7 44.4 %copy-start.16 = (bf16[128,2048]{1,0:T(8,128)(2,1)S(1)}, bf16[128,2048]{1,0:T(8,128)(2,1)}, u32[]{:S(2)}) copy-start(bf16[128,2048]{1,0:T(8,128)(2,1)} %param.13) | copy-start | bytes 1572868
  283.8 174.6 %all-gather.13.cloned.1.call-start = ((), (), s32[]{:S(2)}) async-start(), calls=%async_computation.11 | async-start | bytes 8912896 | tf_op jit(solution)/shard_map/all_gather | solution.py:182
  326.3 164.9 %all-gather.17.cloned.1.call-start = ((), (), s32[]{:S(2)}) async-start(), calls=%async_computation.13 | async-start | bytes 3145728 | tf_op jit(solution)/shard_map/all_gather | solution.py:170
  326.9 241.9 %all-gather.19.cloned.1.call-start = ((), (), s32[]{:S(2)}) async-start(), calls=%async_computation.15 | async-start | bytes 8912896 | tf_op jit(solution)/shard_map/all_gather | solution.py:182
  329.1 369.6 %reduce-scatter.9.cloned.1.call-start = ((), (), s32[]{:S(2)}) async-start(), calls=%async_computation.16 | async-start | bytes 8912896 | tf_op jit(solution)/shard_map/reduce_scatter | solution.py:186
  568.8 15.1 %copy-start.35 = (bf16[2048,1024]{1,0:T(8,128)(2,1)S(1)}, bf16[2048,1024]{1,0:T(8,128)(2,1)}, u32[]{:S(2)}) copy-start(bf16[2048,1024]{1,0:T(8,128)(2,1)} %all-gather.15.cloned.1.call-done) | copy-start | bytes 12582916
  582.6 12.9 %copy-start.41 = (bf16[2048,512]{0,1:T(8,128)(2,1)}, bf16[2048,512]{0,1:T(8,128)(2,1)S(1)}, u32[]{:S(2)}) copy-start(bf16[2048,512]{0,1:T(8,128)(2,1)S(1)} %get-tuple-element.26) | copy-start | bytes 6291460
  595.5 103.1 %copy-start.12 = (bf16[128,2048]{1,0:T(8,128)(2,1)S(1)}, bf16[128,2048]{1,0:T(8,128)(2,1)}, u32[]{:S(2)}) copy-start(bf16[128,2048]{1,0:T(8,128)(2,1)} %reduce-scatter.5.cloned.1.call-done) | copy-start | bytes 1572868
  595.6 181.8 %copy-start.22 = (bf16[128,2048]{1,0:T(8,128)(2,1)S(1)}, bf16[128,2048]{1,0:T(8,128)(2,1)}, u32[]{:S(2)}) copy-start(bf16[128,2048]{1,0:T(8,128)(2,1)} %all_gather.30) | copy-start | bytes 1572868
  595.6 181.8 %all-gather.21.cloned.1.call-start = ((), (), s32[]{:S(2)}) async-start(), calls=%async_computation.17 | async-start | bytes 8912896 | tf_op jit(solution)/shard_map/all_gather | solution.py:182
  702.6 345.7 %reduce-scatter.11.cloned.1.call-start = ((), (), s32[]{:S(2)}) async-start(), calls=%async_computation.18 | async-start | bytes 8912896 | tf_op jit(solution)/shard_map/reduce_scatter | solution.py:186
  816.4 8.9 copy-start.10
  816.4 8.9 copy-start.11
  823.9 5.1 copy-start.37
  825.3 2.7 copy-start.32
  835.8 266.0 %reduce-scatter.7.cloned.1.call-start = ((), (), s32[]{:S(2)}) async-start(), calls=%async_computation.14 | async-start | bytes 8912896 | tf_op jit(solution)/shard_map/reduce_scatter | solution.py:186
  860.4 3.3 copy-start.15
  864.0 48.0 %collective-permute-start.2 = (bf16[1024,1024]{1,0:T(8,128)(2,1)S(1)}, bf16[1024,1024]{1,0:T(8,128)(2,1)}, u32[]{:S(2)}, u32[]{:S(2)}) collective-permute-start(bf16[1024,1024]{1,0:T(8,128)(2,1)S(1)} %dynamic-slice_convert_fusion), channel_id=1, source_target_pairs={{0,16},{16,0},{1,17},{17,1},{2,18},{18,2},{3,19},{19,3},{4,20},{20... | collective-permute-start | bytes 6291464 | tf_op jit(solution)/shard_map/ppermute | solution.py:166
  916.8 58.9 %all-to-all-start.3 = ((bf16[16,64,1024]{2,1,0:T(8,128)(2,1)}), bf16[16,64,1024]{2,1,0:T(8,128)(2,1)S(1)}, u32[]{:S(2)}, u32[]{:S(2)}) async-start(bf16[16,64,1024]{2,1,0:T(8,128)(2,1)} %bitcast.89), calls=%async_computation.7 | async-start | bytes 4194304 | tf_op jit(solution)/shard_map/all_to_all | solution.py:190
  920.8 12.3 %copy-start.29 = (bf16[2048,128]{1,0:T(8,128)(2,1)S(1)}, bf16[2048,128]{1,0:T(8,128)(2,1)}, u32[]{:S(2)}) copy-start(bf16[2048,128]{1,0:T(8,128)(2,1)} %copy-done.28) | copy-start | bytes 1572868
  920.8 12.3 %copy-start.31 = (bf16[2048,128]{1,0:T(8,128)(2,1)S(1)}, bf16[2048,128]{1,0:T(8,128)(2,1)}, u32[]{:S(2)}) copy-start(bf16[2048,128]{1,0:T(8,128)(2,1)} %copy-done.30) | copy-start | bytes 1572868
  920.8 12.3 %copy-start.33 = (bf16[2048,128]{1,0:T(8,128)(2,1)S(1)}, bf16[2048,128]{1,0:T(8,128)(2,1)}, u32[]{:S(2)}) copy-start(bf16[2048,128]{1,0:T(8,128)(2,1)} %copy-done.32) | copy-start | bytes 1572868
  931.6 26.3 %collective-permute-start.3 = (bf16[256,2048]{1,0:T(8,128)(2,1)}, bf16[256,2048]{1,0:T(8,128)(2,1)}, u32[]{:S(2)}, u32[]{:S(2)}) collective-permute-start(bf16[256,2048]{1,0:T(8,128)(2,1)} %dynamic-slice_convert_fusion.1), channel_id=1, source_target_pairs={{0,16},{16,0},{1,17},{17,1},{2,18},{18,2},{3,19},{19,3},{4,20},{20... | collective-permute-start | bytes 3145736 | tf_op jit(solution)/shard_map/ppermute | solution.py:166
  943.0 45.1 %collective-permute-start = (bf16[1024,384]{1,0:T(8,128)(2,1)}, bf16[1024,384]{1,0:T(8,128)(2,1)}, u32[]{:S(2)}, u32[]{:S(2)}) collective-permute-start(bf16[1024,384]{1,0:T(8,128)(2,1)} %dynamic-slice_convert_fusion.2), channel_id=1, source_target_pairs={{0,16},{16,0},{1,17},{17,1},{2,18},{18,2},{3,19},{19,3},{4,20},{20... | collective-permute-start | bytes 2359304 | tf_op jit(solution)/shard_map/ppermute | solution.py:166
  980.9 7.2 copy-start.24
  988.1 13.6 %copy-start.1 = (f32[2048,128]{1,0:T(8,128)S(1)}, f32[2048,128]{1,0:T(8,128)}, u32[]{:S(2)}) copy-start(f32[2048,128]{1,0:T(8,128)} %copy-done) | copy-start | bytes 3145732
  990.5 42.5 %all-to-all-start.2 = ((bf16[16,64,384]{2,1,0:T(8,128)(2,1)}), bf16[16,64,384]{2,1,0:T(8,128)(2,1)}, u32[]{:S(2)}, u32[]{:S(2)}) async-start(bf16[16,64,384]{2,1,0:T(8,128)(2,1)} %bitcast.31), calls=%async_computation.6 | async-start | bytes 1572864 | tf_op jit(solution)/shard_map/all_to_all | solution.py:190
  1001.7 7.5 copy-start.8
  1007.4 8.9 collective-permute-start.1
  1040.7 61.1 %copy-start.14 = (bf16[128,2048]{1,0:T(8,128)(2,1)S(1)}, bf16[128,2048]{1,0:T(8,128)(2,1)}, u32[]{:S(2)}) copy-start(bf16[128,2048]{1,0:T(8,128)(2,1)} %reduce-scatter.9.cloned.1.call-done) | copy-start | bytes 1572868
  1040.7 61.1 %copy-start.17 = (bf16[128,2048]{1,0:T(8,128)(2,1)S(1)}, bf16[128,2048]{1,0:T(8,128)(2,1)}, u32[]{:S(2)}) copy-start(bf16[128,2048]{1,0:T(8,128)(2,1)} %param.13) | copy-start | bytes 1572868
  (14 other events, 20.8 us)
Sparse Core Ops, SparseCore 0:
  10.2 92.3 all-gather.8
  104.7 25.4 all-gather.10
  190.4 132.4 reduce-scatter.4
  324.3 56.4 all-gather.14
  383.4 74.8 all-gather.12
  459.7 31.3 all-gather.16
  493.9 74.8 all-gather.18
  595.7 102.9 reduce-scatter.8
  702.7 74.6 all-gather.20
  835.9 132.7 reduce-scatter.10
  972.8 121.2 reduce-scatter.6

commit v2 on v1

--- a/solution.py
+++ b/solution.py
@@ -14,6 +14,7 @@
 DOCS = 4
 EPS = 1e-05
 NEG = -1e30
+MESH = pl.DeviceIdType.MESH
 F32 = jnp.float32
 BF16 = jnp.bfloat16
 
@@ -159,6 +160,576 @@
             flops=5 * rows * rows * cols, bytes_accessed=20 * rows * cols, transcendentals=0
         ),
     )(queries, keys, values, grads, attended, log_total, opening)
+
+
+class Place:
+    def __init__(self):
+        self.dp = lax.axis_index("dp")
+        seq = lax.axis_index("seq")
+        self.length = lax.axis_size("seq") // 4
+        self.line = lax.div(seq, 4)
+        self.pair = lax.rem(lax.div(seq, 2), 2)
+        self.core = lax.rem(seq, 2)
+
+    def index(self, line, pair, core):
+        return (line * 2 + pair) * 2 + core
+
+    def device(self, line, pair, core):
+        return (self.dp, self.index(line, pair, core))
+
+    def sibling(self):
+        return self.device(self.line, self.pair, 1 - self.core)
+
+    def across(self):
+        return self.device(self.line, 1 - self.pair, self.core)
+
+    def above(self):
+        return self.device(self.line + 1, self.pair, self.core)
+
+    def below(self):
+        return self.device(self.line - 1, self.pair, self.core)
+
+    def greet(self):
+        barrier = pltpu.get_barrier_semaphore()
+
+        def signal(device):
+            pl.semaphore_signal(barrier, inc=1, device_id=device, device_id_type=MESH)
+
+        signal(self.sibling())
+        signal(self.across())
+        pl.when(self.line > 0)(lambda: signal(self.below()))
+        pl.when(self.line < self.length - 1)(lambda: signal(self.above()))
+        inner = (self.line > 0) & (self.line < self.length - 1)
+        pl.semaphore_wait(barrier, jnp.where(inner, 4, 3))
+
+
+def remote(src, dst, send_sem, recv_sem, device):
+    return pltpu.make_async_remote_copy(
+        src_ref=src,
+        dst_ref=dst,
+        send_sem=send_sem,
+        recv_sem=recv_sem,
+        device_id=device,
+        device_id_type=MESH,
+    )
+
+
+def scatter_kernel(
+    transposed,
+    parts,
+    tile,
+    a_ref,
+    b_ref,
+    out_ref,
+    core_out,
+    core_in,
+    pair_out,
+    pair_in,
+    line_out,
+    up_in,
+    down_in,
+    held,
+    core_sems,
+    pair_sems,
+    line_sems,
+    up_sems,
+    down_sems,
+):
+    here = Place()
+    here.greet()
+    length = here.length
+    rows = out_ref.shape[0]
+    width = out_ref.shape[1] // parts
+    tiles = width // tile
+    steps = length * parts
+
+    def target(i):
+        ups = length - 1 - here.line
+        near = here.line < length // 2
+        if_near = jnp.where(i < ups, length - 1 - i, i - ups)
+        if_far = jnp.where(i < here.line, i, length - 1 - (i - here.line))
+        return jnp.where(i == length - 1, here.line, jnp.where(near, if_near, if_far))
+
+    def product(line, pair, core, part, use):
+        first = pl.multiple_of(here.index(line, pair, core) * rows, rows)
+        a = a_ref[pl.ds(first, rows), :]
+
+        @pl.loop(0, tiles)
+        def _(t):
+            into = pl.ds(pl.multiple_of(t * tile, tile), tile)
+            cols = pl.ds(pl.multiple_of(part * width + t * tile, tile), tile)
+            use(dot_t(a, b_ref[cols, :]) if transposed else dot(a, b_ref[:, cols]), into)
+
+    def core_copy(slot):
+        return remote(
+            core_out.at[slot],
+            core_in.at[slot],
+            core_sems.at[0, slot],
+            core_sems.at[1, slot],
+            here.sibling(),
+        )
+
+    def pair_copy(slot):
+        return remote(
+            pair_out.at[slot],
+            pair_in.at[slot],
+            pair_sems.at[0, slot],
+            pair_sems.at[1, slot],
+            here.across(),
+        )
+
+    def up_copy(slot, into):
+        return remote(
+            line_out.at[slot], up_in.at[into], line_sems.at[slot], up_sems.at[into], here.above()
+        )
+
+    def down_copy(slot, into):
+        return remote(
+            line_out.at[slot], down_in.at[into], line_sems.at[slot], down_sems.at[into], here.below()
+        )
+
+    def for_sibling(step, pair, slot):
+        def use(value, cols):
+            core_out[slot, :, cols] = value.astype(BF16)
+
+        product(target(step // parts), pair, 1 - here.core, step % parts, use)
+        core_copy(slot).start()
+
+    for_sibling(0, 1 - here.pair, 0)
+
+    @pl.loop(0, steps)
+    def _(step):
+        pl.when(step < steps - 1)(lambda: for_sibling(step + 1, 1 - here.pair, step + 1))
+        core_copy(step).wait_recv()
+
+        def use(value, cols):
+            pair_out[step, :, cols] = (value + core_in[step, :, cols].astype(F32)).astype(BF16)
+
+        product(target(step // parts), 1 - here.pair, here.core, step % parts, use)
+        pair_copy(step).start()
+
+    for_sibling(0, here.pair, steps)
+
+    @pl.loop(0, steps)
+    def _(step):
+        pl.when(step < steps - 1)(lambda: for_sibling(step + 1, here.pair, steps + step + 1))
+        core_copy(steps + step).wait_recv()
+        line = target(step // parts)
+        part = step % parts
+        into = line * parts + part
+
+        def use(value, cols):
+            held[:, cols] = value + core_in[steps + step, :, cols].astype(F32)
+
+        product(line, here.pair, here.core, part, use)
+        pair_copy(step).wait_recv()
+        from_above = (line <= here.line) & (here.line < length - 1)
+        from_below = (line >= here.line) & (here.line > 0)
+        held[...] += pair_in[step].astype(F32)
+
+        @pl.when(from_above)
+        def _():
+            down_copy(0, into).wait_recv()
+            held[...] += down_in[into].astype(F32)
+
+        @pl.when(from_below)
+        def _():
+            up_copy(0, into).wait_recv()
+            held[...] += up_in[into].astype(F32)
+
+        @pl.when(line == here.line)
+        def _():
+            out_ref[:, pl.ds(pl.multiple_of(part * width, width), width)] = held[...]
+
+        @pl.when(line < here.line)
+        def _():
+            line_out[step] = held[...].astype(BF16)
+            down_copy(step, into).start()
+
+        @pl.when(line > here.line)
+        def _():
+            line_out[step] = held[...].astype(BF16)
+            up_copy(step, into).start()
+
+    @pl.loop(0, steps)
+    def _(step):
+        core_copy(step).wait_send()
+        core_copy(steps + step).wait_send()
+        pair_copy(step).wait_send()
+        line = target(step // parts)
+        pl.when(line < here.line)(lambda: down_copy(step, 0).wait_send())
+        pl.when(line > here.line)(lambda: up_copy(step, 0).wait_send())
+
+
+def product_scatter(a, b, transposed, call_id, parts=2):
+    seq = lax.axis_size("seq")
+    steps = seq // 4 * parts
+    rows = a.shape[0] // seq
+    width = b.shape[0] if transposed else b.shape[1]
+    block = (rows, width // parts)
+    vmem = pl.BlockSpec(memory_space=pltpu.VMEM)
+    return pl.pallas_call(
+        functools.partial(scatter_kernel, transposed, parts, min(width // parts, 512)),
+        out_shape=jax.ShapeDtypeStruct((rows, width), F32),
+        in_specs=[vmem, vmem],
+        out_specs=vmem,
+        scratch_shapes=[
+            pltpu.VMEM((2 * steps, *block), BF16),
+            pltpu.VMEM((2 * steps, *block), BF16),
+            pltpu.VMEM((steps, *block), BF16),
+            pltpu.VMEM((steps, *block), BF16),
+            pltpu.VMEM((steps, *block), BF16),
+            pltpu.VMEM((steps, *block), BF16),
+            pltpu.VMEM((steps, *block), BF16),
+            pltpu.VMEM(block, F32),
+            pltpu.SemaphoreType.DMA((2, 2 * steps)),
+            pltpu.SemaphoreType.DMA((2, steps)),
+            pltpu.SemaphoreType.DMA((steps,)),
+            pltpu.SemaphoreType.DMA((steps,)),
+            pltpu.SemaphoreType.DMA((steps,)),
+        ],
+        compiler_params=pltpu.CompilerParams(
+            collective_id=call_id, has_side_effects=True, vmem_limit_bytes=48 << 20
+        ),
+        cost_estimate=pl.CostEstimate(
+            flops=2 * a.shape[0] * a.shape[1] * width,
+            bytes_accessed=4 * a.shape[0] * width,
+            transcendentals=0,
+        ),
+    )(a, b)
+
+def gather_units(here, own_ref, buf, send_sems, recv_sems, compute):
+    length = here.length
+    last = length - 1
+    steps = 2 * length
+    half = own_ref.shape[0] // 2
+    mine = here.index(here.line, here.pair, here.core)
+    shorter = jnp.minimum(here.line, last - here.line)
+    longer = jnp.where(here.line < last - here.line, 1, -1)
+
+    def column(j):
+        i = j - 1
+        paired = jnp.where(i % 2 == 0, here.line - i // 2 - 1, here.line + i // 2 + 1)
+        single = here.line + longer * (i - shorter + 1)
+        return jnp.where(j == 0, here.line, jnp.where(i < 2 * shorter, paired, single))
+
+    def copy(way, device, block, part):
+        ref = buf.at[block, part]
+        return remote(
+            ref, ref, send_sems.at[way, block, part], recv_sems.at[block, part], device
+        )
+
+    def up(block, part):
+        return copy(0, here.above(), block, part)
+
+    def down(block, part):
+        return copy(1, here.below(), block, part)
+
+    def across(block, part):
+        return copy(2, here.across(), block, part)
+
+    def sideways(block, part):
+        return copy(3, here.sibling(), block, part)
+
+    for part in range(2):
+        buf[mine, part] = own_ref[pl.ds(part * half, half), :]
+        pl.when(here.line < last)(lambda part=part: up(mine, part).start())
+        pl.when(here.line > 0)(lambda part=part: down(mine, part).start())
+        across(mine, part).start()
+        sideways(mine, part).start()
+
+    @pl.loop(0, steps)
+    def _(step):
+        part = step % 2
+        far = step // 2 + 1
+
+        @pl.when(here.line >= far)
+        def _():
+            block = here.index(here.line - far, here.pair, here.core)
+            up(block, part).wait_recv()
+            pl.when(here.line < last)(lambda: up(block, part).start())
+            sideways(block, part).start()
+
+        @pl.when(here.line + far <= last)
+        def _():
+            block = here.index(here.line + far, here.pair, here.core)
+            down(block, part).wait_recv()
+            pl.when(here.line > 0)(lambda: down(block, part).start())
+            sideways(block, part).start()
+
+        @pl.when(step + 2 < steps)
+        def _():
+            across(here.index(column(step // 2 + 1), here.pair, here.core), part).start()
+
+        block = here.index(column(step // 2), 1 - here.pair, here.core)
+        across(block, part).wait_recv()
+        sideways(block, part).start()
+
+        in_column = (step % 2 == 1) & (step < steps - 1) | (step == 0)
+        order = jnp.where(in_column, (step + 1) // 2, jnp.where(step == steps - 1, last, step // 2 - 1))
+        line = column(order)
+        pair = jnp.where(in_column, here.pair, 1 - here.pair)
+        other = here.index(line, pair, 1 - here.core)
+        sideways(other, 0).wait_recv()
+        sideways(other, 1).wait_recv()
+        compute(step, here.index(line, pair, 0))
+
+    @pl.loop(0, length)
+    def _(line):
+        for part in range(2):
+            block = here.index(line, here.pair, here.core)
+
+            @pl.when((line <= here.line) & (here.line < last))
+            def _():
+                up(block, part).wait_send()
+
+            @pl.when((line >= here.line) & (here.line > 0))
+            def _():
+                down(block, part).wait_send()
+
+            across(block, part).wait_send()
+            sideways(block, part).wait_send()
+            sideways(here.index(line, 1 - here.pair, here.core), part).wait_send()
+
+
+def gather_scratch(seq, rows, width):
+    return [
+        pltpu.VMEM((seq, 2, rows // 2, width), BF16),
+        pltpu.SemaphoreType.DMA((4, seq, 2)),
+        pltpu.SemaphoreType.DMA((seq, 2)),
+    ]
+
+
+def unit_rows(first, rows):
+    return pl.ds(pl.multiple_of(first * rows, 2 * rows), 2 * rows)
+
+
+def take_unit(buf, first):
+    blocks = buf[pl.ds(first, 2)]
+    return blocks.reshape(-1, blocks.shape[-1])
+
+
+def rotated(values, cosine, sine):
+    cols = values.shape[1]
+    lane = lax.broadcasted_iota(jnp.int32, values.shape, 1)
+    ahead = pltpu.roll(values, cols - HEAD_DIM // 2, 1)
+    behind = pltpu.roll(values, HEAD_DIM // 2, 1)
+    swapped = jnp.where(lane % HEAD_DIM < HEAD_DIM // 2, ahead, behind)
+    return values * cosine + swapped * sine
+
+
+def project_kernel(
+    own_ref,
+    gain_ref,
+    weight_ref,
+    cos_ref,
+    sin_ref,
+    normed_ref,
+    q_ref,
+    k_ref,
+    v_ref,
+    buf,
+    send_sems,
+    recv_sems,
+    held,
+    held_sems,
+):
+    here = Place()
+    here.greet()
+    rows = own_ref.shape[0]
+    cols = q_ref.shape[1]
+    chunk = min(32, rows // 2)
+
+    def store(step, first):
+        slot = step % 2
+        return pltpu.make_async_copy(
+            held.at[slot], normed_ref.at[unit_rows(first, rows)], held_sems.at[slot]
+        )
+
+    def compute(step, first):
+        slot = step % 2
+        pl.when(step >= 2)(lambda: store(step, first).wait())
+
+        @pl.loop(0, 2 * rows // chunk)
+        def _(i):
+            at = i * chunk
+            block = lax.div(at, rows)
+            part = lax.div(at % rows, rows // 2)
+            values = buf[first + block, part, pl.ds(at % (rows // 2), chunk), :].astype(F32)
+            factor = lax.rsqrt(jnp.mean(values * values, axis=1, keepdims=True) + EPS)
+            held[slot, pl.ds(at, chunk), :] = (values * factor * gain_ref[...]).astype(BF16)
+
+        store(step, first).start()
+        qkv = dot(held[slot], weight_ref[...])
+        where = unit_rows(first, rows)
+        cosine = cos_ref[where, :]
+        sine = sin_ref[where, :]
+        scale = BF16(1.0 / 8.0)
+        q_ref[where, :] = rotated(qkv[:, :cols], cosine, sine).astype(BF16) * scale
+        k_ref[where, :] = rotated(qkv[:, cols : 2 * cols], cosine, sine).astype(BF16)
+        v_ref[where, :] = qkv[:, 2 * cols :].astype(BF16)
+
+    gather_units(here, own_ref, buf, send_sems, recv_sems, compute)
+    store(0, 0).wait()
+    store(1, 0).wait()
+
+
+def gather_project(own, gain, weight, cosine, sine, call_id):
+    seq = lax.axis_size("seq")
+    rows, width = own.shape
+    cols = cosine.shape[1]
+    vmem = pl.BlockSpec(memory_space=pltpu.VMEM)
+    head = jax.ShapeDtypeStruct((seq * rows, cols), BF16)
+    return pl.pallas_call(
+        project_kernel,
+        out_shape=[jax.ShapeDtypeStruct((seq * rows, width), BF16), head, head, head],
+        in_specs=[vmem] * 5,
+        out_specs=[pl.BlockSpec(memory_space=pl.ANY), vmem, vmem, vmem],
+        scratch_shapes=gather_scratch(seq, rows, width)
+        + [pltpu.VMEM((2, 2 * rows, width), BF16), pltpu.SemaphoreType.DMA((2,))],
+        compiler_params=pltpu.CompilerParams(
+            collective_id=call_id, has_side_effects=True, vmem_limit_bytes=48 << 20
+        ),
+        cost_estimate=pl.CostEstimate(
+            flops=2 * seq * rows * width * weight.shape[1],
+            bytes_accessed=4 * seq * rows * width,
+            transcendentals=0,
+        ),
+    )(own, gain, weight, cosine, sine)
+
+
+def feed_kernel(
+    own_ref,
+    grad_ref,
+    feed_ref,
+    down_ref,
+    normed_ref,
+    hidden_ref,
+    back_ref,
+    buf,
+    send_sems,
+    recv_sems,
+    out_sems,
+):
+    here = Place()
+    here.greet()
+    rows = own_ref.shape[0]
+    hidden = hidden_ref.shape[1]
+    tile = 256
+
+    def store(first, block, part, step):
+        begin = (first + block) * rows + part * (rows // 2)
+        return pltpu.make_async_copy(
+            buf.at[first + block, part],
+            normed_ref.at[pl.ds(pl.multiple_of(begin, rows // 2), rows // 2)],
+            out_sems.at[step, block, part],
+        )
+
+    def stores(first, step):
+        return [store(first, block, part, step) for block in range(2) for part in range(2)]
+
+    def compute(step, first):
+        for one in stores(first, step):
+            one.start()
+        where = unit_rows(first, rows)
+        normed = take_unit(buf, first)
+        grad = grad_ref[where, :]
+
+        @pl.loop(0, hidden // tile)
+        def _(t):
+            cols = pl.ds(pl.multiple_of(t * tile, tile), tile)
+            later = pl.ds(pl.multiple_of(hidden + t * tile, tile), tile)
+            gate = dot(normed, feed_ref[:, cols])
+            upward = dot(normed, feed_ref[:, later])
+            hidden_grad = dot_t(grad, down_ref[cols, :])
+            sigmoid = jax.nn.sigmoid(gate)
+            silu = gate * sigmoid
+            hidden_ref[where, cols] = (silu * upward).astype(BF16)
+            back_ref[where, cols] = (
+                hidden_grad * upward * sigmoid * (1.0 + gate * (1.0 - sigmoid))
+            ).astype(BF16)
+            back_ref[where, later] = (hidden_grad * silu).astype(BF16)
+
+    gather_units(here, own_ref, buf, send_sems, recv_sems, compute)
+
+    @pl.loop(0, 2 * here.length)
+    def _(step):
+        for one in stores(0, step):
+            one.wait()
+
+
+def gather_feed(own, grad_out, feed_weight, down_weight, call_id):
+    seq = lax.axis_size("seq")
+    rows, width = own.shape
+    hidden = down_weight.shape[0]
+    vmem = pl.BlockSpec(memory_space=pltpu.VMEM)
+    return pl.pallas_call(
+        feed_kernel,
+        out_shape=[
+            jax.ShapeDtypeStruct((seq * rows, width), BF16),
+            jax.ShapeDtypeStruct((seq * rows, hidden), BF16),
+            jax.ShapeDtypeStruct((seq * rows, 2 * hidden), BF16),
+        ],
+        in_specs=[vmem] * 4,
+        out_specs=[pl.BlockSpec(memory_space=pl.ANY), vmem, vmem],
+        scratch_shapes=gather_scratch(seq, rows, width)
+        + [pltpu.SemaphoreType.DMA((seq // 2, 2, 2))],
+        compiler_params=pltpu.CompilerParams(
+            collective_id=call_id, has_side_effects=True, vmem_limit_bytes=56 << 20
+        ),
+        cost_estimate=pl.CostEstimate(
+            flops=6 * seq * rows * width * hidden,
+            bytes_accessed=6 * seq * rows * width,
+            transcendentals=0,
+        ),
+    )(own, grad_out, feed_weight, down_weight)
+
+
+def back_kernel(
+    own_ref, weight_ref, attended_ref, grad_ref, part_ref, buf, send_sems, recv_sems
+):
+    here = Place()
+    here.greet()
+    rows = own_ref.shape[0]
+    width = own_ref.shape[1]
+    tile = 512
+    part_ref[...] = jnp.zeros_like(part_ref)
+
+    def compute(step, first):
+        where = unit_rows(first, rows)
+        unit = take_unit(buf, first)
+        grad_ref[where, :] = dot_t(unit, weight_ref[...]).astype(BF16)
+        attended = attended_ref[where, :]
+        for t in range(width // tile):
+            cols = slice(t * tile, (t + 1) * tile)
+            part_ref[:, cols] += t_dot(attended, unit[:, cols])
+
+    gather_units(here, own_ref, buf, send_sems, recv_sems, compute)
+
+
+def gather_back(own, weight, attended, call_id):
+    seq = lax.axis_size("seq")
+    rows, width = own.shape
+    cols = weight.shape[0]
+    vmem = pl.BlockSpec(memory_space=pltpu.VMEM)
+    return pl.pallas_call(
+        back_kernel,
+        out_shape=[
+            jax.ShapeDtypeStruct((seq * rows, cols), BF16),
+            jax.ShapeDtypeStruct((cols, width), F32),
+        ],
+        in_specs=[vmem] * 3,
+        out_specs=[vmem] * 2,
+        scratch_shapes=gather_scratch(seq, rows, width),
+        compiler_params=pltpu.CompilerParams(
+            collective_id=call_id, has_side_effects=True, vmem_limit_bytes=40 << 20
+        ),
+        cost_estimate=pl.CostEstimate(
+            flops=4 * seq * rows * width * cols,
+            bytes_accessed=4 * seq * rows * width,
+            transcendentals=0,
+        ),
+    )(own, weight, attended)
 
 
 def swap_dp(values):
@@ -227,6 +798,7 @@
     half_kv = KV_HEADS // dp
     hidden_dev = down_weight.shape[0]
     block = 512
+    in_kernels = seq % 4 == 0 and 2 * rows * width <= 16 << 20
 
     doc_ends = jnp.cumsum(doc_lengths[0])
     place = jnp.arange(rows, dtype=jnp.int32)
@@ -275,43 +847,64 @@
     ).astype(F32)
     gain_one, gain_two = gains[0], gains[1]
 
-    inputs_all = gather_rows(tokens).astype(F32)
-    normed_one = (inputs_all * norm_factor(inputs_all) * gain_one).astype(BF16)
-    qkv = dot(normed_one, qkv_weight)
+    scale = 1.0 / math.sqrt(HEAD_DIM)
     head_cols = dp * HEAD_DIM
-    query_lin, key_lin = qkv[:, :head_cols], qkv[:, head_cols : 2 * head_cols]
-    values = qkv[:, 2 * head_cols :].astype(BF16)
-    scale = 1.0 / math.sqrt(HEAD_DIM)
-    queries = (query_lin * cos_heads + swap_halves(query_lin) * sin_heads).astype(BF16) * BF16(scale)
-    keys = (key_lin * cos_heads + swap_halves(key_lin) * sin_heads).astype(BF16)
+    if in_kernels:
+        normed_one, queries, keys, values = gather_project(
+            tokens, gain_one[None, :], qkv_weight, cos_heads, sin_heads, 0
+        )
+    else:
+        inputs_all = gather_rows(tokens).astype(F32)
+        normed_one = (inputs_all * norm_factor(inputs_all) * gain_one).astype(BF16)
+        qkv = dot(normed_one, qkv_weight)
+        query_lin, key_lin = qkv[:, :head_cols], qkv[:, head_cols : 2 * head_cols]
+        values = qkv[:, 2 * head_cols :].astype(BF16)
+        queries = query_lin * cos_heads + swap_halves(query_lin) * sin_heads
+        queries = queries.astype(BF16) * BF16(scale)
+        keys = (key_lin * cos_heads + swap_halves(key_lin) * sin_heads).astype(BF16)
     attended_sum, log_total = attention(queries, keys, values, opening[:, None], block)
     if share > 1:
         own_rows = ((place // tok_count) % share == mine % share)[:, None]
         attended_sum = jnp.where(own_rows, attended_sum, 0.0)
     attended = attended_sum.astype(BF16)
     inputs = tokens.astype(F32)
-    middle = inputs + scatter_rows(dot(attended, output_own))
+    if in_kernels:
+        middle = inputs + product_scatter(attended, output_own, False, 1)
+    else:
+        middle = inputs + scatter_rows(dot(attended, output_own))
 
     factor_two = norm_factor(middle)
-    normed_two = gather_rows((middle * factor_two * gain_two).astype(BF16))
+    normed_own = (middle * factor_two * gain_two).astype(BF16)
     grad_own = jnp.where(own_keeping[:, None], cotangent, BF16(0))
     grad_out = gather_rows(grad_own)
-    feed = dot(normed_two, feed_weight)
-    feed_cols = dp * hidden_dev
-    gate_lin, upward = feed[:, :feed_cols], feed[:, feed_cols:]
-    sigmoid = jax.nn.sigmoid(gate_lin)
-    hidden = (gate_lin * sigmoid * upward).astype(BF16)
-    hidden_grad = dot_t(grad_out, down_own)
-    gate_back = (hidden_grad * upward * sigmoid * (1.0 + gate_lin * (1.0 - sigmoid))).astype(BF16)
-    up_back = (hidden_grad * gate_lin * sigmoid).astype(BF16)
-    feed_back = jnp.concatenate([gate_back, up_back], axis=1)
-    normed_two_grad = scatter_rows(dot_t(feed_back, feed_weight))
+    if in_kernels:
+        normed_two, hidden, feed_back = gather_feed(
+            normed_own, grad_out, feed_weight, down_own, 2
+        )
+        normed_two_grad = product_scatter(feed_back, feed_weight.T, False, 3)
+    else:
+        normed_two = gather_rows(normed_own)
+        feed = dot(normed_two, feed_weight)
+        feed_cols = dp * hidden_dev
+        gate_lin, upward = feed[:, :feed_cols], feed[:, feed_cols:]
+        sigmoid = jax.nn.sigmoid(gate_lin)
+        hidden = (gate_lin * sigmoid * upward).astype(BF16)
+        hidden_grad = dot_t(grad_out, down_own)
+        gate_back = hidden_grad * upward * sigmoid * (1.0 + gate_lin * (1.0 - sigmoid))
+        up_back = hidden_grad * gate_lin * sigmoid
+        feed_back = jnp.concatenate([gate_back, up_back], axis=1).astype(BF16)
+        normed_two_grad = scatter_rows(dot_t(feed_back, feed_weight))
     mixed = middle + scatter_rows(dot(hidden, down_own))
     middle_in, gain_two_part = norm_back(middle, factor_two, gain_two, normed_two_grad)
     middle_grad = grad_own.astype(F32) + middle_in
-    middle_back = gather_rows(middle_grad.astype(BF16))
-
-    attended_grad = dot_t(middle_back, output_own).astype(BF16)
+    if in_kernels:
+        attended_grad, output_part = gather_back(
+            middle_grad.astype(BF16), output_own, attended, 4
+        )
+    else:
+        middle_back = gather_rows(middle_grad.astype(BF16))
+        attended_grad = dot_t(middle_back, output_own).astype(BF16)
+        output_part = t_dot(attended, middle_back)
     if share > 1:
         attended_grad = jnp.where(own_rows, attended_grad, BF16(0))
     query_acc, key_acc, value_acc = attention_back(
@@ -321,7 +914,10 @@
     query_back = query_acc * cos_heads - swap_halves(query_acc) * sin_heads
     key_back = key_acc * cos_heads - swap_halves(key_acc) * sin_heads
     qkv_back = jnp.concatenate([query_back, key_back, value_acc], axis=1).astype(BF16)
-    normed_one_grad = scatter_rows(dot_t(qkv_back, qkv_weight))
+    if in_kernels:
+        normed_one_grad = product_scatter(qkv_back, qkv_weight, True, 5)
+    else:
+        normed_one_grad = scatter_rows(dot_t(qkv_back, qkv_weight))
     input_in, gain_one_part = norm_back(inputs, norm_factor(inputs), gain_one, normed_one_grad)
     token_grad = middle_grad + input_in
 
@@ -329,7 +925,6 @@
     feed_grad = feed_grad.reshape(seq, slab, 2, dp, hidden_dev)
     feed_grad = jnp.transpose(feed_grad, (2, 1, 3, 0, 4)).reshape(2, slab, dp * seq * hidden_dev)
     down_grad = sum_dp(t_dot(hidden, grad_out))
-    output_part = t_dot(attended, middle_back)
     if share > 1:
         split = output_part.reshape(dp, share, slab, width)
         split = jnp.transpose(split, (1, 0, 2, 3)).reshape(share * dp * slab, width)

time: 1120 us -> 824 us (0.74)
  waiting for transfers between devices: 557 us -> 91.4 us
  Pallas kernels: 51.8 us -> 419 us
  blocking collectives: 207 us -> 102 us
  matrix products: 107 us -> 31.1 us
  other arithmetic: 54.5 us -> 35.2 us
    pallas_call x0 -> x6, Pallas kernels: none -> 367 us  [the longest x3 194 us: product_scatter(): pl.pallas_call(functools.partial(scatter_kernel, transposed, parts, min(w...]
    all_gather x4 -> x1, waiting for transfers between devices: 231 us -> 0.01 us  [gather_rows(): return lax.all_gather(values, 'seq', axis=0, tiled=True)]
    reduce_scatter x4 -> x1, waiting for transfers between devices: 142 us -> 0.01 us  [scatter_rows(): lax.psum_scatter(partial.astype(BF16), 'seq', scatter_dimension=0, tiled=...]
    all_gather x3, waiting for transfers between devices: 92.3 us -> 0.02 us  [gather_dp(): return lax.all_gather(values, 'dp', axis=0, tiled=True)]
    all_to_all x1 -> x0, blocking collectives: 84.3 us -> none  [exchange(): lax.all_to_all(blocks, 'seq', split_axis=0, concat_axis=0, tiled=True)]
    dot_general x4 -> x0, matrix products: 38.8 us -> none  [dot_t(): lax.dot_general(a, b, (((1,), (1,)), ((), ())), preferred_element_type=F32)]
    dot_general x4 -> x1, matrix products: 36.2 us -> 6.8 us  [dot(): return jnp.dot(a, b, preferred_element_type=F32)]
    ppermute x4, waiting for transfers between devices: 61.7 us -> 38.9 us  [swap_dp(): lax.ppermute(values, 'dp', [(i, (i + 1) % count) for i in range(count)])]
  transfers between devices with their start and end apart: 18 -> 13, of which waited for: 14 -> 4; matrix products, arithmetic and copies ran while one was open for 12% -> 15% of each run, Pallas kernels for 0% -> 37%
where the time goes in v2:
time: 824 us; the launch traced here: 815 us
  Pallas kernels  419 us (51%)
  blocking collectives  102 us (12%)
  local copies, waits for them, and re-layouts  94.5 us (11%)
  waiting for transfers between devices  91.4 us (11%)
  other arithmetic  35.2 us (4%)
  matrix products  31.1 us (4%)
  starting transfers between devices  27.1 us (3%)
  between operations  14.7 us (2%)
    pallas_call x3, Pallas kernels, product_scatter(): pl.pallas_call(functools.partial(scatter_kernel, transposed, parts, min(w...  194 us
    pallas_call x1, Pallas kernels, gather_back(): pl.pallas_call(back_kernel, out_shape=[jax.ShapeDtypeStruct((seq * rows,...  60.9 us
    pallas_call x1, Pallas kernels, gather_feed(): pl.pallas_call(feed_kernel, out_shape=[jax.ShapeDtypeStruct((seq * rows,...  58.5 us
    pallas_call x1, Pallas kernels, gather_project(): pl.pallas_call(project_kernel, out_shape=[jax.ShapeDtypeStruct((seq * row...  53.9 us
    all_to_all x4, waiting for transfers between devices, exchange(): lax.all_to_all(blocks, 'seq', split_axis=0, concat_axis=0, tiled=True)  51 us
    all_gather x1, blocking collectives, shards(): lax.all_gather(jnp.stack([attn_gain, mlp_gain]), ('dp', 'seq'), axis=1, t...  47.4 us
    psum x1, blocking collectives, shards(): lax.psum(jnp.stack([gain_one_part, gain_two_part]), ('dp', 'seq'))  41.9 us
    ppermute x4, waiting for transfers between devices, swap_dp(): lax.ppermute(values, 'dp', [(i, (i + 1) % count) for i in range(count)])  38.9 us
  transfers between devices with their start and end apart: 13, of which 4 were waited for; matrix products, arithmetic and copies ran while one was open for 15% of the time, Pallas kernels for 37%

profile of v2, /device:TPU:0, one launch (start us, length us, event | category | flops | bytes accessed | tf_op | source)
XLA Modules:
  0.0 814.8 jit_solution(2038780645969266608)
XLA Ops:
  14.7 7.5 all-to-all-start
  24.7 2.7 maximum_bitcast_fusion
  27.4 2.7 all_to_all.31
  30.1 10.7 %all-to-all-done = bf16[16,64,384]{2,1,0:T(8,128)(2,1)S(1)} async-done(((bf16[16,64,384]{2,1,0:T(8,128)(2,1)}), bf16[16,64,384]{2,1,0:T(8,128)(2,1)S(1)}, u32[]{:S(2)}, u32[]{:S(2)}) %all-to-all-start) | async-done | bytes 786464 | tf_op jit(solution)/shard_map/all_to_all | solution.py:761
  41.7 5.5 all-to-all-start.1
  48.0 40.3 %all-to-all-done.1 = bf16[16,64,1024]{2,1,0:T(8,128)(2,1)S(1)} async-done(((bf16[16,64,1024]{2,1,0:T(8,128)(2,1)}), bf16[16,64,1024]{2,1,0:T(8,128)(2,1)S(1)}, u32[]{:S(2)}, u32[]{:S(2)}) %all-to-all-start.1) | async-done | bytes 2097184 | tf_op jit(solution)/shard_map/all_to_all | solution.py:761
  88.3 2.5 copy.126
  94.2 47.4 %all-gather = bf16[32,64,2]{1,2,0:T(2,128)(2,1)S(1)} all-gather(bf16[1,64,2]{1,2,0:T(2,128)(2,1)S(1)} %maximum_bitcast_fusion.2), channel_id=1, replica_groups=mesh['dp'=2,'seq'=16] {'dp','seq'}, dimensions={0}, use_global_device_ids=true | all-gather | bytes 8448 | tf_op jit(solution)/shard_map/all_gather | solution.py:845
  147.3 12.6 %all_gather.20.b_ref.weight_ref = bf16[128,2048]{1,0:T(8,128)(2,1)} all-gather(bf16[64,2048]{1,0:T(8,128)(2,1)S(1)} %copy-done.35), channel_id=1, replica_groups=mesh['dp'=2,'seq'=16] {'dp'}, dimensions={0}, use_global_device_ids=true | all-gather | bytes 786432 | tf_op jit(solution)/shard_map/all_gather | solution.py:741
  161.4 53.9 %shard_map.203 = (bf16[2048,2048]{1,0:T(8,128)(2,1)}, bf16[2048,128]{1,0:T(8,128)(2,1)S(1)}, bf16[2048,128]{1,0:T(8,128)(2,1)S(1)}, bf16[2048,128]{1,0:T(8,128)(2,1)S(1)}) custom-call(bf16[128,2048]{1,0:T(8,128)(2,1)S(1)} %copy-done, f32[1,2048]{1,0:T(1,128)S(1)} %get-tuple-element.56.gain_ref, bf16[2048,384]{1,0:T(8,128)(2,1)S(1)} %copy-done.8, ...), custom_call_target="tpu_custom_call" | custom-call | flops 3221225472 | bytes 16777216 | tf_op jit(solution)/shard_map/pallas_call | solution.py:583
  215.4 22.4 %shard_map.204 = (f32[2048,128]{1,0:T(8,128)S(1)}, f32[2048,2]{1,0:T(8,128)S(1)}) custom-call(bf16[2048,128]{1,0:T(8,128)(2,1)S(1)} %get-tuple-element.25.q_ref, bf16[2048,128]{1,0:T(8,128)(2,1)S(1)} %get-tuple-element.26.k_ref, bf16[2048,128]{1,0:T(8,128)(2,1)S(1)} %get-tuple-element.27.v_ref, s32[2048,1]{1,0:T(8,128)S(1)} %copy-done.3), custom_call_target="tpu_custom_call" | custom-call | flops 1073741824 | bytes 2621440 | tf_op jit(solution)/shard_map/pallas_call | solution.py:96
  238.9 71.2 %shard_map.205 = f32[128,2048]{1,0:T(8,128)S(1)} custom-call(bf16[2048,128]{1,0:T(8,128)(2,1)S(1)} %convert_element_type.77.a_ref.attended_ref, bf16[128,2048]{1,0:T(8,128)(2,1)S(1)} %copy-done.6), custom_call_target="tpu_custom_call" | custom-call | flops 1073741824 | bytes 16777216 | tf_op jit(solution)/shard_map/pallas_call | solution.py:371
  312.3 6.4 copy.127.feed_ref
  318.7 58.5 %shard_map.206 = (bf16[2048,2048]{1,0:T(8,128)(2,1)}, bf16[2048,512]{1,0:T(8,128)(2,1)}, bf16[2048,1024]{1,0:T(8,128)(2,1)}) custom-call(bf16[128,2048]{1,0:T(8,128)(2,1)} %multiply_convert_fusion.own_ref, bf16[2048,2048]{1,0:T(8,128)(2,1)} %all-gather.8.cloned.1.call-done.grad_ref, bf16[2048,1024]{1,0:T(8,128)(2,1)} %copy.127.feed_ref, ...), custom_call_target="tpu_custom_call" | custom-call | flops 12884901888 | bytes 25165824 | tf_op jit(solution)/shard_map/pallas_call | solution.py:666
  377.3 2.2 copy-done.15
  379.5 59.6 %shard_map.207 = f32[128,2048]{1,0:T(8,128)S(1)} custom-call(bf16[2048,1024]{1,0:T(8,128)(2,1)S(1)} %copy-done.15, bf16[1024,2048]{1,0:T(8,128)(2,1)} %bitcast.81), custom_call_target="tpu_custom_call" | custom-call | flops 8589934592 | bytes 16777216 | tf_op jit(solution)/shard_map/pallas_call | solution.py:371
  441.6 6.8 convolution_convert_fusion
  450.5 60.9 %shard_map.208 = (bf16[2048,128]{1,0:T(8,128)(2,1)S(1)}, f32[128,2048]{1,0:T(8,128)S(1)}) custom-call(bf16[128,2048]{1,0:T(8,128)(2,1)S(1)} %copy-done.5, bf16[128,2048]{1,0:T(8,128)(2,1)S(1)} %copy-done.7, bf16[2048,128]{1,0:T(8,128)(2,1)S(1)} %convert_element_type.77.a_ref.attended_ref), custom_call_target="tpu_custom_call" | custom-call | flops 2147483648 | bytes 16777216 | tf_op jit(solution)/shard_map/pallas_call | solution.py:715
  513.2 29.1 %shard_map.209 = (f32[2048,128]{1,0:T(8,128)}, f32[2048,128]{1,0:T(8,128)}, f32[2048,128]{1,0:T(8,128)}) custom-call(bf16[2048,128]{1,0:T(8,128)(2,1)} %copy-done.11, bf16[2048,128]{1,0:T(8,128)(2,1)} %copy-done.12, bf16[2048,128]{1,0:T(8,128)(2,1)} %copy-done.13, bf16[2048,128]{1,0:T(8,128)(2,1)} %copy-done.14, f32[2048,128]{1,0:T(8,128)} %copy-done.2, ...), custom_call_target="tpu_custom_call" | custom-call | flops 2684354560 | bytes 5242880 | tf_op jit(solution)/shard_map/pallas_call | solution.py:152
  544.9 2.5 copy.130
  547.4 2.3 rev.6
  549.7 2.5 copy.131
  552.3 2.5 copy.134
  554.8 2.3 rev.7
  557.1 2.5 copy.135
  559.6 3.1 subtract_convert_fusion.1
  562.8 7.8 fusion.11
  572.2 9.0 %fusion.15 = f32[2048,1024]{1,0:T(8,128)S(1)} fusion(bf16[2048,2048]{1,0:T(8,128)(2,1)S(1)} %bitcast.112, bf16[2048,1024]{1,0:T(8,128)(2,1)S(1)} %copy-done.16), kind=kOutput, calls=%fused_computation.63 | convolution fusion | flops 8589934592 | bytes 20971520 | tf_op jit(solution)/shard_map/dot_general | solution.py:48
  581.2 3.3 copy-done.22
  586.7 4.3 collective-permute-done
  591.1 2.5 add_convert_fusion.1
  593.6 4.6 all-to-all-start.2
  601.5 34.6 %collective-permute-done.2 = bf16[1024,1024]{1,0:T(8,128)(2,1)} collective-permute-done((bf16[1024,1024]{1,0:T(8,128)(2,1)}, bf16[1024,1024]{1,0:T(8,128)(2,1)}, u32[]{:S(2)}, u32[]{:S(2)}) %collective-permute-start.2) | collective-permute-done | bytes 2097184 | tf_op jit(solution)/shard_map/ppermute | solution.py:737
  636.1 4.9 add_convert_fusion
  641.0 4.8 all-to-all-start.3
  645.8 7.6 fusion.16
  657.3 63.1 %shard_map.210 = f32[128,2048]{1,0:T(8,128)S(1)} custom-call(bf16[2048,384]{1,0:T(8,128)(2,1)S(1)} %pad_maximum_fusion.a_ref, bf16[2048,384]{1,0:T(8,128)(2,1)S(1)} %copy-done.9), custom_call_target="tpu_custom_call" | custom-call | flops 3221225472 | bytes 16777216 | tf_op jit(solution)/shard_map/pallas_call | solution.py:371
  720.7 41.9 %psum.7 = f32[2,2048]{1,0:T(2,128)S(1)} all-reduce(f32[2,2048]{1,0:T(2,128)S(1)} %pad_maximum_fusion.2), channel_id=1, replica_groups=mesh['dp'=2,'seq'=16] {'dp','seq'}, use_global_device_ids=true, to_apply=%region_9.10 | all-reduce | flops 4096 | bytes 32768 | tf_op jit(solution)/shard_map/psum | solution.py:945
  765.2 3.6 convert_add_fusion
  768.8 3.2 reshape.182
  772.0 3.5 fusion.13
  777.1 2.4 reshape.179
  785.2 6.6 reshape.183
  791.9 4.6 copy.151
  796.5 2.5 fusion.12
  798.9 2.7 squeeze.19
  801.7 2.8 squeeze.20
  804.5 3.6 fusion.5
  (166 shorter events, 55.4 us)
Async XLA Ops:
  14.7 7.5 copy-start.33
  14.7 26.2 %all-to-all-start = ((bf16[16,64,384]{2,1,0:T(8,128)(2,1)}), bf16[16,64,384]{2,1,0:T(8,128)(2,1)S(1)}, u32[]{:S(2)}, u32[]{:S(2)}) async-start(bf16[16,64,384]{2,1,0:T(8,128)(2,1)} %all_to_all.28), calls=%async_computation | async-start | bytes 1572864 | tf_op jit(solution)/shard_map/all_to_all | solution.py:761
  22.2 1.3 copy-start.34
  41.7 46.6 %all-to-all-start.1 = ((bf16[16,64,1024]{2,1,0:T(8,128)(2,1)}), bf16[16,64,1024]{2,1,0:T(8,128)(2,1)S(1)}, u32[]{:S(2)}, u32[]{:S(2)}) async-start(bf16[16,64,1024]{2,1,0:T(8,128)(2,1)} %all_to_all.31), calls=%async_computation.1 | async-start | bytes 4194304 | tf_op jit(solution)/shard_map/all_to_all | solution.py:761
  47.2 112.8 %all-gather.6.cloned.1.call-start = ((), (), s32[]{:S(2)}) async-start(), calls=%async_computation.5 | async-start | bytes 2359296 | tf_op jit(solution)/shard_map/all_gather | solution.py:741
  48.0 264.3 %all-gather.10.cloned.1.call-start = ((), (), s32[]{:S(2)}) async-start(), calls=%async_computation.7 | async-start | bytes 6291456 | tf_op jit(solution)/shard_map/all_gather | solution.py:741
  90.9 2.3 copy-start.19
  90.9 3.2 copy-start.38
  90.9 3.3 copy-start.39
  90.9 227.8 %all-gather.12.cloned.1.call-start = ((), (), s32[]{:S(2)}) async-start(), calls=%async_computation.8 | async-start | bytes 3145728 | tf_op jit(solution)/shard_map/all_gather | solution.py:741
  91.6 227.1 %all-gather.8.cloned.1.call-start = ((), (), s32[]{:S(2)}) async-start(), calls=%async_computation.6 | async-start | bytes 8912896 | tf_op jit(solution)/shard_map/all_gather | solution.py:753
  94.1 710.4 %reduce-scatter.2.cloned.1.call-start = ((), (), s32[]{:S(2)}) async-start(), calls=%async_computation.9 | async-start | bytes 8912896 | tf_op jit(solution)/shard_map/reduce_scatter | solution.py:757
  143.2 4.1 copy-start.35
  144.3 15.7 %copy-start = (bf16[128,2048]{1,0:T(8,128)(2,1)S(1)}, bf16[128,2048]{1,0:T(8,128)(2,1)}, u32[]{:S(2)}) copy-start(bf16[128,2048]{1,0:T(8,128)(2,1)} %own_ref.1) | copy-start | bytes 1572868
  146.0 69.4 %copy-start.1 = (f32[2048,128]{1,0:T(8,128)}, f32[2048,128]{1,0:T(8,128)S(1)}, u32[]{:S(2)}) copy-start(f32[2048,128]{1,0:T(8,128)S(1)} %copy.122.sin_ref) | copy-start | bytes 3145732
  160.0 1.4 copy-start.8
  161.4 54.0 %copy-start.3 = (s32[2048,1]{1,0:T(8,128)S(1)}, s32[2048,1]{1,0:T(8,128)}, u32[]{:S(2)}) copy-start(s32[2048,1]{1,0:T(8,128)} %copy.123.open_ref) | copy-start | bytes 24580
  215.4 22.5 %copy-start.11 = (bf16[2048,128]{1,0:T(8,128)(2,1)}, bf16[2048,128]{1,0:T(8,128)(2,1)S(1)}, u32[]{:S(2)}) copy-start(bf16[2048,128]{1,0:T(8,128)(2,1)S(1)} %get-tuple-element.25.q_ref) | copy-start | bytes 1572868
  215.4 23.5 %copy-start.12 = (bf16[2048,128]{1,0:T(8,128)(2,1)}, bf16[2048,128]{1,0:T(8,128)(2,1)S(1)}, u32[]{:S(2)}) copy-start(bf16[2048,128]{1,0:T(8,128)(2,1)S(1)} %get-tuple-element.26.k_ref) | copy-start | bytes 1572868
  215.4 23.5 %copy-start.13 = (bf16[2048,128]{1,0:T(8,128)(2,1)}, bf16[2048,128]{1,0:T(8,128)(2,1)S(1)}, u32[]{:S(2)}) copy-start(bf16[2048,128]{1,0:T(8,128)(2,1)S(1)} %get-tuple-element.27.v_ref) | copy-start | bytes 1572868
  215.4 23.5 %copy-start.6 = (bf16[128,2048]{1,0:T(8,128)(2,1)S(1)}, bf16[128,2048]{1,0:T(8,128)(2,1)}, u32[]{:S(2)}) copy-start(bf16[128,2048]{1,0:T(8,128)(2,1)} %all_gather.20.b_ref.weight_ref) | copy-start | bytes 1572868
  237.8 72.2 %copy-start.10 = (f32[2048,2]{1,0:T(8,128)}, f32[2048,2]{1,0:T(8,128)S(1)}, u32[]{:S(2)}) copy-start(f32[2048,2]{1,0:T(8,128)S(1)} %get-tuple-element.32.lse_ref) | copy-start | bytes 49156
  377.3 2.2 copy-start.15
  379.5 59.6 %copy-start.18 = (f32[128,2048]{1,0:T(8,128)S(1)}, f32[128,2048]{1,0:T(8,128)}, u32[]{:S(2)}) copy-start(f32[128,2048]{1,0:T(8,128)} %copy-done.17) | copy-start | bytes 3145732
  439.1 1.0 copy-start.20
  439.1 2.3 copy-start.40
  439.4 2.1 copy-start.36
  542.3 1.5 copy-start.23
  543.7 19.1 %copy-start.30 = (bf16[2048,128]{1,0:T(8,128)(2,1)}, bf16[2048,128]{1,0:T(8,128)(2,1)S(1)}, u32[]{:S(2)}) copy-start(bf16[2048,128]{1,0:T(8,128)(2,1)S(1)} %convert.14) | copy-start | bytes 1572868
  559.6 12.5 %slice-start = ((s8[8388608]{0:T(1024)(128)(4,1)}), s8[4194304]{0:T(1024)(128)(4,1)S(1)}, s32[]{:S(2)}) async-start(s8[8388608]{0:T(1024)(128)(4,1)} %bitcast.111), calls=%async_computation.10 | async-start | bytes 8388608
  562.7 7.8 copy-start.26
  562.7 7.8 copy-start.28
  562.7 9.4 %copy-start.16 = (bf16[2048,1024]{1,0:T(8,128)(2,1)S(1)}, bf16[2048,1024]{1,0:T(8,128)(2,1)}, u32[]{:S(2)}) copy-start(bf16[2048,1024]{1,0:T(8,128)(2,1)} %get-tuple-element.30.a_ref) | copy-start | bytes 12582916
  562.8 9.4 %slice-start.1 = ((s8[8388608]{0:T(1024)(128)(4,1)}), s8[4194304]{0:T(1024)(128)(4,1)S(1)}, s32[]{:S(2)}) async-start(s8[8388608]{0:T(1024)(128)(4,1)} %bitcast.111), calls=%async_computation.11 | async-start | bytes 8388608
  570.6 1.6 copy-start.32
  570.7 20.4 %collective-permute-start = (bf16[1024,384]{1,0:T(8,128)(2,1)S(1)}, bf16[1024,384]{1,0:T(8,128)(2,1)S(1)}, u32[]{:S(2)}, u32[]{:S(2)}) collective-permute-start(bf16[1024,384]{1,0:T(8,128)(2,1)S(1)} %dynamic-slice_convert_fusion.2), channel_id=1, source_target_pairs={{0,16},{16,0},{1,17},{17,1},{2,18},{18,2},{3,19},{19,3},{4,20},{20... | collective-permute-start | bytes 2359304 | tf_op jit(solution)/shard_map/ppermute | solution.py:737
  581.1 3.3 copy-start.22
  586.1 50.0 %collective-permute-start.2 = (bf16[1024,1024]{1,0:T(8,128)(2,1)}, bf16[1024,1024]{1,0:T(8,128)(2,1)}, u32[]{:S(2)}, u32[]{:S(2)}) collective-permute-start(bf16[1024,1024]{1,0:T(8,128)(2,1)} %dynamic-slice_convert_fusion), channel_id=1, source_target_pairs={{0,16},{16,0},{1,17},{17,1},{2,18},{18,2},{3,19},{19,3},{4,20},{20... | collective-permute-start | bytes 6291464 | tf_op jit(solution)/shard_map/ppermute | solution.py:737
  593.6 47.5 %all-to-all-start.2 = ((bf16[16,64,384]{2,1,0:T(8,128)(2,1)}), bf16[16,64,384]{2,1,0:T(8,128)(2,1)S(1)}, u32[]{:S(2)}, u32[]{:S(2)}) async-start(bf16[16,64,384]{2,1,0:T(8,128)(2,1)} %bitcast.28), calls=%async_computation.3 | async-start | bytes 1572864 | tf_op jit(solution)/shard_map/all_to_all | solution.py:761
  599.9 163.4 %collective-permute-start.1 = (bf16[64,2048]{1,0:T(8,128)(2,1)}, bf16[64,2048]{1,0:T(8,128)(2,1)}, u32[]{:S(2)}, u32[]{:S(2)}) collective-permute-start(bf16[64,2048]{1,0:T(8,128)(2,1)} %dynamic-slice_convert_fusion.3), channel_id=1, source_target_pairs={{0,16},{16,0},{1,17},{17,1},{2,18},{18,2},{3,19},{19,3},{4,20},{20... | collective-permute-start | bytes 786440 | tf_op jit(solution)/shard_map/ppermute | solution.py:737
  641.0 144.2 %all-to-all-start.3 = ((bf16[16,64,1024]{2,1,0:T(8,128)(2,1)}), bf16[16,64,1024]{2,1,0:T(8,128)(2,1)}, u32[]{:S(2)}, u32[]{:S(2)}) async-start(bf16[16,64,1024]{2,1,0:T(8,128)(2,1)} %bitcast.79), calls=%async_computation.4 | async-start | bytes 4194304 | tf_op jit(solution)/shard_map/all_to_all | solution.py:761
  653.5 2.8 copy-start.25
  653.5 2.8 copy-start.27
  653.5 2.8 copy-start.29
  653.5 2.8 copy-start.31
  654.6 2.7 copy-start.9
  654.6 110.6 %collective-permute-start.3 = (bf16[256,2048]{1,0:T(8,128)(2,1)}, bf16[256,2048]{1,0:T(8,128)(2,1)}, u32[]{:S(2)}, u32[]{:S(2)}) collective-permute-start(bf16[256,2048]{1,0:T(8,128)(2,1)} %dynamic-slice_convert_fusion.1), channel_id=1, source_target_pairs={{0,16},{16,0},{1,17},{17,1},{2,18},{18,2},{3,19},{19,3},{4,20},{20... | collective-permute-start | bytes 3145736 | tf_op jit(solution)/shard_map/ppermute | solution.py:737
  801.7 2.8 copy-start.21
  (8 other events, 7.5 us)
Sparse Core Ops, SparseCore 0:
  50.2 28.5 all-gather.5
  91.0 66.7 all-gather.9
  159.4 35.3 all-gather.11
  196.8 91.4 all-gather.7
  448.5 108.7 reduce-scatter.1

commit v3 on v1

--- a/solution.py
+++ b/solution.py
@@ -14,6 +14,7 @@
 DOCS = 4
 EPS = 1e-05
 NEG = -1e30
+MESH = pl.DeviceIdType.MESH
 F32 = jnp.float32
 BF16 = jnp.bfloat16
 
@@ -161,6 +162,1164 @@
     )(queries, keys, values, grads, attended, log_total, opening)
 
 
+class Place:
+    def __init__(self):
+        self.dp = lax.axis_index("dp")
+        self.mine = lax.axis_index("seq")
+        self.count = lax.axis_size("seq")
+        self.length = self.count // 4
+        self.line = lax.div(self.mine, 4)
+        self.pair = lax.rem(lax.div(self.mine, 2), 2)
+        self.core = lax.rem(self.mine, 2)
+        self.slot = self.line * 2 + self.core
+
+    def index(self, line, pair, core):
+        return (line * 2 + pair) * 2 + core
+
+    def peer(self, slot, same):
+        pair = self.pair if same else 1 - self.pair
+        return self.index(lax.div(slot, 2), pair, lax.rem(slot, 2))
+
+    def device(self, line, pair, core):
+        return (self.dp, self.index(line, pair, core))
+
+    def sibling(self):
+        return self.device(self.line, self.pair, 1 - self.core)
+
+    def across(self):
+        return self.device(self.line, 1 - self.pair, self.core)
+
+    def above(self):
+        return self.device(self.line + 1, self.pair, self.core)
+
+    def below(self):
+        return self.device(self.line - 1, self.pair, self.core)
+
+    def partner(self):
+        return (1 - self.dp, self.mine)
+
+    def greet(self, partner=False):
+        barrier = pltpu.get_barrier_semaphore()
+
+        def signal(device):
+            pl.semaphore_signal(barrier, inc=1, device_id=device, device_id_type=MESH)
+
+        signal(self.sibling())
+        signal(self.across())
+        pl.when(self.line > 0)(lambda: signal(self.below()))
+        pl.when(self.line < self.length - 1)(lambda: signal(self.above()))
+        if partner:
+            signal(self.partner())
+        inner = (self.line > 0) & (self.line < self.length - 1)
+        pl.semaphore_wait(barrier, jnp.where(inner, 4, 3) + (1 if partner else 0))
+
+    def greet_all(self):
+        barrier = pltpu.get_barrier_semaphore()
+
+        def signal(device):
+            pl.semaphore_signal(barrier, inc=1, device_id=device, device_id_type=MESH)
+
+        signal(self.partner())
+
+        @pl.loop(1, self.count)
+        def _(ahead):
+            signal((self.dp, lax.rem(self.mine + ahead, self.count)))
+
+        pl.semaphore_wait(barrier, self.count)
+
+
+def remote(src, dst, send_sem, recv_sem, device):
+    return pltpu.make_async_remote_copy(
+        src_ref=src,
+        dst_ref=dst,
+        send_sem=send_sem,
+        recv_sem=recv_sem,
+        device_id=device,
+        device_id_type=MESH,
+    )
+
+
+class Spread:
+    def __init__(self, here, same, copies):
+        self.here, self.same, self.copies = here, same, copies
+        self.slots = here.count // 2
+
+    def each(self, visit):
+        @pl.loop(1 if self.same else 0, self.slots)
+        def _(ahead):
+            slot = lax.rem(self.here.slot + ahead, self.slots)
+            visit(self.here.peer(slot, self.same), slot)
+
+    def start(self):
+        def visit(peer, slot):
+            for one in self.copies(peer, self.here.mine, self.here.slot, slot):
+                one.start()
+
+        self.each(visit)
+
+    def finish(self):
+        def visit(peer, slot):
+            for one in self.copies(peer, peer, slot, slot):
+                one.wait()
+
+        self.each(visit)
+
+
+def block_spread(here, same, blocks, into, sems):
+    def copies(peer, sender, at, sem):
+        return [
+            remote(
+                blocks.at[peer],
+                into.at[at],
+                sems.at[0, sem],
+                sems.at[1, at],
+                (here.dp, peer),
+            )
+        ]
+
+    return Spread(here, same, copies)
+
+
+def feed_spread(here, same, weights, into, sems):
+    dp = lax.axis_size("dp")
+    columns = into.shape[2] // (dp * len(weights))
+
+    def copies(peer, sender, at, sem):
+        made = []
+        for kind, weight in enumerate(weights):
+            for half in range(dp):
+                part = kind * dp + half
+                begin = pl.multiple_of((half * here.count + peer) * columns, columns)
+                made.append(
+                    remote(
+                        weight.at[:, pl.ds(begin, columns)],
+                        into.at[at, :, pl.ds(part * columns, columns)],
+                        sems.at[0, sem, part],
+                        sems.at[1, at, part],
+                        (here.dp, peer),
+                    )
+                )
+        return made
+
+    return Spread(here, same, copies)
+
+
+def nothing():
+    pass
+
+
+def gather_units(here, own_ref, buf, send_sems, recv_sems, compute, between=None, ready=0):
+    length = here.length
+    last = length - 1
+    steps = 2 * length
+    half = own_ref.shape[0] // 2
+    mine = here.mine
+    shorter = jnp.minimum(here.line, last - here.line)
+    longer = jnp.where(here.line < last - here.line, 1, -1)
+
+    def column(j):
+        i = j - 1
+        paired = jnp.where(i % 2 == 0, here.line - i // 2 - 1, here.line + i // 2 + 1)
+        single = here.line + longer * (i - shorter + 1)
+        return jnp.where(j == 0, here.line, jnp.where(i < 2 * shorter, paired, single))
+
+    def copy(way, device, block, part):
+        ref = buf.at[block, part]
+        return remote(
+            ref, ref, send_sems.at[way, block, part], recv_sems.at[block, part], device
+        )
+
+    def up(block, part):
+        return copy(0, here.above(), block, part)
+
+    def down(block, part):
+        return copy(1, here.below(), block, part)
+
+    def across(block, part):
+        return copy(2, here.across(), block, part)
+
+    def sideways(block, part):
+        return copy(3, here.sibling(), block, part)
+
+    def unit(number):
+        in_column = (number % 2 == 1) & (number < steps - 1) | (number == 0)
+        later = jnp.where(number == steps - 1, last, number // 2 - 1)
+        line = column(jnp.where(in_column, (number + 1) // 2, later))
+        pair = jnp.where(in_column, here.pair, 1 - here.pair)
+        other = here.index(line, pair, 1 - here.core)
+        sideways(other, 0).wait_recv()
+        sideways(other, 1).wait_recv()
+        compute(number, here.index(line, pair, 0))
+
+    for part in range(2):
+        buf[mine, part] = own_ref[pl.ds(part * half, half), :]
+        pl.when(here.line < last)(lambda part=part: up(mine, part).start())
+        pl.when(here.line > 0)(lambda part=part: down(mine, part).start())
+        across(mine, part).start()
+        sideways(mine, part).start()
+
+    @pl.loop(0, steps)
+    def _(step):
+        part = step % 2
+        far = step // 2 + 1
+
+        @pl.when(here.line >= far)
+        def _():
+            block = here.index(here.line - far, here.pair, here.core)
+            up(block, part).wait_recv()
+            pl.when(here.line < last)(lambda: up(block, part).start())
+            sideways(block, part).start()
+
+        @pl.when(here.line + far <= last)
+        def _():
+            block = here.index(here.line + far, here.pair, here.core)
+            down(block, part).wait_recv()
+            pl.when(here.line > 0)(lambda: down(block, part).start())
+            sideways(block, part).start()
+
+        @pl.when(step + 2 < steps)
+        def _():
+            across(here.index(column(step // 2 + 1), here.pair, here.core), part).start()
+
+        block = here.index(column(step // 2), 1 - here.pair, here.core)
+        across(block, part).wait_recv()
+        sideways(block, part).start()
+
+        if between is None:
+            unit(step)
+        else:
+            between(step)
+            begin = jnp.where(step == ready, 0, step)
+            end = jnp.where(step < ready, step, step + 1)
+
+            @pl.loop(begin, end)
+            def _(number):
+                unit(number)
+
+    @pl.loop(0, length)
+    def _(line):
+        for part in range(2):
+            block = here.index(line, here.pair, here.core)
+
+            @pl.when((line <= here.line) & (here.line < last))
+            def _():
+                up(block, part).wait_send()
+
+            @pl.when((line >= here.line) & (here.line > 0))
+            def _():
+                down(block, part).wait_send()
+
+            across(block, part).wait_send()
+            sideways(block, part).wait_send()
+            sideways(here.index(line, 1 - here.pair, here.core), part).wait_send()
+
+
+def gather_scratch(seq, rows, width):
+    return [
+        pltpu.VMEM((seq, 2, rows // 2, width), BF16),
+        pltpu.SemaphoreType.DMA((4, seq, 2)),
+        pltpu.SemaphoreType.DMA((seq, 2)),
+    ]
+
+
+def unit_rows(first, rows):
+    return pl.ds(pl.multiple_of(first * rows, 2 * rows), 2 * rows)
+
+
+def take_unit(buf, first):
+    blocks = buf[pl.ds(first, 2)]
+    return blocks.reshape(-1, blocks.shape[-1])
+
+
+class UnitStore:
+    def __init__(self, buf, out_ref, sems):
+        self.buf, self.out_ref, self.sems = buf, out_ref, sems
+
+    def copies(self, number, first):
+        half = self.buf.shape[2]
+        made = []
+        for block in range(2):
+            for part in range(2):
+                begin = ((first + block) * 2 + part) * half
+                made.append(
+                    pltpu.make_async_copy(
+                        self.buf.at[first + block, part],
+                        self.out_ref.at[pl.ds(pl.multiple_of(begin, half), half)],
+                        self.sems.at[number, block, part],
+                    )
+                )
+        return made
+
+    def start(self, number, first):
+        for one in self.copies(number, first):
+            one.start()
+
+    def finish(self):
+        @pl.loop(0, self.sems.shape[0])
+        def _(number):
+            for one in self.copies(number, 0):
+                one.wait()
+
+
+def params(call_id, mebibytes):
+    return pltpu.CompilerParams(
+        collective_id=call_id, has_side_effects=True, vmem_limit_bytes=mebibytes << 20
+    )
+
+
+def cost(flops, bytes_accessed):
+    return pl.CostEstimate(flops=flops, bytes_accessed=bytes_accessed, transcendentals=0)
+
+
+VMEM = pl.BlockSpec(memory_space=pltpu.VMEM)
+HBM = pl.BlockSpec(memory_space=pl.ANY)
+
+
+def rotated(values, cosine, sine):
+    cols = values.shape[1]
+    lane = lax.broadcasted_iota(jnp.int32, values.shape, 1)
+    ahead = pltpu.roll(values, cols - HEAD_DIM // 2, 1)
+    behind = pltpu.roll(values, HEAD_DIM // 2, 1)
+    swapped = jnp.where(lane % HEAD_DIM < HEAD_DIM // 2, ahead, behind)
+    return values * cosine + swapped * sine
+
+
+def project_kernel(
+    own_ref,
+    blocks_ref,
+    gate_ref,
+    up_ref,
+    down_ref,
+    output_ref,
+    cos_ref,
+    sin_ref,
+    normed_ref,
+    q_ref,
+    k_ref,
+    v_ref,
+    weight_ref,
+    feed_ref,
+    down_out_ref,
+    output_out_ref,
+    buf,
+    send_sems,
+    recv_sems,
+    store_sems,
+    near_sems,
+    far_sems,
+    feed_sems,
+    swap_sems,
+    local_sems,
+    pair_sems,
+):
+    here = Place()
+    here.greet_all()
+    cols = q_ref.shape[1]
+    rows = own_ref.shape[0]
+    dp = here.dp
+
+    def weight_spread(same, sems):
+        def copies(peer, sender, at, sem):
+            return [
+                remote(
+                    blocks_ref.at[peer],
+                    weight_ref.at[dp, sender],
+                    sems.at[0, sem],
+                    sems.at[1, at],
+                    (dp, peer),
+                )
+            ]
+
+        return Spread(here, same, copies)
+
+    near = weight_spread(True, near_sems)
+    far = weight_spread(False, far_sems)
+    far.start()
+    near.start()
+    weight_ref[dp, here.mine] = blocks_ref[here.mine]
+    swaps = []
+    for number, (src, dst) in enumerate([(down_ref, down_out_ref), (output_ref, output_out_ref)]):
+        swaps.append(
+            remote(src, dst.at[dp], swap_sems.at[0, number], swap_sems.at[1, number], here.partner())
+        )
+        swaps.append(pltpu.make_async_copy(src, dst.at[dp], local_sems.at[number]))
+    for one in swaps:
+        one.start()
+    feed = feed_spread(here, True, (gate_ref, up_ref), feed_ref, feed_sems)
+    columns = feed_ref.shape[2] // 4
+    own_feed = []
+    for kind, weight in enumerate((gate_ref, up_ref)):
+        for half in range(2):
+            part = kind * 2 + half
+            begin = pl.multiple_of((half * here.count + here.mine) * columns, columns)
+            own_feed.append(
+                pltpu.make_async_copy(
+                    weight.at[:, pl.ds(begin, columns)],
+                    feed_ref.at[here.slot, :, pl.ds(part * columns, columns)],
+                    local_sems.at[2 + part],
+                )
+            )
+    for one in own_feed:
+        one.start()
+
+    def pair_copy(source, sender):
+        return remote(
+            weight_ref.at[source, sender],
+            weight_ref.at[source, sender],
+            pair_sems.at[0, sender],
+            pair_sems.at[1, sender],
+            here.partner(),
+        )
+
+    def between(step):
+        @pl.when(step == 0)
+        def _():
+            feed.start()
+
+        @pl.when(step == 1)
+        def _():
+            near.finish()
+            far.finish()
+
+            @pl.loop(0, here.count)
+            def _(sender):
+                pair_copy(dp, sender).start()
+
+        @pl.when(step == 3)
+        def _():
+            @pl.loop(0, here.count)
+            def _(sender):
+                pair_copy(1 - dp, sender).wait_recv()
+
+    store = UnitStore(buf, normed_ref, store_sems)
+
+    def compute(number, first):
+        store.start(number, first)
+        weight = weight_ref[...].reshape(-1, weight_ref.shape[-1])
+        qkv = dot(take_unit(buf, first), weight)
+        where = unit_rows(first, rows)
+        cosine = cos_ref[where, :]
+        sine = sin_ref[where, :]
+        scale = BF16(1.0 / math.sqrt(HEAD_DIM))
+        q_ref[where, :] = rotated(qkv[:, :cols], cosine, sine).astype(BF16) * scale
+        k_ref[where, :] = rotated(qkv[:, cols : 2 * cols], cosine, sine).astype(BF16)
+        v_ref[where, :] = qkv[:, 2 * cols :].astype(BF16)
+
+    gather_units(here, own_ref, buf, send_sems, recv_sems, compute, between, 3)
+
+    @pl.loop(0, here.count)
+    def _(sender):
+        pair_copy(dp, sender).wait_send()
+
+    store.finish()
+    feed.finish()
+    for one in swaps + own_feed:
+        one.wait()
+
+
+def gather_project(own, blocks, gate, up, down, output, cosine, sine, call_id):
+    seq = lax.axis_size("seq")
+    rows, width = own.shape
+    cols = cosine.shape[1]
+    slab = gate.shape[0]
+    head = jax.ShapeDtypeStruct((seq * rows, cols), BF16)
+    feed_cols = 4 * down.shape[0]
+    dma = pltpu.SemaphoreType.DMA
+    return pl.pallas_call(
+        project_kernel,
+        out_shape=[
+            jax.ShapeDtypeStruct((seq * rows, width), BF16),
+            head,
+            head,
+            head,
+            jax.ShapeDtypeStruct((2, *blocks.shape), BF16),
+            jax.ShapeDtypeStruct((seq // 2, slab, feed_cols), BF16),
+            jax.ShapeDtypeStruct((2, *down.shape), BF16),
+            jax.ShapeDtypeStruct((2, *output.shape), BF16),
+        ],
+        in_specs=[VMEM, VMEM, HBM, HBM, HBM, HBM, VMEM, VMEM],
+        out_specs=[HBM, VMEM, VMEM, VMEM, VMEM, HBM, HBM, HBM],
+        scratch_shapes=gather_scratch(seq, rows, width)
+        + [
+            dma((seq // 2, 2, 2)),
+            dma((2, seq // 2)),
+            dma((2, seq // 2)),
+            dma((2, seq // 2, 4)),
+            dma((2, 2)),
+            dma((6,)),
+            dma((2, seq)),
+        ],
+        compiler_params=params(call_id, 40),
+        cost_estimate=cost(2 * seq * rows * width * 3 * cols, 4 * seq * rows * width),
+    )(own, blocks, gate, up, down, output, cosine, sine)
+
+
+def attention_feed_kernel(
+    block,
+    q_ref,
+    k_ref,
+    v_ref,
+    open_ref,
+    gate_ref,
+    up_ref,
+    out_ref,
+    lse_ref,
+    feed_ref,
+    feed_sems,
+):
+    here = Place()
+    feed = feed_spread(here, False, (gate_ref, up_ref), feed_ref, feed_sems)
+
+    @pl.when(pl.program_id(0) == 0)
+    def _():
+        here.greet_all()
+        feed.start()
+
+    attention_kernel(block, q_ref, k_ref, v_ref, open_ref, out_ref, lse_ref)
+
+    @pl.when(pl.program_id(0) == pl.num_programs(0) - 1)
+    def _():
+        feed.finish()
+
+
+def attention_feed(queries, keys, values, opening, gate, up, feed_cols, block, call_id):
+    seq = lax.axis_size("seq")
+    rows, cols = queries.shape
+    heads = cols // HEAD_DIM
+    tiled = lambda width: pl.BlockSpec((block, width), lambda i: (i, 0))
+    whole = pl.BlockSpec((rows, cols), lambda i: (0, 0))
+    return pl.pallas_call(
+        functools.partial(attention_feed_kernel, block),
+        grid=(rows // block,),
+        in_specs=[tiled(cols), whole, whole, tiled(1), HBM, HBM],
+        out_specs=[tiled(cols), tiled(heads), HBM],
+        out_shape=[
+            jax.ShapeDtypeStruct((rows, cols), F32),
+            jax.ShapeDtypeStruct((rows, heads), F32),
+            jax.ShapeDtypeStruct((seq // 2, gate.shape[0], feed_cols), BF16),
+        ],
+        scratch_shapes=[pltpu.SemaphoreType.DMA((2, seq // 2, 4))],
+        compiler_params=params(call_id, 48),
+        cost_estimate=cost(2 * rows * rows * cols, 10 * rows * cols),
+    )(queries, keys, values, opening, gate, up)
+
+
+def scatter_rows_of_product(
+    here,
+    transposed,
+    parts,
+    tile,
+    a_ref,
+    b_ref,
+    out_ref,
+    core_out,
+    core_in,
+    pair_out,
+    pair_in,
+    line_out,
+    up_in,
+    down_in,
+    held,
+    core_sems,
+    pair_sems,
+    line_sems,
+    up_sems,
+    down_sems,
+    between=nothing,
+    middle=nothing,
+):
+    length = here.length
+    rows = out_ref.shape[0]
+    width = out_ref.shape[1] // parts
+    tiles = width // tile
+    steps = length * parts
+
+    def target(i):
+        ups = length - 1 - here.line
+        near = here.line < length // 2
+        if_near = jnp.where(i < ups, length - 1 - i, i - ups)
+        if_far = jnp.where(i < here.line, i, length - 1 - (i - here.line))
+        return jnp.where(i == length - 1, here.line, jnp.where(near, if_near, if_far))
+
+    def product(line, pair, core, part, use):
+        first = pl.multiple_of(here.index(line, pair, core) * rows, rows)
+        a = a_ref[pl.ds(first, rows), :]
+
+        @pl.loop(0, tiles)
+        def _(t):
+            into = pl.ds(pl.multiple_of(t * tile, tile), tile)
+            cols = pl.ds(pl.multiple_of(part * width + t * tile, tile), tile)
+            use(dot_t(a, b_ref[cols, :]) if transposed else dot(a, b_ref[:, cols]), into)
+
+    def core_copy(slot):
+        return remote(
+            core_out.at[slot],
+            core_in.at[slot],
+            core_sems.at[0, slot],
+            core_sems.at[1, slot],
+            here.sibling(),
+        )
+
+    def pair_copy(slot):
+        return remote(
+            pair_out.at[slot],
+            pair_in.at[slot],
+            pair_sems.at[0, slot],
+            pair_sems.at[1, slot],
+            here.across(),
+        )
+
+    def up_copy(slot, into):
+        return remote(
+            line_out.at[slot], up_in.at[into], line_sems.at[slot], up_sems.at[into], here.above()
+        )
+
+    def down_copy(slot, into):
+        return remote(
+            line_out.at[slot], down_in.at[into], line_sems.at[slot], down_sems.at[into], here.below()
+        )
+
+    def for_sibling(step, pair, slot):
+        def use(value, cols):
+            core_out[slot, :, cols] = value.astype(BF16)
+
+        product(target(step // parts), pair, 1 - here.core, step % parts, use)
+        core_copy(slot).start()
+
+    for_sibling(0, 1 - here.pair, 0)
+
+    @pl.loop(0, steps)
+    def _(step):
+        pl.when(step < steps - 1)(lambda: for_sibling(step + 1, 1 - here.pair, step + 1))
+        core_copy(step).wait_recv()
+
+        def use(value, cols):
+            pair_out[step, :, cols] = (value + core_in[step, :, cols].astype(F32)).astype(BF16)
+
+        product(target(step // parts), 1 - here.pair, here.core, step % parts, use)
+        pair_copy(step).start()
+
+    for_sibling(0, here.pair, steps)
+    between()
+
+    @pl.loop(0, steps)
+    def _(step):
+        pl.when(step < steps - 1)(lambda: for_sibling(step + 1, here.pair, steps + step + 1))
+        core_copy(steps + step).wait_recv()
+        line = target(step // parts)
+        part = step % parts
+        into = line * parts + part
+
+        def use(value, cols):
+            held[:, cols] = value + core_in[steps + step, :, cols].astype(F32)
+
+        product(line, here.pair, here.core, part, use)
+        pair_copy(step).wait_recv()
+        from_above = (line <= here.line) & (here.line < length - 1)
+        from_below = (line >= here.line) & (here.line > 0)
+        held[...] += pair_in[step].astype(F32)
+
+        @pl.when(from_above)
+        def _():
+            down_copy(0, into).wait_recv()
+            held[...] += down_in[into].astype(F32)
+
+        @pl.when(from_below)
+        def _():
+            up_copy(0, into).wait_recv()
+            held[...] += up_in[into].astype(F32)
+
+        @pl.when(line == here.line)
+        def _():
+            out_ref[:, pl.ds(pl.multiple_of(part * width, width), width)] = held[...]
+
+        @pl.when(line < here.line)
+        def _():
+            line_out[step] = held[...].astype(BF16)
+            down_copy(step, into).start()
+
+        @pl.when(line > here.line)
+        def _():
+            line_out[step] = held[...].astype(BF16)
+            up_copy(step, into).start()
+
+        if middle is not nothing:
+            pl.when(step == steps // 2)(middle)
+
+    @pl.loop(0, steps)
+    def _(step):
+        core_copy(step).wait_send()
+        core_copy(steps + step).wait_send()
+        pair_copy(step).wait_send()
+        line = target(step // parts)
+        pl.when(line < here.line)(lambda: down_copy(step, 0).wait_send())
+        pl.when(line > here.line)(lambda: up_copy(step, 0).wait_send())
+
+
+SCATTER_PARTS = 2
+SCATTER_SCRATCH = 13
+
+
+def scatter_scratch(seq, rows, width):
+    steps = seq // 4 * SCATTER_PARTS
+    block = (rows, width // SCATTER_PARTS)
+    dma = pltpu.SemaphoreType.DMA
+    return [
+        pltpu.VMEM((2 * steps, *block), BF16),
+        pltpu.VMEM((2 * steps, *block), BF16),
+        pltpu.VMEM((steps, *block), BF16),
+        pltpu.VMEM((steps, *block), BF16),
+        pltpu.VMEM((steps, *block), BF16),
+        pltpu.VMEM((steps, *block), BF16),
+        pltpu.VMEM((steps, *block), BF16),
+        pltpu.VMEM(block, F32),
+        dma((2, 2 * steps)),
+        dma((2, steps)),
+        dma((steps,)),
+        dma((steps,)),
+        dma((steps,)),
+    ]
+
+
+def scatter_tile(width):
+    return min(width // SCATTER_PARTS, 512)
+
+
+def scatter_cost(a, width):
+    return cost(2 * a.shape[0] * a.shape[1] * width, 4 * a.shape[0] * width)
+
+
+def scatter_kernel(tile, a_ref, b_ref, out_ref, *scratch):
+    here = Place()
+    here.greet()
+    scatter_rows_of_product(here, False, SCATTER_PARTS, tile, a_ref, b_ref, out_ref, *scratch)
+
+
+def product_scatter(a, b, call_id):
+    seq = lax.axis_size("seq")
+    rows = a.shape[0] // seq
+    width = b.shape[1]
+    return pl.pallas_call(
+        functools.partial(scatter_kernel, scatter_tile(width)),
+        out_shape=jax.ShapeDtypeStruct((rows, width), F32),
+        in_specs=[VMEM, VMEM],
+        out_specs=VMEM,
+        scratch_shapes=scatter_scratch(seq, rows, width),
+        compiler_params=params(call_id, 48),
+        cost_estimate=scatter_cost(a, width),
+    )(a, b)
+
+
+def scatter_feed_kernel(tile, a_ref, b_ref, near_ref, far_ref, out_ref, feed_ref, *scratch):
+    here = Place()
+    here.greet(partner=True)
+    swap_sems, local_sems = scratch[SCATTER_SCRATCH:]
+    slots = near_ref.shape[0]
+
+    def copies(half, ref, slot):
+        place = feed_ref.at[here.dp, here.peer(slot, half == 0)]
+        return (
+            remote(
+                ref.at[slot],
+                place,
+                swap_sems.at[0, half, slot],
+                swap_sems.at[1, half, slot],
+                here.partner(),
+            ),
+            pltpu.make_async_copy(ref.at[slot], place, local_sems.at[half, slot]),
+        )
+
+    @pl.loop(0, slots)
+    def _(slot):
+        for half, ref in enumerate((near_ref, far_ref)):
+            for one in copies(half, ref, slot):
+                one.start()
+
+    scatter_rows_of_product(
+        here, False, SCATTER_PARTS, tile, a_ref, b_ref, out_ref, *scratch[:SCATTER_SCRATCH]
+    )
+
+    @pl.loop(0, slots)
+    def _(slot):
+        for half, ref in enumerate((near_ref, far_ref)):
+            for one in copies(half, ref, slot):
+                one.wait()
+
+
+def product_scatter_feed(a, b, near, far, call_id):
+    seq = lax.axis_size("seq")
+    rows = a.shape[0] // seq
+    width = b.shape[1]
+    dma = pltpu.SemaphoreType.DMA
+    return pl.pallas_call(
+        functools.partial(scatter_feed_kernel, scatter_tile(width)),
+        out_shape=[
+            jax.ShapeDtypeStruct((rows, width), F32),
+            jax.ShapeDtypeStruct((2, seq, *near.shape[1:]), BF16),
+        ],
+        in_specs=[VMEM, VMEM, HBM, HBM],
+        out_specs=[VMEM, HBM],
+        scratch_shapes=scatter_scratch(seq, rows, width)
+        + [dma((2, 2, seq // 2)), dma((2, seq // 2))],
+        compiler_params=params(call_id, 40),
+        cost_estimate=scatter_cost(a, width),
+    )(a, b, near, far)
+
+
+def feed_kernel(
+    own_ref,
+    grad_ref,
+    feed_ref,
+    down_ref,
+    normed_ref,
+    hidden_ref,
+    back_ref,
+    buf,
+    send_sems,
+    recv_sems,
+    store_sems,
+):
+    here = Place()
+    here.greet()
+    rows = own_ref.shape[0]
+    hidden = hidden_ref.shape[1]
+    tile = 256
+    store = UnitStore(buf, normed_ref, store_sems)
+
+    def compute(number, first):
+        store.start(number, first)
+        where = unit_rows(first, rows)
+        normed = take_unit(buf, first)
+        grad = grad_ref[where, :]
+
+        @pl.loop(0, hidden // tile)
+        def _(t):
+            cols = pl.ds(pl.multiple_of(t * tile, tile), tile)
+            later = pl.ds(pl.multiple_of(hidden + t * tile, tile), tile)
+            gate = dot(normed, feed_ref[:, cols])
+            upward = dot(normed, feed_ref[:, later])
+            hidden_grad = dot_t(grad, down_ref[cols, :])
+            sigmoid = jax.nn.sigmoid(gate)
+            silu = gate * sigmoid
+            hidden_ref[where, cols] = (silu * upward).astype(BF16)
+            back_ref[where, cols] = (
+                hidden_grad * upward * sigmoid * (1.0 + gate * (1.0 - sigmoid))
+            ).astype(BF16)
+            back_ref[where, later] = (hidden_grad * silu).astype(BF16)
+
+    gather_units(here, own_ref, buf, send_sems, recv_sems, compute)
+    store.finish()
+
+
+def gather_feed(own, grad_out, feed_weight, down_weight, call_id):
+    seq = lax.axis_size("seq")
+    rows, width = own.shape
+    hidden = down_weight.shape[0]
+    return pl.pallas_call(
+        feed_kernel,
+        out_shape=[
+            jax.ShapeDtypeStruct((seq * rows, width), BF16),
+            jax.ShapeDtypeStruct((seq * rows, hidden), BF16),
+            jax.ShapeDtypeStruct((seq * rows, 2 * hidden), BF16),
+        ],
+        in_specs=[VMEM] * 4,
+        out_specs=[HBM, VMEM, VMEM],
+        scratch_shapes=gather_scratch(seq, rows, width)
+        + [pltpu.SemaphoreType.DMA((seq // 2, 2, 2))],
+        compiler_params=params(call_id, 56),
+        cost_estimate=cost(6 * seq * rows * width * hidden, 6 * seq * rows * width),
+    )(own, grad_out, feed_weight, down_weight)
+
+
+def back_kernel(
+    own_ref,
+    weight_ref,
+    attended_ref,
+    share_ref,
+    grad_ref,
+    part_ref,
+    came_ref,
+    buf,
+    send_sems,
+    recv_sems,
+    swap_sems,
+):
+    here = Place()
+    here.greet(partner=True)
+    rows = own_ref.shape[0]
+    width = own_ref.shape[1]
+    tile = 512
+    swap = remote(
+        share_ref.at[1 - here.dp], came_ref, swap_sems.at[0], swap_sems.at[1], here.partner()
+    )
+    swap.start()
+    part_ref[...] = jnp.zeros_like(part_ref)
+
+    def compute(number, first):
+        where = unit_rows(first, rows)
+        unit = take_unit(buf, first)
+        grad_ref[where, :] = dot_t(unit, weight_ref[...]).astype(BF16)
+        attended = attended_ref[where, :]
+        for t in range(width // tile):
+            cols = slice(t * tile, (t + 1) * tile)
+            part_ref[:, cols] += t_dot(attended, unit[:, cols])
+
+    gather_units(here, own_ref, buf, send_sems, recv_sems, compute)
+    swap.wait()
+
+
+def gather_back(own, weight, attended, share, call_id):
+    seq = lax.axis_size("seq")
+    rows, width = own.shape
+    cols = weight.shape[0]
+    return pl.pallas_call(
+        back_kernel,
+        out_shape=[
+            jax.ShapeDtypeStruct((seq * rows, cols), BF16),
+            jax.ShapeDtypeStruct((cols, width), F32),
+            jax.ShapeDtypeStruct(share.shape[1:], BF16),
+        ],
+        in_specs=[VMEM] * 3 + [HBM],
+        out_specs=[VMEM] * 2 + [HBM],
+        scratch_shapes=gather_scratch(seq, rows, width) + [pltpu.SemaphoreType.DMA((2,))],
+        compiler_params=params(call_id, 40),
+        cost_estimate=cost(4 * seq * rows * width * cols, 4 * seq * rows * width),
+    )(own, weight, attended, share)
+
+
+def attention_back_feed_kernel(
+    block,
+    q_ref,
+    k_ref,
+    v_ref,
+    g_ref,
+    att_ref,
+    lse_ref,
+    open_ref,
+    cos_ref,
+    sin_ref,
+    blocks_ref,
+    down_ref,
+    output_ref,
+    back_ref,
+    feed_ref,
+    down_out_ref,
+    output_out_ref,
+    dq_ref,
+    dk_ref,
+    dv_ref,
+    feed_sems,
+    swap_sems,
+):
+    here = Place()
+    tile = pl.program_id(0)
+    cols = q_ref.shape[1]
+    feed = block_spread(here, False, blocks_ref, feed_ref, feed_sems)
+    swaps = [
+        remote(src, dst, swap_sems.at[0, number], swap_sems.at[1, number], here.partner())
+        for number, (src, dst) in enumerate(
+            [(down_ref, down_out_ref), (output_ref, output_out_ref)]
+        )
+    ]
+
+    @pl.when(tile == 0)
+    def _():
+        here.greet_all()
+        feed.start()
+        for one in swaps:
+            one.start()
+
+    attention_back_kernel(
+        block, q_ref, k_ref, v_ref, g_ref, att_ref, lse_ref, open_ref, dq_ref, dk_ref, dv_ref
+    )
+    where = pl.ds(pl.multiple_of(tile * block, block), block)
+    scale = 1.0 / math.sqrt(HEAD_DIM)
+    cosine = cos_ref[where, :]
+    sine = sin_ref[where, :]
+    back_ref[where, :cols] = rotated(dq_ref[...] * scale, cosine, -sine).astype(BF16)
+
+    @pl.when(tile == pl.num_programs(0) - 1)
+    def _():
+        @pl.loop(0, pl.num_programs(0))
+        def _(i):
+            rows = pl.ds(pl.multiple_of(i * block, block), block)
+            keys = rotated(dk_ref[rows, :], cos_ref[rows, :], -sin_ref[rows, :])
+            back_ref[rows, cols : 2 * cols] = keys.astype(BF16)
+            back_ref[rows, 2 * cols :] = dv_ref[rows, :].astype(BF16)
+
+        feed.finish()
+        for one in swaps:
+            one.wait()
+
+
+def attention_back_feed(
+    queries,
+    keys,
+    values,
+    grads,
+    attended,
+    log_total,
+    opening,
+    cosine,
+    sine,
+    blocks,
+    down,
+    output,
+    block,
+    call_id,
+):
+    seq = lax.axis_size("seq")
+    rows, cols = queries.shape
+    heads = cols // HEAD_DIM
+    tiled = lambda width: pl.BlockSpec((block, width), lambda i: (i, 0))
+    whole = pl.BlockSpec((rows, cols), lambda i: (0, 0))
+    dma = pltpu.SemaphoreType.DMA
+    return pl.pallas_call(
+        functools.partial(attention_back_feed_kernel, block),
+        grid=(rows // block,),
+        in_specs=[tiled(cols), whole, whole, tiled(cols), tiled(cols), tiled(heads), tiled(1)]
+        + [whole, whole, HBM, HBM, HBM],
+        out_specs=[pl.BlockSpec((rows, 3 * cols), lambda i: (0, 0)), HBM, HBM, HBM],
+        out_shape=[
+            jax.ShapeDtypeStruct((rows, 3 * cols), BF16),
+            jax.ShapeDtypeStruct((seq // 2, *blocks.shape[1:]), BF16),
+            jax.ShapeDtypeStruct(down.shape, BF16),
+            jax.ShapeDtypeStruct(output.shape, BF16),
+        ],
+        scratch_shapes=[
+            pltpu.VMEM((block, cols), F32),
+            pltpu.VMEM((rows, cols), F32),
+            pltpu.VMEM((rows, cols), F32),
+            dma((2, seq // 2)),
+            dma((2, 2)),
+        ],
+        compiler_params=params(call_id, 60),
+        cost_estimate=cost(5 * rows * rows * cols, 20 * rows * cols),
+    )(
+        queries,
+        keys,
+        values,
+        grads,
+        attended,
+        log_total,
+        opening,
+        cosine,
+        sine,
+        blocks,
+        down,
+        output,
+    )
+
+
+def scatter_last_kernel(
+    tile,
+    a_ref,
+    b_ref,
+    normed_ref,
+    blocks_ref,
+    out_ref,
+    feed_ref,
+    qkv_ref,
+    *scratch,
+):
+    here = Place()
+    here.greet_all()
+    whole, away, came, sums, feed_sems, near_sems, far_sems, swap_sems, local_sem = scratch[
+        SCATTER_SCRATCH:
+    ]
+    feed = block_spread(here, True, blocks_ref, feed_ref, feed_sems)
+    feed.start()
+    own_feed = pltpu.make_async_copy(
+        blocks_ref.at[here.mine], feed_ref.at[here.slot], local_sem.at[0]
+    )
+    own_feed.start()
+    swap = remote(away, came, swap_sems.at[0], swap_sems.at[1], here.partner())
+    near = block_spread(here, True, sums, qkv_ref.at[0], near_sems)
+    far = block_spread(here, False, sums, qkv_ref.at[1], far_sems)
+    half = away.shape[0]
+    chunk = min(half, 512)
+    chunks = half // chunk
+
+    def between():
+        @pl.loop(0, 2 * chunks)
+        def _(i):
+            first = pl.multiple_of(i * chunk, chunk)
+            part = t_dot(normed_ref[:, pl.ds(first, chunk)], a_ref[...])
+            whole[pl.ds(first, chunk), :] = part
+
+        @pl.loop(0, chunks)
+        def _(i):
+            into = pl.ds(pl.multiple_of(i * chunk, chunk), chunk)
+            first = pl.multiple_of((1 - here.dp) * half + i * chunk, chunk)
+            away[into, :] = whole[pl.ds(first, chunk), :].astype(BF16)
+
+        swap.start()
+
+    def middle():
+        swap.wait_recv()
+        slab = sums.shape[1]
+
+        @pl.loop(0, here.count)
+        def _(i):
+            rows = pl.ds(pl.multiple_of(i * slab, slab), slab)
+            own = pl.ds(pl.multiple_of(here.dp * half + i * slab, slab), slab)
+            sums[i] = (whole[own, :] + came[rows, :].astype(F32)).astype(BF16)
+
+        qkv_ref[0, here.slot] = sums[here.mine]
+        far.start()
+        near.start()
+
+    scatter_rows_of_product(
+        here,
+        True,
+        SCATTER_PARTS,
+        tile,
+        a_ref,
+        b_ref,
+        out_ref,
+        *scratch[:SCATTER_SCRATCH],
+        between,
+        middle,
+    )
+    swap.wait_send()
+    near.finish()
+    far.finish()
+    feed.finish()
+    own_feed.wait()
+
+
+def product_scatter_last(a, b, normed, blocks, call_id):
+    seq = lax.axis_size("seq")
+    rows = a.shape[0] // seq
+    width, cols = b.shape
+    slab = blocks.shape[1]
+    dma = pltpu.SemaphoreType.DMA
+    return pl.pallas_call(
+        functools.partial(scatter_last_kernel, scatter_tile(width)),
+        out_shape=[
+            jax.ShapeDtypeStruct((rows, width), F32),
+            jax.ShapeDtypeStruct((seq // 2, *blocks.shape[1:]), BF16),
+            jax.ShapeDtypeStruct((2, seq // 2, slab, cols), BF16),
+        ],
+        in_specs=[VMEM, VMEM, VMEM, HBM],
+        out_specs=[VMEM, HBM, VMEM],
+        scratch_shapes=scatter_scratch(seq, rows, width)
+        + [
+            pltpu.VMEM((width, cols), F32),
+            pltpu.VMEM((width // 2, cols), BF16),
+            pltpu.VMEM((width // 2, cols), BF16),
+            pltpu.VMEM((seq, slab, cols), BF16),
+            dma((2, seq // 2)),
+            dma((2, seq // 2)),
+            dma((2, seq // 2)),
+            dma((2,)),
+            dma((1,)),
+        ],
+        compiler_params=params(call_id, 56),
+        cost_estimate=scatter_cost(a, width),
+    )(a, b, normed, blocks)
+
+
 def swap_dp(values):
     count = lax.axis_size("dp")
     return lax.ppermute(values, "dp", [(i, (i + 1) % count) for i in range(count)])
@@ -202,7 +1361,7 @@
     return grad_in, grad_gain
 
 
-def shards(
+def plain_shards(
     tokens,
     cotangent,
     doc_lengths,
@@ -365,13 +1524,216 @@
     )
 
 
+def shards(
+    tokens,
+    cotangent,
+    doc_lengths,
+    attn_gain,
+    mlp_gain,
+    query_weight,
+    key_weight,
+    value_weight,
+    output_weight,
+    gate_weight,
+    up_weight,
+    down_weight,
+):
+    dp = lax.axis_size("dp")
+    seq = lax.axis_size("seq")
+    data = lax.axis_index("dp")
+    mine = lax.axis_index("seq")
+    tok_count, width = tokens.shape
+    rows = tok_count * seq
+    slab = query_weight.shape[0]
+    half_heads = HEADS // dp
+    half_kv = KV_HEADS // dp
+    hidden_dev = down_weight.shape[0]
+    block = 512
+
+    doc_ends = jnp.cumsum(doc_lengths[0])
+    place = jnp.arange(rows, dtype=jnp.int32)
+    passed = doc_ends[None, :] <= place[:, None]
+    opening = jnp.max(jnp.where(passed, doc_ends[None, :], 0), axis=1)
+    position = place - opening
+    keeping = place < doc_ends[DOCS - 1]
+    angles = position.astype(F32)[:, None] * rotary_table(HEAD_DIM)[None, :]
+    cosine = jnp.cos(angles)
+    sine = jnp.sin(angles)
+    cos_heads = jnp.tile(cosine, (1, 2 * dp))
+    sin_heads = jnp.tile(jnp.concatenate([-sine, sine], axis=1), (1, dp))
+    own_keeping = lax.dynamic_slice_in_dim(keeping, mine * tok_count, tok_count, 0)
+    grad_own = jnp.where(own_keeping[:, None], cotangent, BF16(0))
+    grad_out = gather_rows(grad_own)
+
+    gain_one = attn_gain.astype(F32)[:, None]
+    gain_two = mlp_gain.astype(F32)[:, None]
+
+    def scaled(weight, gain):
+        return (weight.astype(F32) * gain).astype(BF16)
+
+    def head_columns(weight, kept):
+        split = scaled(weight, gain_one).reshape(slab, dp, kept, HEAD_DIM)
+        return jnp.repeat(split, seq // kept, axis=2)
+
+    qkv_blocks = jnp.stack(
+        [
+            head_columns(query_weight, half_heads),
+            head_columns(key_weight, half_kv),
+            head_columns(value_weight, half_kv),
+        ],
+        axis=1,
+    )
+    qkv_blocks = jnp.transpose(qkv_blocks, (3, 0, 1, 2, 4)).reshape(seq, slab, 3 * dp * HEAD_DIM)
+    gate_scaled = scaled(gate_weight, gain_two)
+    up_scaled = scaled(up_weight, gain_two)
+
+    inputs = tokens.astype(F32)
+    factor_one = norm_factor(inputs)
+    (normed_one, queries, keys, values, qkv_weight, feed_near, down_own, output_own) = (
+        gather_project(
+            (inputs * factor_one).astype(BF16),
+            qkv_blocks,
+            gate_scaled,
+            up_scaled,
+            down_weight,
+            output_weight,
+            cos_heads,
+            sin_heads,
+            0,
+        )
+    )
+    qkv_weight = qkv_weight.reshape(width, -1)
+    down_own = down_own.reshape(-1, width)
+    output_own = output_own.reshape(-1, width)
+    attended_sum, log_total, feed_far = attention_feed(
+        queries,
+        keys,
+        values,
+        opening[:, None],
+        gate_scaled,
+        up_scaled,
+        feed_near.shape[2],
+        block,
+        1,
+    )
+    attended = attended_sum.astype(BF16)
+    attended_out, feed_weight = product_scatter_feed(attended, output_own, feed_near, feed_far, 2)
+    feed_weight = feed_weight.reshape(width, -1)
+    middle = inputs + attended_out
+
+    factor_two = norm_factor(middle)
+    normed_two, hidden, feed_back = gather_feed(
+        (middle * factor_two).astype(BF16), grad_out, feed_weight, down_own, 3
+    )
+    mixed = middle + scatter_rows(dot(hidden, down_own))
+
+    def norm_input_grad(values, factor, upstream):
+        inner_mean = jnp.mean(upstream * values, axis=-1, keepdims=True)
+        return factor * upstream - values * factor * factor * factor * inner_mean
+
+    middle_in = norm_input_grad(middle, factor_two, product_scatter(feed_back, feed_weight.T, 4))
+    middle_grad = grad_own.astype(F32) + middle_in
+    feed_part = t_dot(normed_two, feed_back).astype(BF16).reshape(dp, width // dp, -1)
+    attended_grad, output_part, feed_came = gather_back(
+        middle_grad.astype(BF16), output_own, attended, feed_part, 5
+    )
+
+    def halves(part):
+        half = part.shape[0] // dp
+        kept = lax.dynamic_slice_in_dim(part, data * half, half, 0)
+        return kept, lax.dynamic_slice_in_dim(part, (1 - data) * half, half, 0).astype(BF16)
+
+    def both(kept, came):
+        return kept.astype(F32) + came.astype(F32)
+
+    feed_kept = lax.dynamic_index_in_dim(feed_part, data, 0, keepdims=False)
+    feed_sums = both(feed_kept, feed_came).astype(BF16).reshape(seq, slab, -1)
+    down_kept, down_away = halves(t_dot(hidden, grad_out))
+    output_kept, output_away = halves(output_part)
+    qkv_back, feed_grad_far, down_came, output_came = attention_back_feed(
+        queries,
+        keys,
+        values,
+        attended_grad,
+        attended_sum,
+        log_total,
+        opening[:, None],
+        cos_heads,
+        sin_heads,
+        feed_sums,
+        down_away,
+        output_away,
+        block,
+        6,
+    )
+    down_grad = both(down_kept, down_came)
+    output_grad = both(output_kept, output_came)
+    normed_one_grad, feed_grad_near, qkv_grads = product_scatter_last(
+        qkv_back, qkv_weight, normed_one, feed_sums, 7
+    )
+    token_grad = middle_grad + norm_input_grad(inputs, factor_one, normed_one_grad)
+
+    pair = (mine // 2) % 2
+
+    def by_sender(near, far):
+        first = jnp.where(pair == 0, near, far)
+        second = jnp.where(pair == 0, far, near)
+        split = jnp.stack([first, second]).reshape(2, seq // 4, 2, *near.shape[1:])
+        return jnp.swapaxes(split, 0, 1).reshape(seq, *near.shape[1:])
+
+    feed_grad = by_sender(feed_grad_near, feed_grad_far).reshape(seq, slab, 2, dp, hidden_dev)
+    feed_grad = jnp.transpose(feed_grad, (2, 1, 3, 0, 4)).reshape(2, slab, -1).astype(F32)
+    qkv_grad = by_sender(qkv_grads[0], qkv_grads[1]).astype(F32)
+    qkv_grad = qkv_grad.reshape(seq, slab, 3, dp, HEAD_DIM)
+
+    def own_columns(part, kept):
+        summed = jnp.sum(part.reshape(kept, seq // kept, slab, dp, HEAD_DIM), axis=1)
+        return jnp.transpose(summed, (1, 2, 0, 3)).reshape(slab, dp * kept * HEAD_DIM)
+
+    query_grad = own_columns(qkv_grad[:, :, 0], half_heads)
+    key_grad = own_columns(qkv_grad[:, :, 1], half_kv)
+    value_grad = own_columns(qkv_grad[:, :, 2], half_kv)
+
+    def along(weight, grad):
+        return jnp.sum(weight.astype(F32) * grad, axis=1)
+
+    attn_gain_grad = (
+        along(query_weight, query_grad)
+        + along(key_weight, key_grad)
+        + along(value_weight, value_grad)
+    )
+    mlp_gain_grad = along(gate_weight, feed_grad[0]) + along(up_weight, feed_grad[1])
+    return (
+        mixed,
+        token_grad,
+        attn_gain_grad,
+        mlp_gain_grad,
+        query_grad * gain_one,
+        key_grad * gain_one,
+        value_grad * gain_one,
+        output_grad,
+        feed_grad[0] * gain_two,
+        feed_grad[1] * gain_two,
+        down_grad,
+    )
+
+
 def solution(mesh):
     both = P(("dp", "seq"), None)
     line = P(("dp", "seq"))
-    return jax.shard_map(
-        shards,
-        mesh=mesh,
-        in_specs=(both, both, P("dp", None), line, line) + (both,) * 7,
-        out_specs=(both, both, line, line) + (both,) * 7,
-        check_vma=False,
-    )
+    dp, seq = mesh.shape["dp"], mesh.shape["seq"]
+
+    def run(*args):
+        tokens = args[0].shape[0]
+        width = args[0].shape[1]
+        suits = dp == 2 and seq % 4 == 0 and width == dp * seq * HEAD_DIM
+        suits = suits and 2 * (tokens // dp) * width <= 16 << 20
+        return jax.shard_map(
+            shards if suits else plain_shards,
+            mesh=mesh,
+            in_specs=(both, both, P("dp", None), line, line) + (both,) * 7,
+            out_specs=(both, both, line, line) + (both,) * 7,
+            check_vma=False,
+        )(*args)
+
+    return run

time: 1120 us -> 701 us (0.63)
  waiting for transfers between devices: 557 us -> 0.04 us
  Pallas kernels: 51.8 us -> 544 us
  blocking collectives: 207 us -> 0 us
  matrix products: 107 us -> 26.7 us
  starting transfers between devices: 28.6 us -> 0.08 us
  local copies, waits for them, and re-layouts: 91.1 us -> 63.3 us
  other arithmetic: 54.5 us -> 42.9 us
    pallas_call x2 -> x8, Pallas kernels: 51.8 us -> 544 us  [the longest x1 130 us: gather_project(): pl.pallas_call(project_kernel, out_shape=[jax.ShapeDtypeStruct((seq * row...]
    all_gather x4 -> x1, waiting for transfers between devices: 231 us -> 0.01 us  [gather_rows(): return lax.all_gather(values, 'seq', axis=0, tiled=True)]
    reduce_scatter x4 -> x1, waiting for transfers between devices: 142 us -> 0.01 us  [scatter_rows(): lax.psum_scatter(partial.astype(BF16), 'seq', scatter_dimension=0, tiled=...]
    all_gather x3 -> x0, waiting for transfers between devices: 92.3 us -> none  [gather_dp(): return lax.all_gather(values, 'dp', axis=0, tiled=True)]
    all_to_all x1 -> x0, blocking collectives: 84.3 us -> none  [exchange(): lax.all_to_all(blocks, 'seq', split_axis=0, concat_axis=0, tiled=True)]
    all_gather x2 -> x0, blocking collectives: 70.6 us -> none  [the longest x1 60.8 us: shards(): lax.all_gather(jnp.stack([attn_gain, mlp_gain]), ('dp', 'seq'), axis=1, t...]
    ppermute x4 -> x0, waiting for transfers between devices: 61.7 us -> none  [swap_dp(): lax.ppermute(values, 'dp', [(i, (i + 1) % count) for i in range(count)])]
    psum x1 -> x0, blocking collectives: 51.6 us -> none  [shards(): lax.psum(jnp.stack([gain_one_part, gain_two_part]), ('dp', 'seq'))]
  transfers between devices with their start and end apart: 18 -> 2, of which waited for: 14 -> 0; matrix products, arithmetic and copies ran while one was open for 12% -> 16% of each run, Pallas kernels for 0% -> 70%
where the time goes in v3:
time: 701 us; the launch traced here: 692 us
  Pallas kernels  544 us (78%)
  local copies, waits for them, and re-layouts  63.3 us (9%)
  other arithmetic  42.9 us (6%)
  matrix products  26.7 us (4%)
  between operations  15.3 us (2%)
    pallas_call x1, Pallas kernels, gather_project(): pl.pallas_call(project_kernel, out_shape=[jax.ShapeDtypeStruct((seq * row...  130 us
    pallas_call x1, Pallas kernels, product_scatter(): pl.pallas_call(functools.partial(scatter_kernel, scatter_tile(width)), ou...  86.2 us
    pallas_call x1, Pallas kernels, product_scatter_last(): pl.pallas_call(functools.partial(scatter_last_kernel, scatter_tile(width)...  78.5 us
    pallas_call x1, Pallas kernels, gather_back(): pl.pallas_call(back_kernel, out_shape=[jax.ShapeDtypeStruct((seq * rows,...  64.2 us
    pallas_call x1, Pallas kernels, gather_feed(): pl.pallas_call(feed_kernel, out_shape=[jax.ShapeDtypeStruct((seq * rows,...  59.6 us
    pallas_call x1, Pallas kernels, product_scatter_feed(): pl.pallas_call(functools.partial(scatter_feed_kernel, scatter_tile(width)...  55.9 us
    pallas_call x1, Pallas kernels, attention_back_feed(): pl.pallas_call(functools.partial(attention_back_feed_kernel, block), grid...  36.8 us
    pallas_call x1, Pallas kernels, attention_feed(): pl.pallas_call(functools.partial(attention_feed_kernel, block), grid=(row...  32.4 us
  transfers between devices with their start and end apart: 2, of which 0 were waited for; matrix products, arithmetic and copies ran while one was open for 16% of the time, Pallas kernels for 70%

profile of v3, /device:TPU:0, one launch (start us, length us, event | category | flops | bytes accessed | tf_op | source)
XLA Modules:
  0.0 692.1 jit_solution(7083759964338190770)
XLA Ops:
  9.3 2.0 broadcast_select_fusion.2
  15.5 3.1 maximum_bitcast_fusion
  18.5 1.7 reshape.183.blocks_ref
  20.4 1.0 fusion.19
  23.0 1.7 fusion.11
  24.7 1.2 fusion.6.own_ref
  26.0 1.8 fusion.3
  27.9 130.1 %shard_map.203 = (bf16[2048,2048]{1,0:T(8,128)(2,1)}, bf16[2048,128]{1,0:T(8,128)(2,1)S(1)}, bf16[2048,128]{1,0:T(8,128)(2,1)S(1)}, bf16[2048,128]{1,0:T(8,128)(...) custom-call(bf16[128,2048]{1,0:T(8,128)(2,1)S(1)} %fusion.6.own_ref,, ...), custom_call_target="tpu_custom_call" | custom-call | flops 3221225472 | bytes 16777216 | tf_op jit(solution)/shard_map/pallas_call | solution.py:628
  158.1 1.1 copy-done.10
  159.2 1.3 copy-done.18
  160.6 32.4 %shard_map.204 = (f32[2048,128]{1,0:T(8,128)S(1)}, f32[2048,2]{1,0:T(8,128)S(1)}, bf16[8,64,1024]{2,1,0:T(8,128)(2,1)S(1)}) custom-call(bf16[2048,128]{1,0:T(8,128)(2,1)S(1)} %get-tuple-element.37.q_ref, bf16[2048,128]{1,0:T(8,128)(2,1)S(1)} %get-tuple-element.38.k_ref, bf16[2048,128]{1,0:T(8,128)(2,1)S(1)} %get-tuple-element.39.v_ref, ...), custom_call_target="tpu_custom_call" | custom-call | flops 1073741824 | bytes 2621440 | tf_op jit(solution)/shard_map/pallas_call | solution.py:691
  193.1 55.9 %shard_map.205 = (f32[128,2048]{1,0:T(8,128)S(1)}, bf16[2,16,64,1024]{3,2,1,0:T(8,128)(2,1)S(1)}) custom-call(bf16[2048,128]{1,0:T(8,128)(2,1)S(1)} %convert_element_type.137.a_ref.attended_ref, bf16[128,2048]{1,0:T(8,128)(2,1)S(1)} %bitcast.68, bf16[8,64,1024]{2,1,0:T(8,128)(2,1)S(1)} %get-tuple-element.42.near_ref, ...), custom_call_target="tpu_custom_call" | custom-call | flops 1073741824 | bytes 16777216 | tf_op jit(solution)/shard_map/pallas_call | solution.py:954
  249.0 2.1 copy-done.1
  252.3 59.6 %shard_map.206 = (bf16[2048,2048]{1,0:T(8,128)(2,1)}, bf16[2048,512]{1,0:T(8,128)(2,1)}, bf16[2048,1024]{1,0:T(8,128)(2,1)}) custom-call(bf16[128,2048]{1,0:T(8,128)(2,1)} %multiply_convert_fusion.own_ref, bf16[2048,2048]{1,0:T(8,128)(2,1)} %all-gather.2.cloned.1.call-done.grad_ref, bf16[2048,1024]{1,0:T(8,128)(2,1)} %bitcast.61, bf16[512,2048]{1,0:T(8,128)(2,1)} %bitcast.66), custom_call_target="tpu_custom_call" | custom-call | flops 12884901888 | bytes 25165824 | tf_op jit(solution)/shard_map/pallas_call | solution.py:1018
  311.9 8.4 %convolution_convert_fusion = bf16[2048,2048]{1,0:T(8,128)(2,1)} fusion(bf16[2048,512]{1,0:T(8,128)(2,1)} %get-tuple-element.47, bf16[512,2048]{1,0:T(8,128)(2,1)S(1)} %bitcast.67), kind=kOutput, calls=%fused_computation | convolution fusion | flops 4299161600 | bytes 12582912 | tf_op jit(solution)/shard_map/dot_general | solution.py:40
  320.3 6.5 copy.103
  326.8 2.7 copy-done.22
  329.5 86.2 %shard_map.207 = f32[128,2048]{1,0:T(8,128)S(1)} custom-call(bf16[2048,1024]{1,0:T(8,128)(2,1)S(1)} %copy-done.22, bf16[1024,2048]{1,0:T(8,128)(2,1)} %bitcast.74), custom_call_target="tpu_custom_call" | custom-call | flops 8589934592 | bytes 16777216 | tf_op jit(solution)/shard_map/pallas_call | solution.py:902
  416.4 1.5 copy-done.23
  417.9 12.2 %convolution_convert_fusion.1 = bf16[2048,1024]{1,0:T(8,128)(2,1)S(1)} fusion(bf16[2048,2048]{1,0:T(8,128)(2,1)} %get-tuple-element.49, bf16[2048,1024]{1,0:T(8,128)(2,1)S(1)} %copy-done.23), kind=kOutput, calls=%fused_computation.4 | convolution fusion | flops 8592031744 | bytes 16777216 | tf_op jit(solution)/shard_map/dot_general | solution.py:48
  430.1 64.2 %shard_map.208 = (bf16[2048,128]{1,0:T(8,128)(2,1)S(1)}, f32[128,2048]{1,0:T(8,128)S(1)}, bf16[1024,1024]{1,0:T(8,128)(2,1)S(1)}) custom-call(bf16[128,2048]{1,0:T(8,128)(2,1)S(1)} %fusion.20.own_ref, bf16[128,2048]{1,0:T(8,128)(2,1)S(1)} %bitcast.69, bf16[2048,128]{1,0:T(8,128)(2,1)S(1)} %copy-done.14, bf16[2,1024,1024]{2,1,0:T(8,128)(2,1)S(1)} %bitcast.64), custom_call_target="tpu_custom_call" | custom-call | flops 2147483648 | bytes 16777216 | tf_op jit(solution)/shard_map/pallas_call | solution.py:1075
  495.1 6.2 fusion.23
  501.3 1.3 dynamic-slice_convert_fusion.down_ref
  502.7 2.3 fusion
  504.9 36.8 %shard_map.209 = (bf16[2048,384]{1,0:T(8,128)(2,1)}, bf16[8,64,1024]{2,1,0:T(8,128)(2,1)}, bf16[256,2048]{1,0:T(8,128)(2,1)}, bf16[64,2048]{1,0:T(8,128)(2,1)}) custom-call(bf16[2048,128]{1,0:T(8,128)(2,1)} %copy-done.7, bf16[2048,128]{1,0:T(8,128)(2,1)} %copy-done.8, bf16[2048,128]{1,0:T(8,128)(2,1)} %copy-done.9, bf16[2048,128]{1,0:T(8,128)(2,1)} %copy-done.15, ...), custom_call_target="tpu_custom_call" | custom-call | flops 2684354560 | bytes 5242880 | tf_op jit(solution)/shard_map/pallas_call | solution.py:1177
  541.8 78.5 %shard_map.210 = (f32[128,2048]{1,0:T(8,128)}, bf16[8,64,1024]{2,1,0:T(8,128)(2,1)}, bf16[2,8,64,384]{3,2,1,0:T(8,128)(2,1)}) custom-call(bf16[2048,384]{1,0:T(8,128)(2,1)} %get-tuple-element.54.a_ref, bf16[2048,384]{1,0:T(8,128)(2,1)} %bitcast.63, bf16[2048,2048]{1,0:T(8,128)(2,1)} %get-tuple-element.56.normed_ref, bf16[16,64,1024]{2,1,0:T(8,128)(2,1)} %bitcast.71), custom_call_target="tpu_custom_call" | custom-call | flops 3221225472 | bytes 16777216 | tf_op jit(solution)/shard_map/pallas_call | solution.py:1297
  620.3 1.4 broadcast_select_fusion.1
  621.7 2.3 convert_bitcast_fusion
  624.0 6.6 reshape.196
  630.6 5.2 fusion.21
  635.7 2.5 copy.115
  638.2 2.7 squeeze.18
  641.0 4.1 copy.114
  645.1 2.7 squeeze.9
  647.8 1.2 broadcast_select_fusion.4
  649.0 1.2 convert_bitcast_fusion.1
  650.3 4.5 reshape.195
  654.7 3.5 fusion.22
  658.2 1.6 copy.109
  659.8 2.4 reshape.191
  662.2 1.9 reduce_sum.111
  664.9 1.1 reshape.192
  666.0 1.9 reduce_sum.113
  668.8 1.1 reshape.193
  670.0 5.7 broadcast_multiply_fusion
  677.9 1.2 broadcast_multiply_fusion.2
  679.7 1.6 convert_add_fusion.1
  681.4 3.4 fusion.10
  (138 shorter events, 15.2 us)
Async XLA Ops:
  7.2 6.3 copy-start.36
  7.2 245.1 %all-gather.2.cloned.1.call-start = ((), (), s32[]{:S(2)}) async-start(), calls=%async_computation.1 | async-start | bytes 8912896 | tf_op jit(solution)/shard_map/all_gather | solution.py:1341
  11.3 670.0 %reduce-scatter.2.cloned.1.call-start = ((), (), s32[]{:S(2)}) async-start(), calls=%async_computation.2 | async-start | bytes 8912896 | tf_op jit(solution)/shard_map/reduce_scatter | solution.py:1345
  21.9 6.0 copy-start.4
  22.6 5.3 copy-start.5
  22.6 5.2 copy-start.41
  23.0 137.6 %copy-start = (s32[2048,1]{1,0:T(8,128)}, s32[2048,1]{1,0:T(8,128)S(1)}, u32[]{:S(2)}) copy-start(s32[2048,1]{1,0:T(8,128)S(1)} %copy.102.open_ref) | copy-start | bytes 24580
  23.0 2.9 copy-start.30
  25.9 1.9 copy-start.12
  26.0 1.9 copy-start.16
  26.0 1.9 copy-start.17
  27.8 130.2 %copy-start.2 = (bf16[64,8192]{1,0:T(8,128)(2,1)}, bf16[64,8192]{1,0:T(8,128)(2,1)S(1)}, u32[]{:S(2)}) copy-start(bf16[64,8192]{1,0:T(8,128)(2,1)S(1)} %get-tuple-element.91.up_ref) | copy-start | bytes 3145732
  27.8 130.2 %copy-start.3 = (bf16[64,8192]{1,0:T(8,128)(2,1)}, bf16[64,8192]{1,0:T(8,128)(2,1)S(1)}, u32[]{:S(2)}) copy-start(bf16[64,8192]{1,0:T(8,128)(2,1)S(1)} %get-tuple-element.92.gate_ref) | copy-start | bytes 3145732
  159.2 1.3 copy-start.18
  160.5 32.4 %copy-start.7 = (bf16[2048,128]{1,0:T(8,128)(2,1)}, bf16[2048,128]{1,0:T(8,128)(2,1)S(1)}, u32[]{:S(2)}) copy-start(bf16[2048,128]{1,0:T(8,128)(2,1)S(1)} %get-tuple-element.37.q_ref) | copy-start | bytes 1572868
  160.5 32.4 %copy-start.8 = (bf16[2048,128]{1,0:T(8,128)(2,1)}, bf16[2048,128]{1,0:T(8,128)(2,1)S(1)}, u32[]{:S(2)}) copy-start(bf16[2048,128]{1,0:T(8,128)(2,1)S(1)} %get-tuple-element.38.k_ref) | copy-start | bytes 1572868
  160.5 32.4 %copy-start.9 = (bf16[2048,128]{1,0:T(8,128)(2,1)}, bf16[2048,128]{1,0:T(8,128)(2,1)S(1)}, u32[]{:S(2)}) copy-start(bf16[2048,128]{1,0:T(8,128)(2,1)S(1)} %get-tuple-element.39.v_ref) | copy-start | bytes 1572868
  160.5 32.5 %copy-start.20 = (bf16[2,64,2048]{2,1,0:T(8,128)(2,1)}, bf16[2,64,2048]{2,1,0:T(8,128)(2,1)S(1)}, u32[]{:S(2)}) copy-start(bf16[2,64,2048]{2,1,0:T(8,128)(2,1)S(1)} %get-tuple-element.41) | copy-start | bytes 1572868
  193.0 56.0 %copy-start.6 = (f32[2048,128]{1,0:T(8,128)}, f32[2048,128]{1,0:T(8,128)S(1)}, u32[]{:S(2)}) copy-start(f32[2048,128]{1,0:T(8,128)S(1)} %get-tuple-element.40.att_ref) | copy-start | bytes 3145732
  193.0 56.0 %copy-start.11 = (f32[2048,2]{1,0:T(8,128)}, f32[2048,2]{1,0:T(8,128)S(1)}, u32[]{:S(2)}) copy-start(f32[2048,2]{1,0:T(8,128)S(1)} %get-tuple-element.51.lse_ref) | copy-start | bytes 49156
  193.1 58.2 %copy-start.13 = (bf16[2048,128]{1,0:T(8,128)(2,1)}, bf16[2048,128]{1,0:T(8,128)(2,1)S(1)}, u32[]{:S(2)}) copy-start(bf16[2048,128]{1,0:T(8,128)(2,1)S(1)} %convert_element_type.137.a_ref.attended_ref) | copy-start | bytes 1572868
  193.1 58.0 %copy-start.24 = (bf16[128,2048]{1,0:T(8,128)(2,1)S(1)}, bf16[128,2048]{1,0:T(8,128)(2,1)}, u32[]{:S(2)}) copy-start(bf16[128,2048]{1,0:T(8,128)(2,1)} %param.12) | copy-start | bytes 1572868
  249.0 2.1 copy-start.1
  252.3 59.6 %copy-start.19 = (bf16[2,256,2048]{2,1,0:T(8,128)(2,1)S(1)}, bf16[2,256,2048]{2,1,0:T(8,128)(2,1)}, u32[]{:S(2)}) copy-start(bf16[2,256,2048]{2,1,0:T(8,128)(2,1)} %copy-done.18) | copy-start | bytes 6291460
  326.8 2.7 copy-start.22
  329.5 86.5 %copy-start.27 = (bf16[128,2048]{1,0:T(8,128)(2,1)S(1)}, bf16[128,2048]{1,0:T(8,128)(2,1)}, u32[]{:S(2)}) copy-start(bf16[128,2048]{1,0:T(8,128)(2,1)} %param.13) | copy-start | bytes 1572868
  415.7 2.2 copy-start.23
  416.0 14.1 %copy-start.42 = (f32[128]{0:T(128)}, f32[128]{0:T(128)S(1)}, u32[]{:S(2)}) copy-start(f32[128]{0:T(128)S(1)} %broadcast_multiply_fusion.6) | copy-start | bytes 1540
  416.0 79.2 %slice-start = ((s8[8388608]{0:T(1024)(128)(4,1)}), s8[4194304]{0:T(1024)(128)(4,1)S(1)}, s32[]{:S(2)}) async-start(s8[8388608]{0:T(1024)(128)(4,1)} %bitcast.88), calls=%async_computation.3 | async-start | bytes 8388608
  417.9 12.2 %copy-start.14 = (bf16[2048,128]{1,0:T(8,128)(2,1)S(1)}, bf16[2048,128]{1,0:T(8,128)(2,1)}, u32[]{:S(2)}) copy-start(bf16[2048,128]{1,0:T(8,128)(2,1)} %copy-done.13) | copy-start | bytes 1572868
  417.9 12.2 %copy-start.21 = (bf16[2,64,2048]{2,1,0:T(8,128)(2,1)S(1)}, bf16[2,64,2048]{2,1,0:T(8,128)(2,1)}, u32[]{:S(2)}) copy-start(bf16[2,64,2048]{2,1,0:T(8,128)(2,1)} %copy-done.20) | copy-start | bytes 1572868
  417.9 77.2 %slice-start.1 = ((s8[8388608]{0:T(1024)(128)(4,1)}), s8[4194304]{0:T(1024)(128)(4,1)S(1)}, s32[]{:S(2)}) async-start(s8[8388608]{0:T(1024)(128)(4,1)} %bitcast.88), calls=%async_computation.4 | async-start | bytes 8388608
  494.3 7.0 %copy-start.15 = (bf16[2048,128]{1,0:T(8,128)(2,1)}, bf16[2048,128]{1,0:T(8,128)(2,1)S(1)}, u32[]{:S(2)}) copy-start(bf16[2048,128]{1,0:T(8,128)(2,1)S(1)} %get-tuple-element.50.g_ref) | copy-start | bytes 1572868
  501.3 3.6 copy-start.31
  541.8 78.5 %copy-start.34 = (bf16[8,64,1024]{2,1,0:T(8,128)(2,1)S(1)}, bf16[8,64,1024]{2,1,0:T(8,128)(2,1)}, u32[]{:S(2)}) copy-start(bf16[8,64,1024]{2,1,0:T(8,128)(2,1)} %get-tuple-element.60) | copy-start | bytes 3145732
  669.9 6.3 copy-start.25
  669.9 6.3 copy-start.29
  669.9 7.0 %copy-start.38 = (bf16[64,512]{1,0:T(8,128)(2,1)S(1)}, bf16[64,512]{1,0:T(8,128)(2,1)}, u32[]{:S(2)}) copy-start(bf16[64,512]{1,0:T(8,128)(2,1)} %param.18) | copy-start | bytes 196612
  670.0 7.0 %copy-start.39 = (bf16[64,512]{1,0:T(8,128)(2,1)S(1)}, bf16[64,512]{1,0:T(8,128)(2,1)}, u32[]{:S(2)}) copy-start(bf16[64,512]{1,0:T(8,128)(2,1)} %param.19) | copy-start | bytes 196612
  670.0 7.9 %copy-start.37 = (bf16[64,2048]{1,0:T(8,128)(2,1)S(1)}, bf16[64,2048]{1,0:T(8,128)(2,1)}, u32[]{:S(2)}) copy-start(bf16[64,2048]{1,0:T(8,128)(2,1)} %param.17) | copy-start | bytes 786436
  670.0 7.9 %copy-start.40 = (bf16[64,2048]{1,0:T(8,128)(2,1)S(1)}, bf16[64,2048]{1,0:T(8,128)(2,1)}, u32[]{:S(2)}) copy-start(bf16[64,2048]{1,0:T(8,128)(2,1)} %get-tuple-element.61) | copy-start | bytes 786436
  670.0 9.7 %copy-start.35 = (bf16[256,2048]{1,0:T(8,128)(2,1)S(1)}, bf16[256,2048]{1,0:T(8,128)(2,1)}, u32[]{:S(2)}) copy-start(bf16[256,2048]{1,0:T(8,128)(2,1)} %get-tuple-element.62) | copy-start | bytes 3145732
  675.7 2.2 copy-start.33
  676.3 3.4 copy-start.32
  679.7 1.7 copy-start.26
  679.7 1.7 copy-start.28
  679.7 1.7 copy-start.43
  679.7 1.6 copy-start.44
  (2 other events, 1.8 us)
Sparse Core Ops, SparseCore 0:
  11.4 115.2 all-gather.1
  320.4 141.6 reduce-scatter.1

commit v4 on v3

--- a/solution.py
+++ b/solution.py
@@ -727,6 +727,7 @@
     down_sems,
     between=nothing,
     middle=nothing,
+    filler=None,
 ):
     length = here.length
     rows = out_ref.shape[0]
@@ -814,6 +815,8 @@
             held[:, cols] = value + core_in[steps + step, :, cols].astype(F32)
 
         product(line, here.pair, here.core, part, use)
+        if filler is not None:
+            filler(step)
         pair_copy(step).wait_recv()
         from_above = (line <= here.line) & (here.line < length - 1)
         from_below = (line >= here.line) & (here.line > 0)
@@ -889,25 +892,44 @@
     return cost(2 * a.shape[0] * a.shape[1] * width, 4 * a.shape[0] * width)
 
 
-def scatter_kernel(tile, a_ref, b_ref, out_ref, *scratch):
+def scatter_grad_kernel(tile, a_ref, b_ref, normed_ref, out_ref, grad_ref, *scratch):
     here = Place()
     here.greet()
-    scatter_rows_of_product(here, False, SCATTER_PARTS, tile, a_ref, b_ref, out_ref, *scratch)
-
-
-def product_scatter(a, b, call_id):
+    cols = normed_ref.shape[1] // (here.length * SCATTER_PARTS)
+
+    def filler(step):
+        some = pl.ds(pl.multiple_of(step * cols, cols), cols)
+        grad_ref[some, :] = t_dot(normed_ref[:, some], a_ref[...]).astype(BF16)
+
+    scatter_rows_of_product(
+        here,
+        False,
+        SCATTER_PARTS,
+        tile,
+        a_ref,
+        b_ref,
+        out_ref,
+        *scratch,
+        filler=filler,
+    )
+
+
+def product_scatter_grad(a, b, normed, call_id):
     seq = lax.axis_size("seq")
     rows = a.shape[0] // seq
     width = b.shape[1]
     return pl.pallas_call(
-        functools.partial(scatter_kernel, scatter_tile(width)),
-        out_shape=jax.ShapeDtypeStruct((rows, width), F32),
-        in_specs=[VMEM, VMEM],
-        out_specs=VMEM,
+        functools.partial(scatter_grad_kernel, scatter_tile(width)),
+        out_shape=[
+            jax.ShapeDtypeStruct((rows, width), F32),
+            jax.ShapeDtypeStruct((width, a.shape[1]), BF16),
+        ],
+        in_specs=[VMEM] * 3,
+        out_specs=[VMEM] * 2,
         scratch_shapes=scatter_scratch(seq, rows, width),
-        compiler_params=params(call_id, 48),
-        cost_estimate=scatter_cost(a, width),
-    )(a, b)
+        compiler_params=params(call_id, 56),
+        cost_estimate=scatter_cost(a, 2 * width),
+    )(a, b, normed)
 
 
 def scatter_feed_kernel(tile, a_ref, b_ref, near_ref, far_ref, out_ref, feed_ref, *scratch):
@@ -974,20 +996,33 @@
     normed_ref,
     hidden_ref,
     back_ref,
+    turned_ref,
+    mixed_ref,
     buf,
     send_sems,
     recv_sems,
     store_sems,
+    mixed_buf,
+    mixed_sems,
 ):
     here = Place()
     here.greet()
     rows = own_ref.shape[0]
+    width = own_ref.shape[1]
     hidden = hidden_ref.shape[1]
     tile = 256
+    wide = 512
     store = UnitStore(buf, normed_ref, store_sems)
+
+    def mixed_copy(number, first):
+        slot = number % 2
+        return pltpu.make_async_copy(
+            mixed_buf.at[slot], mixed_ref.at[unit_rows(first, rows)], mixed_sems.at[slot]
+        )
 
     def compute(number, first):
         store.start(number, first)
+        pl.when(number >= 2)(lambda: mixed_copy(number, first).wait())
         where = unit_rows(first, rows)
         normed = take_unit(buf, first)
         grad = grad_ref[where, :]
@@ -1007,7 +1042,20 @@
             ).astype(BF16)
             back_ref[where, later] = (hidden_grad * silu).astype(BF16)
 
+        @pl.loop(0, width // wide)
+        def _(t):
+            cols = pl.ds(pl.multiple_of(t * wide, wide), wide)
+            part = dot(hidden_ref[where, :], down_ref[:, cols])
+            mixed_buf[number % 2, :, cols] = part.astype(BF16)
+
+        mixed_copy(number, first).start()
+        share = width // (2 * here.length)
+        some = pl.ds(pl.multiple_of(number * share, share), share)
+        turned_ref[:, some] = feed_ref[some, :].T
+
     gather_units(here, own_ref, buf, send_sems, recv_sems, compute)
+    mixed_copy(0, 0).wait()
+    mixed_copy(1, 0).wait()
     store.finish()
 
 
@@ -1021,13 +1069,19 @@
             jax.ShapeDtypeStruct((seq * rows, width), BF16),
             jax.ShapeDtypeStruct((seq * rows, hidden), BF16),
             jax.ShapeDtypeStruct((seq * rows, 2 * hidden), BF16),
+            jax.ShapeDtypeStruct((2 * hidden, width), BF16),
+            jax.ShapeDtypeStruct((seq * rows, width), BF16),
         ],
         in_specs=[VMEM] * 4,
-        out_specs=[HBM, VMEM, VMEM],
+        out_specs=[HBM, VMEM, VMEM, VMEM, HBM],
         scratch_shapes=gather_scratch(seq, rows, width)
-        + [pltpu.SemaphoreType.DMA((seq // 2, 2, 2))],
+        + [
+            pltpu.SemaphoreType.DMA((seq // 2, 2, 2)),
+            pltpu.VMEM((2, 2 * rows, width), BF16),
+            pltpu.SemaphoreType.DMA((2,)),
+        ],
         compiler_params=params(call_id, 56),
-        cost_estimate=cost(6 * seq * rows * width * hidden, 6 * seq * rows * width),
+        cost_estimate=cost(8 * seq * rows * width * hidden, 8 * seq * rows * width),
     )(own, grad_out, feed_weight, down_weight)
 
 
@@ -1035,14 +1089,20 @@
     own_ref,
     weight_ref,
     attended_ref,
+    hidden_ref,
+    out_grad_ref,
     share_ref,
     grad_ref,
-    part_ref,
+    output_kept_ref,
+    output_away_ref,
+    down_kept_ref,
+    down_away_ref,
     came_ref,
     buf,
     send_sems,
     recv_sems,
     swap_sems,
+    part,
 ):
     here = Place()
     here.greet(partner=True)
@@ -1053,7 +1113,14 @@
         share_ref.at[1 - here.dp], came_ref, swap_sems.at[0], swap_sems.at[1], here.partner()
     )
     swap.start()
-    part_ref[...] = jnp.zeros_like(part_ref)
+    part[...] = jnp.zeros_like(part)
+    share = width // (2 * here.length)
+
+    def split(values, kept_ref, away_ref, cols):
+        half = values.shape[0] // 2
+        top, bottom = values[:half], values[half:]
+        kept_ref[:, cols] = jnp.where(here.dp == 0, top, bottom)
+        away_ref[:, cols] = jnp.where(here.dp == 0, bottom, top).astype(BF16)
 
     def compute(number, first):
         where = unit_rows(first, rows)
@@ -1062,13 +1129,18 @@
         attended = attended_ref[where, :]
         for t in range(width // tile):
             cols = slice(t * tile, (t + 1) * tile)
-            part_ref[:, cols] += t_dot(attended, unit[:, cols])
+            part[:, cols] += t_dot(attended, unit[:, cols])
+        some = pl.ds(pl.multiple_of(number * share, share), share)
+        split(t_dot(hidden_ref[...], out_grad_ref[:, some]), down_kept_ref, down_away_ref, some)
 
     gather_units(here, own_ref, buf, send_sems, recv_sems, compute)
+    for t in range(width // tile):
+        cols = slice(t * tile, (t + 1) * tile)
+        split(part[:, cols], output_kept_ref, output_away_ref, cols)
     swap.wait()
 
 
-def gather_back(own, weight, attended, share, call_id):
+def gather_back(own, weight, attended, hidden, grad_out, share, call_id):
     seq = lax.axis_size("seq")
     rows, width = own.shape
     cols = weight.shape[0]
@@ -1076,15 +1148,19 @@
         back_kernel,
         out_shape=[
             jax.ShapeDtypeStruct((seq * rows, cols), BF16),
-            jax.ShapeDtypeStruct((cols, width), F32),
+            jax.ShapeDtypeStruct((cols // 2, width), F32),
+            jax.ShapeDtypeStruct((cols // 2, width), BF16),
+            jax.ShapeDtypeStruct((hidden.shape[1] // 2, width), F32),
+            jax.ShapeDtypeStruct((hidden.shape[1] // 2, width), BF16),
             jax.ShapeDtypeStruct(share.shape[1:], BF16),
         ],
-        in_specs=[VMEM] * 3 + [HBM],
-        out_specs=[VMEM] * 2 + [HBM],
-        scratch_shapes=gather_scratch(seq, rows, width) + [pltpu.SemaphoreType.DMA((2,))],
-        compiler_params=params(call_id, 40),
-        cost_estimate=cost(4 * seq * rows * width * cols, 4 * seq * rows * width),
-    )(own, weight, attended, share)
+        in_specs=[VMEM] * 5 + [HBM],
+        out_specs=[VMEM] * 5 + [HBM],
+        scratch_shapes=gather_scratch(seq, rows, width)
+        + [pltpu.SemaphoreType.DMA((2,)), pltpu.VMEM((cols, width), F32)],
+        compiler_params=params(call_id, 48),
+        cost_estimate=cost(8 * seq * rows * width * cols, 6 * seq * rows * width),
+    )(own, weight, attended, hidden, grad_out, share)
 
 
 def attention_back_feed_kernel(
@@ -1320,6 +1396,117 @@
     )(a, b, normed, blocks)
 
 
+def unpack_kernel(
+    pair_ref,
+    near_gate_ref,
+    far_gate_ref,
+    near_up_ref,
+    far_up_ref,
+    gate_ref,
+    up_ref,
+    qkv_ref,
+    query_ref,
+    key_ref,
+    value_ref,
+    gain_one_ref,
+    gain_two_ref,
+    gate_out_ref,
+    up_out_ref,
+    query_out_ref,
+    key_out_ref,
+    value_out_ref,
+    one_out_ref,
+    two_out_ref,
+):
+    pair = pair_ref[0]
+    dp = lax.axis_size("dp")
+    length = qkv_ref.shape[1] // 2
+    slab = qkv_ref.shape[2]
+    step = pl.program_id(0) * pl.num_programs(1) + pl.program_id(1)
+    columns = near_gate_ref.shape[2]
+
+    def along(grad, weight):
+        return jnp.sum(grad * weight.astype(F32), axis=1, keepdims=True)
+
+    @pl.when(step == 0)
+    def _():
+        two_out_ref[...] = jnp.zeros_like(two_out_ref)
+        total = jnp.zeros((slab, 1), F32)
+        gain = gain_one_ref[...]
+
+        def put(out_ref, weight_ref, begin, grad):
+            cols = slice(begin, begin + grad.shape[1])
+            out_ref[:, cols] = grad * gain
+            return along(grad, weight_ref[:, cols])
+
+        pairs = [{}, {}]
+        for line in range(length):
+            rows = []
+            for number in range(4):
+                slot = line * 2 + number % 2
+                near, far = qkv_ref[0, slot].astype(F32), qkv_ref[1, slot].astype(F32)
+                rows.append(jnp.where(number // 2 == pair, near, far))
+            kv = rows[0] + rows[1] + rows[2] + rows[3]
+            for half in range(dp):
+                cols = slice(half * HEAD_DIM, (half + 1) * HEAD_DIM)
+                for number in (0, 2):
+                    two = jnp.concatenate([rows[number][:, cols], rows[number + 1][:, cols]], axis=1)
+                    begin = (half * length * 4 + line * 4 + number) * HEAD_DIM
+                    total = total + put(query_out_ref, query_ref, begin, two)
+                for kind in range(2):
+                    begin = ((kind + 1) * dp + half) * HEAD_DIM
+                    pairs[kind][half, line] = kv[:, begin : begin + HEAD_DIM]
+        for kind, (out_ref, weight_ref) in enumerate(
+            [(key_out_ref, key_ref), (value_out_ref, value_ref)]
+        ):
+            for half in range(dp):
+                for line in range(0, length, 2):
+                    two = [pairs[kind][half, line], pairs[kind][half, line + 1]]
+                    begin = (half * length + line) * HEAD_DIM
+                    total = total + put(
+                        out_ref, weight_ref, begin, jnp.concatenate(two, axis=1)
+                    )
+        one_out_ref[...] = total
+
+    total = jnp.zeros((slab, 1), F32)
+    for near_ref, far_ref, weight_ref, out_ref in (
+        (near_gate_ref, far_gate_ref, gate_ref, gate_out_ref),
+        (near_up_ref, far_up_ref, up_ref, up_out_ref),
+    ):
+        for number in range(4):
+            core = number % 2
+            near, far = near_ref[core].astype(F32), far_ref[core].astype(F32)
+            grad = jnp.where(number // 2 == pair, near, far)
+            cols = slice(number * columns, (number + 1) * columns)
+            total = total + along(grad, weight_ref[:, cols])
+            out_ref[:, cols] = grad * gain_two_ref[...]
+    two_out_ref[...] += total
+
+
+def unpack(pair, near, far, gate, up, qkv, query, key, value, gain_one, gain_two):
+    dp = lax.axis_size("dp")
+    seq = lax.axis_size("seq")
+    slab, ff = gate.shape
+    length = seq // 4
+    columns = ff // (dp * seq)
+    whole = lambda array: pl.BlockSpec(array.shape, lambda j, i: (0,) * array.ndim)
+    block = lambda kind: pl.BlockSpec((2, slab, columns), lambda j, i: (i, 0, kind * dp + j))
+    tile = pl.BlockSpec((slab, 4 * columns), lambda j, i: (0, j * length + i))
+    f32 = lambda array: jax.ShapeDtypeStruct(array.shape, F32)
+    outs = [f32(gate), f32(up), f32(query), f32(key), f32(value), f32(gain_one), f32(gain_two)]
+    return pl.pallas_call(
+        unpack_kernel,
+        grid=(dp, length),
+        in_specs=[pl.BlockSpec(memory_space=pltpu.SMEM)]
+        + [block(0), block(0), block(1), block(1), tile, tile]
+        + [whole(array) for array in (qkv, query, key, value, gain_one, gain_two)],
+        out_specs=[tile, tile] + [whole(array) for array in outs[2:]],
+        out_shape=outs,
+        compiler_params=pltpu.CompilerParams(vmem_limit_bytes=40 << 20),
+        cost_estimate=cost(slab * ff, 16 * slab * ff),
+    )(pair, near, far, near, far, gate, up, qkv, query, key, value, gain_one, gain_two)
+
+
 def swap_dp(values):
     count = lax.axis_size("dp")
     return lax.ppermute(values, "dp", [(i, (i + 1) % count) for i in range(count)])
@@ -1622,34 +1809,27 @@
     middle = inputs + attended_out
 
     factor_two = norm_factor(middle)
-    normed_two, hidden, feed_back = gather_feed(
+    normed_two, hidden, feed_back, feed_turned, mixed_part = gather_feed(
         (middle * factor_two).astype(BF16), grad_out, feed_weight, down_own, 3
     )
-    mixed = middle + scatter_rows(dot(hidden, down_own))
+    mixed = middle + scatter_rows(mixed_part)
 
     def norm_input_grad(values, factor, upstream):
         inner_mean = jnp.mean(upstream * values, axis=-1, keepdims=True)
         return factor * upstream - values * factor * factor * factor * inner_mean
 
-    middle_in = norm_input_grad(middle, factor_two, product_scatter(feed_back, feed_weight.T, 4))
-    middle_grad = grad_own.astype(F32) + middle_in
-    feed_part = t_dot(normed_two, feed_back).astype(BF16).reshape(dp, width // dp, -1)
-    attended_grad, output_part, feed_came = gather_back(
-        middle_grad.astype(BF16), output_own, attended, feed_part, 5
-    )
-
-    def halves(part):
-        half = part.shape[0] // dp
-        kept = lax.dynamic_slice_in_dim(part, data * half, half, 0)
-        return kept, lax.dynamic_slice_in_dim(part, (1 - data) * half, half, 0).astype(BF16)
+    normed_two_grad, feed_part = product_scatter_grad(feed_back, feed_turned, normed_two, 4)
+    middle_grad = grad_own.astype(F32) + norm_input_grad(middle, factor_two, normed_two_grad)
+    feed_part = feed_part.reshape(dp, width // dp, -1)
+    attended_grad, output_kept, output_away, down_kept, down_away, feed_came = gather_back(
+        middle_grad.astype(BF16), output_own, attended, hidden, grad_out, feed_part, 5
+    )
 
     def both(kept, came):
         return kept.astype(F32) + came.astype(F32)
 
     feed_kept = lax.dynamic_index_in_dim(feed_part, data, 0, keepdims=False)
     feed_sums = both(feed_kept, feed_came).astype(BF16).reshape(seq, slab, -1)
-    down_kept, down_away = halves(t_dot(hidden, grad_out))
-    output_kept, output_away = halves(output_part)
     qkv_back, feed_grad_far, down_came, output_came = attention_back_feed(
         queries,
         keys,
@@ -1673,47 +1853,31 @@
     )
     token_grad = middle_grad + norm_input_grad(inputs, factor_one, normed_one_grad)
 
-    pair = (mine // 2) % 2
-
-    def by_sender(near, far):
-        first = jnp.where(pair == 0, near, far)
-        second = jnp.where(pair == 0, far, near)
-        split = jnp.stack([first, second]).reshape(2, seq // 4, 2, *near.shape[1:])
-        return jnp.swapaxes(split, 0, 1).reshape(seq, *near.shape[1:])
-
-    feed_grad = by_sender(feed_grad_near, feed_grad_far).reshape(seq, slab, 2, dp, hidden_dev)
-    feed_grad = jnp.transpose(feed_grad, (2, 1, 3, 0, 4)).reshape(2, slab, -1).astype(F32)
-    qkv_grad = by_sender(qkv_grads[0], qkv_grads[1]).astype(F32)
-    qkv_grad = qkv_grad.reshape(seq, slab, 3, dp, HEAD_DIM)
-
-    def own_columns(part, kept):
-        summed = jnp.sum(part.reshape(kept, seq // kept, slab, dp, HEAD_DIM), axis=1)
-        return jnp.transpose(summed, (1, 2, 0, 3)).reshape(slab, dp * kept * HEAD_DIM)
-
-    query_grad = own_columns(qkv_grad[:, :, 0], half_heads)
-    key_grad = own_columns(qkv_grad[:, :, 1], half_kv)
-    value_grad = own_columns(qkv_grad[:, :, 2], half_kv)
-
-    def along(weight, grad):
-        return jnp.sum(weight.astype(F32) * grad, axis=1)
-
-    attn_gain_grad = (
-        along(query_weight, query_grad)
-        + along(key_weight, key_grad)
-        + along(value_weight, value_grad)
-    )
-    mlp_gain_grad = along(gate_weight, feed_grad[0]) + along(up_weight, feed_grad[1])
+    pair = ((mine // 2) % 2).reshape(1)
+    gate_grad, up_grad, query_grad, key_grad, value_grad, attn_gain_grad, mlp_gain_grad = unpack(
+        pair,
+        feed_grad_near,
+        feed_grad_far,
+        gate_weight,
+        up_weight,
+        qkv_grads,
+        query_weight,
+        key_weight,
+        value_weight,
+        gain_one,
+        gain_two,
+    )
     return (
         mixed,
         token_grad,
-        attn_gain_grad,
-        mlp_gain_grad,
-        query_grad * gain_one,
-        key_grad * gain_one,
-        value_grad * gain_one,
+        attn_gain_grad[:, 0],
+        mlp_gain_grad[:, 0],
+        query_grad,
+        key_grad,
+        value_grad,
         output_grad,
-        feed_grad[0] * gain_two,
-        feed_grad[1] * gain_two,
+        gate_grad,
+        up_grad,
         down_grad,
     )
 

time: 701 us -> 632 us (0.902); the launches traced: 692 us -> 631 us
  local copies, waits for them, and re-layouts: 63.3 us -> 19.8 us
  matrix products: 26.7 us -> 0 us
  Pallas kernels: 544 us -> 562 us
  other arithmetic: 42.9 us -> 35.1 us
    dot_general x3 -> x0, matrix products: 26.7 us -> none  [the longest x2 18.3 us: t_dot(): lax.dot_general(a, b, (((0,), (0,)), ((), ())), preferred_element_type=F32)]
    slice x4 -> x0, local copies, waits for them, and re-layouts: 15.3 us -> none  [the longest x2 7.7 us: shards(): feed_grad[1]]
    convert_element_type x4 -> x0, local copies, waits for them, and re-layouts: 13.2 us -> none  [the longest x1 6.58 us: shards(): jnp.transpose(feed_grad, (2, 1, 3, 0, 4)).reshape(2, slab, -1).astype(F32)]
    pallas_call x1 -> x2, Pallas kernels: 86.2 us -> 99 us  [the longest x1 92.1 us: product_scatter_grad(): pl.pallas_call(functools.partial(scatter_grad_kernel, scatter_tile(width)...]
    reshape x4 -> x0, local copies, waits for them, and re-layouts: 11.1 us -> none  [the longest x1 6.51 us: shards(): feed_weight = feed_weight.reshape(width, -1)]
    mul x3 -> x0, other arithmetic: 7.85 us -> none  [the longest x1 5.73 us: shards(): feed_grad[1] * gain_two]
  transfers between devices with their start and end apart: 2 -> 2, of which waited for: 0 -> 0; matrix products, arithmetic and copies ran while one was open for 16% -> 6% of each run, Pallas kernels for 70% -> 79%
where the time goes in v4:
time: 632 us; the launch traced here: 631 us
  Pallas kernels  562 us (89%)
  other arithmetic  35.1 us (6%)
  local copies, waits for them, and re-layouts  19.8 us (3%)
  between operations  14.8 us (2%)
    pallas_call x1, Pallas kernels, gather_project(): pl.pallas_call(project_kernel, out_shape=[jax.ShapeDtypeStruct((seq * row...  127 us
    pallas_call x1, Pallas kernels, product_scatter_grad(): pl.pallas_call(functools.partial(scatter_grad_kernel, scatter_tile(width)...  92.1 us
    pallas_call x1, Pallas kernels, product_scatter_last(): pl.pallas_call(functools.partial(scatter_last_kernel, scatter_tile(width)...  79.1 us
    pallas_call x1, Pallas kernels, gather_back(): pl.pallas_call(back_kernel, out_shape=[jax.ShapeDtypeStruct((seq * rows,...  68.4 us
    pallas_call x1, Pallas kernels, gather_feed(): pl.pallas_call(feed_kernel, out_shape=[jax.ShapeDtypeStruct((seq * rows,...  62.8 us
    pallas_call x1, Pallas kernels, product_scatter_feed(): pl.pallas_call(functools.partial(scatter_feed_kernel, scatter_tile(width)...  55.7 us
    pallas_call x1, Pallas kernels, attention_back_feed(): pl.pallas_call(functools.partial(attention_back_feed_kernel, block), grid...  37 us
    pallas_call x1, Pallas kernels, attention_feed(): pl.pallas_call(functools.partial(attention_feed_kernel, block), grid=(row...  32.3 us
  transfers between devices with their start and end apart: 2, of which 0 were waited for; matrix products, arithmetic and copies ran while one was open for 6% of the time, Pallas kernels for 79%

profile of v4, /device:TPU:0, one launch (start us, length us, event | category | flops | bytes accessed | tf_op | source)
XLA Modules:
  0.0 631.3 jit_solution(1089524371348674365)
XLA Ops:
  7.2 0.8 reduce-window.4
  8.1 0.6 slice.4
  8.6 0.7 add_compare_fusion
  9.3 1.9 broadcast_select_fusion
  11.5 1.8 fusion.9
  13.4 1.3 copy.43.sin_ref
  15.5 0.5 stack_reshape_broadcast_in_dim_reshape.3
  16.0 0.5 copy.41
  16.5 0.4 broadcast_in_dim.30
  16.9 0.4 broadcast_in_dim.31
  17.3 3.1 maximum_bitcast_fusion
  20.4 1.7 reshape.154.blocks_ref
  22.3 1.3 copy.42.cos_ref
  24.0 1.6 fusion.7
  25.5 1.2 convert_bitcast_fusion
  26.7 1.2 fusion.2.own_ref
  28.0 0.5 multiply_convert_fusion
  28.5 0.7 copy-done.6
  29.2 0.5 copy-done.7
  29.7 0.8 copy-done.20
  30.9 127.2 %shard_map.203 = (bf16[2048,2048]{1,0:T(8,128)(2,1)}, bf16[2048,128]{1,0:T(8,128)(2,1)S(1)}, bf16[2048,128]{1,0:T(8,128)(2,1)S(1)}, bf16[2048,128]{1,0:T(8,128)(...) custom-call(bf16[128,2048]{1,0:T(8,128)(2,1)S(1)} %fusion.2.own_ref,, ...), custom_call_target="tpu_custom_call" | custom-call | flops 3221225472 | bytes 16777216 | tf_op jit(solution)/shard_map/pallas_call | solution.py:628
  158.1 1.1 copy-done.16
  159.3 32.3 %shard_map.204 = (f32[2048,128]{1,0:T(8,128)S(1)}, f32[2048,2]{1,0:T(8,128)S(1)}, bf16[8,64,1024]{2,1,0:T(8,128)(2,1)S(1)}) custom-call(bf16[2048,128]{1,0:T(8,128)(2,1)S(1)} %get-tuple-element.51.q_ref, bf16[2048,128]{1,0:T(8,128)(2,1)S(1)} %get-tuple-element.52.k_ref, bf16[2048,128]{1,0:T(8,128)(2,1)S(1)} %get-tuple-element.53.v_ref, ...), custom_call_target="tpu_custom_call" | custom-call | flops 1073741824 | bytes 2621440 | tf_op jit(solution)/shard_map/pallas_call | solution.py:691
  191.8 55.7 %shard_map.205 = (f32[128,2048]{1,0:T(8,128)S(1)}, bf16[2,16,64,1024]{3,2,1,0:T(8,128)(2,1)S(1)}) custom-call(bf16[2048,128]{1,0:T(8,128)(2,1)S(1)} %convert_element_type.97.a_ref.attended_ref, bf16[128,2048]{1,0:T(8,128)(2,1)S(1)} %bitcast.25, bf16[8,64,1024]{2,1,0:T(8,128)(2,1)S(1)} %get-tuple-element.56.near_ref, ...), custom_call_target="tpu_custom_call" | custom-call | flops 1073741824 | bytes 16777216 | tf_op jit(solution)/shard_map/pallas_call | solution.py:976
  247.5 2.0 copy-done.35
  249.7 1.0 multiply_convert_fusion.2.own_ref
  250.7 62.8 %shard_map.206 = (bf16[2048,2048]{1,0:T(8,128)(2,1)}, bf16[2048,512]{1,0:T(8,128)(2,1)}, bf16[2048,1024]{1,0:T(8,128)(2,1)}, bf16[1024,2048]{1,0:T(8,128)(2,1)}, bf16[2048,2048]{1,0:T(8,128)(2,1)}) custom-call(bf16[128,2048]{1,0:T(8,128)(2,1)} %multiply_convert_fusion.2.own_ref, bf16[2048,2048]{1,0:T(8,128)(2,1)} %all-gather.2.cloned.1.call-done.grad_ref.out_grad_ref, ...), custom_call_target="tpu_custom_call" | custom-call | flops 17179869184 | bytes 33554432 | tf_op jit(solution)/shard_map/pallas_call | solution.py:1066
  313.6 0.7 copy.48.gain_one_ref
  314.3 1.4 copy.49.gain_two_ref
  315.6 92.1 %shard_map.207 = (f32[128,2048]{1,0:T(8,128)}, bf16[2048,1024]{1,0:T(8,128)(2,1)}) custom-call(bf16[2048,1024]{1,0:T(8,128)(2,1)} %get-tuple-element.62.a_ref, bf16[1024,2048]{1,0:T(8,128)(2,1)} %get-tuple-element.63.b_ref, bf16[2048,2048]{1,0:T(8,128)(2,1)} %get-tuple-element.64.normed_ref), custom_call_target="tpu_custom_call" | custom-call | flops 17179869184 | bytes 33554432 | tf_op jit(solution)/shard_map/pallas_call | solution.py:921
  407.8 1.6 multiply_reduce_fusion
  409.6 0.4 fusion.10.own_ref
  410.0 0.5 copy-done.23
  410.5 68.4 %shard_map.208 = (bf16[2048,128]{1,0:T(8,128)(2,1)S(1)}, f32[64,2048]{1,0:T(8,128)S(1)}, bf16[64,2048]{1,0:T(8,128)(2,1)S(1)}, f32[256,2048]{1,0:T(8,128)S(1)}, ...) custom-call(bf16[128,2048]{1,0:T(8,128)(2,1)S(1)} %fusion.10.own_ref, bf16[128,2048]{1,0:T(8,128)(2,1)S(1)} %bitcast.26, ...), custom_call_target="tpu_custom_call" | custom-call | flops 4294967296 | bytes 25165824 | tf_op jit(solution)/shard_map/pallas_call | solution.py:1147
  479.0 5.4 fusion
  484.4 37.0 %shard_map.209 = (bf16[2048,384]{1,0:T(8,128)(2,1)}, bf16[8,64,1024]{2,1,0:T(8,128)(2,1)}, bf16[256,2048]{1,0:T(8,128)(2,1)}, bf16[64,2048]{1,0:T(8,128)(2,1)}) custom-call(bf16[2048,128]{1,0:T(8,128)(2,1)} %copy-done.13, bf16[2048,128]{1,0:T(8,128)(2,1)} %copy-done.14, bf16[2048,128]{1,0:T(8,128)(2,1)} %copy-done.15, bf16[2048,128]{1,0:T(8,128)(2,1)} %copy-done.25, ...), custom_call_target="tpu_custom_call" | custom-call | flops 2684354560 | bytes 5242880 | tf_op jit(solution)/shard_map/pallas_call | solution.py:1253
  521.5 79.1 %shard_map.210 = (f32[128,2048]{1,0:T(8,128)}, bf16[8,64,1024]{2,1,0:T(8,128)(2,1)}, bf16[2,8,64,384]{3,2,1,0:T(8,128)(2,1)}) custom-call(bf16[2048,384]{1,0:T(8,128)(2,1)} %get-tuple-element.73.a_ref, bf16[2048,384]{1,0:T(8,128)(2,1)} %bitcast.24, bf16[2048,2048]{1,0:T(8,128)(2,1)} %get-tuple-element.75.normed_ref, bf16[16,64,1024]{2,1,0:T(8,128)(2,1)} %bitcast.30), custom_call_target="tpu_custom_call" | custom-call | flops 3221225472 | bytes 16777216 | tf_op jit(solution)/shard_map/pallas_call | solution.py:1373
  600.7 1.2 copy-done.10
  601.9 1.1 copy-done.21
  603.0 6.9 %shard_map.211 = (f32[64,8192]{1,0:T(8,128)}, f32[64,8192]{1,0:T(8,128)}, f32[64,2048]{1,0:T(8,128)}, f32[64,512]{1,0:T(8,128)}, f32[64,512]{1,0:T(8,128)}, /*index=5*/f32[64,1]{1,0:T(8,128)S(1)}, f32[64,1]{1,0:T(8,128)S(1)}) custom-call(s32[1]{0:T(128)} %bitcast.16.pair_ref, bf16[8,64,1024]{2,1,0:T(8,128)(2,1)S(1)} %copy-done.10, ...), custom_call_target="tpu_custom_call" | custom-call | flops 524288 | bytes 8388608 | tf_op jit(solution)/shard_map/pallas_call | solution.py:1497
  610.0 0.6 copy-done.31
  610.6 0.6 copy-done.32
  611.2 1.5 reduce
  612.7 1.4 reduce.1
  614.1 1.5 fusion.8
  615.6 1.9 convert_add_fusion.4
  617.6 2.8 convert_add_fusion.1
  620.4 4.1 fusion.6
  (104 shorter events, 2.6 us)
Async XLA Ops:
  7.2 243.5 %all-gather.2.cloned.1.call-start = ((), (), s32[]{:S(2)}) async-start(), calls=%async_computation.1 | async-start | bytes 8912896 | tf_op jit(solution)/shard_map/all_gather | solution.py:1528
  11.3 609.1 %reduce-scatter.2.cloned.1.call-start = ((), (), s32[]{:S(2)}) async-start(), calls=%async_computation.2 | async-start | bytes 8912896 | tf_op jit(solution)/shard_map/reduce_scatter | solution.py:1532
  13.3 1.5 copy-start.43
  13.3 1.5 copy-start.26
  13.3 1.5 copy-start.27
  13.3 2.0 copy-start.19
  20.4 1.7 copy-start.42
  22.2 5.7 copy-start.3
  22.3 5.7 copy-start.4
  23.9 135.3 %copy-start = (s32[2048,1]{1,0:T(8,128)}, s32[2048,1]{1,0:T(8,128)S(1)}, u32[]{:S(2)}) copy-start(s32[2048,1]{1,0:T(8,128)S(1)} %copy.44.open_ref) | copy-start | bytes 24580
  27.9 1.2 copy-start.6
  27.9 1.8 copy-start.7
  28.0 2.5 copy-start.20
  28.0 2.9 copy-start.33
  28.0 2.9 copy-start.34
  28.5 129.6 %copy-start.1 = (bf16[64,8192]{1,0:T(8,128)(2,1)}, bf16[64,8192]{1,0:T(8,128)(2,1)S(1)}, u32[]{:S(2)}) copy-start(bf16[64,8192]{1,0:T(8,128)(2,1)S(1)} %get-tuple-element.100.up_ref) | copy-start | bytes 3145732
  28.5 129.6 %copy-start.2 = (bf16[64,8192]{1,0:T(8,128)(2,1)}, bf16[64,8192]{1,0:T(8,128)(2,1)S(1)}, u32[]{:S(2)}) copy-start(bf16[64,8192]{1,0:T(8,128)(2,1)S(1)} %get-tuple-element.101.gate_ref) | copy-start | bytes 3145732
  158.1 1.1 copy-start.16
  159.3 32.4 %copy-start.13 = (bf16[2048,128]{1,0:T(8,128)(2,1)}, bf16[2048,128]{1,0:T(8,128)(2,1)S(1)}, u32[]{:S(2)}) copy-start(bf16[2048,128]{1,0:T(8,128)(2,1)S(1)} %get-tuple-element.51.q_ref) | copy-start | bytes 1572868
  159.3 32.4 %copy-start.14 = (bf16[2048,128]{1,0:T(8,128)(2,1)}, bf16[2048,128]{1,0:T(8,128)(2,1)S(1)}, u32[]{:S(2)}) copy-start(bf16[2048,128]{1,0:T(8,128)(2,1)S(1)} %get-tuple-element.52.k_ref) | copy-start | bytes 1572868
  159.3 32.4 %copy-start.15 = (bf16[2048,128]{1,0:T(8,128)(2,1)}, bf16[2048,128]{1,0:T(8,128)(2,1)S(1)}, u32[]{:S(2)}) copy-start(bf16[2048,128]{1,0:T(8,128)(2,1)S(1)} %get-tuple-element.53.v_ref) | copy-start | bytes 1572868
  159.3 32.4 %copy-start.36 = (bf16[2,256,2048]{2,1,0:T(8,128)(2,1)}, bf16[2,256,2048]{2,1,0:T(8,128)(2,1)S(1)}, u32[]{:S(2)}) copy-start(bf16[2,256,2048]{2,1,0:T(8,128)(2,1)S(1)} %get-tuple-element.60) | copy-start | bytes 6291460
  159.3 32.5 %copy-start.22 = (bf16[2,64,2048]{2,1,0:T(8,128)(2,1)}, bf16[2,64,2048]{2,1,0:T(8,128)(2,1)S(1)}, u32[]{:S(2)}) copy-start(bf16[2,64,2048]{2,1,0:T(8,128)(2,1)S(1)} %get-tuple-element.55) | copy-start | bytes 1572868
  191.7 55.8 %copy-start.8 = (f32[2048,128]{1,0:T(8,128)}, f32[2048,128]{1,0:T(8,128)S(1)}, u32[]{:S(2)}) copy-start(f32[2048,128]{1,0:T(8,128)S(1)} %get-tuple-element.54.att_ref) | copy-start | bytes 3145732
  191.7 55.8 %copy-start.17 = (f32[2048,2]{1,0:T(8,128)}, f32[2048,2]{1,0:T(8,128)S(1)}, u32[]{:S(2)}) copy-start(f32[2048,2]{1,0:T(8,128)S(1)} %get-tuple-element.69.lse_ref) | copy-start | bytes 49156
  191.7 57.8 %copy-start.37 = (bf16[128,2048]{1,0:T(8,128)(2,1)S(1)}, bf16[128,2048]{1,0:T(8,128)(2,1)}, u32[]{:S(2)}) copy-start(bf16[128,2048]{1,0:T(8,128)(2,1)} %param.12) | copy-start | bytes 1572868
  247.5 2.1 copy-start.35
  407.8 1.6 copy-start.38
  407.8 1.7 copy-start.39
  407.8 1.8 copy-start.41
  409.4 1.1 copy-start.23
  410.5 68.4 %copy-start.40 = (bf16[2048,1024]{1,0:T(8,128)(2,1)S(1)}, bf16[2048,1024]{1,0:T(8,128)(2,1)}, u32[]{:S(2)}) copy-start(bf16[2048,1024]{1,0:T(8,128)(2,1)} %get-tuple-element.67) | copy-start | bytes 12582916
  478.9 5.5 copy-start.11
  478.9 5.5 copy-start.18
  478.9 5.5 copy-start.25
  478.9 5.5 copy-start.28
  478.9 5.5 copy-start.24
  521.5 79.2 %copy-start.5 = (bf16[64,8192]{1,0:T(8,128)(2,1)S(1)}, bf16[64,8192]{1,0:T(8,128)(2,1)}, u32[]{:S(2)}) copy-start(bf16[64,8192]{1,0:T(8,128)(2,1)} %gate_ref.1) | copy-start | bytes 3145732
  521.5 79.2 %copy-start.9 = (bf16[8,64,1024]{2,1,0:T(8,128)(2,1)S(1)}, bf16[8,64,1024]{2,1,0:T(8,128)(2,1)}, u32[]{:S(2)}) copy-start(bf16[8,64,1024]{2,1,0:T(8,128)(2,1)} %get-tuple-element.78.far_gate_ref.far_up_ref) | copy-start | bytes 3145732
  521.5 79.2 %copy-start.29 = (f32[64,1]{1,0:T(8,128)S(1)}, f32[64,1]{1,0:T(8,128)}, u32[]{:S(2)}) copy-start(f32[64,1]{1,0:T(8,128)} %copy.48.gain_one_ref) | copy-start | bytes 772
  521.5 79.2 %copy-start.30 = (f32[64,1]{1,0:T(8,128)S(1)}, f32[64,1]{1,0:T(8,128)}, u32[]{:S(2)}) copy-start(f32[64,1]{1,0:T(8,128)} %copy.49.gain_two_ref) | copy-start | bytes 772
  600.7 1.2 copy-start.10
  601.9 1.1 copy-start.21
  609.9 0.6 copy-start.31
  610.6 0.6 copy-start.32
  611.2 6.4 %copy-start.12 = (f32[256,2048]{1,0:T(8,128)S(1)}, f32[256,2048]{1,0:T(8,128)}, u32[]{:S(2)}) copy-start(f32[256,2048]{1,0:T(8,128)} %copy-done.11) | copy-start | bytes 6291460
Sparse Core Ops, SparseCore 0:
  11.4 109.7 all-gather.1
  313.6 138.9 reduce-scatter.1

commit v5 on v4

--- a/solution.py
+++ b/solution.py
@@ -162,6 +162,10 @@
     )(queries, keys, values, grads, attended, log_total, opening)
 
 
+def nothing():
+    pass
+
+
 class Place:
     def __init__(self):
         self.dp = lax.axis_index("dp")
@@ -213,7 +217,7 @@
         inner = (self.line > 0) & (self.line < self.length - 1)
         pl.semaphore_wait(barrier, jnp.where(inner, 4, 3) + (1 if partner else 0))
 
-    def greet_all(self):
+    def greet_all(self, meanwhile=nothing):
         barrier = pltpu.get_barrier_semaphore()
 
         def signal(device):
@@ -225,6 +229,7 @@
         def _(ahead):
             signal((self.dp, lax.rem(self.mine + ahead, self.count)))
 
+        meanwhile()
         pl.semaphore_wait(barrier, self.count)
 
 
@@ -304,15 +309,10 @@
     return Spread(here, same, copies)
 
 
-def nothing():
-    pass
-
-
-def gather_units(here, own_ref, buf, send_sems, recv_sems, compute, between=None, ready=0):
+def gather_units(here, buf, send_sems, recv_sems, compute, between=None, ready=0, started=nothing):
     length = here.length
     last = length - 1
     steps = 2 * length
-    half = own_ref.shape[0] // 2
     mine = here.mine
     shorter = jnp.minimum(here.line, last - here.line)
     longer = jnp.where(here.line < last - here.line, 1, -1)
@@ -352,11 +352,11 @@
         compute(number, here.index(line, pair, 0))
 
     for part in range(2):
-        buf[mine, part] = own_ref[pl.ds(part * half, half), :]
         pl.when(here.line < last)(lambda part=part: up(mine, part).start())
         pl.when(here.line > 0)(lambda part=part: down(mine, part).start())
         across(mine, part).start()
         sideways(mine, part).start()
+    started()
 
     @pl.loop(0, steps)
     def _(step):
@@ -414,9 +414,15 @@
             sideways(here.index(line, 1 - here.pair, here.core), part).wait_send()
 
 
+def put_own(here, own_ref, buf):
+    half = buf.shape[2]
+    for part in range(2):
+        buf[here.mine, part] = own_ref[pl.ds(part * half, half), :]
+
+
 def gather_scratch(seq, rows, width):
     return [
-        pltpu.VMEM((seq, 2, rows // 2, width), BF16),
+        pltpu.VMEM((seq, 2, rows, width), BF16),
         pltpu.SemaphoreType.DMA((4, seq, 2)),
         pltpu.SemaphoreType.DMA((seq, 2)),
     ]
@@ -485,25 +491,37 @@
 
 
 def project_kernel(
-    own_ref,
-    blocks_ref,
+    lengths_ref,
+    tokens_ref,
+    cotangent_ref,
+    query_ref,
+    key_ref,
+    value_ref,
     gate_ref,
     up_ref,
+    gain_one_ref,
+    gain_two_ref,
+    freq_ref,
     down_ref,
     output_ref,
-    cos_ref,
-    sin_ref,
     normed_ref,
+    grads_ref,
     q_ref,
     k_ref,
     v_ref,
+    cos_ref,
+    sin_ref,
+    open_ref,
     weight_ref,
+    gate_out_ref,
+    up_out_ref,
     feed_ref,
     down_out_ref,
     output_out_ref,
     buf,
     send_sems,
     recv_sems,
+    blocks,
     store_sems,
     near_sems,
     far_sems,
@@ -513,16 +531,52 @@
     pair_sems,
 ):
     here = Place()
-    here.greet_all()
     cols = q_ref.shape[1]
-    rows = own_ref.shape[0]
+    rows = tokens_ref.shape[0]
     dp = here.dp
+    ends = [lengths_ref[0, 0]]
+    for j in range(1, DOCS):
+        ends.append(ends[-1] + lengths_ref[0, j])
+
+    def own_rows():
+        chunk = 32
+
+        @pl.loop(0, rows // chunk)
+        def _(i):
+            some = pl.ds(pl.multiple_of(i * chunk, chunk), chunk)
+            values = tokens_ref[some, :].astype(F32)
+            factor = lax.rsqrt(jnp.mean(values * values, axis=1, keepdims=True) + EPS)
+            buf[here.mine, 0, some, :] = (values * factor).astype(BF16)
+            shape = (chunk, cotangent_ref.shape[1])
+            place = here.mine * rows + i * chunk + lax.broadcasted_iota(jnp.int32, shape, 0)
+            grads = cotangent_ref[some, :].astype(F32)
+            buf[here.mine, 1, some, :] = jnp.where(place < ends[-1], grads, 0.0).astype(BF16)
+
+    def own_blocks():
+        gain = gain_one_ref[...]
+        query = query_ref[...].astype(F32) * gain
+        key = key_ref[...].astype(F32) * gain
+        value = value_ref[...].astype(F32) * gain
+
+        def heads(array, number, kept):
+            parts = []
+            for half in range(2):
+                head = half * kept + number * kept // blocks.shape[0]
+                parts.append(array[:, head * HEAD_DIM : (head + 1) * HEAD_DIM])
+            return jnp.concatenate(parts, axis=1).astype(BF16)
+
+        for number in range(blocks.shape[0]):
+            blocks[number, :, :cols] = heads(query, number, HEADS // 2)
+            blocks[number, :, cols : 2 * cols] = heads(key, number, KV_HEADS // 2)
+            blocks[number, :, 2 * cols :] = heads(value, number, KV_HEADS // 2)
+
+    here.greet_all(own_rows)
 
     def weight_spread(same, sems):
         def copies(peer, sender, at, sem):
             return [
                 remote(
-                    blocks_ref.at[peer],
+                    blocks.at[peer],
                     weight_ref.at[dp, sender],
                     sems.at[0, sem],
                     sems.at[1, at],
@@ -534,21 +588,16 @@
 
     near = weight_spread(True, near_sems)
     far = weight_spread(False, far_sems)
-    far.start()
-    near.start()
-    weight_ref[dp, here.mine] = blocks_ref[here.mine]
     swaps = []
     for number, (src, dst) in enumerate([(down_ref, down_out_ref), (output_ref, output_out_ref)]):
         swaps.append(
             remote(src, dst.at[dp], swap_sems.at[0, number], swap_sems.at[1, number], here.partner())
         )
         swaps.append(pltpu.make_async_copy(src, dst.at[dp], local_sems.at[number]))
-    for one in swaps:
-        one.start()
-    feed = feed_spread(here, True, (gate_ref, up_ref), feed_ref, feed_sems)
+    feed = feed_spread(here, True, (gate_out_ref, up_out_ref), feed_ref, feed_sems)
     columns = feed_ref.shape[2] // 4
     own_feed = []
-    for kind, weight in enumerate((gate_ref, up_ref)):
+    for kind, weight in enumerate((gate_out_ref, up_out_ref)):
         for half in range(2):
             part = kind * 2 + half
             begin = pl.multiple_of((half * here.count + here.mine) * columns, columns)
@@ -559,8 +608,6 @@
                     local_sems.at[2 + part],
                 )
             )
-    for one in own_feed:
-        one.start()
 
     def pair_copy(source, sender):
         return remote(
@@ -571,11 +618,45 @@
             here.partner(),
         )
 
+    def own_tables():
+        chunk = 128
+
+        @pl.loop(0, open_ref.shape[0] // chunk)
+        def _(i):
+            some = pl.ds(pl.multiple_of(i * chunk, chunk), chunk)
+            place = i * chunk + lax.broadcasted_iota(jnp.int32, (chunk, 1), 0)
+            opening = jnp.zeros((chunk, 1), jnp.int32)
+            for end in ends:
+                opening = jnp.where(place >= end, end, opening)
+            open_ref[some, :] = opening
+            angles = (place - opening).astype(F32) * freq_ref[...]
+            lane = lax.broadcasted_iota(jnp.int32, angles.shape, 1)
+            sine = jnp.sin(angles)
+            cos_ref[some, :] = jnp.cos(angles)
+            sin_ref[some, :] = jnp.where(lane % HEAD_DIM < HEAD_DIM // 2, -sine, sine)
+
+    def started():
+        own_blocks()
+        far.start()
+        near.start()
+        weight_ref[dp, here.mine] = blocks[here.mine]
+        for one in swaps:
+            one.start()
+        chunk = 512
+
+        @pl.loop(0, gate_ref.shape[1] // chunk)
+        def _(i):
+            some = pl.ds(pl.multiple_of(i * chunk, chunk), chunk)
+            gain = gain_two_ref[...]
+            gate_out_ref[:, some] = (gate_ref[:, some].astype(F32) * gain).astype(BF16)
+            up_out_ref[:, some] = (up_ref[:, some].astype(F32) * gain).astype(BF16)
+
+        for one in own_feed:
+            one.start()
+        feed.start()
+        own_tables()
+
     def between(step):
-        @pl.when(step == 0)
-        def _():
-            feed.start()
-
         @pl.when(step == 1)
         def _():
             near.finish()
@@ -591,12 +672,26 @@
             def _(sender):
                 pair_copy(1 - dp, sender).wait_recv()
 
-    store = UnitStore(buf, normed_ref, store_sems)
+    def stores(number, first):
+        made = []
+        for block in range(2):
+            where = pl.ds(pl.multiple_of((first + block) * rows, rows), rows)
+            for part, out_ref in enumerate((normed_ref, grads_ref)):
+                made.append(
+                    pltpu.make_async_copy(
+                        buf.at[first + block, part],
+                        out_ref.at[where],
+                        store_sems.at[number, block, part],
+                    )
+                )
+        return made
 
     def compute(number, first):
-        store.start(number, first)
+        for one in stores(number, first):
+            one.start()
         weight = weight_ref[...].reshape(-1, weight_ref.shape[-1])
-        qkv = dot(take_unit(buf, first), weight)
+        unit = buf[pl.ds(first, 2), 0]
+        qkv = dot(unit.reshape(-1, unit.shape[-1]), weight)
         where = unit_rows(first, rows)
         cosine = cos_ref[where, :]
         sine = sin_ref[where, :]
@@ -605,42 +700,56 @@
         k_ref[where, :] = rotated(qkv[:, cols : 2 * cols], cosine, sine).astype(BF16)
         v_ref[where, :] = qkv[:, 2 * cols :].astype(BF16)
 
-    gather_units(here, own_ref, buf, send_sems, recv_sems, compute, between, 3)
+    gather_units(here, buf, send_sems, recv_sems, compute, between, 3, started)
 
     @pl.loop(0, here.count)
     def _(sender):
         pair_copy(dp, sender).wait_send()
 
-    store.finish()
+    @pl.loop(0, here.count // 2)
+    def _(number):
+        for one in stores(number, 0):
+            one.wait()
+
     feed.finish()
     for one in swaps + own_feed:
         one.wait()
 
 
-def gather_project(own, blocks, gate, up, down, output, cosine, sine, call_id):
+def gather_project(
+    lengths, tokens, cotangent, query, key, value, gate, up, gains, freq, down, output, call_id
+):
     seq = lax.axis_size("seq")
-    rows, width = own.shape
-    cols = cosine.shape[1]
-    slab = gate.shape[0]
-    head = jax.ShapeDtypeStruct((seq * rows, cols), BF16)
-    feed_cols = 4 * down.shape[0]
+    rows, width = tokens.shape
+    cols = 2 * HEAD_DIM
+    slab, ff = gate.shape
+    bf16 = lambda *shape: jax.ShapeDtypeStruct(shape, BF16)
+    f32 = lambda *shape: jax.ShapeDtypeStruct(shape, F32)
+    all_rows = seq * rows
     dma = pltpu.SemaphoreType.DMA
     return pl.pallas_call(
         project_kernel,
         out_shape=[
-            jax.ShapeDtypeStruct((seq * rows, width), BF16),
-            head,
-            head,
-            head,
-            jax.ShapeDtypeStruct((2, *blocks.shape), BF16),
-            jax.ShapeDtypeStruct((seq // 2, slab, feed_cols), BF16),
-            jax.ShapeDtypeStruct((2, *down.shape), BF16),
-            jax.ShapeDtypeStruct((2, *output.shape), BF16),
+            bf16(all_rows, width),
+            bf16(all_rows, width),
+            bf16(all_rows, cols),
+            bf16(all_rows, cols),
+            bf16(all_rows, cols),
+            f32(all_rows, cols),
+            f32(all_rows, cols),
+            jax.ShapeDtypeStruct((all_rows, 1), jnp.int32),
+            bf16(2, seq, slab, 3 * cols),
+            bf16(slab, ff),
+            bf16(slab, ff),
+            bf16(seq // 2, slab, 4 * down.shape[0]),
+            bf16(2, *down.shape),
+            bf16(2, *output.shape),
         ],
-        in_specs=[VMEM, VMEM, HBM, HBM, HBM, HBM, VMEM, VMEM],
-        out_specs=[HBM, VMEM, VMEM, VMEM, VMEM, HBM, HBM, HBM],
+        in_specs=[pl.BlockSpec(memory_space=pltpu.SMEM)] + [VMEM] * 10 + [HBM] * 2,
+        out_specs=[HBM] * 2 + [VMEM] * 9 + [HBM] * 3,
         scratch_shapes=gather_scratch(seq, rows, width)
         + [
+            pltpu.VMEM((seq, slab, 3 * cols), BF16),
             dma((seq // 2, 2, 2)),
             dma((2, seq // 2)),
             dma((2, seq // 2)),
@@ -649,9 +758,9 @@
             dma((6,)),
             dma((2, seq)),
         ],
-        compiler_params=params(call_id, 40),
-        cost_estimate=cost(2 * seq * rows * width * 3 * cols, 4 * seq * rows * width),
-    )(own, blocks, gate, up, down, output, cosine, sine)
+        compiler_params=params(call_id, 56),
+        cost_estimate=cost(2 * all_rows * width * 3 * cols, 8 * all_rows * width),
+    )(lengths, tokens, cotangent, query, key, value, gate, up, *gains, freq, down, output)
 
 
 def attention_feed_kernel(
@@ -892,8 +1001,11 @@
     return cost(2 * a.shape[0] * a.shape[1] * width, 4 * a.shape[0] * width)
 
 
-def scatter_grad_kernel(tile, a_ref, b_ref, normed_ref, out_ref, grad_ref, *scratch):
+def scatter_grad_kernel(tile, a_ref, b_ref, normed_hbm, out_ref, grad_ref, *scratch):
     here = Place()
+    normed_ref, fetch_sem = scratch[SCATTER_SCRATCH:]
+    fetch = pltpu.make_async_copy(normed_hbm, normed_ref, fetch_sem.at[0])
+    fetch.start()
     here.greet()
     cols = normed_ref.shape[1] // (here.length * SCATTER_PARTS)
 
@@ -909,7 +1021,8 @@
         a_ref,
         b_ref,
         out_ref,
-        *scratch,
+        *scratch[:SCATTER_SCRATCH],
+        between=fetch.wait,
         filler=filler,
     )
 
@@ -924,9 +1037,10 @@
             jax.ShapeDtypeStruct((rows, width), F32),
             jax.ShapeDtypeStruct((width, a.shape[1]), BF16),
         ],
-        in_specs=[VMEM] * 3,
+        in_specs=[VMEM, VMEM, HBM],
         out_specs=[VMEM] * 2,
-        scratch_shapes=scatter_scratch(seq, rows, width),
+        scratch_shapes=scatter_scratch(seq, rows, width)
+        + [pltpu.VMEM(normed.shape, BF16), pltpu.SemaphoreType.DMA((1,))],
         compiler_params=params(call_id, 56),
         cost_estimate=scatter_cost(a, 2 * width),
     )(a, b, normed)
@@ -990,13 +1104,13 @@
 
 def feed_kernel(
     own_ref,
-    grad_ref,
-    feed_ref,
-    down_ref,
+    grad_hbm,
+    feed_hbm,
+    down_hbm,
     normed_ref,
-    hidden_ref,
-    back_ref,
-    turned_ref,
+    hidden_out_ref,
+    back_out_ref,
+    turned_out_ref,
     mixed_ref,
     buf,
     send_sems,
@@ -1004,8 +1118,25 @@
     store_sems,
     mixed_buf,
     mixed_sems,
+    grad_ref,
+    feed_ref,
+    down_ref,
+    hidden_ref,
+    back_ref,
+    turned_ref,
+    fetch_sems,
+    out_sems,
 ):
     here = Place()
+    fetches = [
+        pltpu.make_async_copy(src, dst, fetch_sems.at[number])
+        for number, (src, dst) in enumerate(
+            [(feed_hbm, feed_ref), (down_hbm, down_ref), (grad_hbm, grad_ref)]
+        )
+    ]
+    for one in fetches:
+        one.start()
+    put_own(here, own_ref, buf)
     here.greet()
     rows = own_ref.shape[0]
     width = own_ref.shape[1]
@@ -1020,8 +1151,29 @@
             mixed_buf.at[slot], mixed_ref.at[unit_rows(first, rows)], mixed_sems.at[slot]
         )
 
+    def outs(number, first):
+        where = unit_rows(first, rows)
+        share = width // (2 * here.length)
+        some = pl.ds(pl.multiple_of(number * share, share), share)
+        return [
+            pltpu.make_async_copy(src, dst, out_sems.at[number, i])
+            for i, (src, dst) in enumerate(
+                [
+                    (hidden_ref.at[where], hidden_out_ref.at[where]),
+                    (back_ref.at[where], back_out_ref.at[where]),
+                    (turned_ref.at[:, some], turned_out_ref.at[:, some]),
+                ]
+            )
+        ]
+
     def compute(number, first):
         store.start(number, first)
+
+        @pl.when(number == 0)
+        def _():
+            for one in fetches:
+                one.wait()
+
         pl.when(number >= 2)(lambda: mixed_copy(number, first).wait())
         where = unit_rows(first, rows)
         normed = take_unit(buf, first)
@@ -1052,8 +1204,16 @@
         share = width // (2 * here.length)
         some = pl.ds(pl.multiple_of(number * share, share), share)
         turned_ref[:, some] = feed_ref[some, :].T
-
-    gather_units(here, own_ref, buf, send_sems, recv_sems, compute)
+        for one in outs(number, first):
+            one.start()
+
+    gather_units(here, buf, send_sems, recv_sems, compute)
+
+    @pl.loop(0, here.count // 2)
+    def _(number):
+        for one in outs(number, 0):
+            one.wait()
+
     mixed_copy(0, 0).wait()
     mixed_copy(1, 0).wait()
     store.finish()
@@ -1072,13 +1232,21 @@
             jax.ShapeDtypeStruct((2 * hidden, width), BF16),
             jax.ShapeDtypeStruct((seq * rows, width), BF16),
         ],
-        in_specs=[VMEM] * 4,
-        out_specs=[HBM, VMEM, VMEM, VMEM, HBM],
-        scratch_shapes=gather_scratch(seq, rows, width)
+        in_specs=[VMEM] + [HBM] * 3,
+        out_specs=[HBM] * 5,
+        scratch_shapes=gather_scratch(seq, rows // 2, width)
         + [
             pltpu.SemaphoreType.DMA((seq // 2, 2, 2)),
             pltpu.VMEM((2, 2 * rows, width), BF16),
             pltpu.SemaphoreType.DMA((2,)),
+            pltpu.VMEM((seq * rows, width), BF16),
+            pltpu.VMEM((width, 2 * hidden), BF16),
+            pltpu.VMEM((hidden, width), BF16),
+            pltpu.VMEM((seq * rows, hidden), BF16),
+            pltpu.VMEM((seq * rows, 2 * hidden), BF16),
+            pltpu.VMEM((2 * hidden, width), BF16),
+            pltpu.SemaphoreType.DMA((3,)),
+            pltpu.SemaphoreType.DMA((seq // 2, 3)),
         ],
         compiler_params=params(call_id, 56),
         cost_estimate=cost(8 * seq * rows * width * hidden, 8 * seq * rows * width),
@@ -1089,8 +1257,8 @@
     own_ref,
     weight_ref,
     attended_ref,
-    hidden_ref,
-    out_grad_ref,
+    hidden_hbm,
+    out_grad_hbm,
     share_ref,
     grad_ref,
     output_kept_ref,
@@ -1103,8 +1271,18 @@
     recv_sems,
     swap_sems,
     part,
+    hidden_ref,
+    out_grad_ref,
+    fetch_sems,
 ):
     here = Place()
+    fetches = [
+        pltpu.make_async_copy(hidden_hbm, hidden_ref, fetch_sems.at[0]),
+        pltpu.make_async_copy(out_grad_hbm, out_grad_ref, fetch_sems.at[1]),
+    ]
+    for one in fetches:
+        one.start()
+    put_own(here, own_ref, buf)
     here.greet(partner=True)
     rows = own_ref.shape[0]
     width = own_ref.shape[1]
@@ -1131,9 +1309,15 @@
             cols = slice(t * tile, (t + 1) * tile)
             part[:, cols] += t_dot(attended, unit[:, cols])
         some = pl.ds(pl.multiple_of(number * share, share), share)
+
+        @pl.when(number == 0)
+        def _():
+            for one in fetches:
+                one.wait()
+
         split(t_dot(hidden_ref[...], out_grad_ref[:, some]), down_kept_ref, down_away_ref, some)
 
-    gather_units(here, own_ref, buf, send_sems, recv_sems, compute)
+    gather_units(here, buf, send_sems, recv_sems, compute)
     for t in range(width // tile):
         cols = slice(t * tile, (t + 1) * tile)
         split(part[:, cols], output_kept_ref, output_away_ref, cols)
@@ -1154,10 +1338,16 @@
             jax.ShapeDtypeStruct((hidden.shape[1] // 2, width), BF16),
             jax.ShapeDtypeStruct(share.shape[1:], BF16),
         ],
-        in_specs=[VMEM] * 5 + [HBM],
+        in_specs=[VMEM] * 3 + [HBM] * 3,
         out_specs=[VMEM] * 5 + [HBM],
-        scratch_shapes=gather_scratch(seq, rows, width)
-        + [pltpu.SemaphoreType.DMA((2,)), pltpu.VMEM((cols, width), F32)],
+        scratch_shapes=gather_scratch(seq, rows // 2, width)
+        + [
+            pltpu.SemaphoreType.DMA((2,)),
+            pltpu.VMEM((cols, width), F32),
+            pltpu.VMEM(hidden.shape, BF16),
+            pltpu.VMEM(grad_out.shape, BF16),
+            pltpu.SemaphoreType.DMA((2,)),
+        ],
         compiler_params=params(call_id, 48),
         cost_estimate=cost(8 * seq * rows * width * cols, 6 * seq * rows * width),
     )(own, weight, attended, hidden, grad_out, share)
@@ -1291,7 +1481,7 @@
     tile,
     a_ref,
     b_ref,
-    normed_ref,
+    normed_hbm,
     blocks_ref,
     out_ref,
     feed_ref,
@@ -1299,37 +1489,43 @@
     *scratch,
 ):
     here = Place()
+    normed_ref, kept, away, came, sums, feed_sems, near_sems, far_sems, swap_sems, local_sems = (
+        scratch[SCATTER_SCRATCH:]
+    )
+    fetch = pltpu.make_async_copy(normed_hbm, normed_ref, local_sems.at[1])
+    fetch.start()
     here.greet_all()
-    whole, away, came, sums, feed_sems, near_sems, far_sems, swap_sems, local_sem = scratch[
-        SCATTER_SCRATCH:
-    ]
     feed = block_spread(here, True, blocks_ref, feed_ref, feed_sems)
     feed.start()
     own_feed = pltpu.make_async_copy(
-        blocks_ref.at[here.mine], feed_ref.at[here.slot], local_sem.at[0]
+        blocks_ref.at[here.mine], feed_ref.at[here.slot], local_sems.at[0]
     )
     own_feed.start()
     swap = remote(away, came, swap_sems.at[0], swap_sems.at[1], here.partner())
     near = block_spread(here, True, sums, qkv_ref.at[0], near_sems)
     far = block_spread(here, False, sums, qkv_ref.at[1], far_sems)
     half = away.shape[0]
-    chunk = min(half, 512)
-    chunks = half // chunk
+    chunk = 256
+
+    def part(dp, i):
+        first = pl.multiple_of(dp * half + i * chunk, chunk)
+        return t_dot(normed_ref[:, pl.ds(first, chunk)], a_ref[...])
 
     def between():
-        @pl.loop(0, 2 * chunks)
+        fetch.wait()
+
+        @pl.loop(0, half // chunk)
         def _(i):
-            first = pl.multiple_of(i * chunk, chunk)
-            part = t_dot(normed_ref[:, pl.ds(first, chunk)], a_ref[...])
-            whole[pl.ds(first, chunk), :] = part
-
-        @pl.loop(0, chunks)
-        def _(i):
-            into = pl.ds(pl.multiple_of(i * chunk, chunk), chunk)
-            first = pl.multiple_of((1 - here.dp) * half + i * chunk, chunk)
-            away[into, :] = whole[pl.ds(first, chunk), :].astype(BF16)
+            away[pl.ds(pl.multiple_of(i * chunk, chunk), chunk), :] = part(1 - here.dp, i).astype(
+                BF16
+            )
 
         swap.start()
+
+    def filler(step):
+        @pl.when(step < half // chunk)
+        def _():
+            kept[pl.ds(pl.multiple_of(step * chunk, chunk), chunk), :] = part(here.dp, step)
 
     def middle():
         swap.wait_recv()
@@ -1338,8 +1534,7 @@
         @pl.loop(0, here.count)
         def _(i):
             rows = pl.ds(pl.multiple_of(i * slab, slab), slab)
-            own = pl.ds(pl.multiple_of(here.dp * half + i * slab, slab), slab)
-            sums[i] = (whole[own, :] + came[rows, :].astype(F32)).astype(BF16)
+            sums[i] = (kept[rows, :] + came[rows, :].astype(F32)).astype(BF16)
 
         qkv_ref[0, here.slot] = sums[here.mine]
         far.start()
@@ -1356,6 +1551,7 @@
         *scratch[:SCATTER_SCRATCH],
         between,
         middle,
+        filler,
     )
     swap.wait_send()
     near.finish()
@@ -1377,11 +1573,12 @@
             jax.ShapeDtypeStruct((seq // 2, *blocks.shape[1:]), BF16),
             jax.ShapeDtypeStruct((2, seq // 2, slab, cols), BF16),
         ],
-        in_specs=[VMEM, VMEM, VMEM, HBM],
+        in_specs=[VMEM, VMEM, HBM, HBM],
         out_specs=[VMEM, HBM, VMEM],
         scratch_shapes=scatter_scratch(seq, rows, width)
         + [
-            pltpu.VMEM((width, cols), F32),
+            pltpu.VMEM(normed.shape, BF16),
+            pltpu.VMEM((width // 2, cols), F32),
             pltpu.VMEM((width // 2, cols), BF16),
             pltpu.VMEM((width // 2, cols), BF16),
             pltpu.VMEM((seq, slab, cols), BF16),
@@ -1389,7 +1586,7 @@
             dma((2, seq // 2)),
             dma((2, seq // 2)),
             dma((2,)),
-            dma((1,)),
+            dma((2,)),
         ],
         compiler_params=params(call_id, 56),
         cost_estimate=scatter_cost(a, width),
@@ -1730,65 +1927,46 @@
     data = lax.axis_index("dp")
     mine = lax.axis_index("seq")
     tok_count, width = tokens.shape
-    rows = tok_count * seq
     slab = query_weight.shape[0]
-    half_heads = HEADS // dp
-    half_kv = KV_HEADS // dp
-    hidden_dev = down_weight.shape[0]
     block = 512
-
-    doc_ends = jnp.cumsum(doc_lengths[0])
-    place = jnp.arange(rows, dtype=jnp.int32)
-    passed = doc_ends[None, :] <= place[:, None]
-    opening = jnp.max(jnp.where(passed, doc_ends[None, :], 0), axis=1)
-    position = place - opening
-    keeping = place < doc_ends[DOCS - 1]
-    angles = position.astype(F32)[:, None] * rotary_table(HEAD_DIM)[None, :]
-    cosine = jnp.cos(angles)
-    sine = jnp.sin(angles)
-    cos_heads = jnp.tile(cosine, (1, 2 * dp))
-    sin_heads = jnp.tile(jnp.concatenate([-sine, sine], axis=1), (1, dp))
-    own_keeping = lax.dynamic_slice_in_dim(keeping, mine * tok_count, tok_count, 0)
-    grad_own = jnp.where(own_keeping[:, None], cotangent, BF16(0))
-    grad_out = gather_rows(grad_own)
-
     gain_one = attn_gain.astype(F32)[:, None]
     gain_two = mlp_gain.astype(F32)[:, None]
 
-    def scaled(weight, gain):
-        return (weight.astype(F32) * gain).astype(BF16)
-
-    def head_columns(weight, kept):
-        split = scaled(weight, gain_one).reshape(slab, dp, kept, HEAD_DIM)
-        return jnp.repeat(split, seq // kept, axis=2)
-
-    qkv_blocks = jnp.stack(
-        [
-            head_columns(query_weight, half_heads),
-            head_columns(key_weight, half_kv),
-            head_columns(value_weight, half_kv),
-        ],
-        axis=1,
-    )
-    qkv_blocks = jnp.transpose(qkv_blocks, (3, 0, 1, 2, 4)).reshape(seq, slab, 3 * dp * HEAD_DIM)
-    gate_scaled = scaled(gate_weight, gain_two)
-    up_scaled = scaled(up_weight, gain_two)
-
+    (
+        normed_one,
+        grad_out,
+        queries,
+        keys,
+        values,
+        cosine,
+        sine,
+        opening,
+        qkv_weight,
+        gate_scaled,
+        up_scaled,
+        feed_near,
+        down_own,
+        output_own,
+    ) = gather_project(
+        doc_lengths,
+        tokens,
+        cotangent,
+        query_weight,
+        key_weight,
+        value_weight,
+        gate_weight,
+        up_weight,
+        (gain_one, gain_two),
+        jnp.tile(rotary_table(HEAD_DIM), 2 * dp)[None, :],
+        down_weight,
+        output_weight,
+        0,
+    )
     inputs = tokens.astype(F32)
     factor_one = norm_factor(inputs)
-    (normed_one, queries, keys, values, qkv_weight, feed_near, down_own, output_own) = (
-        gather_project(
-            (inputs * factor_one).astype(BF16),
-            qkv_blocks,
-            gate_scaled,
-            up_scaled,
-            down_weight,
-            output_weight,
-            cos_heads,
-            sin_heads,
-            0,
-        )
-    )
+    own_place = mine * tok_count + jnp.arange(tok_count, dtype=jnp.int32)
+    own_keeping = own_place < jnp.sum(doc_lengths)
+    grad_own = jnp.where(own_keeping[:, None], cotangent, BF16(0))
     qkv_weight = qkv_weight.reshape(width, -1)
     down_own = down_own.reshape(-1, width)
     output_own = output_own.reshape(-1, width)
@@ -1796,7 +1974,7 @@
         queries,
         keys,
         values,
-        opening[:, None],
+        opening,
         gate_scaled,
         up_scaled,
         feed_near.shape[2],
@@ -1837,9 +2015,9 @@
         attended_grad,
         attended_sum,
         log_total,
-        opening[:, None],
-        cos_heads,
-        sin_heads,
+        opening,
+        cosine,
+        sine,
         feed_sums,
         down_away,
         output_away,

time: 632 us -> 619 us (0.979)
  waiting for transfers between devices: 0.04 us -> 34.4 us
  Pallas kernels: 562 us -> 539 us
  other arithmetic: 35.1 us -> 19.8 us
  local copies, waits for them, and re-layouts: 19.8 us -> 11.6 us
    reduce_scatter x1, waiting for transfers between devices: 0.01 us -> 34.4 us  [scatter_rows(): lax.psum_scatter(partial.astype(BF16), 'seq', scatter_dimension=0, tiled=...]
    pallas_call x1, Pallas kernels: 68.4 us -> 51.7 us  [gather_back(): pl.pallas_call(back_kernel, out_shape=[jax.ShapeDtypeStruct((seq * rows,...]
    pallas_call x1, Pallas kernels: 62.8 us -> 55.8 us  [gather_feed(): pl.pallas_call(feed_kernel, out_shape=[jax.ShapeDtypeStruct((seq * rows,...]
  transfers between devices with their start and end apart: 2 -> 1, of which waited for: 0 -> 1; matrix products, arithmetic and copies ran while one was open for 6% -> 0% of each run, Pallas kernels for 79% -> 14%
where the time goes in v5:
time: 619 us
  Pallas kernels  539 us (87%)
  waiting for transfers between devices  34.4 us (6%)
  other arithmetic  19.8 us (3%)
  between operations  14.4 us (2%)
  local copies, waits for them, and re-layouts  11.6 us (2%)
    pallas_call x1, Pallas kernels, gather_project(): pl.pallas_call(project_kernel, out_shape=[bf16(all_rows, width), bf16(all...  127 us
    pallas_call x1, Pallas kernels, product_scatter_grad(): pl.pallas_call(functools.partial(scatter_grad_kernel, scatter_tile(width)...  89 us
    pallas_call x1, Pallas kernels, product_scatter_last(): pl.pallas_call(functools.partial(scatter_last_kernel, scatter_tile(width)...  75.7 us
    pallas_call x1, Pallas kernels, gather_feed(): pl.pallas_call(feed_kernel, out_shape=[jax.ShapeDtypeStruct((seq * rows,...  55.8 us
    pallas_call x1, Pallas kernels, product_scatter_feed(): pl.pallas_call(functools.partial(scatter_feed_kernel, scatter_tile(width)...  55.5 us
    pallas_call x1, Pallas kernels, gather_back(): pl.pallas_call(back_kernel, out_shape=[jax.ShapeDtypeStruct((seq * rows,...  51.7 us
    pallas_call x1, Pallas kernels, attention_feed(): pl.pallas_call(functools.partial(attention_feed_kernel, block), grid=(row...  38.2 us
    pallas_call x1, Pallas kernels, attention_back_feed(): pl.pallas_call(functools.partial(attention_back_feed_kernel, block), grid...  38.1 us
  transfers between devices with their start and end apart: 1, of which 1 were waited for; matrix products, arithmetic and copies ran while one was open for 0% of the time, Pallas kernels for 14%

profile of v5, /device:TPU:0, one launch (start us, length us, event | category | flops | bytes accessed | tf_op | source)
XLA Modules:
  0.0 618.8 jit_solution(2090467086596591256)
XLA Ops:
  7.2 0.0 reduce-scatter.2.cloned.1.call-start
  7.2 0.7 bitcast_convert_fusion.1
  7.9 0.7 copy.27.gain_one_ref
  8.6 0.7 bitcast_convert_fusion
  9.3 0.7 copy.28.gain_two_ref
  10.0 0.6 broadcast_in_dim_tile.3.freq_ref
  10.6 127.5 %shard_map.203 = (bf16[2048,2048]{1,0:T(8,128)(2,1)}, bf16[2048,2048]{1,0:T(8,128)(2,1)}, bf16[2048,128]{1,0:T(8,128)(2,1)}, bf16[2048,128]{1,0:T(8,128)(2,1)}, ...) custom-call(s32[1,4]{1,0:T(1,128)} %lengths_ref.1, ...), custom_call_target="tpu_custom_call" | custom-call | flops 3221225472 | bytes 33554432 | tf_op jit(solution)/shard_map/pallas_call | solution.py:730
  138.1 1.2 copy-done.1
  139.3 1.0 copy-done.4
  140.3 1.0 copy-done.5
  141.4 1.0 copy-done.6
  142.4 38.2 %shard_map.204 = (f32[2048,128]{1,0:T(8,128)S(1)}, f32[2048,2]{1,0:T(8,128)S(1)}, bf16[8,64,1024]{2,1,0:T(8,128)(2,1)S(1)}) custom-call(bf16[2048,128]{1,0:T(8,128)(2,1)S(1)} %copy-done.4, bf16[2048,128]{1,0:T(8,128)(2,1)S(1)} %copy-done.5, bf16[2048,128]{1,0:T(8,128)(2,1)S(1)} %copy-done.6, s32[2048,1]{1,0:T(8,128)S(1)} %copy-done.1, ...), custom_call_target="tpu_custom_call" | custom-call | flops 1073741824 | bytes 2621440 | tf_op jit(solution)/shard_map/pallas_call | solution.py:800
  180.7 0.0 copy-start
  180.7 0.0 copy-start.9
  180.7 0.1 convert_element_type.39.a_ref.attended_ref
  180.8 55.5 %shard_map.205 = (f32[128,2048]{1,0:T(8,128)S(1)}, bf16[2,16,64,1024]{3,2,1,0:T(8,128)(2,1)S(1)}) custom-call(bf16[2048,128]{1,0:T(8,128)(2,1)S(1)} %convert_element_type.39.a_ref.attended_ref, bf16[128,2048]{1,0:T(8,128)(2,1)S(1)} %bitcast.16, bf16[8,64,1024]{2,1,0:T(8,128)(2,1)S(1)} %copy-done.23, bf16[8,64,1024]{2,1,0:T(8,128)(2,1)S(1)} %get-tuple-element.66.far_ref), custom_call_target="tpu_custom_call" | custom-call | flops 1073741824 | bytes 16777216 | tf_op jit(solution)/shard_map/pallas_call | solution.py:1090
  236.3 2.1 copy-done.22
  238.4 0.2 multiply_reduce_fusion.1
  238.6 0.9 multiply_convert_fusion.own_ref
  239.6 55.8 %shard_map.206 = (bf16[2048,2048]{1,0:T(8,128)(2,1)}, bf16[2048,512]{1,0:T(8,128)(2,1)}, bf16[2048,1024]{1,0:T(8,128)(2,1)}, bf16[1024,2048]{1,0:T(8,128)(2,1)}, bf16[2048,2048]{1,0:T(8,128)(2,1)}) custom-call(bf16[128,2048]{1,0:T(8,128)(2,1)} %multiply_convert_fusion.own_ref, bf16[2048,2048]{1,0:T(8,128)(2,1)} %get-tuple-element.68.grad_hbm.out_grad_hbm, ...), custom_call_target="tpu_custom_call" | custom-call | flops 17179869184 | bytes 33554432 | tf_op jit(solution)/shard_map/pallas_call | solution.py:1226
  295.4 0.0 copy-start.33
  295.5 0.0 reduce-scatter.2.cloned.1.call-update
  295.5 0.6 copy-done.33
  296.1 0.6 reduce_sum.46
  296.7 0.7 add_compare_fusion
  297.4 0.0 copy-start.25
  297.4 89.0 %shard_map.207 = (f32[128,2048]{1,0:T(8,128)}, bf16[2048,1024]{1,0:T(8,128)(2,1)}) custom-call(bf16[2048,1024]{1,0:T(8,128)(2,1)} %get-tuple-element.72.a_ref, bf16[1024,2048]{1,0:T(8,128)(2,1)} %get-tuple-element.73.b_ref, bf16[2048,2048]{1,0:T(8,128)(2,1)} %get-tuple-element.74.normed_hbm), custom_call_target="tpu_custom_call" | custom-call | flops 17179869184 | bytes 33554432 | tf_op jit(solution)/shard_map/pallas_call | solution.py:1034
  386.5 1.6 fusion.1
  388.0 34.4 %reduce-scatter.2.cloned.1.call-done = bf16[128,2048]{1,0:T(8,128)(2,1)} async-done(((bf16[2048,2048]{1,0:T(8,128)(2,1)}), bf16[128,2048]{1,0:T(8,128)(2,1)}) %reduce-scatter.2.cloned.1.call-update) | async-done | bytes 524304 | tf_op jit(solution)/shard_map/reduce_scatter | solution.py:1729
  422.4 3.2 fusion.8
  425.6 51.7 %shard_map.208 = (bf16[2048,128]{1,0:T(8,128)(2,1)S(1)}, f32[64,2048]{1,0:T(8,128)S(1)}, bf16[64,2048]{1,0:T(8,128)(2,1)S(1)}, f32[256,2048]{1,0:T(8,128)S(1)}, ...) custom-call(bf16[128,2048]{1,0:T(8,128)(2,1)S(1)} %get-tuple-element.105.own_ref, ...), custom_call_target="tpu_custom_call" | custom-call | flops 4294967296 | bytes 25165824 | tf_op jit(solution)/shard_map/pallas_call | solution.py:1331
  477.3 0.0 copy-start.17
  477.4 4.7 fusion
  482.1 38.1 %shard_map.209 = (bf16[2048,384]{1,0:T(8,128)(2,1)}, bf16[8,64,1024]{2,1,0:T(8,128)(2,1)}, bf16[256,2048]{1,0:T(8,128)(2,1)}, bf16[64,2048]{1,0:T(8,128)(2,1)}) custom-call(bf16[2048,128]{1,0:T(8,128)(2,1)} %get-tuple-element.57.q_ref, bf16[2048,128]{1,0:T(8,128)(2,1)} %get-tuple-element.58.k_ref, bf16[2048,128]{1,0:T(8,128)(2,1)} %get-tuple-element.59.v_ref, ...), custom_call_target="tpu_custom_call" | custom-call | flops 2684354560 | bytes 5242880 | tf_op jit(solution)/shard_map/pallas_call | solution.py:1443
  520.2 0.0 copy-start.7
  520.2 0.0 copy-start.8
  520.2 75.7 %shard_map.210 = (f32[128,2048]{1,0:T(8,128)}, bf16[8,64,1024]{2,1,0:T(8,128)(2,1)}, bf16[2,8,64,384]{3,2,1,0:T(8,128)(2,1)}) custom-call(bf16[2048,384]{1,0:T(8,128)(2,1)} %get-tuple-element.85.a_ref, bf16[2048,384]{1,0:T(8,128)(2,1)} %bitcast.23, bf16[2048,2048]{1,0:T(8,128)(2,1)} %get-tuple-element.87.normed_hbm, bf16[16,64,1024]{2,1,0:T(8,128)(2,1)} %bitcast.20), custom_call_target="tpu_custom_call" | custom-call | flops 3221225472 | bytes 16777216 | tf_op jit(solution)/shard_map/pallas_call | solution.py:1569
  596.1 1.2 copy-done.3
  597.3 1.1 copy-done.11
  598.4 6.9 %shard_map.211 = (f32[64,8192]{1,0:T(8,128)}, f32[64,8192]{1,0:T(8,128)}, f32[64,2048]{1,0:T(8,128)}, f32[64,512]{1,0:T(8,128)}, f32[64,512]{1,0:T(8,128)}, /*index=5*/f32[64,1]{1,0:T(8,128)S(1)}, f32[64,1]{1,0:T(8,128)S(1)}) custom-call(s32[1]{0:T(128)} %bitcast.9.pair_ref, bf16[8,64,1024]{2,1,0:T(8,128)(2,1)S(1)} %copy-done.3, ...), custom_call_target="tpu_custom_call" | custom-call | flops 524288 | bytes 8388608 | tf_op jit(solution)/shard_map/pallas_call | solution.py:1694
  605.3 0.6 reduce
  606.0 0.6 reduce.1
  606.6 1.5 fusion.7
  608.1 0.0 copy-done.30
  608.1 1.6 convert_add_fusion.1
  609.8 0.9 convert_add_fusion.4
  610.6 0.0 copy-done.29
  610.7 1.3 fusion.6
  (56 shorter events, 0.2 us)
Async XLA Ops:
  7.2 415.2 %reduce-scatter.2.cloned.1.call-start = ((), (), s32[]{:S(2)}) async-start(), calls=%async_computation.1 | async-start | bytes 8912896 | tf_op jit(solution)/shard_map/reduce_scatter | solution.py:1729
  138.1 1.2 copy-start.1
  139.3 1.0 copy-start.4
  140.3 1.0 copy-start.5
  141.4 1.0 copy-start.6
  142.4 38.3 %copy-start.12 = (bf16[2,64,2048]{2,1,0:T(8,128)(2,1)S(1)}, bf16[2,64,2048]{2,1,0:T(8,128)(2,1)}, u32[]{:S(2)}) copy-start(bf16[2,64,2048]{2,1,0:T(8,128)(2,1)} %get-tuple-element.64) | copy-start | bytes 1572868
  142.4 38.3 %copy-start.23 = (bf16[8,64,1024]{2,1,0:T(8,128)(2,1)S(1)}, bf16[8,64,1024]{2,1,0:T(8,128)(2,1)}, u32[]{:S(2)}) copy-start(bf16[8,64,1024]{2,1,0:T(8,128)(2,1)} %get-tuple-element.65.near_ref) | copy-start | bytes 3145732
  180.7 55.6 %copy-start = (f32[2048,128]{1,0:T(8,128)}, f32[2048,128]{1,0:T(8,128)S(1)}, u32[]{:S(2)}) copy-start(f32[2048,128]{1,0:T(8,128)S(1)} %get-tuple-element.63.att_ref) | copy-start | bytes 3145732
  180.7 55.6 %copy-start.9 = (f32[2048,2]{1,0:T(8,128)}, f32[2048,2]{1,0:T(8,128)S(1)}, u32[]{:S(2)}) copy-start(f32[2048,2]{1,0:T(8,128)S(1)} %get-tuple-element.79.lse_ref) | copy-start | bytes 49156
  180.7 57.7 %copy-start.24 = (bf16[128,2048]{1,0:T(8,128)(2,1)S(1)}, bf16[128,2048]{1,0:T(8,128)(2,1)}, u32[]{:S(2)}) copy-start(bf16[128,2048]{1,0:T(8,128)(2,1)} %tokens_ref.1) | copy-start | bytes 1572868
  236.3 2.1 copy-start.22
  295.4 0.7 copy-start.33
  297.4 89.1 %copy-start.25 = (bf16[128,2048]{1,0:T(8,128)(2,1)S(1)}, bf16[128,2048]{1,0:T(8,128)(2,1)}, u32[]{:S(2)}) copy-start(bf16[128,2048]{1,0:T(8,128)(2,1)} %tokens_ref.1) | copy-start | bytes 1572868
  386.4 36.0 %copy-start.31 = (bf16[128,2048]{1,0:T(8,128)(2,1)S(1)}, bf16[128,2048]{1,0:T(8,128)(2,1)}, u32[]{:S(2)}) copy-start(bf16[128,2048]{1,0:T(8,128)(2,1)} %cotangent_ref.1) | copy-start | bytes 1572868
  425.6 51.8 %copy-start.27 = (bf16[2048,1024]{1,0:T(8,128)(2,1)S(1)}, bf16[2048,1024]{1,0:T(8,128)(2,1)}, u32[]{:S(2)}) copy-start(bf16[2048,1024]{1,0:T(8,128)(2,1)} %get-tuple-element.77) | copy-start | bytes 12582916
  477.3 4.7 copy-start.10
  477.3 4.7 copy-start.13
  477.3 4.7 copy-start.15
  477.3 4.7 copy-start.17
  520.2 75.8 %copy-start.2 = (bf16[8,64,1024]{2,1,0:T(8,128)(2,1)S(1)}, bf16[8,64,1024]{2,1,0:T(8,128)(2,1)}, u32[]{:S(2)}) copy-start(bf16[8,64,1024]{2,1,0:T(8,128)(2,1)} %get-tuple-element.90.far_gate_ref.far_up_ref) | copy-start | bytes 3145732
  520.2 75.8 %copy-start.7 = (bf16[64,8192]{1,0:T(8,128)(2,1)S(1)}, bf16[64,8192]{1,0:T(8,128)(2,1)}, u32[]{:S(2)}) copy-start(bf16[64,8192]{1,0:T(8,128)(2,1)} %gate_ref.3) | copy-start | bytes 3145732
  520.2 75.8 %copy-start.8 = (bf16[64,8192]{1,0:T(8,128)(2,1)S(1)}, bf16[64,8192]{1,0:T(8,128)(2,1)}, u32[]{:S(2)}) copy-start(bf16[64,8192]{1,0:T(8,128)(2,1)} %up_ref.3) | copy-start | bytes 3145732
  520.2 75.8 %copy-start.16 = (bf16[64,2048]{1,0:T(8,128)(2,1)S(1)}, bf16[64,2048]{1,0:T(8,128)(2,1)}, u32[]{:S(2)}) copy-start(bf16[64,2048]{1,0:T(8,128)(2,1)} %query_ref.3) | copy-start | bytes 786436
  520.2 75.8 %copy-start.18 = (f32[64,1]{1,0:T(8,128)S(1)}, f32[64,1]{1,0:T(8,128)}, u32[]{:S(2)}) copy-start(f32[64,1]{1,0:T(8,128)} %copy.27.gain_one_ref) | copy-start | bytes 772
  520.2 75.8 %copy-start.19 = (f32[64,1]{1,0:T(8,128)S(1)}, f32[64,1]{1,0:T(8,128)}, u32[]{:S(2)}) copy-start(f32[64,1]{1,0:T(8,128)} %copy.28.gain_two_ref) | copy-start | bytes 772
  520.2 75.8 %copy-start.20 = (bf16[64,512]{1,0:T(8,128)(2,1)S(1)}, bf16[64,512]{1,0:T(8,128)(2,1)}, u32[]{:S(2)}) copy-start(bf16[64,512]{1,0:T(8,128)(2,1)} %key_ref.3) | copy-start | bytes 196612
  520.2 75.8 %copy-start.21 = (bf16[64,512]{1,0:T(8,128)(2,1)S(1)}, bf16[64,512]{1,0:T(8,128)(2,1)}, u32[]{:S(2)}) copy-start(bf16[64,512]{1,0:T(8,128)(2,1)} %value_ref.3) | copy-start | bytes 196612
  596.1 1.2 copy-start.3
  597.3 1.1 copy-start.11
  598.4 8.2 %copy-start.26 = (bf16[128,2048]{1,0:T(8,128)(2,1)S(1)}, bf16[128,2048]{1,0:T(8,128)(2,1)}, u32[]{:S(2)}) copy-start(bf16[128,2048]{1,0:T(8,128)(2,1)} %tokens_ref.1) | copy-start | bytes 1572868
  606.6 1.5 copy-start.30
  608.1 1.6 copy-start.14
  608.1 1.6 copy-start.32
  608.1 2.5 copy-start.28
  608.1 2.5 copy-start.29
Sparse Core Ops, SparseCore 0:
  295.6 126.7 reduce-scatter.1

commit v6 on v5

--- a/solution.py
+++ b/solution.py
@@ -389,8 +389,8 @@
             unit(step)
         else:
             between(step)
-            begin = jnp.where(step == ready, 0, step)
-            end = jnp.where(step < ready, step, step + 1)
+            begin = jnp.maximum(2 * (step - ready), 0)
+            end = jnp.maximum(2 * (step + 1 - ready), 0)
 
             @pl.loop(begin, end)
             def _(number):
@@ -570,7 +570,11 @@
             blocks[number, :, cols : 2 * cols] = heads(key, number, KV_HEADS // 2)
             blocks[number, :, 2 * cols :] = heads(value, number, KV_HEADS // 2)
 
-    here.greet_all(own_rows)
+    def own_parts():
+        own_blocks()
+        own_rows()
+
+    here.greet_all(own_parts)
 
     def weight_spread(same, sems):
         def copies(peer, sender, at, sem):
@@ -636,9 +640,6 @@
             sin_ref[some, :] = jnp.where(lane % HEAD_DIM < HEAD_DIM // 2, -sine, sine)
 
     def started():
-        own_blocks()
-        far.start()
-        near.start()
         weight_ref[dp, here.mine] = blocks[here.mine]
         for one in swaps:
             one.start()
@@ -657,7 +658,7 @@
         own_tables()
 
     def between(step):
-        @pl.when(step == 1)
+        @pl.when(step == 2)
         def _():
             near.finish()
             far.finish()
@@ -666,7 +667,7 @@
             def _(sender):
                 pair_copy(dp, sender).start()
 
-        @pl.when(step == 3)
+        @pl.when(step == 4)
         def _():
             @pl.loop(0, here.count)
             def _(sender):
@@ -700,7 +701,9 @@
         k_ref[where, :] = rotated(qkv[:, cols : 2 * cols], cosine, sine).astype(BF16)
         v_ref[where, :] = qkv[:, 2 * cols :].astype(BF16)
 
-    gather_units(here, buf, send_sems, recv_sems, compute, between, 3, started)
+    far.start()
+    near.start()
+    gather_units(here, buf, send_sems, recv_sems, compute, between, here.length, started)
 
     @pl.loop(0, here.count)
     def _(sender):
@@ -813,34 +816,33 @@
     )(queries, keys, values, opening, gate, up)
 
 
-def scatter_rows_of_product(
+SCATTER_PARTS = 2
+SCATTER_RING = 4
+SCATTER_SCRATCH = 11
+
+
+def scatter_rows_of_products(
     here,
-    transposed,
-    parts,
-    tile,
-    a_ref,
-    b_ref,
-    out_ref,
+    products,
     core_out,
     core_in,
     pair_out,
     pair_in,
     line_out,
-    up_in,
-    down_in,
+    line_in,
     held,
     core_sems,
     pair_sems,
     line_sems,
-    up_sems,
-    down_sems,
+    came_sems,
     between=nothing,
     middle=nothing,
     filler=None,
 ):
     length = here.length
-    rows = out_ref.shape[0]
-    width = out_ref.shape[1] // parts
+    parts = SCATTER_PARTS * len(products)
+    rows, width = held.shape
+    tile = min(width, 512)
     tiles = width // tile
     steps = length * parts
 
@@ -853,17 +855,24 @@
 
     def product(line, pair, core, part, use):
         first = pl.multiple_of(here.index(line, pair, core) * rows, rows)
-        a = a_ref[pl.ds(first, rows), :]
-
-        @pl.loop(0, tiles)
-        def _(t):
-            into = pl.ds(pl.multiple_of(t * tile, tile), tile)
-            cols = pl.ds(pl.multiple_of(part * width + t * tile, tile), tile)
-            use(dot_t(a, b_ref[cols, :]) if transposed else dot(a, b_ref[:, cols]), into)
+
+        def one(number):
+            transposed, a_ref, b_ref, _ = products[number]
+            a = a_ref[pl.ds(first, rows), :]
+            begin = (part - number * SCATTER_PARTS) * width
+
+            @pl.loop(0, tiles)
+            def _(t):
+                into = pl.ds(pl.multiple_of(t * tile, tile), tile)
+                cols = pl.ds(pl.multiple_of(begin + t * tile, tile), tile)
+                use(dot_t(a, b_ref[cols, :]) if transposed else dot(a, b_ref[:, cols]), into)
+
+        for number in range(len(products)):
+            pl.when(part // SCATTER_PARTS == number)(functools.partial(one, number))
 
     def core_copy(slot):
         return remote(
-            core_out.at[slot],
+            core_out.at[slot % SCATTER_RING],
             core_in.at[slot],
             core_sems.at[0, slot],
             core_sems.at[1, slot],
@@ -879,24 +888,28 @@
             here.across(),
         )
 
-    def up_copy(slot, into):
+    def up_copy(slot, line, part):
+        into = (line + 1) * parts + part
         return remote(
-            line_out.at[slot], up_in.at[into], line_sems.at[slot], up_sems.at[into], here.above()
+            line_out.at[slot], line_in.at[into], line_sems.at[slot], came_sems.at[into], here.above()
         )
 
-    def down_copy(slot, into):
+    def down_copy(slot, line, part):
+        into = line * parts + part
         return remote(
-            line_out.at[slot], down_in.at[into], line_sems.at[slot], down_sems.at[into], here.below()
+            line_out.at[slot], line_in.at[into], line_sems.at[slot], came_sems.at[into], here.below()
         )
 
     def for_sibling(step, pair, slot):
+        pl.when(slot >= SCATTER_RING)(lambda: core_copy(slot - SCATTER_RING).wait_send())
+
         def use(value, cols):
-            core_out[slot, :, cols] = value.astype(BF16)
+            core_out[slot % SCATTER_RING, :, cols] = value.astype(BF16)
 
         product(target(step // parts), pair, 1 - here.core, step % parts, use)
         core_copy(slot).start()
 
-    for_sibling(0, 1 - here.pair, 0)
+    for_sibling(jnp.int32(0), 1 - here.pair, jnp.int32(0))
 
     @pl.loop(0, steps)
     def _(step):
@@ -909,7 +922,7 @@
         product(target(step // parts), 1 - here.pair, here.core, step % parts, use)
         pair_copy(step).start()
 
-    for_sibling(0, here.pair, steps)
+    for_sibling(jnp.int32(0), here.pair, jnp.int32(steps))
     between()
 
     @pl.loop(0, steps)
@@ -918,7 +931,6 @@
         core_copy(steps + step).wait_recv()
         line = target(step // parts)
         part = step % parts
-        into = line * parts + part
 
         def use(value, cols):
             held[:, cols] = value + core_in[steps + step, :, cols].astype(F32)
@@ -933,120 +945,163 @@
 
         @pl.when(from_above)
         def _():
-            down_copy(0, into).wait_recv()
-            held[...] += down_in[into].astype(F32)
+            down_copy(0, line, part).wait_recv()
+            held[...] += line_in[line * parts + part].astype(F32)
 
         @pl.when(from_below)
         def _():
-            up_copy(0, into).wait_recv()
-            held[...] += up_in[into].astype(F32)
-
-        @pl.when(line == here.line)
-        def _():
-            out_ref[:, pl.ds(pl.multiple_of(part * width, width), width)] = held[...]
+            up_copy(0, line, part).wait_recv()
+            held[...] += line_in[(line + 1) * parts + part].astype(F32)
+
+        for number, (_, _, _, out_ref) in enumerate(products):
+
+            @pl.when((line == here.line) & (part // SCATTER_PARTS == number))
+            def _():
+                begin = (part - number * SCATTER_PARTS) * width
+                out_ref[:, pl.ds(pl.multiple_of(begin, width), width)] = held[...]
 
         @pl.when(line < here.line)
         def _():
             line_out[step] = held[...].astype(BF16)
-            down_copy(step, into).start()
+            down_copy(step, line, part).start()
 
         @pl.when(line > here.line)
         def _():
             line_out[step] = held[...].astype(BF16)
-            up_copy(step, into).start()
+            up_copy(step, line, part).start()
 
         if middle is not nothing:
             pl.when(step == steps // 2)(middle)
 
+    @pl.loop(2 * steps - SCATTER_RING, 2 * steps)
+    def _(slot):
+        core_copy(slot).wait_send()
+
     @pl.loop(0, steps)
     def _(step):
-        core_copy(step).wait_send()
-        core_copy(steps + step).wait_send()
         pair_copy(step).wait_send()
         line = target(step // parts)
-        pl.when(line < here.line)(lambda: down_copy(step, 0).wait_send())
-        pl.when(line > here.line)(lambda: up_copy(step, 0).wait_send())
-
-
-SCATTER_PARTS = 2
-SCATTER_SCRATCH = 13
-
-
-def scatter_scratch(seq, rows, width):
-    steps = seq // 4 * SCATTER_PARTS
+        pl.when(line < here.line)(lambda: down_copy(step, 0, 0).wait_send())
+        pl.when(line > here.line)(lambda: up_copy(step, 0, 0).wait_send())
+
+
+def scatter_scratch(seq, rows, width, count=1):
+    length = seq // 4
+    parts = SCATTER_PARTS * count
+    steps = length * parts
     block = (rows, width // SCATTER_PARTS)
     dma = pltpu.SemaphoreType.DMA
     return [
-        pltpu.VMEM((2 * steps, *block), BF16),
+        pltpu.VMEM((SCATTER_RING, *block), BF16),
         pltpu.VMEM((2 * steps, *block), BF16),
         pltpu.VMEM((steps, *block), BF16),
         pltpu.VMEM((steps, *block), BF16),
         pltpu.VMEM((steps, *block), BF16),
-        pltpu.VMEM((steps, *block), BF16),
-        pltpu.VMEM((steps, *block), BF16),
+        pltpu.VMEM(((length + 1) * parts, *block), BF16),
         pltpu.VMEM(block, F32),
         dma((2, 2 * steps)),
         dma((2, steps)),
         dma((steps,)),
-        dma((steps,)),
-        dma((steps,)),
+        dma(((length + 1) * parts,)),
     ]
-
-
-def scatter_tile(width):
-    return min(width // SCATTER_PARTS, 512)
 
 
 def scatter_cost(a, width):
     return cost(2 * a.shape[0] * a.shape[1] * width, 4 * a.shape[0] * width)
 
 
-def scatter_grad_kernel(tile, a_ref, b_ref, normed_hbm, out_ref, grad_ref, *scratch):
+def scatter_both_kernel(
+    back_ref,
+    turned_ref,
+    hidden_ref,
+    down_ref,
+    normed_hbm,
+    out_ref,
+    mixed_ref,
+    sums_ref,
+    *scratch,
+):
     here = Place()
-    normed_ref, fetch_sem = scratch[SCATTER_SCRATCH:]
-    fetch = pltpu.make_async_copy(normed_hbm, normed_ref, fetch_sem.at[0])
-    fetch.start()
-    here.greet()
-    cols = normed_ref.shape[1] // (here.length * SCATTER_PARTS)
+    here.greet(partner=True)
+    normed, away, came, fetch_sems, swap_sems = scratch[SCATTER_SCRATCH:]
+    chunk = normed.shape[2]
+    half = normed_hbm.shape[1] // 2
+    chunks = half // chunk
+
+    def fetch(number):
+        dp = jnp.where(number < chunks, 1 - here.dp, here.dp)
+        begin = dp * half + number % chunks * chunk
+        return pltpu.make_async_copy(
+            normed_hbm.at[:, pl.ds(pl.multiple_of(begin, chunk), chunk)],
+            normed.at[number % 2],
+            fetch_sems.at[number % 2],
+        )
+
+    def swap(i):
+        some = pl.ds(pl.multiple_of(i * chunk, chunk), chunk)
+        return remote(
+            away.at[some], came.at[some], swap_sems.at[0, i], swap_sems.at[1, i], here.partner()
+        )
+
+    def part(number):
+        fetch(number).wait()
+        pl.when(number + 1 < 2 * chunks)(lambda: fetch(number + 1).start())
+        return t_dot(normed[number % 2], back_ref[...])
 
     def filler(step):
-        some = pl.ds(pl.multiple_of(step * cols, cols), cols)
-        grad_ref[some, :] = t_dot(normed_ref[:, some], a_ref[...]).astype(BF16)
-
-    scatter_rows_of_product(
+        @pl.when(step < chunks)
+        def _():
+            some = pl.ds(pl.multiple_of(step * chunk, chunk), chunk)
+            away[some, :] = part(step).astype(BF16)
+            swap(step).start()
+
+        @pl.when((step >= chunks) & (step < 3 * chunks) & (step % 2 == 0))
+        def _():
+            i = (step - chunks) // 2
+            some = pl.ds(pl.multiple_of(i * chunk, chunk), chunk)
+            kept = part(chunks + i)
+            swap(i).wait()
+            sums_ref[some, :] = (kept + came[some, :].astype(F32)).astype(BF16)
+
+    fetch(jnp.int32(0)).start()
+    scatter_rows_of_products(
         here,
-        False,
-        SCATTER_PARTS,
-        tile,
-        a_ref,
-        b_ref,
-        out_ref,
+        [(False, back_ref, turned_ref, out_ref), (False, hidden_ref, down_ref, mixed_ref)],
         *scratch[:SCATTER_SCRATCH],
-        between=fetch.wait,
         filler=filler,
     )
 
 
-def product_scatter_grad(a, b, normed, call_id):
+def product_scatter_both(back, turned, hidden, down, normed, call_id):
     seq = lax.axis_size("seq")
-    rows = a.shape[0] // seq
-    width = b.shape[1]
+    rows = back.shape[0] // seq
+    width = turned.shape[1]
+    cols = back.shape[1]
+    chunk = width // 8
+    dma = pltpu.SemaphoreType.DMA
     return pl.pallas_call(
-        functools.partial(scatter_grad_kernel, scatter_tile(width)),
+        scatter_both_kernel,
         out_shape=[
             jax.ShapeDtypeStruct((rows, width), F32),
-            jax.ShapeDtypeStruct((width, a.shape[1]), BF16),
+            jax.ShapeDtypeStruct((rows, width), F32),
+            jax.ShapeDtypeStruct((width // 2, cols), BF16),
         ],
-        in_specs=[VMEM, VMEM, HBM],
-        out_specs=[VMEM] * 2,
-        scratch_shapes=scatter_scratch(seq, rows, width)
-        + [pltpu.VMEM(normed.shape, BF16), pltpu.SemaphoreType.DMA((1,))],
-        compiler_params=params(call_id, 56),
-        cost_estimate=scatter_cost(a, 2 * width),
-    )(a, b, normed)
-
-
-def scatter_feed_kernel(tile, a_ref, b_ref, near_ref, far_ref, out_ref, feed_ref, *scratch):
+        in_specs=[VMEM] * 4 + [HBM],
+        out_specs=[VMEM] * 3,
+        scratch_shapes=scatter_scratch(seq, rows, width, 2)
+        + [
+            pltpu.VMEM((2, normed.shape[0], chunk), BF16),
+            pltpu.VMEM((width // 2, cols), BF16),
+            pltpu.VMEM((width // 2, cols), BF16),
+            dma((2,)),
+            dma((2, 4)),
+        ],
+        compiler_params=params(call_id, 60),
+        cost_estimate=scatter_cost(back, 3 * width),
+    )(back, turned, hidden, down, normed)
+
+
+def scatter_feed_kernel(a_ref, b_ref, near_ref, far_ref, out_ref, feed_ref, *scratch):
     here = Place()
     here.greet(partner=True)
     swap_sems, local_sems = scratch[SCATTER_SCRATCH:]
@@ -1071,8 +1126,8 @@
             for one in copies(half, ref, slot):
                 one.start()
 
-    scatter_rows_of_product(
-        here, False, SCATTER_PARTS, tile, a_ref, b_ref, out_ref, *scratch[:SCATTER_SCRATCH]
+    scatter_rows_of_products(
+        here, [(False, a_ref, b_ref, out_ref)], *scratch[:SCATTER_SCRATCH]
     )
 
     @pl.loop(0, slots)
@@ -1088,7 +1143,7 @@
     width = b.shape[1]
     dma = pltpu.SemaphoreType.DMA
     return pl.pallas_call(
-        functools.partial(scatter_feed_kernel, scatter_tile(width)),
+        scatter_feed_kernel,
         out_shape=[
             jax.ShapeDtypeStruct((rows, width), F32),
             jax.ShapeDtypeStruct((2, seq, *near.shape[1:]), BF16),
@@ -1111,13 +1166,10 @@
     hidden_out_ref,
     back_out_ref,
     turned_out_ref,
-    mixed_ref,
     buf,
     send_sems,
     recv_sems,
     store_sems,
-    mixed_buf,
-    mixed_sems,
     grad_ref,
     feed_ref,
     down_ref,
@@ -1142,14 +1194,7 @@
     width = own_ref.shape[1]
     hidden = hidden_ref.shape[1]
     tile = 256
-    wide = 512
     store = UnitStore(buf, normed_ref, store_sems)
-
-    def mixed_copy(number, first):
-        slot = number % 2
-        return pltpu.make_async_copy(
-            mixed_buf.at[slot], mixed_ref.at[unit_rows(first, rows)], mixed_sems.at[slot]
-        )
 
     def outs(number, first):
         where = unit_rows(first, rows)
@@ -1174,7 +1219,6 @@
             for one in fetches:
                 one.wait()
 
-        pl.when(number >= 2)(lambda: mixed_copy(number, first).wait())
         where = unit_rows(first, rows)
         normed = take_unit(buf, first)
         grad = grad_ref[where, :]
@@ -1194,13 +1238,6 @@
             ).astype(BF16)
             back_ref[where, later] = (hidden_grad * silu).astype(BF16)
 
-        @pl.loop(0, width // wide)
-        def _(t):
-            cols = pl.ds(pl.multiple_of(t * wide, wide), wide)
-            part = dot(hidden_ref[where, :], down_ref[:, cols])
-            mixed_buf[number % 2, :, cols] = part.astype(BF16)
-
-        mixed_copy(number, first).start()
         share = width // (2 * here.length)
         some = pl.ds(pl.multiple_of(number * share, share), share)
         turned_ref[:, some] = feed_ref[some, :].T
@@ -1214,8 +1251,6 @@
         for one in outs(number, 0):
             one.wait()
 
-    mixed_copy(0, 0).wait()
-    mixed_copy(1, 0).wait()
     store.finish()
 
 
@@ -1230,15 +1265,12 @@
             jax.ShapeDtypeStruct((seq * rows, hidden), BF16),
             jax.ShapeDtypeStruct((seq * rows, 2 * hidden), BF16),
             jax.ShapeDtypeStruct((2 * hidden, width), BF16),
-            jax.ShapeDtypeStruct((seq * rows, width), BF16),
         ],
         in_specs=[VMEM] + [HBM] * 3,
-        out_specs=[HBM] * 5,
+        out_specs=[HBM] * 4,
         scratch_shapes=gather_scratch(seq, rows // 2, width)
         + [
             pltpu.SemaphoreType.DMA((seq // 2, 2, 2)),
-            pltpu.VMEM((2, 2 * rows, width), BF16),
-            pltpu.SemaphoreType.DMA((2,)),
             pltpu.VMEM((seq * rows, width), BF16),
             pltpu.VMEM((width, 2 * hidden), BF16),
             pltpu.VMEM((hidden, width), BF16),
@@ -1259,17 +1291,18 @@
     attended_ref,
     hidden_hbm,
     out_grad_hbm,
-    share_ref,
+    blocks_ref,
     grad_ref,
     output_kept_ref,
     output_away_ref,
     down_kept_ref,
     down_away_ref,
-    came_ref,
+    near_ref,
     buf,
     send_sems,
     recv_sems,
-    swap_sems,
+    near_sems,
+    own_sem,
     part,
     hidden_ref,
     out_grad_ref,
@@ -1283,14 +1316,17 @@
     for one in fetches:
         one.start()
     put_own(here, own_ref, buf)
-    here.greet(partner=True)
+    here.greet_all()
     rows = own_ref.shape[0]
     width = own_ref.shape[1]
     tile = 512
-    swap = remote(
-        share_ref.at[1 - here.dp], came_ref, swap_sems.at[0], swap_sems.at[1], here.partner()
-    )
-    swap.start()
+    near = block_spread(here, True, blocks_ref, near_ref, near_sems)
+    own = pltpu.make_async_copy(blocks_ref.at[here.mine], near_ref.at[here.slot], own_sem.at[0])
+
+    def started():
+        near.start()
+        own.start()
+
     part[...] = jnp.zeros_like(part)
     share = width // (2 * here.length)
 
@@ -1317,14 +1353,15 @@
 
         split(t_dot(hidden_ref[...], out_grad_ref[:, some]), down_kept_ref, down_away_ref, some)
 
-    gather_units(here, buf, send_sems, recv_sems, compute)
+    gather_units(here, buf, send_sems, recv_sems, compute, started=started)
     for t in range(width // tile):
         cols = slice(t * tile, (t + 1) * tile)
         split(part[:, cols], output_kept_ref, output_away_ref, cols)
-    swap.wait()
-
-
-def gather_back(own, weight, attended, hidden, grad_out, share, call_id):
+    near.finish()
+    own.wait()
+
+
+def gather_back(own, weight, attended, hidden, grad_out, blocks, call_id):
     seq = lax.axis_size("seq")
     rows, width = own.shape
     cols = weight.shape[0]
@@ -1336,13 +1373,14 @@
             jax.ShapeDtypeStruct((cols // 2, width), BF16),
             jax.ShapeDtypeStruct((hidden.shape[1] // 2, width), F32),
             jax.ShapeDtypeStruct((hidden.shape[1] // 2, width), BF16),
-            jax.ShapeDtypeStruct(share.shape[1:], BF16),
+            jax.ShapeDtypeStruct((seq // 2, *blocks.shape[1:]), BF16),
         ],
         in_specs=[VMEM] * 3 + [HBM] * 3,
         out_specs=[VMEM] * 5 + [HBM],
         scratch_shapes=gather_scratch(seq, rows // 2, width)
         + [
-            pltpu.SemaphoreType.DMA((2,)),
+            pltpu.SemaphoreType.DMA((2, seq // 2)),
+            pltpu.SemaphoreType.DMA((1,)),
             pltpu.VMEM((cols, width), F32),
             pltpu.VMEM(hidden.shape, BF16),
             pltpu.VMEM(grad_out.shape, BF16),
@@ -1350,7 +1388,7 @@
         ],
         compiler_params=params(call_id, 48),
         cost_estimate=cost(8 * seq * rows * width * cols, 6 * seq * rows * width),
-    )(own, weight, attended, hidden, grad_out, share)
+    )(own, weight, attended, hidden, grad_out, blocks)
 
 
 def attention_back_feed_kernel(
@@ -1477,30 +1515,14 @@
     )
 
 
-def scatter_last_kernel(
-    tile,
-    a_ref,
-    b_ref,
-    normed_hbm,
-    blocks_ref,
-    out_ref,
-    feed_ref,
-    qkv_ref,
-    *scratch,
-):
+def scatter_last_kernel(a_ref, b_ref, normed_hbm, out_ref, qkv_ref, *scratch):
     here = Place()
-    normed_ref, kept, away, came, sums, feed_sems, near_sems, far_sems, swap_sems, local_sems = (
-        scratch[SCATTER_SCRATCH:]
-    )
-    fetch = pltpu.make_async_copy(normed_hbm, normed_ref, local_sems.at[1])
+    normed_ref, kept, away, came, sums, near_sems, far_sems, swap_sems, fetch_sems = scratch[
+        SCATTER_SCRATCH:
+    ]
+    fetch = pltpu.make_async_copy(normed_hbm, normed_ref, fetch_sems.at[0])
     fetch.start()
     here.greet_all()
-    feed = block_spread(here, True, blocks_ref, feed_ref, feed_sems)
-    feed.start()
-    own_feed = pltpu.make_async_copy(
-        blocks_ref.at[here.mine], feed_ref.at[here.slot], local_sems.at[0]
-    )
-    own_feed.start()
     swap = remote(away, came, swap_sems.at[0], swap_sems.at[1], here.partner())
     near = block_spread(here, True, sums, qkv_ref.at[0], near_sems)
     far = block_spread(here, False, sums, qkv_ref.at[1], far_sems)
@@ -1540,14 +1562,9 @@
         far.start()
         near.start()
 
-    scatter_rows_of_product(
+    scatter_rows_of_products(
         here,
-        True,
-        SCATTER_PARTS,
-        tile,
-        a_ref,
-        b_ref,
-        out_ref,
+        [(True, a_ref, b_ref, out_ref)],
         *scratch[:SCATTER_SCRATCH],
         between,
         middle,
@@ -1556,25 +1573,22 @@
     swap.wait_send()
     near.finish()
     far.finish()
-    feed.finish()
-    own_feed.wait()
-
-
-def product_scatter_last(a, b, normed, blocks, call_id):
+
+
+def product_scatter_last(a, b, normed, call_id):
     seq = lax.axis_size("seq")
     rows = a.shape[0] // seq
     width, cols = b.shape
-    slab = blocks.shape[1]
+    slab = width // (2 * seq)
     dma = pltpu.SemaphoreType.DMA
     return pl.pallas_call(
-        functools.partial(scatter_last_kernel, scatter_tile(width)),
+        scatter_last_kernel,
         out_shape=[
             jax.ShapeDtypeStruct((rows, width), F32),
-            jax.ShapeDtypeStruct((seq // 2, *blocks.shape[1:]), BF16),
             jax.ShapeDtypeStruct((2, seq // 2, slab, cols), BF16),
         ],
-        in_specs=[VMEM, VMEM, HBM, HBM],
-        out_specs=[VMEM, HBM, VMEM],
+        in_specs=[VMEM, VMEM, HBM],
+        out_specs=[VMEM, VMEM],
         scratch_shapes=scatter_scratch(seq, rows, width)
         + [
             pltpu.VMEM(normed.shape, BF16),
@@ -1584,13 +1598,12 @@
             pltpu.VMEM((seq, slab, cols), BF16),
             dma((2, seq // 2)),
             dma((2, seq // 2)),
-            dma((2, seq // 2)),
             dma((2,)),
-            dma((2,)),
+            dma((1,)),
         ],
         compiler_params=params(call_id, 56),
         cost_estimate=scatter_cost(a, width),
-    )(a, b, normed, blocks)
+    )(a, b, normed)
 
 
 def unpack_kernel(
@@ -1924,7 +1937,6 @@
 ):
     dp = lax.axis_size("dp")
     seq = lax.axis_size("seq")
-    data = lax.axis_index("dp")
     mine = lax.axis_index("seq")
     tok_count, width = tokens.shape
     slab = query_weight.shape[0]
@@ -1987,27 +1999,27 @@
     middle = inputs + attended_out
 
     factor_two = norm_factor(middle)
-    normed_two, hidden, feed_back, feed_turned, mixed_part = gather_feed(
+    normed_two, hidden, feed_back, feed_turned = gather_feed(
         (middle * factor_two).astype(BF16), grad_out, feed_weight, down_own, 3
     )
-    mixed = middle + scatter_rows(mixed_part)
 
     def norm_input_grad(values, factor, upstream):
         inner_mean = jnp.mean(upstream * values, axis=-1, keepdims=True)
         return factor * upstream - values * factor * factor * factor * inner_mean
 
-    normed_two_grad, feed_part = product_scatter_grad(feed_back, feed_turned, normed_two, 4)
+    normed_two_grad, mixed_sum, feed_sums = product_scatter_both(
+        feed_back, feed_turned, hidden, down_own, normed_two, 4
+    )
+    mixed = middle + mixed_sum
+    feed_sums = feed_sums.reshape(seq, slab, -1)
     middle_grad = grad_own.astype(F32) + norm_input_grad(middle, factor_two, normed_two_grad)
-    feed_part = feed_part.reshape(dp, width // dp, -1)
-    attended_grad, output_kept, output_away, down_kept, down_away, feed_came = gather_back(
-        middle_grad.astype(BF16), output_own, attended, hidden, grad_out, feed_part, 5
+    attended_grad, output_kept, output_away, down_kept, down_away, feed_grad_near = gather_back(
+        middle_grad.astype(BF16), output_own, attended, hidden, grad_out, feed_sums, 5
     )
 
     def both(kept, came):
         return kept.astype(F32) + came.astype(F32)
 
-    feed_kept = lax.dynamic_index_in_dim(feed_part, data, 0, keepdims=False)
-    feed_sums = both(feed_kept, feed_came).astype(BF16).reshape(seq, slab, -1)
     qkv_back, feed_grad_far, down_came, output_came = attention_back_feed(
         queries,
         keys,
@@ -2026,9 +2038,7 @@
     )
     down_grad = both(down_kept, down_came)
     output_grad = both(output_kept, output_came)
-    normed_one_grad, feed_grad_near, qkv_grads = product_scatter_last(
-        qkv_back, qkv_weight, normed_one, feed_sums, 7
-    )
+    normed_one_grad, qkv_grads = product_scatter_last(qkv_back, qkv_weight, normed_one, 7)
     token_grad = middle_grad + norm_input_grad(inputs, factor_one, normed_one_grad)
 
     pair = ((mine // 2) % 2).reshape(1)

time: 619 us -> 612 us (0.989)
  Pallas kernels: 539 us -> 576 us
  waiting for transfers between devices: 34.4 us -> 0 us
  between operations: 14.4 us -> 0.99 us
    reduce_scatter x1 -> x0, waiting for transfers between devices: 34.4 us -> none  [scatter_rows(): lax.psum_scatter(partial.astype(BF16), 'seq', scatter_dimension=0, tiled=...]
    pallas_call x3, Pallas kernels: 220 us -> 240 us  [the longest x1 109 us: product_scatter_both(): pl.pallas_call(scatter_both_kernel, out_shape=[jax.ShapeDtypeStruct((rows...]
    pallas_call x1, Pallas kernels: 51.7 us -> 67.6 us  [gather_back(): pl.pallas_call(back_kernel, out_shape=[jax.ShapeDtypeStruct((seq * rows,...]
    unnamed x68 -> x58, local copies, waits for them, and re-layouts: 9.6 us -> 13.3 us
  transfers between devices with their start and end apart: 1 -> 0, of which waited for: 1 -> 0; matrix products, arithmetic and copies ran while one was open for 0% -> 0% of each run, Pallas kernels for 14% -> 0%
where the time goes in v6:
time: 612 us
  Pallas kernels  576 us (94%)
  other arithmetic  19.5 us (3%)
  local copies, waits for them, and re-layouts  15.4 us (3%)
    pallas_call x1, Pallas kernels, gather_project(): pl.pallas_call(project_kernel, out_shape=[bf16(all_rows, width), bf16(all...  128 us
    pallas_call x1, Pallas kernels, product_scatter_both(): pl.pallas_call(scatter_both_kernel, out_shape=[jax.ShapeDtypeStruct((rows...  109 us
    pallas_call x1, Pallas kernels, product_scatter_last(): pl.pallas_call(scatter_last_kernel, out_shape=[jax.ShapeDtypeStruct((rows...  75.1 us
    pallas_call x1, Pallas kernels, gather_back(): pl.pallas_call(back_kernel, out_shape=[jax.ShapeDtypeStruct((seq * rows,...  67.6 us
    pallas_call x1, Pallas kernels, product_scatter_feed(): pl.pallas_call(scatter_feed_kernel, out_shape=[jax.ShapeDtypeStruct((rows...  55.7 us
    pallas_call x1, Pallas kernels, gather_feed(): pl.pallas_call(feed_kernel, out_shape=[jax.ShapeDtypeStruct((seq * rows,...  54.5 us
    pallas_call x1, Pallas kernels, attention_back_feed(): pl.pallas_call(functools.partial(attention_back_feed_kernel, block), grid...  41.6 us
    pallas_call x1, Pallas kernels, attention_feed(): pl.pallas_call(functools.partial(attention_feed_kernel, block), grid=(row...  37.2 us

profile of v6, /device:TPU:0, one launch (start us, length us, event | category | flops | bytes accessed | tf_op | source)
XLA Modules:
  0.0 611.6 jit_solution(11446000689544934889)
XLA Ops:
  0.6 0.7 bitcast_convert_fusion.1
  1.3 0.7 copy.27.gain_one_ref
  2.0 0.7 bitcast_convert_fusion
  2.7 0.7 copy.28.gain_two_ref
  3.4 0.6 broadcast_in_dim_tile.3.freq_ref
  4.0 128.3 %shard_map.203 = (bf16[2048,2048]{1,0:T(8,128)(2,1)}, bf16[2048,2048]{1,0:T(8,128)(2,1)}, bf16[2048,128]{1,0:T(8,128)(2,1)}, bf16[2048,128]{1,0:T(8,128)(2,1)}, ...) custom-call(s32[1,4]{1,0:T(1,128)} %lengths_ref.1, ...), custom_call_target="tpu_custom_call" | custom-call | flops 3221225472 | bytes 33554432 | tf_op jit(solution)/shard_map/pallas_call | solution.py:733
  132.3 1.2 copy-done.1
  133.5 1.0 copy-done.3
  134.6 1.0 copy-done.4
  135.6 1.0 copy-done.5
  136.7 37.2 %shard_map.204 = (f32[2048,128]{1,0:T(8,128)S(1)}, f32[2048,2]{1,0:T(8,128)S(1)}, bf16[8,64,1024]{2,1,0:T(8,128)(2,1)S(1)}) custom-call(bf16[2048,128]{1,0:T(8,128)(2,1)S(1)} %copy-done.3, bf16[2048,128]{1,0:T(8,128)(2,1)S(1)} %copy-done.4, bf16[2048,128]{1,0:T(8,128)(2,1)S(1)} %copy-done.5, s32[2048,1]{1,0:T(8,128)S(1)} %copy-done.1, ...), custom_call_target="tpu_custom_call" | custom-call | flops 1073741824 | bytes 2621440 | tf_op jit(solution)/shard_map/pallas_call | solution.py:803
  173.8 0.0 copy-start
  173.8 0.0 copy-start.8
  173.9 0.1 convert_element_type.24.a_ref.attended_ref
  173.9 0.0 copy-start.23
  174.0 55.7 %shard_map.205 = (f32[128,2048]{1,0:T(8,128)S(1)}, bf16[2,16,64,1024]{3,2,1,0:T(8,128)(2,1)S(1)}) custom-call(bf16[2048,128]{1,0:T(8,128)(2,1)S(1)} %convert_element_type.24.a_ref.attended_ref, bf16[128,2048]{1,0:T(8,128)(2,1)S(1)} %bitcast.13, bf16[8,64,1024]{2,1,0:T(8,128)(2,1)S(1)} %copy-done.22, bf16[8,64,1024]{2,1,0:T(8,128)(2,1)S(1)} %get-tuple-element.65.far_ref), custom_call_target="tpu_custom_call" | custom-call | flops 1073741824 | bytes 16777216 | tf_op jit(solution)/shard_map/pallas_call | solution.py:1145
  229.7 2.1 copy-done.20
  231.8 0.2 multiply_reduce_fusion.1
  232.0 0.9 multiply_convert_fusion.own_ref
  233.0 54.5 %shard_map.206 = (bf16[2048,2048]{1,0:T(8,128)(2,1)}, bf16[2048,512]{1,0:T(8,128)(2,1)}, bf16[2048,1024]{1,0:T(8,128)(2,1)}, bf16[1024,2048]{1,0:T(8,128)(2,1)}) custom-call(bf16[128,2048]{1,0:T(8,128)(2,1)} %multiply_convert_fusion.own_ref, bf16[2048,2048]{1,0:T(8,128)(2,1)} %get-tuple-element.67.grad_hbm.out_grad_hbm, bf16[2048,1024]{1,0:T(8,128)(2,1)} %bitcast.12, ...), custom_call_target="tpu_custom_call" | custom-call | flops 17179869184 | bytes 33554432 | tf_op jit(solution)/shard_map/pallas_call | solution.py:1261
  287.4 108.9 %shard_map.207 = (f32[128,2048]{1,0:T(8,128)}, f32[128,2048]{1,0:T(8,128)}, bf16[1024,1024]{1,0:T(8,128)(2,1)}) custom-call(bf16[2048,1024]{1,0:T(8,128)(2,1)} %get-tuple-element.70.back_ref, bf16[1024,2048]{1,0:T(8,128)(2,1)} %get-tuple-element.71.turned_ref, bf16[2048,512]{1,0:T(8,128)(2,1)} %get-tuple-element.72.hidden_ref.hidden_hbm, ...), custom_call_target="tpu_custom_call" | custom-call | flops 25769803776 | bytes 50331648 | tf_op jit(solution)/shard_map/pallas_call | solution.py:1082
  396.3 0.0 copy-start.28
  396.3 0.0 copy-start.26
  396.3 1.6 fusion
  397.9 0.6 reduce_sum.46
  398.6 0.7 add_compare_fusion
  399.2 3.3 fusion.8
  402.6 67.6 %shard_map.208 = (bf16[2048,128]{1,0:T(8,128)(2,1)S(1)}, f32[64,2048]{1,0:T(8,128)S(1)}, bf16[64,2048]{1,0:T(8,128)(2,1)S(1)}, f32[256,2048]{1,0:T(8,128)}, bf16...) custom-call(bf16[128,2048]{1,0:T(8,128)(2,1)S(1)} %get-tuple-element.103.own_ref, ...), custom_call_target="tpu_custom_call" | custom-call | flops 4294967296 | bytes 25165824 | tf_op jit(solution)/shard_map/pallas_call | solution.py:1368
  470.2 0.0 copy-start.9
  470.2 1.0 copy-done.9
  471.2 0.8 copy-done.11
  472.0 0.7 copy-done.13
  472.7 41.6 %shard_map.209 = (bf16[2048,384]{1,0:T(8,128)(2,1)}, bf16[8,64,1024]{2,1,0:T(8,128)(2,1)}, bf16[256,2048]{1,0:T(8,128)(2,1)}, bf16[64,2048]{1,0:T(8,128)(2,1)}) custom-call(bf16[2048,128]{1,0:T(8,128)(2,1)} %get-tuple-element.56.q_ref, bf16[2048,128]{1,0:T(8,128)(2,1)} %get-tuple-element.57.k_ref, bf16[2048,128]{1,0:T(8,128)(2,1)} %get-tuple-element.58.v_ref, ...), custom_call_target="tpu_custom_call" | custom-call | flops 2684354560 | bytes 5242880 | tf_op jit(solution)/shard_map/pallas_call | solution.py:1481
  514.3 2.8 convert_add_fusion
  517.1 0.9 convert_add_fusion.2
  518.0 0.0 copy-start.15
  518.0 75.1 %shard_map.210 = (f32[128,2048]{1,0:T(8,128)}, bf16[2,8,64,384]{3,2,1,0:T(8,128)(2,1)}) custom-call(bf16[2048,384]{1,0:T(8,128)(2,1)} %get-tuple-element.83.a_ref, bf16[2048,384]{1,0:T(8,128)(2,1)} %bitcast.19, bf16[2048,2048]{1,0:T(8,128)(2,1)} %get-tuple-element.85.normed_hbm), custom_call_target="tpu_custom_call" | custom-call | flops 3221225472 | bytes 16777216 | tf_op jit(solution)/shard_map/pallas_call | solution.py:1584
  593.2 0.0 copy-start.7
  593.2 1.2 copy-done.7
  594.5 1.1 copy-done.10
  595.6 0.8 copy-done.17
  596.4 6.9 %shard_map.211 = (f32[64,8192]{1,0:T(8,128)}, f32[64,8192]{1,0:T(8,128)}, f32[64,2048]{1,0:T(8,128)}, f32[64,512]{1,0:T(8,128)}, f32[64,512]{1,0:T(8,128)}, /*index=5*/f32[64,1]{1,0:T(8,128)S(1)}, f32[64,1]{1,0:T(8,128)S(1)}) custom-call(s32[1]{0:T(128)} %bitcast.7.pair_ref, bf16[8,64,1024]{2,1,0:T(8,128)(2,1)S(1)} %get-tuple-element.87.near_gate_ref.near_up_ref, ...), custom_call_target="tpu_custom_call" | custom-call | flops 524288 | bytes 8388608 | tf_op jit(solution)/shard_map/pallas_call | solution.py:1707
  603.3 0.6 copy-done.18
  603.9 0.6 copy-done.19
  604.5 1.5 reduce
  606.0 1.4 reduce.1
  607.4 1.5 fusion.6
  609.0 2.7 fusion.5
  (42 shorter events, 0.1 us)
Async XLA Ops:
  132.3 1.2 copy-start.1
  133.5 1.0 copy-start.3
  134.6 1.0 copy-start.4
  135.6 1.0 copy-start.5
  136.7 37.3 %copy-start.21 = (bf16[2,64,2048]{2,1,0:T(8,128)(2,1)S(1)}, bf16[2,64,2048]{2,1,0:T(8,128)(2,1)}, u32[]{:S(2)}) copy-start(bf16[2,64,2048]{2,1,0:T(8,128)(2,1)} %get-tuple-element.63) | copy-start | bytes 1572868
  136.7 37.3 %copy-start.22 = (bf16[8,64,1024]{2,1,0:T(8,128)(2,1)S(1)}, bf16[8,64,1024]{2,1,0:T(8,128)(2,1)}, u32[]{:S(2)}) copy-start(bf16[8,64,1024]{2,1,0:T(8,128)(2,1)} %get-tuple-element.64.near_ref) | copy-start | bytes 3145732
  173.8 55.9 %copy-start = (f32[2048,128]{1,0:T(8,128)}, f32[2048,128]{1,0:T(8,128)S(1)}, u32[]{:S(2)}) copy-start(f32[2048,128]{1,0:T(8,128)S(1)} %get-tuple-element.62.att_ref) | copy-start | bytes 3145732
  173.8 55.9 %copy-start.8 = (f32[2048,2]{1,0:T(8,128)}, f32[2048,2]{1,0:T(8,128)S(1)}, u32[]{:S(2)}) copy-start(f32[2048,2]{1,0:T(8,128)S(1)} %get-tuple-element.78.lse_ref) | copy-start | bytes 49156
  173.9 57.9 %copy-start.23 = (bf16[128,2048]{1,0:T(8,128)(2,1)S(1)}, bf16[128,2048]{1,0:T(8,128)(2,1)}, u32[]{:S(2)}) copy-start(bf16[128,2048]{1,0:T(8,128)(2,1)} %tokens_ref.1) | copy-start | bytes 1572868
  229.7 2.1 copy-start.20
  396.3 1.6 copy-start.28
  396.3 2.9 copy-start.26
  470.2 1.0 copy-start.9
  471.2 0.8 copy-start.11
  472.0 0.7 copy-start.13
  472.7 41.6 %copy-start.25 = (f32[256,2048]{1,0:T(8,128)S(1)}, f32[256,2048]{1,0:T(8,128)}, u32[]{:S(2)}) copy-start(f32[256,2048]{1,0:T(8,128)} %get-tuple-element.99) | copy-start | bytes 6291460
  514.3 2.9 copy-start.27
  518.0 75.2 %copy-start.2 = (bf16[8,64,1024]{2,1,0:T(8,128)(2,1)S(1)}, bf16[8,64,1024]{2,1,0:T(8,128)(2,1)}, u32[]{:S(2)}) copy-start(bf16[8,64,1024]{2,1,0:T(8,128)(2,1)} %get-tuple-element.88.far_gate_ref.far_up_ref) | copy-start | bytes 3145732
  518.0 75.2 %copy-start.6 = (bf16[64,8192]{1,0:T(8,128)(2,1)S(1)}, bf16[64,8192]{1,0:T(8,128)(2,1)}, u32[]{:S(2)}) copy-start(bf16[64,8192]{1,0:T(8,128)(2,1)} %gate_ref.3) | copy-start | bytes 3145732
  518.0 75.2 %copy-start.12 = (bf16[64,2048]{1,0:T(8,128)(2,1)S(1)}, bf16[64,2048]{1,0:T(8,128)(2,1)}, u32[]{:S(2)}) copy-start(bf16[64,2048]{1,0:T(8,128)(2,1)} %query_ref.3) | copy-start | bytes 786436
  518.0 75.2 %copy-start.14 = (f32[64,1]{1,0:T(8,128)S(1)}, f32[64,1]{1,0:T(8,128)}, u32[]{:S(2)}) copy-start(f32[64,1]{1,0:T(8,128)} %copy.27.gain_one_ref) | copy-start | bytes 772
  518.0 75.2 %copy-start.15 = (f32[64,1]{1,0:T(8,128)S(1)}, f32[64,1]{1,0:T(8,128)}, u32[]{:S(2)}) copy-start(f32[64,1]{1,0:T(8,128)} %copy.28.gain_two_ref) | copy-start | bytes 772
  518.0 75.2 %copy-start.16 = (bf16[64,512]{1,0:T(8,128)(2,1)S(1)}, bf16[64,512]{1,0:T(8,128)(2,1)}, u32[]{:S(2)}) copy-start(bf16[64,512]{1,0:T(8,128)(2,1)} %key_ref.3) | copy-start | bytes 196612
  593.2 1.2 copy-start.7
  594.5 1.1 copy-start.10
  595.6 0.8 copy-start.17
  603.3 0.6 copy-start.18
  603.9 0.6 copy-start.19
  604.5 4.4 copy-start.24

commit v7 on v6

--- a/solution.py
+++ b/solution.py
@@ -3,6 +3,7 @@
 
 import jax
 import jax.numpy as jnp
+import numpy as np
 from jax import lax
 from jax.experimental import pallas as pl
 from jax.experimental.pallas import tpu as pltpu
@@ -68,7 +69,7 @@
             allowed = allowed_tile(opening, tile * block, first, scores.shape)
             scores = jnp.where(allowed, scores, NEG)
             new_peak = jnp.maximum(peak, jnp.max(scores, axis=1, keepdims=True))
-            spread = jnp.where(allowed, jnp.exp(scores - new_peak), 0.0)
+            spread = jnp.exp(scores - new_peak)
             fade = jnp.exp(peak - new_peak)
             total = total * fade + jnp.sum(spread, axis=1, keepdims=True)
             acc = acc * fade + dot(spread.astype(BF16), v_ref[pl.ds(first, block), lanes])
@@ -255,12 +256,22 @@
             slot = lax.rem(self.here.slot + ahead, self.slots)
             visit(self.here.peer(slot, self.same), slot)
 
+    def start_one(self, ahead):
+        slot = lax.rem(self.here.slot + ahead, self.slots)
+        peer = self.here.peer(slot, self.same)
+        for one in self.copies(peer, self.here.mine, self.here.slot, slot):
+            one.start()
+
     def start(self):
-        def visit(peer, slot):
-            for one in self.copies(peer, self.here.mine, self.here.slot, slot):
-                one.start()
-
-        self.each(visit)
+        pl.loop(1 if self.same else 0, self.slots)(self.start_one)
+
+    def start_some(self, number, each):
+        first = 1 if self.same else 0
+
+        @pl.loop(0, each)
+        def _(i):
+            ahead = first + number * each + i
+            pl.when((number >= 0) & (ahead < self.slots))(lambda: self.start_one(ahead))
 
     def finish(self):
         def visit(peer, slot):
@@ -309,7 +320,7 @@
     return Spread(here, same, copies)
 
 
-def gather_units(here, buf, send_sems, recv_sems, compute, between=None, ready=0, started=nothing):
+def gather_units(here, buf, send_sems, recv_sems, compute, between=None, ready=None, started=nothing):
     length = here.length
     last = length - 1
     steps = 2 * length
@@ -385,10 +396,11 @@
         across(block, part).wait_recv()
         sideways(block, part).start()
 
-        if between is None:
+        if between is not None:
+            between(step)
+        if ready is None:
             unit(step)
         else:
-            between(step)
             begin = jnp.maximum(2 * (step - ready), 0)
             end = jnp.maximum(2 * (step + 1 - ready), 0)
 
@@ -488,6 +500,20 @@
     behind = pltpu.roll(values, HEAD_DIM // 2, 1)
     swapped = jnp.where(lane % HEAD_DIM < HEAD_DIM // 2, ahead, behind)
     return values * cosine + swapped * sine
+
+
+def upright(row):
+    count = row.shape[1]
+    shape = (count, count)
+    same = lax.broadcasted_iota(jnp.int32, shape, 0) == lax.broadcasted_iota(jnp.int32, shape, 1)
+    return jnp.sum(jnp.where(same, row.astype(F32), 0.0), axis=1, keepdims=True)
+
+
+def flat(column):
+    count = column.shape[0]
+    shape = (count, count)
+    same = lax.broadcasted_iota(jnp.int32, shape, 0) == lax.broadcasted_iota(jnp.int32, shape, 1)
+    return jnp.sum(jnp.where(same, column, 0.0), axis=0, keepdims=True)
 
 
 def project_kernel(
@@ -553,7 +579,7 @@
             buf[here.mine, 1, some, :] = jnp.where(place < ends[-1], grads, 0.0).astype(BF16)
 
     def own_blocks():
-        gain = gain_one_ref[...]
+        gain = upright(gain_one_ref[...])
         query = query_ref[...].astype(F32) * gain
         key = key_ref[...].astype(F32) * gain
         value = value_ref[...].astype(F32) * gain
@@ -648,16 +674,17 @@
         @pl.loop(0, gate_ref.shape[1] // chunk)
         def _(i):
             some = pl.ds(pl.multiple_of(i * chunk, chunk), chunk)
-            gain = gain_two_ref[...]
+            gain = upright(gain_two_ref[...])
             gate_out_ref[:, some] = (gate_ref[:, some].astype(F32) * gain).astype(BF16)
             up_out_ref[:, some] = (up_ref[:, some].astype(F32) * gain).astype(BF16)
 
         for one in own_feed:
             one.start()
-        feed.start()
         own_tables()
 
     def between(step):
+        feed.start_some(step - (2 * here.length - 3), 3)
+
         @pl.when(step == 2)
         def _():
             near.finish()
@@ -761,7 +788,7 @@
             dma((6,)),
             dma((2, seq)),
         ],
-        compiler_params=params(call_id, 56),
+        compiler_params=params(call_id, 60),
         cost_estimate=cost(2 * all_rows * width * 3 * cols, 8 * all_rows * width),
     )(lengths, tokens, cotangent, query, key, value, gate, up, *gains, freq, down, output)
 
@@ -777,6 +804,7 @@
     out_ref,
     lse_ref,
     feed_ref,
+    low_ref,
     feed_sems,
 ):
     here = Place()
@@ -788,6 +816,7 @@
         feed.start()
 
     attention_kernel(block, q_ref, k_ref, v_ref, open_ref, out_ref, lse_ref)
+    low_ref[...] = out_ref[...].astype(BF16)
 
     @pl.when(pl.program_id(0) == pl.num_programs(0) - 1)
     def _():
@@ -804,16 +833,32 @@
         functools.partial(attention_feed_kernel, block),
         grid=(rows // block,),
         in_specs=[tiled(cols), whole, whole, tiled(1), HBM, HBM],
-        out_specs=[tiled(cols), tiled(heads), HBM],
+        out_specs=[tiled(cols), tiled(heads), HBM, tiled(cols)],
         out_shape=[
             jax.ShapeDtypeStruct((rows, cols), F32),
             jax.ShapeDtypeStruct((rows, heads), F32),
             jax.ShapeDtypeStruct((seq // 2, gate.shape[0], feed_cols), BF16),
+            jax.ShapeDtypeStruct((rows, cols), BF16),
         ],
         scratch_shapes=[pltpu.SemaphoreType.DMA((2, seq // 2, 4))],
-        compiler_params=params(call_id, 48),
+        compiler_params=params(call_id, 60),
         cost_estimate=cost(2 * rows * rows * cols, 10 * rows * cols),
     )(queries, keys, values, opening, gate, up)
+
+
+ROW_CHUNK = 32
+
+
+def norm_input_grad(values, upstream):
+    factor = norm_factor(values)
+    inner_mean = jnp.mean(upstream * values, axis=-1, keepdims=True)
+    return factor * upstream - values * factor * factor * factor * inner_mean
+
+
+def in_row_chunks(rows, chunk, visit):
+    @pl.loop(0, rows // chunk)
+    def _(i):
+        visit(pl.ds(pl.multiple_of(i * chunk, chunk), chunk))
 
 
 SCATTER_PARTS = 2
@@ -835,8 +880,8 @@
     pair_sems,
     line_sems,
     came_sems,
+    early=None,
     between=nothing,
-    middle=nothing,
     filler=None,
 ):
     length = here.length
@@ -921,6 +966,8 @@
 
         product(target(step // parts), 1 - here.pair, here.core, step % parts, use)
         pair_copy(step).start()
+        if early is not None:
+            early(step)
 
     for_sibling(jnp.int32(0), here.pair, jnp.int32(steps))
     between()
@@ -969,9 +1016,6 @@
         def _():
             line_out[step] = held[...].astype(BF16)
             up_copy(step, line, part).start()
-
-        if middle is not nothing:
-            pl.when(step == steps // 2)(middle)
 
     @pl.loop(2 * steps - SCATTER_RING, 2 * steps)
     def _(slot):
@@ -1015,15 +1059,23 @@
     turned_ref,
     hidden_ref,
     down_ref,
+    middle_ref,
+    grads_hbm,
     normed_hbm,
-    out_ref,
+    grad_ref,
+    low_ref,
     mixed_ref,
     sums_ref,
     *scratch,
 ):
     here = Place()
+    normed, away, came, own, fetch_sems, swap_sems, own_sem = scratch[SCATTER_SCRATCH:]
+    rows = grad_ref.shape[0]
+    own_copy = pltpu.make_async_copy(
+        grads_hbm.at[pl.ds(pl.multiple_of(here.mine * rows, rows), rows)], own, own_sem.at[0]
+    )
+    own_copy.start()
     here.greet(partner=True)
-    normed, away, came, fetch_sems, swap_sems = scratch[SCATTER_SCRATCH:]
     chunk = normed.shape[2]
     half = normed_hbm.shape[1] // 2
     chunks = half // chunk
@@ -1066,13 +1118,21 @@
     fetch(jnp.int32(0)).start()
     scatter_rows_of_products(
         here,
-        [(False, back_ref, turned_ref, out_ref), (False, hidden_ref, down_ref, mixed_ref)],
+        [(False, back_ref, turned_ref, grad_ref), (False, hidden_ref, down_ref, mixed_ref)],
         *scratch[:SCATTER_SCRATCH],
         filler=filler,
     )
-
-
-def product_scatter_both(back, turned, hidden, down, normed, call_id):
+    own_copy.wait()
+
+    def add(some):
+        grad = own[some, :].astype(F32) + norm_input_grad(middle_ref[some, :], grad_ref[some, :])
+        grad_ref[some, :] = grad
+        low_ref[some, :] = grad.astype(BF16)
+
+    in_row_chunks(rows, ROW_CHUNK, add)
+
+
+def product_scatter_both(back, turned, hidden, down, middle, grads, normed, call_id):
     seq = lax.axis_size("seq")
     rows = back.shape[0] // seq
     width = turned.shape[1]
@@ -1083,25 +1143,30 @@
         scatter_both_kernel,
         out_shape=[
             jax.ShapeDtypeStruct((rows, width), F32),
+            jax.ShapeDtypeStruct((rows, width), BF16),
             jax.ShapeDtypeStruct((rows, width), F32),
             jax.ShapeDtypeStruct((width // 2, cols), BF16),
         ],
-        in_specs=[VMEM] * 4 + [HBM],
-        out_specs=[VMEM] * 3,
+        in_specs=[VMEM] * 5 + [HBM] * 2,
+        out_specs=[VMEM] * 4,
         scratch_shapes=scatter_scratch(seq, rows, width, 2)
         + [
             pltpu.VMEM((2, normed.shape[0], chunk), BF16),
             pltpu.VMEM((width // 2, cols), BF16),
             pltpu.VMEM((width // 2, cols), BF16),
+            pltpu.VMEM((rows, width), BF16),
             dma((2,)),
             dma((2, 4)),
+            dma((1,)),
         ],
         compiler_params=params(call_id, 60),
         cost_estimate=scatter_cost(back, 3 * width),
-    )(back, turned, hidden, down, normed)
-
-
-def scatter_feed_kernel(a_ref, b_ref, near_ref, far_ref, out_ref, feed_ref, *scratch):
+    )(back, turned, hidden, down, middle, grads, normed)
+
+
+def scatter_feed_kernel(
+    a_ref, b_ref, tokens_ref, near_ref, far_ref, middle_ref, normed_ref, feed_ref, *scratch
+):
     here = Place()
     here.greet(partner=True)
     swap_sems, local_sems = scratch[SCATTER_SCRATCH:]
@@ -1127,8 +1192,15 @@
                 one.start()
 
     scatter_rows_of_products(
-        here, [(False, a_ref, b_ref, out_ref)], *scratch[:SCATTER_SCRATCH]
-    )
+        here, [(False, a_ref, b_ref, middle_ref)], *scratch[:SCATTER_SCRATCH]
+    )
+
+    def add(some):
+        middle = tokens_ref[some, :].astype(F32) + middle_ref[some, :]
+        middle_ref[some, :] = middle
+        normed_ref[some, :] = (middle * norm_factor(middle)).astype(BF16)
+
+    in_row_chunks(middle_ref.shape[0], ROW_CHUNK, add)
 
     @pl.loop(0, slots)
     def _(slot):
@@ -1137,7 +1209,7 @@
                 one.wait()
 
 
-def product_scatter_feed(a, b, near, far, call_id):
+def product_scatter_feed(a, b, tokens, near, far, call_id):
     seq = lax.axis_size("seq")
     rows = a.shape[0] // seq
     width = b.shape[1]
@@ -1146,15 +1218,16 @@
         scatter_feed_kernel,
         out_shape=[
             jax.ShapeDtypeStruct((rows, width), F32),
+            jax.ShapeDtypeStruct((rows, width), BF16),
             jax.ShapeDtypeStruct((2, seq, *near.shape[1:]), BF16),
         ],
-        in_specs=[VMEM, VMEM, HBM, HBM],
-        out_specs=[VMEM, HBM],
+        in_specs=[VMEM, VMEM, VMEM, HBM, HBM],
+        out_specs=[VMEM, VMEM, HBM],
         scratch_shapes=scatter_scratch(seq, rows, width)
         + [dma((2, 2, seq // 2)), dma((2, seq // 2))],
         compiler_params=params(call_id, 40),
         cost_estimate=scatter_cost(a, width),
-    )(a, b, near, far)
+    )(a, b, tokens, near, far)
 
 
 def feed_kernel(
@@ -1280,7 +1353,7 @@
             pltpu.SemaphoreType.DMA((3,)),
             pltpu.SemaphoreType.DMA((seq // 2, 3)),
         ],
-        compiler_params=params(call_id, 56),
+        compiler_params=params(call_id, 60),
         cost_estimate=cost(8 * seq * rows * width * hidden, 8 * seq * rows * width),
     )(own, grad_out, feed_weight, down_weight)
 
@@ -1323,9 +1396,10 @@
     near = block_spread(here, True, blocks_ref, near_ref, near_sems)
     own = pltpu.make_async_copy(blocks_ref.at[here.mine], near_ref.at[here.slot], own_sem.at[0])
 
-    def started():
-        near.start()
-        own.start()
+    own.start()
+
+    def between(step):
+        near.start_some(step - here.length, 2)
 
     part[...] = jnp.zeros_like(part)
     share = width // (2 * here.length)
@@ -1353,7 +1427,7 @@
 
         split(t_dot(hidden_ref[...], out_grad_ref[:, some]), down_kept_ref, down_away_ref, some)
 
-    gather_units(here, buf, send_sems, recv_sems, compute, started=started)
+    gather_units(here, buf, send_sems, recv_sems, compute, between)
     for t in range(width // tile):
         cols = slice(t * tile, (t + 1) * tile)
         split(part[:, cols], output_kept_ref, output_away_ref, cols)
@@ -1386,7 +1460,7 @@
             pltpu.VMEM(grad_out.shape, BF16),
             pltpu.SemaphoreType.DMA((2,)),
         ],
-        compiler_params=params(call_id, 48),
+        compiler_params=params(call_id, 60),
         cost_estimate=cost(8 * seq * rows * width * cols, 6 * seq * rows * width),
     )(own, weight, attended, hidden, grad_out, blocks)
 
@@ -1533,41 +1607,56 @@
         first = pl.multiple_of(dp * half + i * chunk, chunk)
         return t_dot(normed_ref[:, pl.ds(first, chunk)], a_ref[...])
 
+    def early(step):
+        @pl.when(step == 1)
+        def _():
+            fetch.wait()
+
+            @pl.loop(0, half // chunk)
+            def _(i):
+                some = pl.ds(pl.multiple_of(i * chunk, chunk), chunk)
+                away[some, :] = part(1 - here.dp, i).astype(BF16)
+
+            swap.start()
+
     def between():
-        fetch.wait()
-
         @pl.loop(0, half // chunk)
         def _(i):
-            away[pl.ds(pl.multiple_of(i * chunk, chunk), chunk), :] = part(1 - here.dp, i).astype(
-                BF16
-            )
-
-        swap.start()
+            kept[pl.ds(pl.multiple_of(i * chunk, chunk), chunk), :] = part(here.dp, i)
+
+    begin = 2
+    each = 3
 
     def filler(step):
-        @pl.when(step < half // chunk)
+        @pl.when(step == begin)
         def _():
-            kept[pl.ds(pl.multiple_of(step * chunk, chunk), chunk), :] = part(here.dp, step)
-
-    def middle():
-        swap.wait_recv()
-        slab = sums.shape[1]
-
-        @pl.loop(0, here.count)
-        def _(i):
-            rows = pl.ds(pl.multiple_of(i * slab, slab), slab)
-            sums[i] = (kept[rows, :] + came[rows, :].astype(F32)).astype(BF16)
-
-        qkv_ref[0, here.slot] = sums[here.mine]
-        far.start()
-        near.start()
+            swap.wait_recv()
+            slab = sums.shape[1]
+
+            @pl.loop(0, here.count)
+            def _(i):
+                rows = pl.ds(pl.multiple_of(i * slab, slab), slab)
+                sums[i] = (kept[rows, :] + came[rows, :].astype(F32)).astype(BF16)
+
+            qkv_ref[0, here.slot] = sums[here.mine]
+
+        @pl.when(step > begin)
+        def _():
+            @pl.loop(0, each)
+            def _(i):
+                number = (step - begin - 1) * each + i
+                pl.when(number < far.slots)(lambda: far.start_one(number))
+
+                @pl.when((number >= far.slots) & (number < 2 * far.slots - 1))
+                def _():
+                    near.start_one(number - far.slots + 1)
 
     scatter_rows_of_products(
         here,
         [(True, a_ref, b_ref, out_ref)],
         *scratch[:SCATTER_SCRATCH],
+        early,
         between,
-        middle,
         filler,
     )
     swap.wait_send()
@@ -1601,7 +1690,7 @@
             dma((2,)),
             dma((1,)),
         ],
-        compiler_params=params(call_id, 56),
+        compiler_params=params(call_id, 60),
         cost_estimate=scatter_cost(a, width),
     )(a, b, normed)
 
@@ -1620,6 +1709,15 @@
     value_ref,
     gain_one_ref,
     gain_two_ref,
+    tokens_ref,
+    middle_ref,
+    mixed_sum_ref,
+    middle_grad_ref,
+    upstream_ref,
+    down_kept_ref,
+    down_came_ref,
+    output_kept_ref,
+    output_came_ref,
     gate_out_ref,
     up_out_ref,
     query_out_ref,
@@ -1627,6 +1725,11 @@
     value_out_ref,
     one_out_ref,
     two_out_ref,
+    mixed_ref,
+    token_grad_ref,
+    down_out_ref,
+    output_out_ref,
+    total_two,
 ):
     pair = pair_ref[0]
     dp = lax.axis_size("dp")
@@ -1640,9 +1743,9 @@
 
     @pl.when(step == 0)
     def _():
-        two_out_ref[...] = jnp.zeros_like(two_out_ref)
+        total_two[...] = jnp.zeros_like(total_two)
         total = jnp.zeros((slab, 1), F32)
-        gain = gain_one_ref[...]
+        gain = upright(gain_one_ref[...])
 
         def put(out_ref, weight_ref, begin, grad):
             cols = slice(begin, begin + grad.shape[1])
@@ -1676,8 +1779,15 @@
                     total = total + put(
                         out_ref, weight_ref, begin, jnp.concatenate(two, axis=1)
                     )
-        one_out_ref[...] = total
-
+        one_out_ref[...] = flat(total)
+
+    mixed_ref[...] = middle_ref[...] + mixed_sum_ref[...]
+    token_grad_ref[...] = middle_grad_ref[...] + norm_input_grad(
+        tokens_ref[...].astype(F32), upstream_ref[...]
+    )
+    down_out_ref[...] = down_kept_ref[...] + down_came_ref[...].astype(F32)
+    output_out_ref[...] = output_kept_ref[...] + output_came_ref[...].astype(F32)
+    gain_two = upright(gain_two_ref[...])
     total = jnp.zeros((slab, 1), F32)
     for near_ref, far_ref, weight_ref, out_ref in (
         (near_gate_ref, far_gate_ref, gate_ref, gate_out_ref),
@@ -1689,11 +1799,15 @@
             grad = jnp.where(number // 2 == pair, near, far)
             cols = slice(number * columns, (number + 1) * columns)
             total = total + along(grad, weight_ref[:, cols])
-            out_ref[:, cols] = grad * gain_two_ref[...]
-    two_out_ref[...] += total
-
-
-def unpack(pair, near, far, gate, up, qkv, query, key, value, gain_one, gain_two):
+            out_ref[:, cols] = grad * gain_two
+    total_two[...] += total
+
+    @pl.when(step == pl.num_programs(0) * pl.num_programs(1) - 1)
+    def _():
+        two_out_ref[...] = flat(total_two[...])
+
+
+def unpack(pair, near, far, gate, up, qkv, query, key, value, gain_one, gain_two, *rows):
     dp = lax.axis_size("dp")
     seq = lax.axis_size("seq")
     slab, ff = gate.shape
@@ -1704,17 +1818,41 @@
     tile = pl.BlockSpec((slab, 4 * columns), lambda j, i: (0, j * length + i))
     f32 = lambda array: jax.ShapeDtypeStruct(array.shape, F32)
     outs = [f32(gate), f32(up), f32(query), f32(key), f32(value), f32(gain_one), f32(gain_two)]
+    sums = [f32(rows[0]), f32(rows[0]), f32(rows[5]), f32(rows[7])]
+    steps = dp * length
+    strip = lambda array: pl.BlockSpec(
+        (array.shape[0] // steps, array.shape[1]), lambda j, i: (j * length + i, 0)
+    )
     return pl.pallas_call(
         unpack_kernel,
         grid=(dp, length),
         in_specs=[pl.BlockSpec(memory_space=pltpu.SMEM)]
         + [block(0), block(0), block(1), block(1), tile, tile]
-        + [whole(array) for array in (qkv, query, key, value, gain_one, gain_two)],
-        out_specs=[tile, tile] + [whole(array) for array in outs[2:]],
-        out_shape=outs,
+        + [whole(array) for array in (qkv, query, key, value, gain_one, gain_two)]
+        + [strip(array) for array in rows],
+        out_specs=[tile, tile]
+        + [whole(array) for array in outs[2:]]
+        + [strip(array) for array in sums],
+        out_shape=outs + sums,
+        scratch_shapes=[pltpu.VMEM((slab, 1), F32)],
         compiler_params=pltpu.CompilerParams(vmem_limit_bytes=40 << 20),
         cost_estimate=cost(slab * ff, 16 * slab * ff),
-    )(pair, near, far, near, far, gate, up, qkv, query, key, value, gain_one, gain_two)
+    )(
+        pair,
+        near,
+        far,
+        near,
+        far,
+        gate,
+        up,
+        qkv,
+        query,
+        key,
+        value,
+        gain_one,
+        gain_two,
+        *rows,
+    )
 
 
 def swap_dp(values):
@@ -1921,6 +2059,23 @@
     )
 
 
+def frequencies():
+    exponent = np.arange(0, HEAD_DIM, 2, dtype=np.float32) / np.float32(HEAD_DIM)
+    inverse = np.power(np.float32(500000.0), -exponent)
+    wavelength = np.float32(2.0 * math.pi) / inverse
+    smooth = (np.float32(8192.0) / wavelength - np.float32(1.0)) / np.float32(3.0)
+    blended = (np.float32(1.0) - smooth) * inverse / np.float32(32.0) + smooth * inverse
+    scaled = np.where(
+        wavelength < 2048.0,
+        inverse,
+        np.where(wavelength > 8192.0, inverse / np.float32(32.0), blended),
+    )
+    return np.tile(scaled.astype(np.float32), 4)
+
+
+FREQUENCIES = frequencies()
+
+
 def shards(
     tokens,
     cotangent,
@@ -1941,8 +2096,8 @@
     tok_count, width = tokens.shape
     slab = query_weight.shape[0]
     block = 512
-    gain_one = attn_gain.astype(F32)[:, None]
-    gain_two = mlp_gain.astype(F32)[:, None]
+    gain_one = attn_gain[None, :]
+    gain_two = mlp_gain[None, :]
 
     (
         normed_one,
@@ -1969,20 +2124,15 @@
         gate_weight,
         up_weight,
         (gain_one, gain_two),
-        jnp.tile(rotary_table(HEAD_DIM), 2 * dp)[None, :],
+        jnp.asarray(FREQUENCIES)[None, :],
         down_weight,
         output_weight,
         0,
     )
-    inputs = tokens.astype(F32)
-    factor_one = norm_factor(inputs)
-    own_place = mine * tok_count + jnp.arange(tok_count, dtype=jnp.int32)
-    own_keeping = own_place < jnp.sum(doc_lengths)
-    grad_own = jnp.where(own_keeping[:, None], cotangent, BF16(0))
     qkv_weight = qkv_weight.reshape(width, -1)
     down_own = down_own.reshape(-1, width)
     output_own = output_own.reshape(-1, width)
-    attended_sum, log_total, feed_far = attention_feed(
+    attended_sum, log_total, feed_far, attended = attention_feed(
         queries,
         keys,
         values,
@@ -1993,32 +2143,21 @@
         block,
         1,
     )
-    attended = attended_sum.astype(BF16)
-    attended_out, feed_weight = product_scatter_feed(attended, output_own, feed_near, feed_far, 2)
+    middle, middle_normed, feed_weight = product_scatter_feed(
+        attended, output_own, tokens, feed_near, feed_far, 2
+    )
     feed_weight = feed_weight.reshape(width, -1)
-    middle = inputs + attended_out
-
-    factor_two = norm_factor(middle)
+
     normed_two, hidden, feed_back, feed_turned = gather_feed(
-        (middle * factor_two).astype(BF16), grad_out, feed_weight, down_own, 3
-    )
-
-    def norm_input_grad(values, factor, upstream):
-        inner_mean = jnp.mean(upstream * values, axis=-1, keepdims=True)
-        return factor * upstream - values * factor * factor * factor * inner_mean
-
-    normed_two_grad, mixed_sum, feed_sums = product_scatter_both(
-        feed_back, feed_turned, hidden, down_own, normed_two, 4
-    )
-    mixed = middle + mixed_sum
+        middle_normed, grad_out, feed_weight, down_own, 3
+    )
+    middle_grad, middle_back, mixed_sum, feed_sums = product_scatter_both(
+        feed_back, feed_turned, hidden, down_own, middle, grad_out, normed_two, 4
+    )
     feed_sums = feed_sums.reshape(seq, slab, -1)
-    middle_grad = grad_own.astype(F32) + norm_input_grad(middle, factor_two, normed_two_grad)
     attended_grad, output_kept, output_away, down_kept, down_away, feed_grad_near = gather_back(
-        middle_grad.astype(BF16), output_own, attended, hidden, grad_out, feed_sums, 5
-    )
-
-    def both(kept, came):
-        return kept.astype(F32) + came.astype(F32)
+        middle_back, output_own, attended, hidden, grad_out, feed_sums, 5
+    )
 
     qkv_back, feed_grad_far, down_came, output_came = attention_back_feed(
         queries,
@@ -2036,13 +2175,22 @@
         block,
         6,
     )
-    down_grad = both(down_kept, down_came)
-    output_grad = both(output_kept, output_came)
     normed_one_grad, qkv_grads = product_scatter_last(qkv_back, qkv_weight, normed_one, 7)
-    token_grad = middle_grad + norm_input_grad(inputs, factor_one, normed_one_grad)
 
     pair = ((mine // 2) % 2).reshape(1)
-    gate_grad, up_grad, query_grad, key_grad, value_grad, attn_gain_grad, mlp_gain_grad = unpack(
+    (
+        gate_grad,
+        up_grad,
+        query_grad,
+        key_grad,
+        value_grad,
+        attn_gain_grad,
+        mlp_gain_grad,
+        mixed,
+        token_grad,
+        down_grad,
+        output_grad,
+    ) = unpack(
         pair,
         feed_grad_near,
         feed_grad_far,
@@ -2054,12 +2202,21 @@
         value_weight,
         gain_one,
         gain_two,
+        tokens,
+        middle,
+        mixed_sum,
+        middle_grad,
+        normed_one_grad,
+        down_kept,
+        down_came,
+        output_kept,
+        output_came,
     )
     return (
         mixed,
         token_grad,
-        attn_gain_grad[:, 0],
-        mlp_gain_grad[:, 0],
+        attn_gain_grad[0],
+        mlp_gain_grad[0],
         query_grad,
         key_grad,
         value_grad,

time: 612 us -> 574 us (0.938)
  Pallas kernels: 576 us -> 553 us
  other arithmetic: 19.5 us -> 0 us
    pallas_call x1, Pallas kernels: 128 us -> 118 us  [gather_project(): pl.pallas_call(project_kernel, out_shape=[bf16(all_rows, width), bf16(all...]
    pallas_call x1, Pallas kernels: 67.6 us -> 60.8 us  [gather_back(): pl.pallas_call(back_kernel, out_shape=[jax.ShapeDtypeStruct((seq * rows,...]
    add x3 -> x0, other arithmetic: 6.37 us -> none  [the longest x2 3.69 us: both(): return kept.astype(F32) + came.astype(F32)]
    unnamed x58 -> x54, local copies, waits for them, and re-layouts: 13.3 us -> 19.2 us
where the time goes in v7:
time: 574 us; the launch traced here: 573 us
  Pallas kernels  553 us (96%)
  local copies, waits for them, and re-layouts  19.2 us (3%)
    pallas_call x1, Pallas kernels, gather_project(): pl.pallas_call(project_kernel, out_shape=[bf16(all_rows, width), bf16(all...  118 us
    pallas_call x1, Pallas kernels, product_scatter_both(): pl.pallas_call(scatter_both_kernel, out_shape=[jax.ShapeDtypeStruct((rows...  110 us
    pallas_call x1, Pallas kernels, product_scatter_last(): pl.pallas_call(scatter_last_kernel, out_shape=[jax.ShapeDtypeStruct((rows...  75.5 us
    pallas_call x1, Pallas kernels, gather_back(): pl.pallas_call(back_kernel, out_shape=[jax.ShapeDtypeStruct((seq * rows,...  60.8 us
    pallas_call x1, Pallas kernels, product_scatter_feed(): pl.pallas_call(scatter_feed_kernel, out_shape=[jax.ShapeDtypeStruct((rows...  56 us
    pallas_call x1, Pallas kernels, gather_feed(): pl.pallas_call(feed_kernel, out_shape=[jax.ShapeDtypeStruct((seq * rows,...  54 us
    pallas_call x1, Pallas kernels, attention_back_feed(): pl.pallas_call(functools.partial(attention_back_feed_kernel, block), grid...  38.5 us
    pallas_call x1, Pallas kernels, attention_feed(): pl.pallas_call(functools.partial(attention_feed_kernel, block), grid=(row...  32 us

profile of v7, /device:TPU:0, one launch (start us, length us, event | category | flops | bytes accessed | tf_op | source)
XLA Modules:
  0.0 572.9 jit_solution(17551731818990382521)
XLA Ops:
  0.6 117.8 %shard_map.212 = (bf16[2048,2048]{1,0:T(8,128)(2,1)}, bf16[2048,2048]{1,0:T(8,128)(2,1)}, bf16[2048,128]{1,0:T(8,128)(2,1)}, bf16[2048,128]{1,0:T(8,128)(2,1)}, ...) custom-call(s32[1,4]{1,0:T(1,128)} %lengths_ref.1, ...), custom_call_target="tpu_custom_call" | custom-call | flops 3221225472 | bytes 33554432 | tf_op jit(solution)/shard_map/pallas_call | solution.py:760
  118.4 0.0 copy-start.12
  118.5 0.0 copy-start.24
  118.5 0.0 copy-start.25
  118.5 32.0 %shard_map.213 = (f32[2048,128]{1,0:T(8,128)}, f32[2048,2]{1,0:T(8,128)}, bf16[8,64,1024]{2,1,0:T(8,128)(2,1)}, bf16[2048,128]{1,0:T(8,128)(2,1)}) custom-call(bf16[2048,128]{1,0:T(8,128)(2,1)} %get-tuple-element.63.q_ref, bf16[2048,128]{1,0:T(8,128)(2,1)} %get-tuple-element.64.k_ref, bf16[2048,128]{1,0:T(8,128)(2,1)} %get-tuple-element.65.v_ref, ...), custom_call_target="tpu_custom_call" | custom-call | flops 1073741824 | bytes 2621440 | tf_op jit(solution)/shard_map/pallas_call | solution.py:832
  150.5 0.0 copy-done.12
  150.5 0.0 copy-done.24
  150.5 1.2 copy-done.21
  151.7 1.0 copy-done.22
  152.8 56.0 %shard_map.214 = (f32[128,2048]{1,0:T(8,128)S(1)}, bf16[128,2048]{1,0:T(8,128)(2,1)S(1)}, bf16[2,16,64,1024]{3,2,1,0:T(8,128)(2,1)S(1)}) custom-call(bf16[2048,128]{1,0:T(8,128)(2,1)S(1)} %copy-done.22, bf16[128,2048]{1,0:T(8,128)(2,1)S(1)} %bitcast.16, bf16[128,2048]{1,0:T(8,128)(2,1)S(1)} %copy-done.12, bf16[8,64,1024]{2,1,0:T(8,128)(2,1)S(1)} %copy-done.25, ...), custom_call_target="tpu_custom_call" | custom-call | flops 1073741824 | bytes 16777216 | tf_op jit(solution)/shard_map/pallas_call | solution.py:1217
  208.8 0.0 copy-start.5
  208.8 1.0 copy-done.5
  209.8 2.0 copy-done.23
  211.8 0.8 copy-done.26
  212.6 54.0 %shard_map.215 = (bf16[2048,2048]{1,0:T(8,128)(2,1)}, bf16[2048,512]{1,0:T(8,128)(2,1)}, bf16[2048,1024]{1,0:T(8,128)(2,1)}, bf16[1024,2048]{1,0:T(8,128)(2,1)}) custom-call(bf16[128,2048]{1,0:T(8,128)(2,1)} %copy-done.26, bf16[2048,2048]{1,0:T(8,128)(2,1)} %get-tuple-element.74.grad_hbm.grads_hbm.out_grad_hbm, bf16[2048,1024]{1,0:T(8,128)(2,1)} %bitcast.14, ...), custom_call_target="tpu_custom_call" | custom-call | flops 17179869184 | bytes 33554432 | tf_op jit(solution)/shard_map/pallas_call | solution.py:1334
  266.6 110.1 %shard_map.216 = (f32[128,2048]{1,0:T(8,128)}, bf16[128,2048]{1,0:T(8,128)(2,1)}, f32[128,2048]{1,0:T(8,128)}, bf16[1024,1024]{1,0:T(8,128)(2,1)}) custom-call(bf16[2048,1024]{1,0:T(8,128)(2,1)} %get-tuple-element.77.back_ref, bf16[1024,2048]{1,0:T(8,128)(2,1)} %get-tuple-element.78.turned_ref, bf16[2048,512]{1,0:T(8,128)(2,1)} %get-tuple-element.79.hidden_ref.hidden_hbm, ...), custom_call_target="tpu_custom_call" | custom-call | flops 25769803776 | bytes 50331648 | tf_op jit(solution)/shard_map/pallas_call | solution.py:1142
  376.7 60.8 %shard_map.217 = (bf16[2048,128]{1,0:T(8,128)(2,1)}, f32[64,2048]{1,0:T(8,128)}, bf16[64,2048]{1,0:T(8,128)(2,1)}, f32[256,2048]{1,0:T(8,128)}, bf16[256,2048]{1,0:T(8,128)(2,1)}, /*index=5*/bf16[8,64,1024]{2,1,0:T(8,128)(2,1)}) custom-call(bf16[128,2048]{1,0:T(8,128)(2,1)} %get-tuple-element.82.own_ref, bf16[128,2048]{1,0:T(8,128)(2,1)} %bitcast.15, ...), custom_call_target="tpu_custom_call" | custom-call | flops 4294967296 | bytes 25165824 | tf_op jit(solution)/shard_map/pallas_call | solution.py:1442
  437.5 38.5 %shard_map.218 = (bf16[2048,384]{1,0:T(8,128)(2,1)}, bf16[8,64,1024]{2,1,0:T(8,128)(2,1)}, bf16[256,2048]{1,0:T(8,128)(2,1)}, bf16[64,2048]{1,0:T(8,128)(2,1)}) custom-call(bf16[2048,128]{1,0:T(8,128)(2,1)} %get-tuple-element.63.q_ref, bf16[2048,128]{1,0:T(8,128)(2,1)} %get-tuple-element.64.k_ref, bf16[2048,128]{1,0:T(8,128)(2,1)} %get-tuple-element.65.v_ref, ...), custom_call_target="tpu_custom_call" | custom-call | flops 2684354560 | bytes 5242880 | tf_op jit(solution)/shard_map/pallas_call | solution.py:1555
  476.1 0.0 copy-start
  476.1 0.0 copy-start.1
  476.1 0.0 copy-start.3
  476.1 0.0 copy-start.15
  476.1 0.0 copy-start.17
  476.1 0.0 copy-start.18
  476.1 0.0 copy-start.19
  476.1 0.0 copy-start.20
  476.1 75.5 %shard_map.219 = (f32[128,2048]{1,0:T(8,128)}, bf16[2,8,64,384]{3,2,1,0:T(8,128)(2,1)}) custom-call(bf16[2048,384]{1,0:T(8,128)(2,1)} %get-tuple-element.93.a_ref, bf16[2048,384]{1,0:T(8,128)(2,1)} %bitcast.23, bf16[2048,2048]{1,0:T(8,128)(2,1)} %get-tuple-element.95.normed_hbm), custom_call_target="tpu_custom_call" | custom-call | flops 3221225472 | bytes 16777216 | tf_op jit(solution)/shard_map/pallas_call | solution.py:1673
  551.7 0.0 copy-done
  551.7 0.0 copy-done.1
  551.7 0.0 copy-done.3
  551.7 0.0 copy-done.15
  551.7 0.0 copy-done.17
  551.7 0.0 copy-done.18
  551.8 0.0 copy-done.19
  551.8 0.0 copy-done.20
  551.8 0.0 copy-start.2
  551.8 1.6 copy-done.2
  553.4 1.2 copy-done.4
  554.6 1.2 copy-done.6
  555.8 1.2 copy-done.7
  557.0 1.2 copy-done.8
  558.3 1.2 copy-done.9
  559.5 1.2 copy-done.10
  560.7 1.1 copy-done.11
  561.9 1.0 copy-done.13
  562.9 1.0 copy-done.14
  563.9 0.9 copy-done.16
  564.9 8.0 %shard_map.220 = (f32[64,8192]{1,0:T(8,128)}, f32[64,8192]{1,0:T(8,128)}, f32[64,2048]{1,0:T(8,128)}, f32[64,512]{1,0:T(8,128)}, f32[64,512]{1,0:T(8,128)}, /*in...) custom-call(s32[1]{0:T(128)} %bitcast.pair_ref, ...), custom_call_target="tpu_custom_call" | custom-call | flops 524288 | bytes 8388608 | tf_op jit(solution)/shard_map/pallas_call | solution.py:1826
  (15 shorter events, 0.0 us)
Async XLA Ops:
  118.4 32.0 %copy-start.12 = (bf16[128,2048]{1,0:T(8,128)(2,1)S(1)}, bf16[128,2048]{1,0:T(8,128)(2,1)}, u32[]{:S(2)}) copy-start(bf16[128,2048]{1,0:T(8,128)(2,1)} %tokens_ref.5) | copy-start | bytes 1572868
  118.5 32.0 %copy-start.24 = (bf16[2,64,2048]{2,1,0:T(8,128)(2,1)S(1)}, bf16[2,64,2048]{2,1,0:T(8,128)(2,1)}, u32[]{:S(2)}) copy-start(bf16[2,64,2048]{2,1,0:T(8,128)(2,1)} %get-tuple-element.70) | copy-start | bytes 1572868
  118.5 32.0 %copy-start.25 = (bf16[8,64,1024]{2,1,0:T(8,128)(2,1)S(1)}, bf16[8,64,1024]{2,1,0:T(8,128)(2,1)}, u32[]{:S(2)}) copy-start(bf16[8,64,1024]{2,1,0:T(8,128)(2,1)} %get-tuple-element.71.near_ref) | copy-start | bytes 3145732
  150.5 1.2 copy-start.21
  151.7 1.0 copy-start.22
  208.8 1.0 copy-start.5
  209.8 2.0 copy-start.23
  211.8 0.8 copy-start.26
  476.1 75.6 %copy-start = (bf16[8,64,1024]{2,1,0:T(8,128)(2,1)S(1)}, bf16[8,64,1024]{2,1,0:T(8,128)(2,1)}, u32[]{:S(2)}) copy-start(bf16[8,64,1024]{2,1,0:T(8,128)(2,1)} %get-tuple-element.84.near_gate_ref.near_up_ref) | copy-start | bytes 3145732
  476.1 75.6 %copy-start.1 = (bf16[8,64,1024]{2,1,0:T(8,128)(2,1)S(1)}, bf16[8,64,1024]{2,1,0:T(8,128)(2,1)}, u32[]{:S(2)}) copy-start(bf16[8,64,1024]{2,1,0:T(8,128)(2,1)} %get-tuple-element.92.far_gate_ref.far_up_ref) | copy-start | bytes 3145732
  476.1 75.6 %copy-start.3 = (bf16[64,8192]{1,0:T(8,128)(2,1)S(1)}, bf16[64,8192]{1,0:T(8,128)(2,1)}, u32[]{:S(2)}) copy-start(bf16[64,8192]{1,0:T(8,128)(2,1)} %gate_ref.3) | copy-start | bytes 3145732
  476.1 75.6 %copy-start.15 = (bf16[64,2048]{1,0:T(8,128)(2,1)S(1)}, bf16[64,2048]{1,0:T(8,128)(2,1)}, u32[]{:S(2)}) copy-start(bf16[64,2048]{1,0:T(8,128)(2,1)} %query_ref.3) | copy-start | bytes 786436
  476.1 75.6 %copy-start.17 = (bf16[64,512]{1,0:T(8,128)(2,1)S(1)}, bf16[64,512]{1,0:T(8,128)(2,1)}, u32[]{:S(2)}) copy-start(bf16[64,512]{1,0:T(8,128)(2,1)} %key_ref.3) | copy-start | bytes 196612
  476.1 75.6 %copy-start.18 = (bf16[64,512]{1,0:T(8,128)(2,1)S(1)}, bf16[64,512]{1,0:T(8,128)(2,1)}, u32[]{:S(2)}) copy-start(bf16[64,512]{1,0:T(8,128)(2,1)} %value_ref.3) | copy-start | bytes 196612
  476.1 75.6 %copy-start.19 = (bf16[64]{0:T(256)(128)(2,1)S(1)}, bf16[64]{0:T(256)(128)(2,1)}, u32[]{:S(2)}) copy-start(bf16[64]{0:T(256)(128)(2,1)} %param.16) | copy-start | bytes 388
  476.1 75.6 %copy-start.20 = (bf16[64]{0:T(256)(128)(2,1)S(1)}, bf16[64]{0:T(256)(128)(2,1)}, u32[]{:S(2)}) copy-start(bf16[64]{0:T(256)(128)(2,1)} %param.17) | copy-start | bytes 388
  551.8 1.6 copy-start.2
  553.4 1.2 copy-start.4
  554.6 1.2 copy-start.6
  555.8 1.2 copy-start.7
  557.0 1.2 copy-start.8
  558.3 1.2 copy-start.9
  559.5 1.2 copy-start.10
  560.7 1.1 copy-start.11
  561.9 1.0 copy-start.13
  562.9 1.0 copy-start.14
  563.9 0.9 copy-start.16

commit v8 on v7

--- a/solution.py
+++ b/solution.py
@@ -58,33 +58,32 @@
 def attention_kernel(block, q_ref, k_ref, v_ref, open_ref, out_ref, lse_ref):
     tile = pl.program_id(0)
     opening = open_ref[...]
-    for head in range(q_ref.shape[1] // HEAD_DIM):
-        lanes = slice(head * HEAD_DIM, (head + 1) * HEAD_DIM)
-        query = q_ref[:, lanes]
-
-        def step(j, carry, lanes=lanes, query=query):
-            peak, total, acc = carry
-            first = pl.multiple_of(j * block, block)
-            scores = dot_t(query, k_ref[pl.ds(first, block), lanes])
-            allowed = allowed_tile(opening, tile * block, first, scores.shape)
+    heads = [
+        slice(i * HEAD_DIM, (i + 1) * HEAD_DIM) for i in range(q_ref.shape[1] // HEAD_DIM)
+    ]
+
+    def step(j, carry):
+        first = pl.multiple_of(j * block, block)
+        allowed = allowed_tile(opening, tile * block, first, (block, block))
+        after = []
+        for lanes, (peak, total, acc) in zip(heads, carry):
+            scores = dot_t(q_ref[:, lanes], k_ref[pl.ds(first, block), lanes])
             scores = jnp.where(allowed, scores, NEG)
             new_peak = jnp.maximum(peak, jnp.max(scores, axis=1, keepdims=True))
             spread = jnp.exp(scores - new_peak)
             fade = jnp.exp(peak - new_peak)
             total = total * fade + jnp.sum(spread, axis=1, keepdims=True)
             acc = acc * fade + dot(spread.astype(BF16), v_ref[pl.ds(first, block), lanes])
-            return new_peak, total, acc
-
-        peak, total, acc = lax.fori_loop(
-            0,
-            tile + 1,
-            step,
-            (
-                jnp.full((block, 1), NEG, F32),
-                jnp.zeros((block, 1), F32),
-                jnp.zeros((block, HEAD_DIM), F32),
-            ),
-        )
+            after.append((new_peak, total, acc))
+        return tuple(after)
+
+    start = (
+        jnp.full((block, 1), NEG, F32),
+        jnp.zeros((block, 1), F32),
+        jnp.zeros((block, HEAD_DIM), F32),
+    )
+    done = lax.fori_loop(0, tile + 1, step, (start,) * len(heads))
+    for head, (lanes, (peak, total, acc)) in enumerate(zip(heads, done)):
         out_ref[:, lanes] = acc / total
         lse_ref[:, head : head + 1] = peak + jnp.log(total)
 
@@ -121,27 +120,32 @@
         dv_ref[...] = jnp.zeros_like(dv_ref)
 
     opening = open_ref[...]
+    heads = []
     for head in range(q_ref.shape[1] // HEAD_DIM):
         lanes = slice(head * HEAD_DIM, (head + 1) * HEAD_DIM)
-        query = q_ref[:, lanes]
-        grad = g_ref[:, lanes]
-        log_total = lse_ref[:, head : head + 1]
-        row_sum = jnp.sum(grad.astype(F32) * att_ref[:, lanes], axis=1, keepdims=True)
-
-        def step(j, acc, lanes=lanes, query=query, grad=grad, log_total=log_total, row_sum=row_sum):
-            first = pl.multiple_of(j * block, block)
-            here = pl.ds(first, block)
-            key = k_ref[here, lanes]
+        grad = g_ref[:, lanes].astype(F32)
+        row_sum = jnp.sum(grad * att_ref[:, lanes], axis=1, keepdims=True)
+        heads.append((lanes, lse_ref[:, head : head + 1], row_sum))
+
+    def step(j, carry):
+        first = pl.multiple_of(j * block, block)
+        here = pl.ds(first, block)
+        allowed = allowed_tile(opening, tile * block, first, (block, block))
+        after = []
+        for (lanes, log_total, row_sum), acc in zip(heads, carry):
+            query, grad, key = q_ref[:, lanes], g_ref[:, lanes], k_ref[here, lanes]
             scores = dot_t(query, key)
-            allowed = allowed_tile(opening, tile * block, first, scores.shape)
             chance = jnp.where(allowed, jnp.exp(scores - log_total), 0.0)
             prob_grad = dot_t(grad, v_ref[here, lanes])
             score_grad = (chance * (prob_grad - row_sum)).astype(BF16)
             dk_ref[here, lanes] += t_dot(score_grad, query)
             dv_ref[here, lanes] += t_dot(chance.astype(BF16), grad)
-            return acc + dot(score_grad, key)
-
-        acc = lax.fori_loop(0, tile + 1, step, jnp.zeros((block, HEAD_DIM), F32))
+            after.append(acc + dot(score_grad, key))
+        return tuple(after)
+
+    start = jnp.zeros((block, HEAD_DIM), F32)
+    done = lax.fori_loop(0, tile + 1, step, (start,) * len(heads))
+    for (lanes, _, _), acc in zip(heads, done):
         dq_ref[:, lanes] = acc
 
 
@@ -219,6 +223,14 @@
         pl.semaphore_wait(barrier, jnp.where(inner, 4, 3) + (1 if partner else 0))
 
     def greet_all(self, meanwhile=nothing):
+        self.call_all()
+        meanwhile()
+        self.await_all()
+
+    def await_all(self):
+        pl.semaphore_wait(pltpu.get_barrier_semaphore(), self.count)
+
+    def call_all(self):
         barrier = pltpu.get_barrier_semaphore()
 
         def signal(device):
@@ -229,9 +241,6 @@
         @pl.loop(1, self.count)
         def _(ahead):
             signal((self.dp, lax.rem(self.mine + ahead, self.count)))
-
-        meanwhile()
-        pl.semaphore_wait(barrier, self.count)
 
 
 def remote(src, dst, send_sem, recv_sem, device):
@@ -555,6 +564,7 @@
     swap_sems,
     local_sems,
     pair_sems,
+    share_sems,
 ):
     here = Place()
     cols = q_ref.shape[1]
@@ -593,8 +603,8 @@
 
         for number in range(blocks.shape[0]):
             blocks[number, :, :cols] = heads(query, number, HEADS // 2)
-            blocks[number, :, cols : 2 * cols] = heads(key, number, KV_HEADS // 2)
-            blocks[number, :, 2 * cols :] = heads(value, number, KV_HEADS // 2)
+            array = value if number % 2 else key
+            blocks[number, :, cols:] = heads(array, number, KV_HEADS // 2)
 
     def own_parts():
         own_blocks()
@@ -700,6 +710,15 @@
             def _(sender):
                 pair_copy(1 - dp, sender).wait_recv()
 
+    def share_copy(ref, number, where):
+        return remote(
+            ref.at[where],
+            ref.at[where],
+            share_sems.at[0, number],
+            share_sems.at[1, number],
+            here.sibling(),
+        )
+
     def stores(number, first):
         made = []
         for block in range(2):
@@ -725,8 +744,13 @@
         sine = sin_ref[where, :]
         scale = BF16(1.0 / math.sqrt(HEAD_DIM))
         q_ref[where, :] = rotated(qkv[:, :cols], cosine, sine).astype(BF16) * scale
-        k_ref[where, :] = rotated(qkv[:, cols : 2 * cols], cosine, sine).astype(BF16)
-        v_ref[where, :] = qkv[:, 2 * cols :].astype(BF16)
+        for core, ref in enumerate((k_ref, v_ref)):
+
+            @pl.when(here.core == core)
+            def _():
+                mine = qkv[:, cols:]
+                ref[where, :] = (mine if core else rotated(mine, cosine, sine)).astype(BF16)
+                share_copy(ref, number, where).start()
 
     far.start()
     near.start()
@@ -740,6 +764,7 @@
     def _(number):
         for one in stores(number, 0):
             one.wait()
+        share_copy(k_ref, number, unit_rows(0, rows)).wait()
 
     feed.finish()
     for one in swaps + own_feed:
@@ -768,7 +793,7 @@
             f32(all_rows, cols),
             f32(all_rows, cols),
             jax.ShapeDtypeStruct((all_rows, 1), jnp.int32),
-            bf16(2, seq, slab, 3 * cols),
+            bf16(2, seq, slab, 2 * cols),
             bf16(slab, ff),
             bf16(slab, ff),
             bf16(seq // 2, slab, 4 * down.shape[0]),
@@ -779,7 +804,7 @@
         out_specs=[HBM] * 2 + [VMEM] * 9 + [HBM] * 3,
         scratch_shapes=gather_scratch(seq, rows, width)
         + [
-            pltpu.VMEM((seq, slab, 3 * cols), BF16),
+            pltpu.VMEM((seq, slab, 2 * cols), BF16),
             dma((seq // 2, 2, 2)),
             dma((2, seq // 2)),
             dma((2, seq // 2)),
@@ -787,9 +812,10 @@
             dma((2, 2)),
             dma((6,)),
             dma((2, seq)),
+            dma((2, seq // 2)),
         ],
         compiler_params=params(call_id, 60),
-        cost_estimate=cost(2 * all_rows * width * 3 * cols, 8 * all_rows * width),
+        cost_estimate=cost(2 * all_rows * width * 2 * cols, 8 * all_rows * width),
     )(lengths, tokens, cotangent, query, key, value, gate, up, *gains, freq, down, output)
 
 
@@ -801,29 +827,36 @@
     open_ref,
     gate_ref,
     up_ref,
+    near_ref,
     out_ref,
     lse_ref,
     feed_ref,
     low_ref,
+    near_out_ref,
     feed_sems,
+    swap_sems,
 ):
     here = Place()
     feed = feed_spread(here, False, (gate_ref, up_ref), feed_ref, feed_sems)
 
+    swap = remote(near_ref, near_out_ref, swap_sems.at[0], swap_sems.at[1], here.partner())
+    pl.when(pl.program_id(0) == 0)(here.call_all)
+    attention_kernel(block, q_ref, k_ref, v_ref, open_ref, out_ref, lse_ref)
+    low_ref[...] = out_ref[...].astype(BF16)
+
     @pl.when(pl.program_id(0) == 0)
     def _():
-        here.greet_all()
+        here.await_all()
         feed.start()
-
-    attention_kernel(block, q_ref, k_ref, v_ref, open_ref, out_ref, lse_ref)
-    low_ref[...] = out_ref[...].astype(BF16)
+        swap.start()
 
     @pl.when(pl.program_id(0) == pl.num_programs(0) - 1)
     def _():
         feed.finish()
-
-
-def attention_feed(queries, keys, values, opening, gate, up, feed_cols, block, call_id):
+        swap.wait()
+
+
+def attention_feed(queries, keys, values, opening, gate, up, near, block, call_id):
     seq = lax.axis_size("seq")
     rows, cols = queries.shape
     heads = cols // HEAD_DIM
@@ -832,18 +865,19 @@
     return pl.pallas_call(
         functools.partial(attention_feed_kernel, block),
         grid=(rows // block,),
-        in_specs=[tiled(cols), whole, whole, tiled(1), HBM, HBM],
-        out_specs=[tiled(cols), tiled(heads), HBM, tiled(cols)],
+        in_specs=[tiled(cols), whole, whole, tiled(1), HBM, HBM, HBM],
+        out_specs=[tiled(cols), tiled(heads), HBM, tiled(cols), HBM],
         out_shape=[
             jax.ShapeDtypeStruct((rows, cols), F32),
             jax.ShapeDtypeStruct((rows, heads), F32),
-            jax.ShapeDtypeStruct((seq // 2, gate.shape[0], feed_cols), BF16),
+            jax.ShapeDtypeStruct(near.shape, BF16),
             jax.ShapeDtypeStruct((rows, cols), BF16),
+            jax.ShapeDtypeStruct(near.shape, BF16),
         ],
-        scratch_shapes=[pltpu.SemaphoreType.DMA((2, seq // 2, 4))],
+        scratch_shapes=[pltpu.SemaphoreType.DMA((2, seq // 2, 4)), pltpu.SemaphoreType.DMA((2,))],
         compiler_params=params(call_id, 60),
         cost_estimate=cost(2 * rows * rows * cols, 10 * rows * cols),
-    )(queries, keys, values, opening, gate, up)
+    )(queries, keys, values, opening, gate, up, near)
 
 
 ROW_CHUNK = 32
@@ -880,7 +914,7 @@
     pair_sems,
     line_sems,
     came_sems,
-    early=None,
+    first=None,
     between=nothing,
     filler=None,
 ):
@@ -958,6 +992,8 @@
 
     @pl.loop(0, steps)
     def _(step):
+        if first is not None:
+            first(step)
         pl.when(step < steps - 1)(lambda: for_sibling(step + 1, 1 - here.pair, step + 1))
         core_copy(step).wait_recv()
 
@@ -966,8 +1002,6 @@
 
         product(target(step // parts), 1 - here.pair, here.core, step % parts, use)
         pair_copy(step).start()
-        if early is not None:
-            early(step)
 
     for_sibling(jnp.int32(0), here.pair, jnp.int32(steps))
     between()
@@ -1055,10 +1089,10 @@
 
 
 def scatter_both_kernel(
-    back_ref,
-    turned_ref,
-    hidden_ref,
-    down_ref,
+    back_hbm,
+    turned_hbm,
+    hidden_hbm,
+    down_hbm,
     middle_ref,
     grads_hbm,
     normed_hbm,
@@ -1069,13 +1103,30 @@
     *scratch,
 ):
     here = Place()
-    normed, away, came, own, fetch_sems, swap_sems, own_sem = scratch[SCATTER_SCRATCH:]
+    factors = scratch[SCATTER_SCRATCH : SCATTER_SCRATCH + 4]
+    back_ref, turned_ref, hidden_ref, down_ref = factors
+    normed, away, came, own, fetch_sems, swap_sems, own_sems = scratch[SCATTER_SCRATCH + 4 :]
     rows = grad_ref.shape[0]
+    loads = [
+        pltpu.make_async_copy(src, dst, own_sems.at[number])
+        for number, (src, dst) in enumerate(
+            zip((back_hbm, turned_hbm, hidden_hbm, down_hbm), factors)
+        )
+    ]
     own_copy = pltpu.make_async_copy(
-        grads_hbm.at[pl.ds(pl.multiple_of(here.mine * rows, rows), rows)], own, own_sem.at[0]
-    )
-    own_copy.start()
+        grads_hbm.at[pl.ds(pl.multiple_of(here.mine * rows, rows), rows)], own, own_sems.at[4]
+    )
+    for one in loads + [own_copy]:
+        one.start()
     here.greet(partner=True)
+    for one in loads[:2]:
+        one.wait()
+
+    def first(step):
+        @pl.when(step == SCATTER_PARTS - 1)
+        def _():
+            for one in loads[2:]:
+                one.wait()
     chunk = normed.shape[2]
     half = normed_hbm.shape[1] // 2
     chunks = half // chunk
@@ -1120,6 +1171,7 @@
         here,
         [(False, back_ref, turned_ref, grad_ref), (False, hidden_ref, down_ref, mixed_ref)],
         *scratch[:SCATTER_SCRATCH],
+        first=first,
         filler=filler,
     )
     own_copy.wait()
@@ -1147,9 +1199,10 @@
             jax.ShapeDtypeStruct((rows, width), F32),
             jax.ShapeDtypeStruct((width // 2, cols), BF16),
         ],
-        in_specs=[VMEM] * 5 + [HBM] * 2,
+        in_specs=[HBM] * 4 + [VMEM] + [HBM] * 2,
         out_specs=[VMEM] * 4,
         scratch_shapes=scatter_scratch(seq, rows, width, 2)
+        + [pltpu.VMEM(array.shape, BF16) for array in (back, turned, hidden, down)]
         + [
             pltpu.VMEM((2, normed.shape[0], chunk), BF16),
             pltpu.VMEM((width // 2, cols), BF16),
@@ -1157,7 +1210,7 @@
             pltpu.VMEM((rows, width), BF16),
             dma((2,)),
             dma((2, 4)),
-            dma((1,)),
+            dma((5,)),
         ],
         compiler_params=params(call_id, 60),
         cost_estimate=scatter_cost(back, 3 * width),
@@ -1165,31 +1218,42 @@
 
 
 def scatter_feed_kernel(
-    a_ref, b_ref, tokens_ref, near_ref, far_ref, middle_ref, normed_ref, feed_ref, *scratch
+    a_ref,
+    b_ref,
+    tokens_ref,
+    near_hbm,
+    other_hbm,
+    far_hbm,
+    middle_ref,
+    normed_ref,
+    feed_ref,
+    *scratch,
 ):
     here = Place()
     here.greet(partner=True)
     swap_sems, local_sems = scratch[SCATTER_SCRATCH:]
-    slots = near_ref.shape[0]
-
-    def copies(half, ref, slot):
-        place = feed_ref.at[here.dp, here.peer(slot, half == 0)]
-        return (
-            remote(
-                ref.at[slot],
-                place,
-                swap_sems.at[0, half, slot],
-                swap_sems.at[1, half, slot],
-                here.partner(),
-            ),
-            pltpu.make_async_copy(ref.at[slot], place, local_sems.at[half, slot]),
+    slots = near_hbm.shape[0]
+
+    def fetch(kind, slot):
+        ref = (near_hbm, other_hbm, far_hbm)[kind]
+        dp = 1 - here.dp if kind == 1 else here.dp
+        return pltpu.make_async_copy(
+            ref.at[slot], feed_ref.at[dp, here.peer(slot, kind < 2)], local_sems.at[kind, slot]
         )
+
+    def swap(slot):
+        place = feed_ref.at[here.dp, here.peer(slot, False)]
+        return remote(
+            place, place, swap_sems.at[0, slot], swap_sems.at[1, slot], here.partner()
+        )
+
+    for kind in (2, 0, 1):
+        pl.loop(0, slots)(lambda slot, kind=kind: fetch(kind, slot).start())
 
     @pl.loop(0, slots)
     def _(slot):
-        for half, ref in enumerate((near_ref, far_ref)):
-            for one in copies(half, ref, slot):
-                one.start()
+        fetch(2, slot).wait()
+        swap(slot).start()
 
     scatter_rows_of_products(
         here, [(False, a_ref, b_ref, middle_ref)], *scratch[:SCATTER_SCRATCH]
@@ -1204,12 +1268,12 @@
 
     @pl.loop(0, slots)
     def _(slot):
-        for half, ref in enumerate((near_ref, far_ref)):
-            for one in copies(half, ref, slot):
-                one.wait()
-
-
-def product_scatter_feed(a, b, tokens, near, far, call_id):
+        swap(slot).wait()
+        for kind in range(2):
+            fetch(kind, slot).wait()
+
+
+def product_scatter_feed(a, b, tokens, near, other, far, call_id):
     seq = lax.axis_size("seq")
     rows = a.shape[0] // seq
     width = b.shape[1]
@@ -1221,13 +1285,13 @@
             jax.ShapeDtypeStruct((rows, width), BF16),
             jax.ShapeDtypeStruct((2, seq, *near.shape[1:]), BF16),
         ],
-        in_specs=[VMEM, VMEM, VMEM, HBM, HBM],
-        out_specs=[VMEM, VMEM, HBM],
+        in_specs=[VMEM, VMEM, VMEM, HBM, HBM, HBM],
+        out_specs=[VMEM, VMEM, VMEM],
         scratch_shapes=scatter_scratch(seq, rows, width)
-        + [dma((2, 2, seq // 2)), dma((2, seq // 2))],
-        compiler_params=params(call_id, 40),
+        + [dma((2, seq // 2)), dma((3, seq // 2))],
+        compiler_params=params(call_id, 60),
         cost_estimate=scatter_cost(a, width),
-    )(a, b, tokens, near, far)
+    )(a, b, tokens, near, other, far)
 
 
 def feed_kernel(
@@ -1486,8 +1550,11 @@
     dq_ref,
     dk_ref,
     dv_ref,
+    share_out,
+    share_in,
     feed_sems,
     swap_sems,
+    share_sems,
 ):
     here = Place()
     tile = pl.program_id(0)
@@ -1500,30 +1567,52 @@
         )
     ]
 
+    pl.when(tile == 0)(here.call_all)
+    attention_back_kernel(
+        block, q_ref, k_ref, v_ref, g_ref, att_ref, lse_ref, open_ref, dq_ref, dk_ref, dv_ref
+    )
+
     @pl.when(tile == 0)
     def _():
-        here.greet_all()
+        here.await_all()
         feed.start()
         for one in swaps:
             one.start()
 
-    attention_back_kernel(
-        block, q_ref, k_ref, v_ref, g_ref, att_ref, lse_ref, open_ref, dq_ref, dk_ref, dv_ref
-    )
     where = pl.ds(pl.multiple_of(tile * block, block), block)
     scale = 1.0 / math.sqrt(HEAD_DIM)
     cosine = cos_ref[where, :]
     sine = sin_ref[where, :]
     back_ref[where, :cols] = rotated(dq_ref[...] * scale, cosine, -sine).astype(BF16)
 
+    def share(i):
+        rows = pl.ds(pl.multiple_of(i * block, block), block)
+        return remote(
+            share_out.at[rows],
+            share_in.at[rows],
+            share_sems.at[0, i],
+            share_sems.at[1, i],
+            here.sibling(),
+        )
+
     @pl.when(tile == pl.num_programs(0) - 1)
     def _():
         @pl.loop(0, pl.num_programs(0))
         def _(i):
             rows = pl.ds(pl.multiple_of(i * block, block), block)
-            keys = rotated(dk_ref[rows, :], cos_ref[rows, :], -sin_ref[rows, :])
-            back_ref[rows, cols : 2 * cols] = keys.astype(BF16)
-            back_ref[rows, 2 * cols :] = dv_ref[rows, :].astype(BF16)
+            away = jnp.where(here.core == 0, dv_ref[rows, :], dk_ref[rows, :])
+            share_out[rows, :] = away.astype(BF16)
+            share(i).start()
+
+        @pl.loop(0, pl.num_programs(0))
+        def _(i):
+            rows = pl.ds(pl.multiple_of(i * block, block), block)
+            share(i).wait()
+            came = share_in[rows, :].astype(F32)
+            keys = rotated(dk_ref[rows, :] + came, cos_ref[rows, :], -sin_ref[rows, :])
+            back_ref[rows, cols:] = jnp.where(here.core == 0, keys, dv_ref[rows, :] + came).astype(
+                BF16
+            )
 
         feed.finish()
         for one in swaps:
@@ -1557,9 +1646,9 @@
         grid=(rows // block,),
         in_specs=[tiled(cols), whole, whole, tiled(cols), tiled(cols), tiled(heads), tiled(1)]
         + [whole, whole, HBM, HBM, HBM],
-        out_specs=[pl.BlockSpec((rows, 3 * cols), lambda i: (0, 0)), HBM, HBM, HBM],
+        out_specs=[pl.BlockSpec((rows, 2 * cols), lambda i: (0, 0)), HBM, HBM, HBM],
         out_shape=[
-            jax.ShapeDtypeStruct((rows, 3 * cols), BF16),
+            jax.ShapeDtypeStruct((rows, 2 * cols), BF16),
             jax.ShapeDtypeStruct((seq // 2, *blocks.shape[1:]), BF16),
             jax.ShapeDtypeStruct(down.shape, BF16),
             jax.ShapeDtypeStruct(output.shape, BF16),
@@ -1568,8 +1657,11 @@
             pltpu.VMEM((block, cols), F32),
             pltpu.VMEM((rows, cols), F32),
             pltpu.VMEM((rows, cols), F32),
+            pltpu.VMEM((rows, cols), BF16),
+            pltpu.VMEM((rows, cols), BF16),
             dma((2, seq // 2)),
             dma((2, 2)),
+            dma((2, rows // block)),
         ],
         compiler_params=params(call_id, 60),
         cost_estimate=cost(5 * rows * rows * cols, 20 * rows * cols),
@@ -1596,7 +1688,6 @@
     ]
     fetch = pltpu.make_async_copy(normed_hbm, normed_ref, fetch_sems.at[0])
     fetch.start()
-    here.greet_all()
     swap = remote(away, came, swap_sems.at[0], swap_sems.at[1], here.partner())
     near = block_spread(here, True, sums, qkv_ref.at[0], near_sems)
     far = block_spread(here, False, sums, qkv_ref.at[1], far_sems)
@@ -1607,17 +1698,16 @@
         first = pl.multiple_of(dp * half + i * chunk, chunk)
         return t_dot(normed_ref[:, pl.ds(first, chunk)], a_ref[...])
 
-    def early(step):
-        @pl.when(step == 1)
-        def _():
-            fetch.wait()
-
-            @pl.loop(0, half // chunk)
-            def _(i):
-                some = pl.ds(pl.multiple_of(i * chunk, chunk), chunk)
-                away[some, :] = part(1 - here.dp, i).astype(BF16)
-
-            swap.start()
+    def meanwhile():
+        fetch.wait()
+
+        @pl.loop(0, half // chunk)
+        def _(i):
+            some = pl.ds(pl.multiple_of(i * chunk, chunk), chunk)
+            away[some, :] = part(1 - here.dp, i).astype(BF16)
+
+    here.greet_all(meanwhile)
+    swap.start()
 
     def between():
         @pl.loop(0, half // chunk)
@@ -1655,9 +1745,8 @@
         here,
         [(True, a_ref, b_ref, out_ref)],
         *scratch[:SCATTER_SCRATCH],
-        early,
-        between,
-        filler,
+        between=between,
+        filler=filler,
     )
     swap.wait_send()
     near.finish()
@@ -1759,7 +1848,7 @@
                 slot = line * 2 + number % 2
                 near, far = qkv_ref[0, slot].astype(F32), qkv_ref[1, slot].astype(F32)
                 rows.append(jnp.where(number // 2 == pair, near, far))
-            kv = rows[0] + rows[1] + rows[2] + rows[3]
+            kv = [rows[core] + rows[core + 2] for core in range(2)]
             for half in range(dp):
                 cols = slice(half * HEAD_DIM, (half + 1) * HEAD_DIM)
                 for number in (0, 2):
@@ -1767,8 +1856,8 @@
                     begin = (half * length * 4 + line * 4 + number) * HEAD_DIM
                     total = total + put(query_out_ref, query_ref, begin, two)
                 for kind in range(2):
-                    begin = ((kind + 1) * dp + half) * HEAD_DIM
-                    pairs[kind][half, line] = kv[:, begin : begin + HEAD_DIM]
+                    begin = (dp + half) * HEAD_DIM
+                    pairs[kind][half, line] = kv[kind][:, begin : begin + HEAD_DIM]
         for kind, (out_ref, weight_ref) in enumerate(
             [(key_out_ref, key_ref), (value_out_ref, value_ref)]
         ):
@@ -1835,7 +1924,7 @@
         + [strip(array) for array in sums],
         out_shape=outs + sums,
         scratch_shapes=[pltpu.VMEM((slab, 1), F32)],
-        compiler_params=pltpu.CompilerParams(vmem_limit_bytes=40 << 20),
+        compiler_params=pltpu.CompilerParams(vmem_limit_bytes=60 << 20),
         cost_estimate=cost(slab * ff, 16 * slab * ff),
     )(
         pair,
@@ -2132,19 +2221,19 @@
     qkv_weight = qkv_weight.reshape(width, -1)
     down_own = down_own.reshape(-1, width)
     output_own = output_own.reshape(-1, width)
-    attended_sum, log_total, feed_far, attended = attention_feed(
+    attended_sum, log_total, feed_far, attended, feed_other = attention_feed(
         queries,
         keys,
         values,
         opening,
         gate_scaled,
         up_scaled,
-        feed_near.shape[2],
+        feed_near,
         block,
         1,
     )
     middle, middle_normed, feed_weight = product_scatter_feed(
-        attended, output_own, tokens, feed_near, feed_far, 2
+        attended, output_own, tokens, feed_near, feed_other, feed_far, 2
     )
     feed_weight = feed_weight.reshape(width, -1)
 

time: 574 us -> 551 us (0.960)
  local copies, waits for them, and re-layouts: 19.2 us -> 0 us
    unnamed x54 -> x0, local copies, waits for them, and re-layouts: 19.2 us -> none
    pallas_call x1, Pallas kernels: 75.5 us -> 68.9 us  [product_scatter_last(): pl.pallas_call(scatter_last_kernel, out_shape=[jax.ShapeDtypeStruct((rows...]
where the time goes in v8:
time: 551 us; the launch traced here: 550 us
  Pallas kernels  549 us (100%)
    pallas_call x1, Pallas kernels, gather_project(): pl.pallas_call(project_kernel, out_shape=[bf16(all_rows, width), bf16(all...  115 us
    pallas_call x1, Pallas kernels, product_scatter_both(): pl.pallas_call(scatter_both_kernel, out_shape=[jax.ShapeDtypeStruct((rows...  110 us
    pallas_call x1, Pallas kernels, product_scatter_last(): pl.pallas_call(scatter_last_kernel, out_shape=[jax.ShapeDtypeStruct((rows...  68.9 us
    pallas_call x1, Pallas kernels, gather_back(): pl.pallas_call(back_kernel, out_shape=[jax.ShapeDtypeStruct((seq * rows,...  60.8 us
    pallas_call x1, Pallas kernels, product_scatter_feed(): pl.pallas_call(scatter_feed_kernel, out_shape=[jax.ShapeDtypeStruct((rows...  57.8 us
    pallas_call x1, Pallas kernels, gather_feed(): pl.pallas_call(feed_kernel, out_shape=[jax.ShapeDtypeStruct((seq * rows,...  53.6 us
    pallas_call x1, Pallas kernels, attention_back_feed(): pl.pallas_call(functools.partial(attention_back_feed_kernel, block), grid...  38.3 us
    pallas_call x1, Pallas kernels, attention_feed(): pl.pallas_call(functools.partial(attention_feed_kernel, block), grid=(row...  32.3 us

profile of v8, /device:TPU:0, one launch (start us, length us, event | category | flops | bytes accessed | tf_op | source)
XLA Modules:
  0.0 550.2 jit_solution(10476839853559569701)
XLA Ops:
  0.6 114.7 %shard_map.212 = (bf16[2048,2048]{1,0:T(8,128)(2,1)}, bf16[2048,2048]{1,0:T(8,128)(2,1)}, bf16[2048,128]{1,0:T(8,128)(2,1)}, bf16[2048,128]{1,0:T(8,128)(2,1)}, ...) custom-call(s32[1,4]{1,0:T(1,128)} %lengths_ref.1, ...), custom_call_target="tpu_custom_call" | custom-call | flops 2147483648 | bytes 33554432 | tf_op jit(solution)/shard_map/pallas_call | solution.py:785
  115.3 32.3 %shard_map.213 = (f32[2048,128]{1,0:T(8,128)}, f32[2048,2]{1,0:T(8,128)}, bf16[8,64,1024]{2,1,0:T(8,128)(2,1)}, bf16[2048,128]{1,0:T(8,128)(2,1)}, bf16[8,64,1024]{2,1,0:T(8,128)(2,1)}) custom-call(bf16[2048,128]{1,0:T(8,128)(2,1)} %get-tuple-element.64.q_ref, bf16[2048,128]{1,0:T(8,128)(2,1)} %get-tuple-element.65.k_ref, ...), custom_call_target="tpu_custom_call" | custom-call | flops 1073741824 | bytes 2621440 | tf_op jit(solution)/shard_map/pallas_call | solution.py:865
  147.7 57.8 %shard_map.214 = (f32[128,2048]{1,0:T(8,128)}, bf16[128,2048]{1,0:T(8,128)(2,1)}, bf16[2,16,64,1024]{3,2,1,0:T(8,128)(2,1)}) custom-call(bf16[2048,128]{1,0:T(8,128)(2,1)} %get-tuple-element.71.a_ref.attended_ref, bf16[128,2048]{1,0:T(8,128)(2,1)} %bitcast.13, bf16[128,2048]{1,0:T(8,128)(2,1)} %tokens_ref.5, ...), custom_call_target="tpu_custom_call" | custom-call | flops 1073741824 | bytes 16777216 | tf_op jit(solution)/shard_map/pallas_call | solution.py:1281
  205.4 53.6 %shard_map.215 = (bf16[2048,2048]{1,0:T(8,128)(2,1)}, bf16[2048,512]{1,0:T(8,128)(2,1)}, bf16[2048,1024]{1,0:T(8,128)(2,1)}, bf16[1024,2048]{1,0:T(8,128)(2,1)}) custom-call(bf16[128,2048]{1,0:T(8,128)(2,1)} %get-tuple-element.75.own_ref, bf16[2048,2048]{1,0:T(8,128)(2,1)} %get-tuple-element.76.grad_hbm.grads_hbm.out_grad_hbm, bf16[2048,1024]{1,0:T(8,128)(2,1)} %bitcast.19, ...), custom_call_target="tpu_custom_call" | custom-call | flops 17179869184 | bytes 33554432 | tf_op jit(solution)/shard_map/pallas_call | solution.py:1398
  259.1 109.6 %shard_map.216 = (f32[128,2048]{1,0:T(8,128)}, bf16[128,2048]{1,0:T(8,128)(2,1)}, f32[128,2048]{1,0:T(8,128)}, bf16[1024,1024]{1,0:T(8,128)(2,1)}) custom-call(bf16[2048,1024]{1,0:T(8,128)(2,1)} %get-tuple-element.79.back_hbm, bf16[1024,2048]{1,0:T(8,128)(2,1)} %get-tuple-element.80.turned_hbm, bf16[2048,512]{1,0:T(8,128)(2,1)} %get-tuple-element.81.hidden_hbm, ...), custom_call_target="tpu_custom_call" | custom-call | flops 25769803776 | bytes 50331648 | tf_op jit(solution)/shard_map/pallas_call | solution.py:1194
  368.6 60.8 %shard_map.217 = (bf16[2048,128]{1,0:T(8,128)(2,1)}, f32[64,2048]{1,0:T(8,128)}, bf16[64,2048]{1,0:T(8,128)(2,1)}, f32[256,2048]{1,0:T(8,128)}, bf16[256,2048]{1,0:T(8,128)(2,1)}, /*index=5*/bf16[8,64,1024]{2,1,0:T(8,128)(2,1)}) custom-call(bf16[128,2048]{1,0:T(8,128)(2,1)} %get-tuple-element.84.own_ref, bf16[128,2048]{1,0:T(8,128)(2,1)} %bitcast.14, ...), custom_call_target="tpu_custom_call" | custom-call | flops 4294967296 | bytes 25165824 | tf_op jit(solution)/shard_map/pallas_call | solution.py:1506
  429.5 38.3 %shard_map.218 = (bf16[2048,256]{1,0:T(8,128)(2,1)}, bf16[8,64,1024]{2,1,0:T(8,128)(2,1)}, bf16[256,2048]{1,0:T(8,128)(2,1)}, bf16[64,2048]{1,0:T(8,128)(2,1)}) custom-call(bf16[2048,128]{1,0:T(8,128)(2,1)} %get-tuple-element.64.q_ref, bf16[2048,128]{1,0:T(8,128)(2,1)} %get-tuple-element.65.k_ref, bf16[2048,128]{1,0:T(8,128)(2,1)} %get-tuple-element.66.v_ref, ...), custom_call_target="tpu_custom_call" | custom-call | flops 2684354560 | bytes 5242880 | tf_op jit(solution)/shard_map/pallas_call | solution.py:1644
  467.8 68.9 %shard_map.219 = (f32[128,2048]{1,0:T(8,128)}, bf16[2,8,64,256]{3,2,1,0:T(8,128)(2,1)}) custom-call(bf16[2048,256]{1,0:T(8,128)(2,1)} %get-tuple-element.95.a_ref, bf16[2048,256]{1,0:T(8,128)(2,1)} %bitcast.12, bf16[2048,2048]{1,0:T(8,128)(2,1)} %get-tuple-element.97.normed_hbm), custom_call_target="tpu_custom_call" | custom-call | flops 2147483648 | bytes 16777216 | tf_op jit(solution)/shard_map/pallas_call | solution.py:1762
  536.7 13.3 %shard_map.220 = (f32[64,8192]{1,0:T(8,128)}, f32[64,8192]{1,0:T(8,128)}, f32[64,2048]{1,0:T(8,128)}, f32[64,512]{1,0:T(8,128)}, f32[64,512]{1,0:T(8,128)}, /*in...) custom-call(s32[1]{0:T(128)} %bitcast.pair_ref, ...), custom_call_target="tpu_custom_call" | custom-call | flops 524288 | bytes 8388608 | tf_op jit(solution)/shard_map/pallas_call | solution.py:1915

commit v9 on v8

--- a/solution.py
+++ b/solution.py
@@ -55,8 +55,9 @@
     return (cols <= rows) & (cols >= opening)
 
 
-def attention_kernel(block, q_ref, k_ref, v_ref, open_ref, out_ref, lse_ref):
-    tile = pl.program_id(0)
+def attention_kernel(block, q_ref, k_ref, v_ref, open_ref, out_ref, lse_ref, tile=None):
+    if tile is None:
+        tile = pl.program_id(0)
     opening = open_ref[...]
     heads = [
         slice(i * HEAD_DIM, (i + 1) * HEAD_DIM) for i in range(q_ref.shape[1] // HEAD_DIM)
@@ -676,6 +677,8 @@
             sin_ref[some, :] = jnp.where(lane % HEAD_DIM < HEAD_DIM // 2, -sine, sine)
 
     def started():
+        far.start()
+        near.start()
         weight_ref[dp, here.mine] = blocks[here.mine]
         for one in swaps:
             one.start()
@@ -752,8 +755,6 @@
                 ref[where, :] = (mine if core else rotated(mine, cosine, sine)).astype(BF16)
                 share_copy(ref, number, where).start()
 
-    far.start()
-    near.start()
     gather_units(here, buf, send_sems, recv_sems, compute, between, here.length, started)
 
     @pl.loop(0, here.count)
@@ -819,67 +820,6 @@
     )(lengths, tokens, cotangent, query, key, value, gate, up, *gains, freq, down, output)
 
 
-def attention_feed_kernel(
-    block,
-    q_ref,
-    k_ref,
-    v_ref,
-    open_ref,
-    gate_ref,
-    up_ref,
-    near_ref,
-    out_ref,
-    lse_ref,
-    feed_ref,
-    low_ref,
-    near_out_ref,
-    feed_sems,
-    swap_sems,
-):
-    here = Place()
-    feed = feed_spread(here, False, (gate_ref, up_ref), feed_ref, feed_sems)
-
-    swap = remote(near_ref, near_out_ref, swap_sems.at[0], swap_sems.at[1], here.partner())
-    pl.when(pl.program_id(0) == 0)(here.call_all)
-    attention_kernel(block, q_ref, k_ref, v_ref, open_ref, out_ref, lse_ref)
-    low_ref[...] = out_ref[...].astype(BF16)
-
-    @pl.when(pl.program_id(0) == 0)
-    def _():
-        here.await_all()
-        feed.start()
-        swap.start()
-
-    @pl.when(pl.program_id(0) == pl.num_programs(0) - 1)
-    def _():
-        feed.finish()
-        swap.wait()
-
-
-def attention_feed(queries, keys, values, opening, gate, up, near, block, call_id):
-    seq = lax.axis_size("seq")
-    rows, cols = queries.shape
-    heads = cols // HEAD_DIM
-    tiled = lambda width: pl.BlockSpec((block, width), lambda i: (i, 0))
-    whole = pl.BlockSpec((rows, cols), lambda i: (0, 0))
-    return pl.pallas_call(
-        functools.partial(attention_feed_kernel, block),
-        grid=(rows // block,),
-        in_specs=[tiled(cols), whole, whole, tiled(1), HBM, HBM, HBM],
-        out_specs=[tiled(cols), tiled(heads), HBM, tiled(cols), HBM],
-        out_shape=[
-            jax.ShapeDtypeStruct((rows, cols), F32),
-            jax.ShapeDtypeStruct((rows, heads), F32),
-            jax.ShapeDtypeStruct(near.shape, BF16),
-            jax.ShapeDtypeStruct((rows, cols), BF16),
-            jax.ShapeDtypeStruct(near.shape, BF16),
-        ],
-        scratch_shapes=[pltpu.SemaphoreType.DMA((2, seq // 2, 4)), pltpu.SemaphoreType.DMA((2,))],
-        compiler_params=params(call_id, 60),
-        cost_estimate=cost(2 * rows * rows * cols, 10 * rows * cols),
-    )(queries, keys, values, opening, gate, up, near)
-
-
 ROW_CHUNK = 32
 
 
@@ -1217,125 +1157,158 @@
     )(back, turned, hidden, down, middle, grads, normed)
 
 
-def scatter_feed_kernel(
-    a_ref,
+def feed_kernel(
+    block,
+    q_ref,
+    k_ref,
+    v_ref,
+    open_ref,
     b_ref,
     tokens_ref,
+    gate_hbm,
+    up_hbm,
     near_hbm,
-    other_hbm,
-    far_hbm,
+    grad_hbm,
+    down_hbm,
+    attended_ref,
+    lse_ref,
+    a_ref,
     middle_ref,
-    normed_ref,
-    feed_ref,
-    *scratch,
-):
-    here = Place()
-    here.greet(partner=True)
-    swap_sems, local_sems = scratch[SCATTER_SCRATCH:]
-    slots = near_hbm.shape[0]
-
-    def fetch(kind, slot):
-        ref = (near_hbm, other_hbm, far_hbm)[kind]
-        dp = 1 - here.dp if kind == 1 else here.dp
-        return pltpu.make_async_copy(
-            ref.at[slot], feed_ref.at[dp, here.peer(slot, kind < 2)], local_sems.at[kind, slot]
-        )
-
-    def swap(slot):
-        place = feed_ref.at[here.dp, here.peer(slot, False)]
-        return remote(
-            place, place, swap_sems.at[0, slot], swap_sems.at[1, slot], here.partner()
-        )
-
-    for kind in (2, 0, 1):
-        pl.loop(0, slots)(lambda slot, kind=kind: fetch(kind, slot).start())
-
-    @pl.loop(0, slots)
-    def _(slot):
-        fetch(2, slot).wait()
-        swap(slot).start()
-
-    scatter_rows_of_products(
-        here, [(False, a_ref, b_ref, middle_ref)], *scratch[:SCATTER_SCRATCH]
-    )
-
-    def add(some):
-        middle = tokens_ref[some, :].astype(F32) + middle_ref[some, :]
-        middle_ref[some, :] = middle
-        normed_ref[some, :] = (middle * norm_factor(middle)).astype(BF16)
-
-    in_row_chunks(middle_ref.shape[0], ROW_CHUNK, add)
-
-    @pl.loop(0, slots)
-    def _(slot):
-        swap(slot).wait()
-        for kind in range(2):
-            fetch(kind, slot).wait()
-
-
-def product_scatter_feed(a, b, tokens, near, other, far, call_id):
-    seq = lax.axis_size("seq")
-    rows = a.shape[0] // seq
-    width = b.shape[1]
-    dma = pltpu.SemaphoreType.DMA
-    return pl.pallas_call(
-        scatter_feed_kernel,
-        out_shape=[
-            jax.ShapeDtypeStruct((rows, width), F32),
-            jax.ShapeDtypeStruct((rows, width), BF16),
-            jax.ShapeDtypeStruct((2, seq, *near.shape[1:]), BF16),
-        ],
-        in_specs=[VMEM, VMEM, VMEM, HBM, HBM, HBM],
-        out_specs=[VMEM, VMEM, VMEM],
-        scratch_shapes=scatter_scratch(seq, rows, width)
-        + [dma((2, seq // 2)), dma((3, seq // 2))],
-        compiler_params=params(call_id, 60),
-        cost_estimate=scatter_cost(a, width),
-    )(a, b, tokens, near, other, far)
-
-
-def feed_kernel(
-    own_ref,
-    grad_hbm,
-    feed_hbm,
-    down_hbm,
     normed_ref,
     hidden_out_ref,
     back_out_ref,
     turned_out_ref,
-    buf,
-    send_sems,
-    recv_sems,
-    store_sems,
-    grad_ref,
-    feed_ref,
-    down_ref,
-    hidden_ref,
-    back_ref,
-    turned_ref,
-    fetch_sems,
-    out_sems,
+    *scratch,
 ):
     here = Place()
+    (
+        feed_ref,
+        swap_sems,
+        local_sems,
+        far_sems,
+        buf,
+        send_sems,
+        recv_sems,
+        store_sems,
+        grad_ref,
+        down_ref,
+        hidden_ref,
+        back_ref,
+        turned_ref,
+        fetch_sems,
+        out_sems,
+    ) = scratch[SCATTER_SCRATCH:]
+    slots, slab = near_hbm.shape[:2]
+    rows, width = middle_ref.shape
+    hidden = hidden_ref.shape[1]
+    tile = 256
+
+    def fetch(slot):
+        return pltpu.make_async_copy(
+            near_hbm.at[slot], feed_ref.at[here.dp, here.peer(slot, True)], local_sems.at[slot]
+        )
+
+    def swap(slot, same):
+        place = feed_ref.at[here.dp, here.peer(slot, same)]
+        half = 0 if same else 1
+        return remote(
+            place,
+            place,
+            swap_sems.at[0, half, slot],
+            swap_sems.at[1, half, slot],
+            here.partner(),
+        )
+
+    columns = hidden // 2
+
+    def far_copies(peer, sender, at, sem):
+        made = []
+        for kind, weight in enumerate((gate_hbm, up_hbm)):
+            for half in range(2):
+                part = kind * 2 + half
+                begin = pl.multiple_of((half * here.count + peer) * columns, columns)
+                made.append(
+                    remote(
+                        weight.at[:, pl.ds(begin, columns)],
+                        feed_ref.at[here.dp, sender, :, pl.ds(part * columns, columns)],
+                        far_sems.at[0, sem, part],
+                        far_sems.at[1, at, part],
+                        (here.dp, peer),
+                    )
+                )
+        return made
+
+    far = Spread(here, False, far_copies)
+
     fetches = [
-        pltpu.make_async_copy(src, dst, fetch_sems.at[number])
-        for number, (src, dst) in enumerate(
-            [(feed_hbm, feed_ref), (down_hbm, down_ref), (grad_hbm, grad_ref)]
-        )
+        pltpu.make_async_copy(down_hbm, down_ref, fetch_sems.at[0]),
+        pltpu.make_async_copy(grad_hbm, grad_ref, fetch_sems.at[1]),
     ]
+    pl.loop(0, slots)(lambda slot: fetch(slot).start())
     for one in fetches:
         one.start()
-    put_own(here, own_ref, buf)
-    here.greet()
-    rows = own_ref.shape[0]
-    width = own_ref.shape[1]
-    hidden = hidden_ref.shape[1]
-    tile = 256
+    here.call_all()
+
+    @pl.loop(0, a_ref.shape[0] // block)
+    def _(tile):
+        some = pl.ds(pl.multiple_of(tile * block, block), block)
+        attention_kernel(
+            block,
+            q_ref.at[some],
+            k_ref,
+            v_ref,
+            open_ref.at[some],
+            attended_ref.at[some],
+            lse_ref.at[some],
+            tile,
+        )
+        a_ref[some, :] = attended_ref[some, :].astype(BF16)
+
+        @pl.when(tile == 0)
+        def _():
+            here.await_all()
+            far.start()
+
+            @pl.loop(0, slots)
+            def _(slot):
+                fetch(slot).wait()
+                swap(slot, True).start()
+
+    def between():
+        far.finish()
+        pl.loop(0, slots)(lambda slot: swap(slot, False).start())
+
+    scatter_rows_of_products(
+        here,
+        [(False, a_ref, b_ref, middle_ref)],
+        *scratch[:SCATTER_SCRATCH],
+        between=between,
+    )
+    half = buf.shape[2]
+    for part in range(2):
+
+        @pl.loop(0, half // ROW_CHUNK)
+        def _(i, part=part):
+            into = pl.ds(pl.multiple_of(i * ROW_CHUNK, ROW_CHUNK), ROW_CHUNK)
+            some = pl.ds(pl.multiple_of(part * half + i * ROW_CHUNK, ROW_CHUNK), ROW_CHUNK)
+            middle = tokens_ref[some, :].astype(F32) + middle_ref[some, :]
+            middle_ref[some, :] = middle
+            buf[here.mine, part, into, :] = (middle * norm_factor(middle)).astype(BF16)
+
+    def started():
+        @pl.loop(0, slots)
+        def _(slot):
+            swap(slot, True).wait()
+            swap(slot, False).wait()
+
+        for one in fetches:
+            one.wait()
+
     store = UnitStore(buf, normed_ref, store_sems)
+    share = width // (2 * here.length)
 
     def outs(number, first):
         where = unit_rows(first, rows)
-        share = width // (2 * here.length)
         some = pl.ds(pl.multiple_of(number * share, share), share)
         return [
             pltpu.make_async_copy(src, dst, out_sems.at[number, i])
@@ -1350,12 +1323,6 @@
 
     def compute(number, first):
         store.start(number, first)
-
-        @pl.when(number == 0)
-        def _():
-            for one in fetches:
-                one.wait()
-
         where = unit_rows(first, rows)
         normed = take_unit(buf, first)
         grad = grad_ref[where, :]
@@ -1364,8 +1331,8 @@
         def _(t):
             cols = pl.ds(pl.multiple_of(t * tile, tile), tile)
             later = pl.ds(pl.multiple_of(hidden + t * tile, tile), tile)
-            gate = dot(normed, feed_ref[:, cols])
-            upward = dot(normed, feed_ref[:, later])
+            gate = dot(normed, feed_ref[:, :, :, cols].reshape(width, tile))
+            upward = dot(normed, feed_ref[:, :, :, later].reshape(width, tile))
             hidden_grad = dot_t(grad, down_ref[cols, :])
             sigmoid = jax.nn.sigmoid(gate)
             silu = gate * sigmoid
@@ -1375,13 +1342,15 @@
             ).astype(BF16)
             back_ref[where, later] = (hidden_grad * silu).astype(BF16)
 
-        share = width // (2 * here.length)
+        slabs = share // slab
+        begin = number * slabs
         some = pl.ds(pl.multiple_of(number * share, share), share)
-        turned_ref[:, some] = feed_ref[some, :].T
+        weights = feed_ref[lax.div(begin, here.count), pl.ds(lax.rem(begin, here.count), slabs)]
+        turned_ref[:, some] = weights.reshape(share, 2 * hidden).T
         for one in outs(number, first):
             one.start()
 
-    gather_units(here, buf, send_sems, recv_sems, compute)
+    gather_units(here, buf, send_sems, recv_sems, compute, started=started)
 
     @pl.loop(0, here.count // 2)
     def _(number):
@@ -1391,35 +1360,52 @@
     store.finish()
 
 
-def gather_feed(own, grad_out, feed_weight, down_weight, call_id):
+def feed_both_ways(
+    queries, keys, values, opening, output, tokens, gate, up, near, grad_out, down, block, call_id
+):
     seq = lax.axis_size("seq")
-    rows, width = own.shape
-    hidden = down_weight.shape[0]
+    rows, width = tokens.shape
+    cols = queries.shape[1]
+    hidden = down.shape[0]
+    all_rows = seq * rows
+    bf16 = lambda *shape: jax.ShapeDtypeStruct(shape, BF16)
+    f32 = lambda *shape: jax.ShapeDtypeStruct(shape, F32)
+    dma = pltpu.SemaphoreType.DMA
     return pl.pallas_call(
-        feed_kernel,
+        functools.partial(feed_kernel, block),
         out_shape=[
-            jax.ShapeDtypeStruct((seq * rows, width), BF16),
-            jax.ShapeDtypeStruct((seq * rows, hidden), BF16),
-            jax.ShapeDtypeStruct((seq * rows, 2 * hidden), BF16),
-            jax.ShapeDtypeStruct((2 * hidden, width), BF16),
+            f32(all_rows, cols),
+            f32(all_rows, cols // HEAD_DIM),
+            bf16(all_rows, cols),
+            f32(rows, width),
+            bf16(all_rows, width),
+            bf16(all_rows, hidden),
+            bf16(all_rows, 2 * hidden),
+            bf16(2 * hidden, width),
         ],
-        in_specs=[VMEM] + [HBM] * 3,
-        out_specs=[HBM] * 4,
-        scratch_shapes=gather_scratch(seq, rows // 2, width)
+        in_specs=[VMEM] * 6 + [HBM] * 5,
+        out_specs=[VMEM] * 4 + [HBM] * 4,
+        scratch_shapes=scatter_scratch(seq, rows, width)
         + [
-            pltpu.SemaphoreType.DMA((seq // 2, 2, 2)),
-            pltpu.VMEM((seq * rows, width), BF16),
-            pltpu.VMEM((width, 2 * hidden), BF16),
+            pltpu.VMEM((2, seq, *near.shape[1:]), BF16),
+            dma((2, 2, seq // 2)),
+            dma((seq // 2,)),
+            dma((2, seq // 2, 4)),
+        ]
+        + gather_scratch(seq, rows // 2, width)
+        + [
+            dma((seq // 2, 2, 2)),
+            pltpu.VMEM((all_rows, width), BF16),
             pltpu.VMEM((hidden, width), BF16),
-            pltpu.VMEM((seq * rows, hidden), BF16),
-            pltpu.VMEM((seq * rows, 2 * hidden), BF16),
+            pltpu.VMEM((all_rows, hidden), BF16),
+            pltpu.VMEM((all_rows, 2 * hidden), BF16),
             pltpu.VMEM((2 * hidden, width), BF16),
-            pltpu.SemaphoreType.DMA((3,)),
-            pltpu.SemaphoreType.DMA((seq // 2, 3)),
+            dma((2,)),
+            dma((seq // 2, 3)),
         ],
-        compiler_params=params(call_id, 60),
-        cost_estimate=cost(8 * seq * rows * width * hidden, 8 * seq * rows * width),
-    )(own, grad_out, feed_weight, down_weight)
+        compiler_params=params(call_id, 62),
+        cost_estimate=cost(8 * all_rows * width * hidden, 8 * all_rows * width),
+    )(queries, keys, values, opening, output, tokens, gate, up, near, grad_out, down)
 
 
 def back_kernel(
@@ -1784,6 +1770,9 @@
     )(a, b, normed)
 
 
+UNPACK_LINES = 4
+
+
 def unpack_kernel(
     pair_ref,
     near_gate_ref,
@@ -1882,10 +1871,10 @@
         (near_gate_ref, far_gate_ref, gate_ref, gate_out_ref),
         (near_up_ref, far_up_ref, up_ref, up_out_ref),
     ):
-        for number in range(4):
-            core = number % 2
-            near, far = near_ref[core].astype(F32), far_ref[core].astype(F32)
-            grad = jnp.where(number // 2 == pair, near, far)
+        for number in range(2 * near_ref.shape[0]):
+            slot = number // 4 * 2 + number % 2
+            near, far = near_ref[slot].astype(F32), far_ref[slot].astype(F32)
+            grad = jnp.where(number // 2 % 2 == pair, near, far)
             cols = slice(number * columns, (number + 1) * columns)
             total = total + along(grad, weight_ref[:, cols])
             out_ref[:, cols] = grad * gain_two
@@ -1900,11 +1889,13 @@
     dp = lax.axis_size("dp")
     seq = lax.axis_size("seq")
     slab, ff = gate.shape
-    length = seq // 4
+    length = seq // 4 // UNPACK_LINES
     columns = ff // (dp * seq)
     whole = lambda array: pl.BlockSpec(array.shape, lambda j, i: (0,) * array.ndim)
-    block = lambda kind: pl.BlockSpec((2, slab, columns), lambda j, i: (i, 0, kind * dp + j))
-    tile = pl.BlockSpec((slab, 4 * columns), lambda j, i: (0, j * length + i))
+    block = lambda kind: pl.BlockSpec(
+        (2 * UNPACK_LINES, slab, columns), lambda j, i: (i, 0, kind * dp + j)
+    )
+    tile = pl.BlockSpec((slab, 4 * UNPACK_LINES * columns), lambda j, i: (0, j * length + i))
     f32 = lambda array: jax.ShapeDtypeStruct(array.shape, F32)
     outs = [f32(gate), f32(up), f32(query), f32(key), f32(value), f32(gain_one), f32(gain_two)]
     sums = [f32(rows[0]), f32(rows[0]), f32(rows[5]), f32(rows[7])]
@@ -2221,25 +2212,24 @@
     qkv_weight = qkv_weight.reshape(width, -1)
     down_own = down_own.reshape(-1, width)
     output_own = output_own.reshape(-1, width)
-    attended_sum, log_total, feed_far, attended, feed_other = attention_feed(
-        queries,
-        keys,
-        values,
-        opening,
-        gate_scaled,
-        up_scaled,
-        feed_near,
-        block,
-        1,
-    )
-    middle, middle_normed, feed_weight = product_scatter_feed(
-        attended, output_own, tokens, feed_near, feed_other, feed_far, 2
-    )
-    feed_weight = feed_weight.reshape(width, -1)
-
-    normed_two, hidden, feed_back, feed_turned = gather_feed(
-        middle_normed, grad_out, feed_weight, down_own, 3
-    )
+    attended_sum, log_total, attended, middle, normed_two, hidden, feed_back, feed_turned = (
+        feed_both_ways(
+            queries,
+            keys,
+            values,
+            opening,
+            output_own,
+            tokens,
+            gate_scaled,
+            up_scaled,
+            feed_near,
+            grad_out,
+            down_own,
+            block,
+            1,
+        )
+    )
+
     middle_grad, middle_back, mixed_sum, feed_sums = product_scatter_both(
         feed_back, feed_turned, hidden, down_own, middle, grad_out, normed_two, 4
     )

time: 551 us -> 537 us (0.975)
  Pallas kernels: 549 us -> 536 us
    pallas_call x3 -> x1, Pallas kernels: 144 us -> 132 us  [feed_both_ways(): pl.pallas_call(functools.partial(feed_kernel, block), out_shape=[f32(all_...]
where the time goes in v9:
time: 537 us; the launch traced here: 536 us
  Pallas kernels  536 us (100%)
    pallas_call x1, Pallas kernels, feed_both_ways(): pl.pallas_call(functools.partial(feed_kernel, block), out_shape=[f32(all_...  132 us
    pallas_call x1, Pallas kernels, gather_project(): pl.pallas_call(project_kernel, out_shape=[bf16(all_rows, width), bf16(all...  115 us
    pallas_call x1, Pallas kernels, product_scatter_both(): pl.pallas_call(scatter_both_kernel, out_shape=[jax.ShapeDtypeStruct((rows...  109 us
    pallas_call x1, Pallas kernels, product_scatter_last(): pl.pallas_call(scatter_last_kernel, out_shape=[jax.ShapeDtypeStruct((rows...  68.8 us
    pallas_call x1, Pallas kernels, gather_back(): pl.pallas_call(back_kernel, out_shape=[jax.ShapeDtypeStruct((seq * rows,...  61.6 us
    pallas_call x1, Pallas kernels, attention_back_feed(): pl.pallas_call(functools.partial(attention_back_feed_kernel, block), grid...  39.2 us

profile of v9, /device:TPU:0, one launch (start us, length us, event | category | flops | bytes accessed | tf_op | source)
XLA Modules:
  0.0 536.4 jit_solution(581345106934027375)
XLA Ops:
  0.6 114.7 %shard_map.212 = (bf16[2048,2048]{1,0:T(8,128)(2,1)}, bf16[2048,2048]{1,0:T(8,128)(2,1)}, bf16[2048,128]{1,0:T(8,128)(2,1)}, bf16[2048,128]{1,0:T(8,128)(2,1)}, ...) custom-call(s32[1,4]{1,0:T(1,128)} %lengths_ref.1, ...), custom_call_target="tpu_custom_call" | custom-call | flops 2147483648 | bytes 33554432 | tf_op jit(solution)/shard_map/pallas_call | solution.py:786
  115.4 132.4 %shard_map.213 = (f32[2048,128]{1,0:T(8,128)}, f32[2048,2]{1,0:T(8,128)}, bf16[2048,128]{1,0:T(8,128)(2,1)}, f32[128,2048]{1,0:T(8,128)}, bf16[2048,2048]{1,0:T(...) custom-call(bf16[2048,128]{1,0:T(8,128)(2,1)} %get-tuple-element.60.q_ref, ...), custom_call_target="tpu_custom_call" | custom-call | flops 17179869184 | bytes 33554432 | tf_op jit(solution)/shard_map/pallas_call | solution.py:1374
  247.8 109.0 %shard_map.214 = (f32[128,2048]{1,0:T(8,128)}, bf16[128,2048]{1,0:T(8,128)(2,1)}, f32[128,2048]{1,0:T(8,128)}, bf16[1024,1024]{1,0:T(8,128)(2,1)}) custom-call(bf16[2048,1024]{1,0:T(8,128)(2,1)} %get-tuple-element.70.back_hbm, bf16[1024,2048]{1,0:T(8,128)(2,1)} %get-tuple-element.71.turned_hbm, bf16[2048,512]{1,0:T(8,128)(2,1)} %get-tuple-element.72.hidden_hbm, ...), custom_call_target="tpu_custom_call" | custom-call | flops 25769803776 | bytes 50331648 | tf_op jit(solution)/shard_map/pallas_call | solution.py:1134
  356.8 61.6 %shard_map.215 = (bf16[2048,128]{1,0:T(8,128)(2,1)}, f32[64,2048]{1,0:T(8,128)}, bf16[64,2048]{1,0:T(8,128)(2,1)}, f32[256,2048]{1,0:T(8,128)}, bf16[256,2048]{1,0:T(8,128)(2,1)}, /*index=5*/bf16[8,64,1024]{2,1,0:T(8,128)(2,1)}) custom-call(bf16[128,2048]{1,0:T(8,128)(2,1)} %get-tuple-element.75.own_ref, bf16[128,2048]{1,0:T(8,128)(2,1)} %bitcast.21, ...), custom_call_target="tpu_custom_call" | custom-call | flops 4294967296 | bytes 25165824 | tf_op jit(solution)/shard_map/pallas_call | solution.py:1492
  418.4 39.2 %shard_map.216 = (bf16[2048,256]{1,0:T(8,128)(2,1)}, bf16[8,64,1024]{2,1,0:T(8,128)(2,1)}, bf16[256,2048]{1,0:T(8,128)(2,1)}, bf16[64,2048]{1,0:T(8,128)(2,1)}) custom-call(bf16[2048,128]{1,0:T(8,128)(2,1)} %get-tuple-element.60.q_ref, bf16[2048,128]{1,0:T(8,128)(2,1)} %get-tuple-element.61.k_ref, bf16[2048,128]{1,0:T(8,128)(2,1)} %get-tuple-element.62.v_ref, ...), custom_call_target="tpu_custom_call" | custom-call | flops 2684354560 | bytes 5242880 | tf_op jit(solution)/shard_map/pallas_call | solution.py:1630
  457.6 68.8 %shard_map.217 = (f32[128,2048]{1,0:T(8,128)}, bf16[2,8,64,256]{3,2,1,0:T(8,128)(2,1)}) custom-call(bf16[2048,256]{1,0:T(8,128)(2,1)} %get-tuple-element.87.a_ref, bf16[2048,256]{1,0:T(8,128)(2,1)} %bitcast.11, bf16[2048,2048]{1,0:T(8,128)(2,1)} %get-tuple-element.89.normed_hbm), custom_call_target="tpu_custom_call" | custom-call | flops 2147483648 | bytes 16777216 | tf_op jit(solution)/shard_map/pallas_call | solution.py:1748
  526.4 9.8 %shard_map.218 = (f32[64,8192]{1,0:T(8,128)}, f32[64,8192]{1,0:T(8,128)}, f32[64,2048]{1,0:T(8,128)}, f32[64,512]{1,0:T(8,128)}, f32[64,512]{1,0:T(8,128)}, /*in...) custom-call(s32[1]{0:T(128)} %bitcast.pair_ref, ...), custom_call_target="tpu_custom_call" | custom-call | flops 524288 | bytes 8388608 | tf_op jit(solution)/shard_map/pallas_call | solution.py:1906

commit v10 on v9

--- a/solution.py
+++ b/solution.py
@@ -111,9 +111,21 @@
 
 
 def attention_back_kernel(
-    block, q_ref, k_ref, v_ref, g_ref, att_ref, lse_ref, open_ref, dq_ref, dk_ref, dv_ref
+    block,
+    q_ref,
+    k_ref,
+    v_ref,
+    g_ref,
+    att_ref,
+    lse_ref,
+    open_ref,
+    dq_ref,
+    dk_ref,
+    dv_ref,
+    tile=None,
 ):
-    tile = pl.program_id(0)
+    if tile is None:
+        tile = pl.program_id(0)
 
     @pl.when(tile == 0)
     def _():
@@ -1409,296 +1421,215 @@
 
 
 def back_kernel(
+    block,
     own_ref,
     weight_ref,
-    attended_ref,
-    hidden_hbm,
-    out_grad_hbm,
-    blocks_ref,
-    grad_ref,
-    output_kept_ref,
-    output_away_ref,
-    down_kept_ref,
-    down_away_ref,
-    near_ref,
-    buf,
-    send_sems,
-    recv_sems,
-    near_sems,
-    own_sem,
-    part,
-    hidden_ref,
-    out_grad_ref,
-    fetch_sems,
-):
-    here = Place()
-    fetches = [
-        pltpu.make_async_copy(hidden_hbm, hidden_ref, fetch_sems.at[0]),
-        pltpu.make_async_copy(out_grad_hbm, out_grad_ref, fetch_sems.at[1]),
-    ]
-    for one in fetches:
-        one.start()
-    put_own(here, own_ref, buf)
-    here.greet_all()
-    rows = own_ref.shape[0]
-    width = own_ref.shape[1]
-    tile = 512
-    near = block_spread(here, True, blocks_ref, near_ref, near_sems)
-    own = pltpu.make_async_copy(blocks_ref.at[here.mine], near_ref.at[here.slot], own_sem.at[0])
-
-    own.start()
-
-    def between(step):
-        near.start_some(step - here.length, 2)
-
-    part[...] = jnp.zeros_like(part)
-    share = width // (2 * here.length)
-
-    def split(values, kept_ref, away_ref, cols):
-        half = values.shape[0] // 2
-        top, bottom = values[:half], values[half:]
-        kept_ref[:, cols] = jnp.where(here.dp == 0, top, bottom)
-        away_ref[:, cols] = jnp.where(here.dp == 0, bottom, top).astype(BF16)
-
-    def compute(number, first):
-        where = unit_rows(first, rows)
-        unit = take_unit(buf, first)
-        grad_ref[where, :] = dot_t(unit, weight_ref[...]).astype(BF16)
-        attended = attended_ref[where, :]
-        for t in range(width // tile):
-            cols = slice(t * tile, (t + 1) * tile)
-            part[:, cols] += t_dot(attended, unit[:, cols])
-        some = pl.ds(pl.multiple_of(number * share, share), share)
-
-        @pl.when(number == 0)
-        def _():
-            for one in fetches:
-                one.wait()
-
-        split(t_dot(hidden_ref[...], out_grad_ref[:, some]), down_kept_ref, down_away_ref, some)
-
-    gather_units(here, buf, send_sems, recv_sems, compute, between)
-    for t in range(width // tile):
-        cols = slice(t * tile, (t + 1) * tile)
-        split(part[:, cols], output_kept_ref, output_away_ref, cols)
-    near.finish()
-    own.wait()
-
-
-def gather_back(own, weight, attended, hidden, grad_out, blocks, call_id):
-    seq = lax.axis_size("seq")
-    rows, width = own.shape
-    cols = weight.shape[0]
-    return pl.pallas_call(
-        back_kernel,
-        out_shape=[
-            jax.ShapeDtypeStruct((seq * rows, cols), BF16),
-            jax.ShapeDtypeStruct((cols // 2, width), F32),
-            jax.ShapeDtypeStruct((cols // 2, width), BF16),
-            jax.ShapeDtypeStruct((hidden.shape[1] // 2, width), F32),
-            jax.ShapeDtypeStruct((hidden.shape[1] // 2, width), BF16),
-            jax.ShapeDtypeStruct((seq // 2, *blocks.shape[1:]), BF16),
-        ],
-        in_specs=[VMEM] * 3 + [HBM] * 3,
-        out_specs=[VMEM] * 5 + [HBM],
-        scratch_shapes=gather_scratch(seq, rows // 2, width)
-        + [
-            pltpu.SemaphoreType.DMA((2, seq // 2)),
-            pltpu.SemaphoreType.DMA((1,)),
-            pltpu.VMEM((cols, width), F32),
-            pltpu.VMEM(hidden.shape, BF16),
-            pltpu.VMEM(grad_out.shape, BF16),
-            pltpu.SemaphoreType.DMA((2,)),
-        ],
-        compiler_params=params(call_id, 60),
-        cost_estimate=cost(8 * seq * rows * width * cols, 6 * seq * rows * width),
-    )(own, weight, attended, hidden, grad_out, blocks)
-
-
-def attention_back_feed_kernel(
-    block,
+    low_ref,
     q_ref,
     k_ref,
     v_ref,
-    g_ref,
     att_ref,
     lse_ref,
     open_ref,
     cos_ref,
     sin_ref,
+    heads_ref,
+    hidden_hbm,
+    out_grad_hbm,
     blocks_ref,
-    down_ref,
-    output_ref,
-    back_ref,
-    feed_ref,
-    down_out_ref,
-    output_out_ref,
-    dq_ref,
-    dk_ref,
-    dv_ref,
-    share_out,
-    share_in,
-    feed_sems,
-    swap_sems,
-    share_sems,
+    normed_hbm,
+    output_kept_ref,
+    output_came_ref,
+    down_kept_ref,
+    down_came_ref,
+    near_ref,
+    far_ref,
+    out_ref,
+    qkv_ref,
+    *scratch,
 ):
     here = Place()
-    tile = pl.program_id(0)
+    (
+        buf,
+        send_sems,
+        recv_sems,
+        part,
+        hidden_ref,
+        out_grad,
+        grad_ref,
+        output_away,
+        down_away,
+        dq_ref,
+        dk_ref,
+        dv_ref,
+        share_out,
+        share_in,
+        back_ref,
+        normed,
+        kept,
+        away,
+        came,
+        sums,
+        near_sems,
+        far_sems,
+        local_sems,
+        swap_sems,
+        share_sems,
+        fetch_sems,
+        sum_sems,
+        sum_near_sems,
+        sum_far_sems,
+    ) = scratch[SCATTER_SCRATCH:]
+    rows, width = own_ref.shape
     cols = q_ref.shape[1]
-    feed = block_spread(here, False, blocks_ref, feed_ref, feed_sems)
+    tile = 512
+    units = 2 * here.length
+    share = width // units
+
+    hidden_copy = pltpu.make_async_copy(hidden_hbm, hidden_ref, local_sems.at[0])
+    own_copy = pltpu.make_async_copy(
+        blocks_ref.at[here.mine], near_ref.at[here.slot], local_sems.at[1]
+    )
+    near = block_spread(here, True, blocks_ref, near_ref, near_sems)
+    far = block_spread(here, False, blocks_ref, far_ref, far_sems)
     swaps = [
         remote(src, dst, swap_sems.at[0, number], swap_sems.at[1, number], here.partner())
         for number, (src, dst) in enumerate(
-            [(down_ref, down_out_ref), (output_ref, output_out_ref)]
+            [(down_away, down_came_ref), (output_away, output_came_ref)]
         )
     ]
 
-    pl.when(tile == 0)(here.call_all)
-    attention_back_kernel(
-        block, q_ref, k_ref, v_ref, g_ref, att_ref, lse_ref, open_ref, dq_ref, dk_ref, dv_ref
-    )
-
-    @pl.when(tile == 0)
-    def _():
-        here.await_all()
-        feed.start()
-        for one in swaps:
-            one.start()
-
-    where = pl.ds(pl.multiple_of(tile * block, block), block)
+    def out_grad_copy(number):
+        some = pl.ds(pl.multiple_of(number * share, share), share)
+        slot = number % 2
+        return pltpu.make_async_copy(
+            out_grad_hbm.at[:, some], out_grad.at[slot], fetch_sems.at[0, slot]
+        )
+
+    hidden_copy.start()
+    own_copy.start()
+    out_grad_copy(jnp.int32(0)).start()
+    here.call_all()
+    put_own(here, own_ref, buf)
+    part[...] = jnp.zeros_like(part)
+    here.await_all()
+
+    def split(values, kept_to, away_to, some):
+        half = values.shape[0] // 2
+        top, bottom = values[:half], values[half:]
+        kept_to[:, some] = jnp.where(here.dp == 0, top, bottom)
+        away_to[:, some] = jnp.where(here.dp == 0, bottom, top).astype(BF16)
+
+    def compute(number, first):
+        where = unit_rows(first, rows)
+        unit = take_unit(buf, first)
+        grad_ref[where, :] = dot_t(unit, weight_ref[...]).astype(BF16)
+        attended = low_ref[where, :]
+        for t in range(width // tile):
+            some = slice(t * tile, (t + 1) * tile)
+            part[:, some] += t_dot(attended, unit[:, some])
+        pl.when(number == 0)(hidden_copy.wait)
+        out_grad_copy(number).wait()
+        pl.when(number + 1 < units)(lambda: out_grad_copy(number + 1).start())
+        some = pl.ds(pl.multiple_of(number * share, share), share)
+        split(t_dot(hidden_ref[...], out_grad[number % 2]), down_kept_ref, down_away, some)
+
+    def between(step):
+        near.start_some(step - here.length, 2)
+
+    gather_units(here, buf, send_sems, recv_sems, compute, between)
+    far.start()
+    for t in range(width // tile):
+        some = slice(t * tile, (t + 1) * tile)
+        split(part[:, some], output_kept_ref, output_away, some)
+    for one in swaps:
+        one.start()
+
+    tiles = q_ref.shape[0] // block
     scale = 1.0 / math.sqrt(HEAD_DIM)
-    cosine = cos_ref[where, :]
-    sine = sin_ref[where, :]
-    back_ref[where, :cols] = rotated(dq_ref[...] * scale, cosine, -sine).astype(BF16)
-
-    def share(i):
-        rows = pl.ds(pl.multiple_of(i * block, block), block)
+
+    @pl.loop(0, tiles)
+    def _(i):
+        some = pl.ds(pl.multiple_of(i * block, block), block)
+        attention_back_kernel(
+            block,
+            q_ref.at[some],
+            k_ref,
+            v_ref,
+            grad_ref.at[some],
+            att_ref.at[some],
+            lse_ref.at[some],
+            open_ref.at[some],
+            dq_ref,
+            dk_ref,
+            dv_ref,
+            i,
+        )
+        turned = rotated(dq_ref[...] * scale, cos_ref[some, :], -sin_ref[some, :])
+        back_ref[some, :cols] = turned.astype(BF16)
+
+    def share_copy(i):
+        some = pl.ds(pl.multiple_of(i * block, block), block)
         return remote(
-            share_out.at[rows],
-            share_in.at[rows],
+            share_out.at[some],
+            share_in.at[some],
             share_sems.at[0, i],
             share_sems.at[1, i],
             here.sibling(),
         )
 
-    @pl.when(tile == pl.num_programs(0) - 1)
-    def _():
-        @pl.loop(0, pl.num_programs(0))
+    @pl.loop(0, tiles)
+    def _(i):
+        some = pl.ds(pl.multiple_of(i * block, block), block)
+        share_out[some, :] = jnp.where(here.core == 0, dv_ref[some, :], dk_ref[some, :]).astype(BF16)
+        share_copy(i).start()
+
+    @pl.loop(0, tiles)
+    def _(i):
+        some = pl.ds(pl.multiple_of(i * block, block), block)
+        share_copy(i).wait()
+        other = share_in[some, :].astype(F32)
+        keys = rotated(dk_ref[some, :] + other, cos_ref[some, :], -sin_ref[some, :])
+        back_ref[some, cols:] = jnp.where(here.core == 0, keys, dv_ref[some, :] + other).astype(BF16)
+
+    swap = remote(away, came, sum_sems.at[0], sum_sems.at[1], here.partner())
+    sum_near = block_spread(here, True, sums, qkv_ref.at[0], sum_near_sems)
+    sum_far = block_spread(here, False, sums, qkv_ref.at[1], sum_far_sems)
+    half = away.shape[0]
+    chunk = normed.shape[2]
+    chunks = half // chunk
+
+    def normed_copy(number):
+        dp = jnp.where(number < chunks, 1 - here.dp, here.dp)
+        begin = dp * half + number % chunks * chunk
+        slot = number % 2
+        return pltpu.make_async_copy(
+            normed_hbm.at[:, pl.ds(pl.multiple_of(begin, chunk), chunk)],
+            normed.at[slot],
+            fetch_sems.at[1, slot],
+        )
+
+    def heads_part(number):
+        normed_copy(number).wait()
+        pl.when(number + 1 < 2 * chunks)(lambda: normed_copy(number + 1).start())
+        return t_dot(normed[number % 2], back_ref[...])
+
+    normed_copy(jnp.int32(0)).start()
+
+    def first(step):
+        @pl.when(step == 2)
+        def _():
+            @pl.loop(0, chunks)
+            def _(i):
+                some = pl.ds(pl.multiple_of(i * chunk, chunk), chunk)
+                away[some, :] = heads_part(i).astype(BF16)
+
+            swap.start()
+
+    def own_share():
+        @pl.loop(0, chunks)
         def _(i):
-            rows = pl.ds(pl.multiple_of(i * block, block), block)
-            away = jnp.where(here.core == 0, dv_ref[rows, :], dk_ref[rows, :])
-            share_out[rows, :] = away.astype(BF16)
-            share(i).start()
-
-        @pl.loop(0, pl.num_programs(0))
-        def _(i):
-            rows = pl.ds(pl.multiple_of(i * block, block), block)
-            share(i).wait()
-            came = share_in[rows, :].astype(F32)
-            keys = rotated(dk_ref[rows, :] + came, cos_ref[rows, :], -sin_ref[rows, :])
-            back_ref[rows, cols:] = jnp.where(here.core == 0, keys, dv_ref[rows, :] + came).astype(
-                BF16
-            )
-
-        feed.finish()
-        for one in swaps:
-            one.wait()
-
-
-def attention_back_feed(
-    queries,
-    keys,
-    values,
-    grads,
-    attended,
-    log_total,
-    opening,
-    cosine,
-    sine,
-    blocks,
-    down,
-    output,
-    block,
-    call_id,
-):
-    seq = lax.axis_size("seq")
-    rows, cols = queries.shape
-    heads = cols // HEAD_DIM
-    tiled = lambda width: pl.BlockSpec((block, width), lambda i: (i, 0))
-    whole = pl.BlockSpec((rows, cols), lambda i: (0, 0))
-    dma = pltpu.SemaphoreType.DMA
-    return pl.pallas_call(
-        functools.partial(attention_back_feed_kernel, block),
-        grid=(rows // block,),
-        in_specs=[tiled(cols), whole, whole, tiled(cols), tiled(cols), tiled(heads), tiled(1)]
-        + [whole, whole, HBM, HBM, HBM],
-        out_specs=[pl.BlockSpec((rows, 2 * cols), lambda i: (0, 0)), HBM, HBM, HBM],
-        out_shape=[
-            jax.ShapeDtypeStruct((rows, 2 * cols), BF16),
-            jax.ShapeDtypeStruct((seq // 2, *blocks.shape[1:]), BF16),
-            jax.ShapeDtypeStruct(down.shape, BF16),
-            jax.ShapeDtypeStruct(output.shape, BF16),
-        ],
-        scratch_shapes=[
-            pltpu.VMEM((block, cols), F32),
-            pltpu.VMEM((rows, cols), F32),
-            pltpu.VMEM((rows, cols), F32),
-            pltpu.VMEM((rows, cols), BF16),
-            pltpu.VMEM((rows, cols), BF16),
-            dma((2, seq // 2)),
-            dma((2, 2)),
-            dma((2, rows // block)),
-        ],
-        compiler_params=params(call_id, 60),
-        cost_estimate=cost(5 * rows * rows * cols, 20 * rows * cols),
-    )(
-        queries,
-        keys,
-        values,
-        grads,
-        attended,
-        log_total,
-        opening,
-        cosine,
-        sine,
-        blocks,
-        down,
-        output,
-    )
-
-
-def scatter_last_kernel(a_ref, b_ref, normed_hbm, out_ref, qkv_ref, *scratch):
-    here = Place()
-    normed_ref, kept, away, came, sums, near_sems, far_sems, swap_sems, fetch_sems = scratch[
-        SCATTER_SCRATCH:
-    ]
-    fetch = pltpu.make_async_copy(normed_hbm, normed_ref, fetch_sems.at[0])
-    fetch.start()
-    swap = remote(away, came, swap_sems.at[0], swap_sems.at[1], here.partner())
-    near = block_spread(here, True, sums, qkv_ref.at[0], near_sems)
-    far = block_spread(here, False, sums, qkv_ref.at[1], far_sems)
-    half = away.shape[0]
-    chunk = 256
-
-    def part(dp, i):
-        first = pl.multiple_of(dp * half + i * chunk, chunk)
-        return t_dot(normed_ref[:, pl.ds(first, chunk)], a_ref[...])
-
-    def meanwhile():
-        fetch.wait()
-
-        @pl.loop(0, half // chunk)
-        def _(i):
-            some = pl.ds(pl.multiple_of(i * chunk, chunk), chunk)
-            away[some, :] = part(1 - here.dp, i).astype(BF16)
-
-    here.greet_all(meanwhile)
-    swap.start()
-
-    def between():
-        @pl.loop(0, half // chunk)
-        def _(i):
-            kept[pl.ds(pl.multiple_of(i * chunk, chunk), chunk), :] = part(here.dp, i)
+            kept[pl.ds(pl.multiple_of(i * chunk, chunk), chunk), :] = heads_part(chunks + i)
 
     begin = 2
     each = 3
@@ -1711,8 +1642,8 @@
 
             @pl.loop(0, here.count)
             def _(i):
-                rows = pl.ds(pl.multiple_of(i * slab, slab), slab)
-                sums[i] = (kept[rows, :] + came[rows, :].astype(F32)).astype(BF16)
+                some = pl.ds(pl.multiple_of(i * slab, slab), slab)
+                sums[i] = (kept[some, :] + came[some, :].astype(F32)).astype(BF16)
 
             qkv_ref[0, here.slot] = sums[here.mine]
 
@@ -1721,53 +1652,123 @@
             @pl.loop(0, each)
             def _(i):
                 number = (step - begin - 1) * each + i
-                pl.when(number < far.slots)(lambda: far.start_one(number))
-
-                @pl.when((number >= far.slots) & (number < 2 * far.slots - 1))
+                pl.when(number < sum_far.slots)(lambda: sum_far.start_one(number))
+
+                @pl.when((number >= sum_far.slots) & (number < 2 * sum_far.slots - 1))
                 def _():
-                    near.start_one(number - far.slots + 1)
+                    sum_near.start_one(number - sum_far.slots + 1)
 
     scatter_rows_of_products(
         here,
-        [(True, a_ref, b_ref, out_ref)],
+        [(True, back_ref, heads_ref, out_ref)],
         *scratch[:SCATTER_SCRATCH],
-        between=between,
+        first=first,
+        between=own_share,
         filler=filler,
     )
     swap.wait_send()
+    for one in swaps:
+        one.wait()
     near.finish()
     far.finish()
-
-
-def product_scatter_last(a, b, normed, call_id):
+    own_copy.wait()
+    sum_near.finish()
+    sum_far.finish()
+
+
+def attention_backwards(
+    own,
+    weight,
+    attended,
+    queries,
+    keys,
+    values,
+    attended_sum,
+    log_total,
+    opening,
+    cosine,
+    sine,
+    heads,
+    hidden,
+    grad_out,
+    blocks,
+    normed,
+    block,
+    call_id,
+):
     seq = lax.axis_size("seq")
-    rows = a.shape[0] // seq
-    width, cols = b.shape
-    slab = width // (2 * seq)
+    rows, width = own.shape
+    all_rows, cols = queries.shape
+    slab = blocks.shape[1]
+    half_hidden = hidden.shape[1] // 2
+    chunk = width // 8
+    bf16 = lambda *shape: jax.ShapeDtypeStruct(shape, BF16)
+    f32 = lambda *shape: jax.ShapeDtypeStruct(shape, F32)
     dma = pltpu.SemaphoreType.DMA
     return pl.pallas_call(
-        scatter_last_kernel,
+        functools.partial(back_kernel, block),
         out_shape=[
-            jax.ShapeDtypeStruct((rows, width), F32),
-            jax.ShapeDtypeStruct((2, seq // 2, slab, cols), BF16),
+            f32(cols // 2, width),
+            bf16(cols // 2, width),
+            f32(half_hidden, width),
+            bf16(half_hidden, width),
+            bf16(seq // 2, *blocks.shape[1:]),
+            bf16(seq // 2, *blocks.shape[1:]),
+            f32(rows, width),
+            bf16(2, seq // 2, slab, 2 * cols),
         ],
-        in_specs=[VMEM, VMEM, HBM],
-        out_specs=[VMEM, VMEM],
+        in_specs=[VMEM] * 12 + [HBM] * 4,
+        out_specs=[VMEM, HBM, VMEM, HBM, HBM, HBM, VMEM, VMEM],
         scratch_shapes=scatter_scratch(seq, rows, width)
+        + gather_scratch(seq, rows // 2, width)
         + [
-            pltpu.VMEM(normed.shape, BF16),
-            pltpu.VMEM((width // 2, cols), F32),
-            pltpu.VMEM((width // 2, cols), BF16),
-            pltpu.VMEM((width // 2, cols), BF16),
-            pltpu.VMEM((seq, slab, cols), BF16),
+            pltpu.VMEM((cols, width), F32),
+            pltpu.VMEM(hidden.shape, BF16),
+            pltpu.VMEM((2, all_rows, width // (seq // 2)), BF16),
+            pltpu.VMEM((all_rows, cols), BF16),
+            pltpu.VMEM((cols // 2, width), BF16),
+            pltpu.VMEM((half_hidden, width), BF16),
+            pltpu.VMEM((block, cols), F32),
+            pltpu.VMEM((all_rows, cols), F32),
+            pltpu.VMEM((all_rows, cols), F32),
+            pltpu.VMEM((all_rows, cols), BF16),
+            pltpu.VMEM((all_rows, cols), BF16),
+            pltpu.VMEM((all_rows, 2 * cols), BF16),
+            pltpu.VMEM((2, all_rows, chunk), BF16),
+            pltpu.VMEM((width // 2, 2 * cols), F32),
+            pltpu.VMEM((width // 2, 2 * cols), BF16),
+            pltpu.VMEM((width // 2, 2 * cols), BF16),
+            pltpu.VMEM((seq, slab, 2 * cols), BF16),
             dma((2, seq // 2)),
             dma((2, seq // 2)),
             dma((2,)),
-            dma((1,)),
+            dma((2, 2)),
+            dma((2, all_rows // block)),
+            dma((2, 2)),
+            dma((2,)),
+            dma((2, seq // 2)),
+            dma((2, seq // 2)),
         ],
-        compiler_params=params(call_id, 60),
-        cost_estimate=scatter_cost(a, width),
-    )(a, b, normed)
+        compiler_params=params(call_id, 62),
+        cost_estimate=cost(12 * all_rows * width * cols, 12 * all_rows * width),
+    )(
+        own,
+        weight,
+        attended,
+        queries,
+        keys,
+        values,
+        attended_sum,
+        log_total,
+        opening,
+        cosine,
+        sine,
+        heads,
+        hidden,
+        grad_out,
+        blocks,
+        normed,
+    )
 
 
 UNPACK_LINES = 4
@@ -2234,27 +2235,35 @@
         feed_back, feed_turned, hidden, down_own, middle, grad_out, normed_two, 4
     )
     feed_sums = feed_sums.reshape(seq, slab, -1)
-    attended_grad, output_kept, output_away, down_kept, down_away, feed_grad_near = gather_back(
-        middle_back, output_own, attended, hidden, grad_out, feed_sums, 5
-    )
-
-    qkv_back, feed_grad_far, down_came, output_came = attention_back_feed(
+    (
+        output_kept,
+        output_came,
+        down_kept,
+        down_came,
+        feed_grad_near,
+        feed_grad_far,
+        normed_one_grad,
+        qkv_grads,
+    ) = attention_backwards(
+        middle_back,
+        output_own,
+        attended,
         queries,
         keys,
         values,
-        attended_grad,
         attended_sum,
         log_total,
         opening,
         cosine,
         sine,
+        qkv_weight,
+        hidden,
+        grad_out,
         feed_sums,
-        down_away,
-        output_away,
+        normed_one,
         block,
-        6,
-    )
-    normed_one_grad, qkv_grads = product_scatter_last(qkv_back, qkv_weight, normed_one, 7)
+        5,
+    )
 
     pair = ((mine // 2) % 2).reshape(1)
     (

time: 537 us -> 521 us (0.970)
  Pallas kernels: 536 us -> 520 us
    pallas_call x3 -> x1, Pallas kernels: 170 us -> 154 us  [attention_backwards(): pl.pallas_call(functools.partial(back_kernel, block), out_shape=[f32(cols...]
where the time goes in v10:
time: 521 us
  Pallas kernels  520 us (100%)
    pallas_call x1, Pallas kernels, attention_backwards(): pl.pallas_call(functools.partial(back_kernel, block), out_shape=[f32(cols...  154 us
    pallas_call x1, Pallas kernels, feed_both_ways(): pl.pallas_call(functools.partial(feed_kernel, block), out_shape=[f32(all_...  132 us
    pallas_call x1, Pallas kernels, gather_project(): pl.pallas_call(project_kernel, out_shape=[bf16(all_rows, width), bf16(all...  115 us
    pallas_call x1, Pallas kernels, product_scatter_both(): pl.pallas_call(scatter_both_kernel, out_shape=[jax.ShapeDtypeStruct((rows...  109 us

profile of v10, /device:TPU:0, one launch (start us, length us, event | category | flops | bytes accessed | tf_op | source)
XLA Modules:
  0.0 521.0 jit_solution(4217146564201609592)
XLA Ops:
  0.6 114.8 %shard_map.212 = (bf16[2048,2048]{1,0:T(8,128)(2,1)}, bf16[2048,2048]{1,0:T(8,128)(2,1)}, bf16[2048,128]{1,0:T(8,128)(2,1)}, bf16[2048,128]{1,0:T(8,128)(2,1)}, ...) custom-call(s32[1,4]{1,0:T(1,128)} %lengths_ref.1, ...), custom_call_target="tpu_custom_call" | custom-call | flops 2147483648 | bytes 33554432 | tf_op jit(solution)/shard_map/pallas_call | solution.py:798
  115.5 132.4 %shard_map.213 = (f32[2048,128]{1,0:T(8,128)}, f32[2048,2]{1,0:T(8,128)}, bf16[2048,128]{1,0:T(8,128)(2,1)}, f32[128,2048]{1,0:T(8,128)}, bf16[2048,2048]{1,0:T(...) custom-call(bf16[2048,128]{1,0:T(8,128)(2,1)} %get-tuple-element.56.q_ref, ...), custom_call_target="tpu_custom_call" | custom-call | flops 17179869184 | bytes 33554432 | tf_op jit(solution)/shard_map/pallas_call | solution.py:1386
  247.9 109.0 %shard_map.214 = (f32[128,2048]{1,0:T(8,128)}, bf16[128,2048]{1,0:T(8,128)(2,1)}, f32[128,2048]{1,0:T(8,128)}, bf16[1024,1024]{1,0:T(8,128)(2,1)}) custom-call(bf16[2048,1024]{1,0:T(8,128)(2,1)} %get-tuple-element.66.back_hbm, bf16[1024,2048]{1,0:T(8,128)(2,1)} %get-tuple-element.67.turned_hbm, bf16[2048,512]{1,0:T(8,128)(2,1)} %get-tuple-element.68.hidden_hbm, ...), custom_call_target="tpu_custom_call" | custom-call | flops 25769803776 | bytes 50331648 | tf_op jit(solution)/shard_map/pallas_call | solution.py:1146
  356.9 154.1 %shard_map.215 = (f32[64,2048]{1,0:T(8,128)}, bf16[64,2048]{1,0:T(8,128)(2,1)}, f32[256,2048]{1,0:T(8,128)}, bf16[256,2048]{1,0:T(8,128)(2,1)}, bf16[8,64,1024]{...) custom-call(bf16[128,2048]{1,0:T(8,128)(2,1)} %get-tuple-element.71.own_ref,, ...), custom_call_target="tpu_custom_call" | custom-call | flops 6442450944 | bytes 50331648 | tf_op jit(solution)/shard_map/pallas_call | solution.py:1708
  511.0 9.8 %shard_map.216 = (f32[64,8192]{1,0:T(8,128)}, f32[64,8192]{1,0:T(8,128)}, f32[64,2048]{1,0:T(8,128)}, f32[64,512]{1,0:T(8,128)}, f32[64,512]{1,0:T(8,128)}, /*in...) custom-call(s32[1]{0:T(128)} %bitcast.pair_ref, ...), custom_call_target="tpu_custom_call" | custom-call | flops 524288 | bytes 8388608 | tf_op jit(solution)/shard_map/pallas_call | solution.py:1907

commit v11 on v10

--- a/solution.py
+++ b/solution.py
@@ -132,28 +132,40 @@
         dk_ref[...] = jnp.zeros_like(dk_ref)
         dv_ref[...] = jnp.zeros_like(dv_ref)
 
-    opening = open_ref[...]
-    heads = []
-    for head in range(q_ref.shape[1] // HEAD_DIM):
+    count = q_ref.shape[1] // HEAD_DIM
+    columns = [open_ref[...].astype(F32), lse_ref[...]]
+    for head in range(count):
         lanes = slice(head * HEAD_DIM, (head + 1) * HEAD_DIM)
         grad = g_ref[:, lanes].astype(F32)
-        row_sum = jnp.sum(grad * att_ref[:, lanes], axis=1, keepdims=True)
-        heads.append((lanes, lse_ref[:, head : head + 1], row_sum))
+        columns.append(jnp.sum(grad * att_ref[:, lanes], axis=1, keepdims=True))
+    columns.append(jnp.zeros((block, 127 - 2 * count), F32))
+    across = jnp.concatenate(columns, axis=1).T
+    opening = across[0:1].astype(jnp.int32)
+    heads = [
+        (
+            slice(head * HEAD_DIM, (head + 1) * HEAD_DIM),
+            across[1 + head : 2 + head],
+            across[1 + count + head : 2 + count + head],
+        )
+        for head in range(count)
+    ]
 
     def step(j, carry):
         first = pl.multiple_of(j * block, block)
         here = pl.ds(first, block)
-        allowed = allowed_tile(opening, tile * block, first, (block, block))
+        keys = first + lax.broadcasted_iota(jnp.int32, (block, block), 0)
+        places = tile * block + lax.broadcasted_iota(jnp.int32, (block, block), 1)
+        allowed = (keys <= places) & (keys >= opening)
         after = []
         for (lanes, log_total, row_sum), acc in zip(heads, carry):
             query, grad, key = q_ref[:, lanes], g_ref[:, lanes], k_ref[here, lanes]
-            scores = dot_t(query, key)
+            scores = dot_t(key, query)
             chance = jnp.where(allowed, jnp.exp(scores - log_total), 0.0)
-            prob_grad = dot_t(grad, v_ref[here, lanes])
+            prob_grad = dot_t(v_ref[here, lanes], grad)
             score_grad = (chance * (prob_grad - row_sum)).astype(BF16)
-            dk_ref[here, lanes] += t_dot(score_grad, query)
-            dv_ref[here, lanes] += t_dot(chance.astype(BF16), grad)
-            after.append(acc + dot(score_grad, key))
+            dk_ref[here, lanes] += dot(score_grad, query)
+            dv_ref[here, lanes] += dot(chance.astype(BF16), grad)
+            after.append(acc + t_dot(score_grad, key))
         return tuple(after)
 
     start = jnp.zeros((block, HEAD_DIM), F32)
@@ -342,7 +354,7 @@
     return Spread(here, same, copies)
 
 
-def gather_units(here, buf, send_sems, recv_sems, compute, between=None, ready=None, started=nothing):
+def gather_units(here, buf, send_sems, recv_sems, compute, between=None, ready=None, started=nothing, level=False):
     length = here.length
     last = length - 1
     steps = 2 * length
@@ -356,23 +368,28 @@
         single = here.line + longer * (i - shorter + 1)
         return jnp.where(j == 0, here.line, jnp.where(i < 2 * shorter, paired, single))
 
-    def copy(way, device, block, part):
-        ref = buf.at[block, part]
-        return remote(
-            ref, ref, send_sems.at[way, block, part], recv_sems.at[block, part], device
-        )
-
-    def up(block, part):
-        return copy(0, here.above(), block, part)
-
-    def down(block, part):
-        return copy(1, here.below(), block, part)
-
-    def across(block, part):
-        return copy(2, here.across(), block, part)
-
-    def sideways(block, part):
-        return copy(3, here.sibling(), block, part)
+    keep = buf.shape[2] * 3 // 4
+
+    def copy(way, device, block, piece):
+        if piece == 2:
+            ref, sem = buf.at[block, 1, pl.ds(0, keep)], 1
+        elif piece == 3:
+            ref, sem = buf.at[block, 1, pl.ds(keep, buf.shape[2] - keep)], 2
+        else:
+            ref, sem = buf.at[block, piece], piece
+        return remote(ref, ref, send_sems.at[way, block, sem], recv_sems.at[block, sem], device)
+
+    def up(block, piece):
+        return copy(0, here.above(), block, piece)
+
+    def down(block, piece):
+        return copy(1, here.below(), block, piece)
+
+    def across(block, piece):
+        return copy(2, here.across(), block, piece)
+
+    def sideways(block, piece):
+        return copy(3, here.sibling(), block, piece)
 
     def unit(number):
         in_column = (number % 2 == 1) & (number < steps - 1) | (number == 0)
@@ -381,71 +398,126 @@
         pair = jnp.where(in_column, here.pair, 1 - here.pair)
         other = here.index(line, pair, 1 - here.core)
         sideways(other, 0).wait_recv()
-        sideways(other, 1).wait_recv()
+        if level:
+            whole = in_column | (line == here.line)
+            pl.when(whole)(lambda: sideways(other, 1).wait_recv())
+
+            @pl.when(jnp.logical_not(whole))
+            def _():
+                sideways(other, 2).wait_recv()
+                sideways(other, 3).wait_recv()
+
+        else:
+            sideways(other, 1).wait_recv()
+
         compute(number, here.index(line, pair, 0))
 
-    for part in range(2):
-        pl.when(here.line < last)(lambda part=part: up(mine, part).start())
-        pl.when(here.line > 0)(lambda part=part: down(mine, part).start())
-        across(mine, part).start()
-        sideways(mine, part).start()
+    for piece in range(2):
+        pl.when(here.line < last)(lambda piece=piece: up(mine, piece).start())
+        pl.when(here.line > 0)(lambda piece=piece: down(mine, piece).start())
+        across(mine, piece).start()
+        sideways(mine, piece).start()
     started()
-
-    @pl.loop(0, steps)
-    def _(step):
-        part = step % 2
-        far = step // 2 + 1
-
+    beside = here.index(here.line, 1 - here.pair, here.core)
+
+    def relay(far, pair, piece):
         @pl.when(here.line >= far)
         def _():
-            block = here.index(here.line - far, here.pair, here.core)
-            up(block, part).wait_recv()
-            pl.when(here.line < last)(lambda: up(block, part).start())
-            sideways(block, part).start()
+            block = here.index(here.line - far, pair, here.core)
+            up(block, piece).wait_recv()
+            pl.when(here.line < last)(lambda: up(block, piece).start())
+            sideways(block, piece).start()
 
         @pl.when(here.line + far <= last)
         def _():
-            block = here.index(here.line + far, here.pair, here.core)
-            down(block, part).wait_recv()
-            pl.when(here.line > 0)(lambda: down(block, part).start())
-            sideways(block, part).start()
-
-        @pl.when(step + 2 < steps)
-        def _():
-            across(here.index(column(step // 2 + 1), here.pair, here.core), part).start()
-
-        block = here.index(column(step // 2), 1 - here.pair, here.core)
-        across(block, part).wait_recv()
-        sideways(block, part).start()
-
-        if between is not None:
-            between(step)
-        if ready is None:
-            unit(step)
-        else:
-            begin = jnp.maximum(2 * (step - ready), 0)
-            end = jnp.maximum(2 * (step + 1 - ready), 0)
-
-            @pl.loop(begin, end)
-            def _(number):
-                unit(number)
+            block = here.index(here.line + far, pair, here.core)
+            down(block, piece).wait_recv()
+            pl.when(here.line > 0)(lambda: down(block, piece).start())
+            sideways(block, piece).start()
+
+    @pl.loop(0, length)
+    def _(round):
+        for part in range(2):
+            step = 2 * round + part
+            relay(round + 1, here.pair, part)
+
+            @pl.when(round < last)
+            def _():
+                block = here.index(column(round + 1), here.pair, here.core)
+                across(block, (2 if level else 1) if part else 0).start()
+
+            block = here.index(column(round), 1 - here.pair, here.core)
+            if part == 0 or not level:
+                across(block, part).wait_recv()
+                sideways(block, part).start()
+            else:
+
+                @pl.when(round == 0)
+                def _():
+                    across(beside, 1).wait_recv()
+                    pl.when(here.line < last)(lambda: up(beside, 3).start())
+                    pl.when(here.line > 0)(lambda: down(beside, 3).start())
+                    sideways(beside, 1).start()
+
+                @pl.when(round > 0)
+                def _():
+                    across(block, 2).wait_recv()
+                    sideways(block, 2).start()
+                    relay(round, 1 - here.pair, 3)
+
+            if between is not None:
+                between(step)
+            if ready is None:
+                unit(step)
+            else:
+                begin = jnp.maximum(2 * (step - ready), 0)
+                end = jnp.maximum(2 * (step + 1 - ready), 0)
+
+                @pl.loop(begin, end)
+                def _(number):
+                    unit(number)
 
     @pl.loop(0, length)
     def _(line):
-        for part in range(2):
-            block = here.index(line, here.pair, here.core)
-
-            @pl.when((line <= here.line) & (here.line < last))
-            def _():
-                up(block, part).wait_send()
-
-            @pl.when((line >= here.line) & (here.line > 0))
-            def _():
-                down(block, part).wait_send()
-
-            across(block, part).wait_send()
-            sideways(block, part).wait_send()
-            sideways(here.index(line, 1 - here.pair, here.core), part).wait_send()
+        own = here.index(line, here.pair, here.core)
+        other = here.index(line, 1 - here.pair, here.core)
+        goes_up = (line <= here.line) & (here.line < last)
+        goes_down = (line >= here.line) & (here.line > 0)
+
+        @pl.when(goes_up)
+        def _():
+            up(own, 0).wait_send()
+            up(own, 1).wait_send()
+            if level:
+                up(other, 3).wait_send()
+
+        @pl.when(goes_down)
+        def _():
+            down(own, 0).wait_send()
+            down(own, 1).wait_send()
+            if level:
+                down(other, 3).wait_send()
+
+        across(own, 0).wait_send()
+        sideways(own, 0).wait_send()
+        sideways(own, 1).wait_send()
+        sideways(other, 0).wait_send()
+
+        if not level:
+            across(own, 1).wait_send()
+            sideways(other, 1).wait_send()
+            return
+
+        @pl.when(line == here.line)
+        def _():
+            across(own, 1).wait_send()
+            sideways(other, 1).wait_send()
+
+        @pl.when(line != here.line)
+        def _():
+            across(own, 2).wait_send()
+            sideways(other, 2).wait_send()
+            sideways(other, 3).wait_send()
 
 
 def put_own(here, own_ref, buf):
@@ -457,8 +529,8 @@
 def gather_scratch(seq, rows, width):
     return [
         pltpu.VMEM((seq, 2, rows, width), BF16),
-        pltpu.SemaphoreType.DMA((4, seq, 2)),
-        pltpu.SemaphoreType.DMA((seq, 2)),
+        pltpu.SemaphoreType.DMA((4, seq, 3)),
+        pltpu.SemaphoreType.DMA((seq, 3)),
     ]
 
 
@@ -1362,7 +1434,7 @@
         for one in outs(number, first):
             one.start()
 
-    gather_units(here, buf, send_sems, recv_sems, compute, started=started)
+    gather_units(here, buf, send_sems, recv_sems, compute, started=started, level=True)
 
     @pl.loop(0, here.count // 2)
     def _(number):
@@ -1534,11 +1606,9 @@
         some = pl.ds(pl.multiple_of(number * share, share), share)
         split(t_dot(hidden_ref[...], out_grad[number % 2]), down_kept_ref, down_away, some)
 
-    def between(step):
-        near.start_some(step - here.length, 2)
-
-    gather_units(here, buf, send_sems, recv_sems, compute, between)
+    gather_units(here, buf, send_sems, recv_sems, compute, level=True)
     far.start()
+    near.start()
     for t in range(width // tile):
         some = slice(t * tile, (t + 1) * tile)
         split(part[:, some], output_kept_ref, output_away, some)

time: 521 us -> 513 us (0.985)
  Pallas kernels: 520 us -> 512 us
    pallas_call x1, Pallas kernels: 154 us -> 147 us  [attention_backwards(): pl.pallas_call(functools.partial(back_kernel, block), out_shape=[f32(cols...]
where the time goes in v11:
time: 513 us
  Pallas kernels  512 us (100%)
    pallas_call x1, Pallas kernels, attention_backwards(): pl.pallas_call(functools.partial(back_kernel, block), out_shape=[f32(cols...  147 us
    pallas_call x1, Pallas kernels, feed_both_ways(): pl.pallas_call(functools.partial(feed_kernel, block), out_shape=[f32(all_...  130 us
    pallas_call x1, Pallas kernels, gather_project(): pl.pallas_call(project_kernel, out_shape=[bf16(all_rows, width), bf16(all...  116 us
    pallas_call x1, Pallas kernels, product_scatter_both(): pl.pallas_call(scatter_both_kernel, out_shape=[jax.ShapeDtypeStruct((rows...  108 us

profile of v11, /device:TPU:0, one launch (start us, length us, event | category | flops | bytes accessed | tf_op | source)
XLA Modules:
  0.0 512.5 jit_solution(11672074526393767055)
XLA Ops:
  0.6 115.5 %shard_map.212 = (bf16[2048,2048]{1,0:T(8,128)(2,1)}, bf16[2048,2048]{1,0:T(8,128)(2,1)}, bf16[2048,128]{1,0:T(8,128)(2,1)}, bf16[2048,128]{1,0:T(8,128)(2,1)}, ...) custom-call(s32[1,4]{1,0:T(1,128)} %lengths_ref.1, ...), custom_call_target="tpu_custom_call" | custom-call | flops 2147483648 | bytes 33554432 | tf_op jit(solution)/shard_map/pallas_call | solution.py:870
  116.2 130.5 %shard_map.213 = (f32[2048,128]{1,0:T(8,128)}, f32[2048,2]{1,0:T(8,128)}, bf16[2048,128]{1,0:T(8,128)(2,1)}, f32[128,2048]{1,0:T(8,128)}, bf16[2048,2048]{1,0:T(...) custom-call(bf16[2048,128]{1,0:T(8,128)(2,1)} %get-tuple-element.56.q_ref, ...), custom_call_target="tpu_custom_call" | custom-call | flops 17179869184 | bytes 33554432 | tf_op jit(solution)/shard_map/pallas_call | solution.py:1458
  246.7 108.4 %shard_map.214 = (f32[128,2048]{1,0:T(8,128)}, bf16[128,2048]{1,0:T(8,128)(2,1)}, f32[128,2048]{1,0:T(8,128)}, bf16[1024,1024]{1,0:T(8,128)(2,1)}) custom-call(bf16[2048,1024]{1,0:T(8,128)(2,1)} %get-tuple-element.66.back_hbm, bf16[1024,2048]{1,0:T(8,128)(2,1)} %get-tuple-element.67.turned_hbm, bf16[2048,512]{1,0:T(8,128)(2,1)} %get-tuple-element.68.hidden_hbm, ...), custom_call_target="tpu_custom_call" | custom-call | flops 25769803776 | bytes 50331648 | tf_op jit(solution)/shard_map/pallas_call | solution.py:1218
  355.1 147.5 %shard_map.215 = (f32[64,2048]{1,0:T(8,128)}, bf16[64,2048]{1,0:T(8,128)(2,1)}, f32[256,2048]{1,0:T(8,128)}, bf16[256,2048]{1,0:T(8,128)(2,1)}, bf16[8,64,1024]{...) custom-call(bf16[128,2048]{1,0:T(8,128)(2,1)} %get-tuple-element.71.own_ref,, ...), custom_call_target="tpu_custom_call" | custom-call | flops 6442450944 | bytes 50331648 | tf_op jit(solution)/shard_map/pallas_call | solution.py:1778
  502.6 9.8 %shard_map.216 = (f32[64,8192]{1,0:T(8,128)}, f32[64,8192]{1,0:T(8,128)}, f32[64,2048]{1,0:T(8,128)}, f32[64,512]{1,0:T(8,128)}, f32[64,512]{1,0:T(8,128)}, /*in...) custom-call(s32[1]{0:T(128)} %bitcast.pair_ref, ...), custom_call_target="tpu_custom_call" | custom-call | flops 524288 | bytes 8388608 | tf_op jit(solution)/shard_map/pallas_call | solution.py:1977

commit v12 on v11

--- a/solution.py
+++ b/solution.py
@@ -326,30 +326,6 @@
                 (here.dp, peer),
             )
         ]
-
-    return Spread(here, same, copies)
-
-
-def feed_spread(here, same, weights, into, sems):
-    dp = lax.axis_size("dp")
-    columns = into.shape[2] // (dp * len(weights))
-
-    def copies(peer, sender, at, sem):
-        made = []
-        for kind, weight in enumerate(weights):
-            for half in range(dp):
-                part = kind * dp + half
-                begin = pl.multiple_of((half * here.count + peer) * columns, columns)
-                made.append(
-                    remote(
-                        weight.at[:, pl.ds(begin, columns)],
-                        into.at[at, :, pl.ds(part * columns, columns)],
-                        sems.at[0, sem, part],
-                        sems.at[1, at, part],
-                        (here.dp, peer),
-                    )
-                )
-        return made
 
     return Spread(here, same, copies)
 
@@ -635,7 +611,6 @@
     weight_ref,
     gate_out_ref,
     up_out_ref,
-    feed_ref,
     down_out_ref,
     output_out_ref,
     buf,
@@ -645,7 +620,6 @@
     store_sems,
     near_sems,
     far_sems,
-    feed_sems,
     swap_sems,
     local_sems,
     pair_sems,
@@ -719,21 +693,6 @@
             remote(src, dst.at[dp], swap_sems.at[0, number], swap_sems.at[1, number], here.partner())
         )
         swaps.append(pltpu.make_async_copy(src, dst.at[dp], local_sems.at[number]))
-    feed = feed_spread(here, True, (gate_out_ref, up_out_ref), feed_ref, feed_sems)
-    columns = feed_ref.shape[2] // 4
-    own_feed = []
-    for kind, weight in enumerate((gate_out_ref, up_out_ref)):
-        for half in range(2):
-            part = kind * 2 + half
-            begin = pl.multiple_of((half * here.count + here.mine) * columns, columns)
-            own_feed.append(
-                pltpu.make_async_copy(
-                    weight.at[:, pl.ds(begin, columns)],
-                    feed_ref.at[here.slot, :, pl.ds(part * columns, columns)],
-                    local_sems.at[2 + part],
-                )
-            )
-
     def pair_copy(source, sender):
         return remote(
             weight_ref.at[source, sender],
@@ -775,13 +734,9 @@
             gate_out_ref[:, some] = (gate_ref[:, some].astype(F32) * gain).astype(BF16)
             up_out_ref[:, some] = (up_ref[:, some].astype(F32) * gain).astype(BF16)
 
-        for one in own_feed:
-            one.start()
         own_tables()
 
     def between(step):
-        feed.start_some(step - (2 * here.length - 3), 3)
-
         @pl.when(step == 2)
         def _():
             near.finish()
@@ -839,7 +794,7 @@
                 ref[where, :] = (mine if core else rotated(mine, cosine, sine)).astype(BF16)
                 share_copy(ref, number, where).start()
 
-    gather_units(here, buf, send_sems, recv_sems, compute, between, here.length, started)
+    gather_units(here, buf, send_sems, recv_sems, compute, between, here.length, started, True)
 
     @pl.loop(0, here.count)
     def _(sender):
@@ -851,8 +806,7 @@
             one.wait()
         share_copy(k_ref, number, unit_rows(0, rows)).wait()
 
-    feed.finish()
-    for one in swaps + own_feed:
+    for one in swaps:
         one.wait()
 
 
@@ -881,21 +835,19 @@
             bf16(2, seq, slab, 2 * cols),
             bf16(slab, ff),
             bf16(slab, ff),
-            bf16(seq // 2, slab, 4 * down.shape[0]),
             bf16(2, *down.shape),
             bf16(2, *output.shape),
         ],
         in_specs=[pl.BlockSpec(memory_space=pltpu.SMEM)] + [VMEM] * 10 + [HBM] * 2,
-        out_specs=[HBM] * 2 + [VMEM] * 9 + [HBM] * 3,
+        out_specs=[HBM] * 2 + [VMEM] * 9 + [HBM] * 2,
         scratch_shapes=gather_scratch(seq, rows, width)
         + [
             pltpu.VMEM((seq, slab, 2 * cols), BF16),
             dma((seq // 2, 2, 2)),
             dma((2, seq // 2)),
             dma((2, seq // 2)),
-            dma((2, seq // 2, 4)),
             dma((2, 2)),
-            dma((6,)),
+            dma((2,)),
             dma((2, seq)),
             dma((2, seq // 2)),
         ],
@@ -1251,7 +1203,6 @@
     tokens_ref,
     gate_hbm,
     up_hbm,
-    near_hbm,
     grad_hbm,
     down_hbm,
     attended_ref,
@@ -1269,6 +1220,7 @@
         feed_ref,
         swap_sems,
         local_sems,
+        near_sems,
         far_sems,
         buf,
         send_sems,
@@ -1282,15 +1234,11 @@
         fetch_sems,
         out_sems,
     ) = scratch[SCATTER_SCRATCH:]
-    slots, slab = near_hbm.shape[:2]
+    slab = feed_ref.shape[2]
+    slots = here.count // 2
     rows, width = middle_ref.shape
     hidden = hidden_ref.shape[1]
     tile = 256
-
-    def fetch(slot):
-        return pltpu.make_async_copy(
-            near_hbm.at[slot], feed_ref.at[here.dp, here.peer(slot, True)], local_sems.at[slot]
-        )
 
     def swap(slot, same):
         place = feed_ref.at[here.dp, here.peer(slot, same)]
@@ -1305,31 +1253,44 @@
 
     columns = hidden // 2
 
-    def far_copies(peer, sender, at, sem):
-        made = []
-        for kind, weight in enumerate((gate_hbm, up_hbm)):
-            for half in range(2):
-                part = kind * 2 + half
-                begin = pl.multiple_of((half * here.count + peer) * columns, columns)
-                made.append(
-                    remote(
-                        weight.at[:, pl.ds(begin, columns)],
-                        feed_ref.at[here.dp, sender, :, pl.ds(part * columns, columns)],
-                        far_sems.at[0, sem, part],
-                        far_sems.at[1, at, part],
-                        (here.dp, peer),
-                    )
+    def columns_of(weight, half, index):
+        begin = pl.multiple_of((half * here.count + index) * columns, columns)
+        return weight.at[:, pl.ds(begin, columns)]
+
+    def place_of(sender, part):
+        return feed_ref.at[here.dp, sender, :, pl.ds(part * columns, columns)]
+
+    sources = [(weight, half) for weight in (gate_hbm, up_hbm) for half in range(2)]
+
+    def feed_spread(same, sems):
+        def copies(peer, sender, at, sem):
+            return [
+                remote(
+                    columns_of(weight, half, peer),
+                    place_of(sender, part),
+                    sems.at[0, sem, part],
+                    sems.at[1, at, part],
+                    (here.dp, peer),
                 )
-        return made
-
-    far = Spread(here, False, far_copies)
+                for part, (weight, half) in enumerate(sources)
+            ]
+
+        return Spread(here, same, copies)
+
+    near = feed_spread(True, near_sems)
+    own_feed = [
+        pltpu.make_async_copy(
+            columns_of(weight, half, here.mine), place_of(here.mine, part), local_sems.at[part]
+        )
+        for part, (weight, half) in enumerate(sources)
+    ]
+    far = feed_spread(False, far_sems)
 
     fetches = [
         pltpu.make_async_copy(down_hbm, down_ref, fetch_sems.at[0]),
         pltpu.make_async_copy(grad_hbm, grad_ref, fetch_sems.at[1]),
     ]
-    pl.loop(0, slots)(lambda slot: fetch(slot).start())
-    for one in fetches:
+    for one in own_feed + fetches:
         one.start()
     here.call_all()
 
@@ -1352,21 +1313,26 @@
         def _():
             here.await_all()
             far.start()
-
-            @pl.loop(0, slots)
-            def _(slot):
-                fetch(slot).wait()
-                swap(slot, True).start()
+            near.start()
 
     def between():
         far.finish()
         pl.loop(0, slots)(lambda slot: swap(slot, False).start())
+
+    def filler(step):
+        @pl.when(step == 2)
+        def _():
+            near.finish()
+            for one in own_feed:
+                one.wait()
+            pl.loop(0, slots)(lambda slot: swap(slot, True).start())
 
     scatter_rows_of_products(
         here,
         [(False, a_ref, b_ref, middle_ref)],
         *scratch[:SCATTER_SCRATCH],
         between=between,
+        filler=filler,
     )
     half = buf.shape[2]
     for part in range(2):
@@ -1445,7 +1411,7 @@
 
 
 def feed_both_ways(
-    queries, keys, values, opening, output, tokens, gate, up, near, grad_out, down, block, call_id
+    queries, keys, values, opening, output, tokens, gate, up, grad_out, down, block, call_id
 ):
     seq = lax.axis_size("seq")
     rows, width = tokens.shape
@@ -1467,13 +1433,14 @@
             bf16(all_rows, 2 * hidden),
             bf16(2 * hidden, width),
         ],
-        in_specs=[VMEM] * 6 + [HBM] * 5,
+        in_specs=[VMEM] * 6 + [HBM] * 4,
         out_specs=[VMEM] * 4 + [HBM] * 4,
         scratch_shapes=scatter_scratch(seq, rows, width)
         + [
-            pltpu.VMEM((2, seq, *near.shape[1:]), BF16),
+            pltpu.VMEM((2, seq, gate.shape[0], 2 * hidden), BF16),
             dma((2, 2, seq // 2)),
-            dma((seq // 2,)),
+            dma((4,)),
+            dma((2, seq // 2, 4)),
             dma((2, seq // 2, 4)),
         ]
         + gather_scratch(seq, rows // 2, width)
@@ -1489,7 +1456,7 @@
         ],
         compiler_params=params(call_id, 62),
         cost_estimate=cost(8 * all_rows * width * hidden, 8 * all_rows * width),
-    )(queries, keys, values, opening, output, tokens, gate, up, near, grad_out, down)
+    )(queries, keys, values, opening, output, tokens, gate, up, grad_out, down)
 
 
 def back_kernel(
@@ -2262,7 +2229,6 @@
         qkv_weight,
         gate_scaled,
         up_scaled,
-        feed_near,
         down_own,
         output_own,
     ) = gather_project(
@@ -2293,7 +2259,6 @@
             tokens,
             gate_scaled,
             up_scaled,
-            feed_near,
             grad_out,
             down_own,
             block,

time: 513 us -> 506 us (0.986)
  Pallas kernels: 512 us -> 504 us
    pallas_call x1, Pallas kernels: 116 us -> 107 us  [gather_project(): pl.pallas_call(project_kernel, out_shape=[bf16(all_rows, width), bf16(all...]
where the time goes in v12:
time: 506 us; the launch traced here: 505 us
  Pallas kernels  504 us (100%)
    pallas_call x1, Pallas kernels, attention_backwards(): pl.pallas_call(functools.partial(back_kernel, block), out_shape=[f32(cols...  149 us
    pallas_call x1, Pallas kernels, feed_both_ways(): pl.pallas_call(functools.partial(feed_kernel, block), out_shape=[f32(all_...  130 us
    pallas_call x1, Pallas kernels, product_scatter_both(): pl.pallas_call(scatter_both_kernel, out_shape=[jax.ShapeDtypeStruct((rows...  109 us
    pallas_call x1, Pallas kernels, gather_project(): pl.pallas_call(project_kernel, out_shape=[bf16(all_rows, width), bf16(all...  107 us

profile of v12, /device:TPU:0, one launch (start us, length us, event | category | flops | bytes accessed | tf_op | source)
XLA Modules:
  0.0 505.2 jit_solution(15798497425740941179)
XLA Ops:
  0.6 107.5 %shard_map.212 = (bf16[2048,2048]{1,0:T(8,128)(2,1)}, bf16[2048,2048]{1,0:T(8,128)(2,1)}, bf16[2048,128]{1,0:T(8,128)(2,1)}, bf16[2048,128]{1,0:T(8,128)(2,1)}, ...) custom-call(s32[1,4]{1,0:T(1,128)} %lengths_ref.1, ...), custom_call_target="tpu_custom_call" | custom-call | flops 2147483648 | bytes 33554432 | tf_op jit(solution)/shard_map/pallas_call | solution.py:824
  108.1 129.6 %shard_map.213 = (f32[2048,128]{1,0:T(8,128)}, f32[2048,2]{1,0:T(8,128)}, bf16[2048,128]{1,0:T(8,128)(2,1)}, f32[128,2048]{1,0:T(8,128)}, bf16[2048,2048]{1,0:T(...) custom-call(bf16[2048,128]{1,0:T(8,128)(2,1)} %get-tuple-element.55.q_ref, ...), custom_call_target="tpu_custom_call" | custom-call | flops 17179869184 | bytes 33554432 | tf_op jit(solution)/shard_map/pallas_call | solution.py:1424
  237.7 108.7 %shard_map.214 = (f32[128,2048]{1,0:T(8,128)}, bf16[128,2048]{1,0:T(8,128)(2,1)}, f32[128,2048]{1,0:T(8,128)}, bf16[1024,1024]{1,0:T(8,128)(2,1)}) custom-call(bf16[2048,1024]{1,0:T(8,128)(2,1)} %get-tuple-element.64.back_hbm, bf16[1024,2048]{1,0:T(8,128)(2,1)} %get-tuple-element.65.turned_hbm, bf16[2048,512]{1,0:T(8,128)(2,1)} %get-tuple-element.66.hidden_hbm, ...), custom_call_target="tpu_custom_call" | custom-call | flops 25769803776 | bytes 50331648 | tf_op jit(solution)/shard_map/pallas_call | solution.py:1170
  346.5 148.8 %shard_map.215 = (f32[64,2048]{1,0:T(8,128)}, bf16[64,2048]{1,0:T(8,128)(2,1)}, f32[256,2048]{1,0:T(8,128)}, bf16[256,2048]{1,0:T(8,128)(2,1)}, bf16[8,64,1024]{...) custom-call(bf16[128,2048]{1,0:T(8,128)(2,1)} %get-tuple-element.69.own_ref,, ...), custom_call_target="tpu_custom_call" | custom-call | flops 6442450944 | bytes 50331648 | tf_op jit(solution)/shard_map/pallas_call | solution.py:1745
  495.3 9.8 %shard_map.216 = (f32[64,8192]{1,0:T(8,128)}, f32[64,8192]{1,0:T(8,128)}, f32[64,2048]{1,0:T(8,128)}, f32[64,512]{1,0:T(8,128)}, f32[64,512]{1,0:T(8,128)}, /*in...) custom-call(s32[1]{0:T(128)} %bitcast.pair_ref, ...), custom_call_target="tpu_custom_call" | custom-call | flops 524288 | bytes 8388608 | tf_op jit(solution)/shard_map/pallas_call | solution.py:1944

commit v13 on v12

--- a/solution.py
+++ b/solution.py
@@ -1127,8 +1127,10 @@
         pl.when(number + 1 < 2 * chunks)(lambda: fetch(number + 1).start())
         return t_dot(normed[number % 2], back_ref[...])
 
-    def filler(step):
-        @pl.when(step < chunks)
+    def filler(place):
+        step = place - 2
+
+        @pl.when((step >= 0) & (step < chunks))
         def _():
             some = pl.ds(pl.multiple_of(step * chunk, chunk), chunk)
             away[some, :] = part(step).astype(BF16)
@@ -1238,7 +1240,7 @@
     slots = here.count // 2
     rows, width = middle_ref.shape
     hidden = hidden_ref.shape[1]
-    tile = 256
+    tile = 512
 
     def swap(slot, same):
         place = feed_ref.at[here.dp, here.peer(slot, same)]

time: 506 us -> 504 us (level)
  no operation moved by 1% of the time
where the time goes in v13:
time: 504 us
  Pallas kernels  503 us (100%)
    pallas_call x1, Pallas kernels, attention_backwards(): pl.pallas_call(functools.partial(back_kernel, block), out_shape=[f32(cols...  149 us
    pallas_call x1, Pallas kernels, feed_both_ways(): pl.pallas_call(functools.partial(feed_kernel, block), out_shape=[f32(all_...  129 us
    pallas_call x1, Pallas kernels, product_scatter_both(): pl.pallas_call(scatter_both_kernel, out_shape=[jax.ShapeDtypeStruct((rows...  108 us
    pallas_call x1, Pallas kernels, gather_project(): pl.pallas_call(project_kernel, out_shape=[bf16(all_rows, width), bf16(all...  107 us

profile of v13, /device:TPU:0, one launch (start us, length us, event | category | flops | bytes accessed | tf_op | source)
XLA Modules:
  0.0 503.7 jit_solution(15732170562014363417)
XLA Ops:
  0.6 107.5 %shard_map.212 = (bf16[2048,2048]{1,0:T(8,128)(2,1)}, bf16[2048,2048]{1,0:T(8,128)(2,1)}, bf16[2048,128]{1,0:T(8,128)(2,1)}, bf16[2048,128]{1,0:T(8,128)(2,1)}, ...) custom-call(s32[1,4]{1,0:T(1,128)} %lengths_ref.1, ...), custom_call_target="tpu_custom_call" | custom-call | flops 2147483648 | bytes 33554432 | tf_op jit(solution)/shard_map/pallas_call | solution.py:824
  108.1 128.9 %shard_map.213 = (f32[2048,128]{1,0:T(8,128)}, f32[2048,2]{1,0:T(8,128)}, bf16[2048,128]{1,0:T(8,128)(2,1)}, f32[128,2048]{1,0:T(8,128)}, bf16[2048,2048]{1,0:T(...) custom-call(bf16[2048,128]{1,0:T(8,128)(2,1)} %get-tuple-element.55.q_ref, ...), custom_call_target="tpu_custom_call" | custom-call | flops 17179869184 | bytes 33554432 | tf_op jit(solution)/shard_map/pallas_call | solution.py:1426
  237.0 107.9 %shard_map.214 = (f32[128,2048]{1,0:T(8,128)}, bf16[128,2048]{1,0:T(8,128)(2,1)}, f32[128,2048]{1,0:T(8,128)}, bf16[1024,1024]{1,0:T(8,128)(2,1)}) custom-call(bf16[2048,1024]{1,0:T(8,128)(2,1)} %get-tuple-element.64.back_hbm, bf16[1024,2048]{1,0:T(8,128)(2,1)} %get-tuple-element.65.turned_hbm, bf16[2048,512]{1,0:T(8,128)(2,1)} %get-tuple-element.66.hidden_hbm, ...), custom_call_target="tpu_custom_call" | custom-call | flops 25769803776 | bytes 50331648 | tf_op jit(solution)/shard_map/pallas_call | solution.py:1172
  345.0 148.7 %shard_map.215 = (f32[64,2048]{1,0:T(8,128)}, bf16[64,2048]{1,0:T(8,128)(2,1)}, f32[256,2048]{1,0:T(8,128)}, bf16[256,2048]{1,0:T(8,128)(2,1)}, bf16[8,64,1024]{...) custom-call(bf16[128,2048]{1,0:T(8,128)(2,1)} %get-tuple-element.69.own_ref,, ...), custom_call_target="tpu_custom_call" | custom-call | flops 6442450944 | bytes 50331648 | tf_op jit(solution)/shard_map/pallas_call | solution.py:1747
  493.7 9.8 %shard_map.216 = (f32[64,8192]{1,0:T(8,128)}, f32[64,8192]{1,0:T(8,128)}, f32[64,2048]{1,0:T(8,128)}, f32[64,512]{1,0:T(8,128)}, f32[64,512]{1,0:T(8,128)}, /*in...) custom-call(s32[1]{0:T(128)} %bitcast.pair_ref, ...), custom_call_target="tpu_custom_call" | custom-call | flops 524288 | bytes 8388608 | tf_op jit(solution)/shard_map/pallas_call | solution.py:1946
